TPU v7x, 32 devices: a whole 2x2x4 slice. The times are simulated.
32 devices in a mesh: facet: 4 (over y, x), bl: 4 (over z), chan: 2 (over core).
Axes of the slice: x: 2, y: 2, z: 4, core: 2. Of those that a mesh axis runs over, the one named last changes fastest.
Arguments:
- visibilities: bfloat16 [128, 8, 2, 128], P(('facet', 'bl'), 'chan'), may hold values from -6 to 6
- coords: bfloat16 [128, 2, 128], P(('facet', 'bl')), may hold values from 4 to 124
- plane_index: int32 [128], P(('facet', 'bl')), may hold values from 0 to 15, as said below
- block_group: int32 [128, 1], P(('facet', 'bl')), may hold values from 0 to 3, as said below
- offsets: int32 [4, 4, 2], replicated, may hold values from 0 to 7
- facet_centre: float32 [4, 2], replicated, may hold values from -8 to 8
- tables: bfloat16 [16, 2, 128, 2, 128], P(('facet', 'bl')), may hold values from -0.5 to 0.5
- antenna_gain: float32 [4, 2, 128], P('bl'), may hold values from 0.1 to 1.9
Outputs:
- subgrids: float32 [4, 4, 128, 2, 128], P('facet', 'bl', 'chan')
Inputs may be any that keep to these rules, and one draw needn't show every extreme that they name: `block_group`: among the 8 blocks of one device at most 4 name the same baseline group, and on every device some group is named by exactly 4 of them. `plane_index`: A block whose baseline group is g names a w-plane p with p modulo 4 equal to g or to (g + 3) modulo 4.
All inputs are finite; a program needn't handle non-finite values.
Results may differ from a plain program's by a relative error of at most 0.0054.
Values may be sent and summed in bfloat16 or wider, within the bound.
No kernel may reach another device: no remote copies, remote signals or barrier semaphores. Data moves between devices by JAX's collectives and lax.ppermute only.
A program may use at most 64 MiB of HBM per device.

v0:
```python
import math

import jax
import jax.numpy as jnp
from jax import lax
from jax.sharding import PartitionSpec as P

SU = 128
CH = 8


kernel_spread = 1.5


def channel_scale(count, first):
    index = (first + jnp.arange(count, dtype=jnp.int32)).astype(jnp.float32)
    return 1.0 + 0.01 * (index - 0.5 * (CH - 1))


def gather_whole(tables):
    whole_table = lax.all_gather(tables, ("facet", "bl"), axis=0, tiled=True)
    return whole_table.reshape(whole_table.shape[0], -1)


def block_grids(samples, place, planes, shifts, centre, flat_table, scale):
    count = samples.shape[0]
    chans = samples.shape[1]
    rows = samples.shape[3]
    planes_total = flat_table.shape[0]
    picks = (planes[:, None] == jnp.arange(planes_total, dtype=jnp.int32)[None, :]).astype(
        jnp.bfloat16
    )
    kernels = jnp.dot(picks, flat_table, preferred_element_type=jnp.float32).astype(jnp.bfloat16)
    kernels = kernels.reshape(count, 2, SU, 2 * SU)
    cells = jnp.arange(SU, dtype=jnp.int32).astype(jnp.float32)
    along_u = place[:, 0].astype(jnp.float32)
    along_v = place[:, 1].astype(jnp.float32)

    def profile(position, offset):
        spot = scale[None, :, None] * position[:, None, :] - offset[:, None, None]
        apart = spot[:, :, :, None] - cells
        return (
            jnp.exp(-apart * apart / (2.0 * kernel_spread * kernel_spread))
            .astype(jnp.bfloat16)
            .reshape(count, chans * rows, SU)
        )

    spread_u = jnp.einsum(
        "bsj,bjk->bsk",
        profile(along_u, shifts[:, 0]),
        kernels[:, 0],
        preferred_element_type=jnp.float32,
    )
    spread_v = jnp.einsum(
        "bsj,bjk->bsk",
        profile(along_v, shifts[:, 1]),
        kernels[:, 1],
        preferred_element_type=jnp.float32,
    ).astype(jnp.bfloat16)
    phase = (
        2.0
        * math.pi
        / SU
        * (scale[None, :, None] * (along_u * centre[0] + along_v * centre[1])[:, None, :])
    )
    phase = phase.reshape(count, chans * rows, 1)
    real_part = samples[:, :, 0].astype(jnp.float32).reshape(count, chans * rows, 1)
    imag_part = samples[:, :, 1].astype(jnp.float32).reshape(count, chans * rows, 1)
    cosine = jnp.cos(phase)
    sine = jnp.sin(phase)
    turned_real = real_part * cosine - imag_part * sine
    turned_imag = real_part * sine + imag_part * cosine
    weighted_real = spread_u[:, :, :SU] * turned_real - spread_u[:, :, SU:] * turned_imag
    weighted_imag = spread_u[:, :, :SU] * turned_imag + spread_u[:, :, SU:] * turned_real
    weighted = jnp.concatenate([weighted_real, weighted_imag], axis=2).astype(jnp.bfloat16)
    product = jnp.einsum("bsj,bsk->bjk", weighted, spread_v, preferred_element_type=jnp.float32)
    grid_real = product[:, :SU, :SU] - product[:, SU:, SU:]
    grid_imag = product[:, :SU, SU:] + product[:, SU:, :SU]
    return jnp.stack([grid_real, grid_imag], axis=2)


def fold_groups(total, arrays, grid_fn):
    count = arrays[0].shape[0]
    step_size = count
    while step_size > 16 and step_size % 2 == 0:
        step_size = step_size // 2
    parts = count // step_size
    shaped = tuple([item.reshape((parts, step_size) + item.shape[1:]) for item in arrays])

    def one_group(carry, group_items):
        return (carry + grid_fn(group_items), None)

    result, _ = lax.scan(one_group, total, shaped)
    return result


def body(
    visibilities, coords, plane_index, block_group, offsets, facet_centre, tables, antenna_gain
):
    facet_count = lax.axis_size("facet")
    group_count = lax.axis_size("bl")
    chan_count = lax.axis_size("chan")
    held = visibilities.shape[0]
    chans = visibilities.shape[1]
    facet_id = lax.axis_index("facet")
    group_id = lax.axis_index("bl")
    scale = channel_scale(chans, lax.axis_index("chan") * chans)
    offsets_here = lax.dynamic_index_in_dim(offsets, facet_id, 0, keepdims=False).astype(
        jnp.float32
    )
    centre = lax.dynamic_index_in_dim(facet_centre, facet_id, 0, keepdims=False)
    rows_out = SU // chan_count
    norm = SU / math.sqrt(visibilities.shape[3] * held * facet_count * CH)
    flat_table = gather_whole(tables)
    capacity = max(2, 2 * held // group_count)
    slots = group_count * capacity
    labels = block_group[:, 0]
    positions = jnp.arange(held, dtype=jnp.int32)
    earlier = positions[:, None] > positions[None, :]
    matching = labels[:, None] == labels[None, :]
    ranking = jnp.sum((earlier & matching).astype(jnp.int32), axis=1)
    target = labels * capacity + ranking
    hits = (target[None, :] == jnp.arange(slots, dtype=jnp.int32)[:, None]).astype(jnp.int32)
    source = jnp.sum(hits * positions[None, :], axis=1)
    filled = jnp.sum(hits, axis=1)
    samples_out = (
        jnp.take(visibilities, source, axis=0) * filled.astype(jnp.bfloat16)[:, None, None, None]
    )
    place_out = jnp.take(coords, source, axis=0)
    planes_out = jnp.where(filled > 0, jnp.take(plane_index, source), -1).astype(jnp.bfloat16)
    samples_in, place_in, planes_in = (
        lax.all_to_all(samples_out, "bl", split_axis=0, concat_axis=0, tiled=True),
        lax.all_to_all(place_out, "bl", split_axis=0, concat_axis=0, tiled=True),
        lax.all_to_all(planes_out, "bl", split_axis=0, concat_axis=0, tiled=True),
    )
    own_shift = lax.dynamic_index_in_dim(offsets_here, group_id, 0, keepdims=False)

    def slot_grid(items):
        piece_samples, piece_place, piece_planes = items
        count = piece_samples.shape[0]
        shifts = jnp.broadcast_to(own_shift[None, :], (count, 2))
        grids = block_grids(
            piece_samples,
            piece_place,
            piece_planes.astype(jnp.int32),
            shifts,
            centre,
            flat_table,
            scale,
        )
        return jnp.sum(grids, axis=0)

    empty = jnp.zeros((SU, 2, SU), jnp.float32)
    raw = fold_groups(
        empty,
        (
            lax.all_gather(samples_in, "facet", axis=0, tiled=True),
            lax.all_gather(place_in, "facet", axis=0, tiled=True),
            lax.all_gather(planes_in, "facet", axis=0, tiled=True),
        ),
        slot_grid,
    )
    rows_sum = lax.psum_scatter(raw, "chan", scatter_dimension=0, tiled=True)
    row_first = lax.axis_index("chan") * rows_out
    gain_u = lax.dynamic_slice_in_dim(antenna_gain[0, 0], row_first, rows_out)
    gain_v = antenna_gain[0, 1]
    gains = gain_u[:, None, None] * gain_v[None, None, :]
    result = rows_sum * gains * norm
    return result.reshape(1, 1, rows_out, 2, SU)


def solution(mesh):
    in_specs = (
        P(("facet", "bl"), "chan", None, None),
        P(("facet", "bl"), None, None),
        P(("facet", "bl")),
        P(("facet", "bl"), None),
        P(),
        P(),
        P(("facet", "bl"), None, None, None, None),
        P("bl", None, None),
    )
    out_specs = P("facet", "bl", "chan", None, None)
    return jax.shard_map(body, mesh=mesh, in_specs=in_specs, out_specs=out_specs, check_vma=False)
```

profile of v0, /device:TPU:0, one launch (start us, length us, event | category | flops | bytes accessed | tf_op | source)
XLA Modules:
  0.0 184.2 jit_solution(3265640481168825798)
XLA Ops:
  6.5 1.6 copy.44
  8.1 0.9 convert_reduce_fusion.1
  9.9 1.3 gather_fusion.1
  12.0 6.3 %all-to-all-start.1 = ((bf16[4,4,1]{1,2,0:T(2,128)(2,1)}), bf16[4,4,1]{1,2,0:T(2,128)(2,1)S(1)}, u32[]{:S(2)}, u32[]{:S(2)}) async-start(bf16[4,4,1]{1,2,0:T(2,128)(2,1)} %copy.43), calls=%async_computation.1 | async-start | bytes 4096 | tf_op jit(solution)/shard_map/all_to_all | solution.py:134
  19.0 1.3 gather_fusion
  20.2 0.8 fusion.54
  22.4 1.3 all-to-all-done.1
  23.7 3.8 %all-to-all-start = ((bf16[16,2,128]{2,1,0:T(2,128)(2,1)}), bf16[16,2,128]{2,1,0:T(2,128)(2,1)S(1)}, u32[]{:S(2)}, u32[]{:S(2)}) async-start(bf16[16,2,128]{2,1,0:T(2,128)(2,1)} %broadcast_select_fusion.1), calls=%async_computation | async-start | bytes 16384 | tf_op jit(solution)/shard_map/all_to_all | solution.py:133
  28.2 5.0 %all-to-all-done = bf16[16,2,128]{2,1,0:T(2,128)(2,1)S(1)} async-done(((bf16[16,2,128]{2,1,0:T(2,128)(2,1)}), bf16[16,2,128]{2,1,0:T(2,128)(2,1)S(1)}, u32[]{:S(2)}, u32[]{:S(2)}) %all-to-all-start) | async-done | bytes 8224 | tf_op jit(solution)/shard_map/all_to_all | solution.py:133
  33.2 3.3 %all-to-all-start.2 = ((bf16[16,4,2,128]{3,2,1,0:T(2,128)(2,1)}), bf16[16,4,2,128]{3,2,1,0:T(2,128)(2,1)S(1)}, u32[]{:S(2)}, u32[]{:S(2)}) async-start(bf16[16,4,2,128]{3,2,1,0:T(2,128)(2,1)} %fusion.48), calls=%async_computation.2 | async-start | bytes 65536 | tf_op jit(solution)/shard_map/all_to_all | solution.py:132
  36.6 0.9 dynamic-slice_reduce_fusion
  37.6 1.3 dynamic-slice.2
  39.6 1.3 dynamic-slice.3
  41.9 9.8 %all-reduce = bf16[64]{0:T(256)(128)(2,1)S(1)} all-reduce(bf16[64]{0:T(256)(128)(2,1)S(1)} %dynamic-update-slice), channel_id=1, replica_groups=mesh['facet'=4,'bl'=4,'chan'=2] {'facet'}, use_global_device_ids=true, to_apply=%add | all-reduce | flops 64 | bytes 256
  51.8 7.3 %all_gather.12 = bf16[64,2,128]{2,1,0:T(2,128)(2,1)S(1)} all-gather(bf16[16,2,128]{2,1,0:T(2,128)(2,1)S(1)} %all-to-all-done), channel_id=1, replica_groups=mesh['facet'=4,'bl'=4,'chan'=2] {'facet'}, dimensions={0}, use_global_device_ids=true | all-gather | bytes 40960 | tf_op jit(solution)/shard_map/all_gather | solution.py:158
  59.1 8.7 %all_gather.15 = bf16[64,4,2,128]{3,1,2,0:T(4,128)(2,1)S(1)} all-gather(bf16[16,4,2,128]{3,1,2,0:T(4,128)(2,1)S(1)} %copy.46), channel_id=1, replica_groups=mesh['facet'=4,'bl'=4,'chan'=2] {'facet'}, dimensions={0}, use_global_device_ids=true | all-gather | bytes 163840 | tf_op jit(solution)/shard_map/all_gather | solution.py:157
  67.8 6.6 %all-gather.2.cloned.1.call-done = bf16[16,2,128,2,128]{4,2,3,1,0:T(8,128)(2,1)} async-done(((bf16[1,2,128,2,128]{4,2,3,1,0:T(8,128)(2,1)}), bf16[16,2,128,2,128]{4,2,3,1,0:T(8,128)(2,1)}) %all-gather.2.cloned.1.call-update) | async-done | bytes 2097168 | tf_op jit(solution)/shard_map/all_gather | solution.py:21
  74.4 5.1 %copy.45 = bf16[16,2,128,2,128]{4,3,2,1,0:T(2,128)(2,1)} copy(bf16[16,2,128,2,128]{4,2,3,1,0:T(8,128)(2,1)} %all-gather.2.cloned.1.call-done) | data formatting | bytes 4194304 | tf_op jit(solution)/shard_map/all_gather | solution.py:21
  79.5 2.9 %reshape.289 = bf16[16,65536]{1,0:T(8,128)(2,1)S(1)} reshape(bf16[16,2,128,2,128]{4,3,2,1,0:T(2,128)(2,1)} %copy.45) | data formatting | bytes 4194304 | tf_op jit(solution)/shard_map/reshape | solution.py:22
  82.4 76.0 %while.11 = (s32[]{:T(128)}, f32[128,2,128]{2,0,1:T(8,128)S(1)}, bf16[4,16,2,128]{3,2,1,0:T(2,128)(2,1)S(1)}, f32[2]{0:T(128)S(1)}, bf16[4,16]{1,0:T(4,128)(2,1)...) while((s32[]{:T(128)}, f32[128,2,128]{2,0,1:T(8,128)S(1)}, ...), condition=%wide.region_5.6_spmd.clone, body=%wide.region_3.5_spmd.clone.sunk | while | flops 2213181952 | bytes 66328492 | solution.py:93
  83.1 1.2 fusion.74
  84.5 1.5 fusion.75
  86.0 0.8 convolution_convert_fusion.2
  87.3 2.1 %fusion.77 = f32[16,512,256]{1,2,0:T(8,128)S(1)} fusion(f32[128]{0:T(128)S(1)} %iota_convert_fusion.2, f32[16,512]{1,0:T(8,128)S(1)} %get-tuple-element.250, bf16[16,2,128,256]{3,2,1,0:T(8,128)(2,1)S(1)} %bitcast.152), kind=kOutput, calls=%fused_computation.21.clone.1 | convolution fusion | flops 542113792 | bytes 9470464 | tf_op jit(solution)/shard_map/while/body/eval_jaxpr/bsj,bjk->bsk/dot_general | solution.py:48
  89.3 3.6 %subtract_convert_fusion.2 = (bf16[16,512,128]{1,2,0:T(8,128)(2,1)}, bf16[16,512,128]{1,2,0:T(8,128)(2,1)}) fusion(f32[16,512,256]{1,2,0:T(8,128)S(1)} %fusion.77, f32[16,512]{1,0:T(8,128)S(1)} %get-tuple-element.251, f32[16,512]{1,0:T(8,128)S(1)} %get-tuple-element.252), kind=kLoop, calls=%fused_computation.19.clone.1 | loop fusion | flops 8388608 | bytes 12648448 | tf_op jit(solution)/shard_map/convert.3
  93.0 5.5 %fusion.78 = f32[16,256,256]{2,1,0:T(8,128)} fusion(bf16[16,512,128]{1,2,0:T(8,128)(2,1)} %get-tuple-element.253, bf16[16,512,128]{1,2,0:T(8,128)(2,1)} %get-tuple-element.254, f32[16,512]{1,0:T(8,128)S(1)} %get-tuple-element.255, f32[128]{0:T(128)S(1)} %iota_convert_fusion.2, bf16[16,2,128,256]{3,2,1,0:T(8,128)(2,1)S(1)} %bitcast.153), kind=kOutput, calls=%fused_computation.13.clone.1 | convolution fusion | flops 1626341376 | bytes 9470464 | tf_op jit(solution)/shard_map/while/body/eval_jaxpr/bsj,bsk->bjk/dot_general | solution.py:76
  98.5 2.7 %fusion.79 = (f32[16,128,1,128]{3,1,0,2:T(8,128)S(1)}, f32[16,128,1,128]{3,1,0,2:T(8,128)S(1)}) fusion(f32[16,256,256]{2,1,0:T(8,128)} %fusion.78), kind=kLoop, calls=%fused_computation.32.clone.1 | loop fusion | flops 524288 | bytes 6291456 | tf_op jit(solution)/shard_map/while/body/eval_jaxpr/stack | solution.py:79
  102.1 1.2 fusion.74
  103.5 1.5 fusion.75
  106.3 2.1 %fusion.77 = f32[16,512,256]{1,2,0:T(8,128)S(1)} fusion(f32[128]{0:T(128)S(1)} %iota_convert_fusion.2, f32[16,512]{1,0:T(8,128)S(1)} %get-tuple-element.250, bf16[16,2,128,256]{3,2,1,0:T(8,128)(2,1)S(1)} %bitcast.152), kind=kOutput, calls=%fused_computation.21.clone.1 | convolution fusion | flops 542113792 | bytes 9470464 | tf_op jit(solution)/shard_map/while/body/eval_jaxpr/bsj,bjk->bsk/dot_general | solution.py:48
  108.3 3.6 %subtract_convert_fusion.2 = (bf16[16,512,128]{1,2,0:T(8,128)(2,1)}, bf16[16,512,128]{1,2,0:T(8,128)(2,1)}) fusion(f32[16,512,256]{1,2,0:T(8,128)S(1)} %fusion.77, f32[16,512]{1,0:T(8,128)S(1)} %get-tuple-element.251, f32[16,512]{1,0:T(8,128)S(1)} %get-tuple-element.252), kind=kLoop, calls=%fused_computation.19.clone.1 | loop fusion | flops 8388608 | bytes 12648448 | tf_op jit(solution)/shard_map/convert.3
  112.0 5.5 %fusion.78 = f32[16,256,256]{2,1,0:T(8,128)} fusion(bf16[16,512,128]{1,2,0:T(8,128)(2,1)} %get-tuple-element.253, bf16[16,512,128]{1,2,0:T(8,128)(2,1)} %get-tuple-element.254, f32[16,512]{1,0:T(8,128)S(1)} %get-tuple-element.255, f32[128]{0:T(128)S(1)} %iota_convert_fusion.2, bf16[16,2,128,256]{3,2,1,0:T(8,128)(2,1)S(1)} %bitcast.153), kind=kOutput, calls=%fused_computation.13.clone.1 | convolution fusion | flops 1626341376 | bytes 9470464 | tf_op jit(solution)/shard_map/while/body/eval_jaxpr/bsj,bsk->bjk/dot_general | solution.py:76
  117.5 2.7 %fusion.79 = (f32[16,128,1,128]{3,1,0,2:T(8,128)S(1)}, f32[16,128,1,128]{3,1,0,2:T(8,128)S(1)}) fusion(f32[16,256,256]{2,1,0:T(8,128)} %fusion.78), kind=kLoop, calls=%fused_computation.32.clone.1 | loop fusion | flops 524288 | bytes 6291456 | tf_op jit(solution)/shard_map/while/body/eval_jaxpr/stack | solution.py:79
  121.1 1.2 fusion.74
  122.5 1.5 fusion.75
  125.3 2.1 %fusion.77 = f32[16,512,256]{1,2,0:T(8,128)S(1)} fusion(f32[128]{0:T(128)S(1)} %iota_convert_fusion.2, f32[16,512]{1,0:T(8,128)S(1)} %get-tuple-element.250, bf16[16,2,128,256]{3,2,1,0:T(8,128)(2,1)S(1)} %bitcast.152), kind=kOutput, calls=%fused_computation.21.clone.1 | convolution fusion | flops 542113792 | bytes 9470464 | tf_op jit(solution)/shard_map/while/body/eval_jaxpr/bsj,bjk->bsk/dot_general | solution.py:48
  127.3 3.6 %subtract_convert_fusion.2 = (bf16[16,512,128]{1,2,0:T(8,128)(2,1)}, bf16[16,512,128]{1,2,0:T(8,128)(2,1)}) fusion(f32[16,512,256]{1,2,0:T(8,128)S(1)} %fusion.77, f32[16,512]{1,0:T(8,128)S(1)} %get-tuple-element.251, f32[16,512]{1,0:T(8,128)S(1)} %get-tuple-element.252), kind=kLoop, calls=%fused_computation.19.clone.1 | loop fusion | flops 8388608 | bytes 12648448 | tf_op jit(solution)/shard_map/convert.3
  131.0 5.5 %fusion.78 = f32[16,256,256]{2,1,0:T(8,128)} fusion(bf16[16,512,128]{1,2,0:T(8,128)(2,1)} %get-tuple-element.253, bf16[16,512,128]{1,2,0:T(8,128)(2,1)} %get-tuple-element.254, f32[16,512]{1,0:T(8,128)S(1)} %get-tuple-element.255, f32[128]{0:T(128)S(1)} %iota_convert_fusion.2, bf16[16,2,128,256]{3,2,1,0:T(8,128)(2,1)S(1)} %bitcast.153), kind=kOutput, calls=%fused_computation.13.clone.1 | convolution fusion | flops 1626341376 | bytes 9470464 | tf_op jit(solution)/shard_map/while/body/eval_jaxpr/bsj,bsk->bjk/dot_general | solution.py:76
  136.5 2.7 %fusion.79 = (f32[16,128,1,128]{3,1,0,2:T(8,128)S(1)}, f32[16,128,1,128]{3,1,0,2:T(8,128)S(1)}) fusion(f32[16,256,256]{2,1,0:T(8,128)} %fusion.78), kind=kLoop, calls=%fused_computation.32.clone.1 | loop fusion | flops 524288 | bytes 6291456 | tf_op jit(solution)/shard_map/while/body/eval_jaxpr/stack | solution.py:79
  140.1 1.2 fusion.74
  141.5 1.5 fusion.75
  144.3 2.1 %fusion.77 = f32[16,512,256]{1,2,0:T(8,128)S(1)} fusion(f32[128]{0:T(128)S(1)} %iota_convert_fusion.2, f32[16,512]{1,0:T(8,128)S(1)} %get-tuple-element.250, bf16[16,2,128,256]{3,2,1,0:T(8,128)(2,1)S(1)} %bitcast.152), kind=kOutput, calls=%fused_computation.21.clone.1 | convolution fusion | flops 542113792 | bytes 9470464 | tf_op jit(solution)/shard_map/while/body/eval_jaxpr/bsj,bjk->bsk/dot_general | solution.py:48
  146.3 3.6 %subtract_convert_fusion.2 = (bf16[16,512,128]{1,2,0:T(8,128)(2,1)}, bf16[16,512,128]{1,2,0:T(8,128)(2,1)}) fusion(f32[16,512,256]{1,2,0:T(8,128)S(1)} %fusion.77, f32[16,512]{1,0:T(8,128)S(1)} %get-tuple-element.251, f32[16,512]{1,0:T(8,128)S(1)} %get-tuple-element.252), kind=kLoop, calls=%fused_computation.19.clone.1 | loop fusion | flops 8388608 | bytes 12648448 | tf_op jit(solution)/shard_map/convert.3
  150.0 5.5 %fusion.78 = f32[16,256,256]{2,1,0:T(8,128)} fusion(bf16[16,512,128]{1,2,0:T(8,128)(2,1)} %get-tuple-element.253, bf16[16,512,128]{1,2,0:T(8,128)(2,1)} %get-tuple-element.254, f32[16,512]{1,0:T(8,128)S(1)} %get-tuple-element.255, f32[128]{0:T(128)S(1)} %iota_convert_fusion.2, bf16[16,2,128,256]{3,2,1,0:T(8,128)(2,1)S(1)} %bitcast.153), kind=kOutput, calls=%fused_computation.13.clone.1 | convolution fusion | flops 1626341376 | bytes 9470464 | tf_op jit(solution)/shard_map/while/body/eval_jaxpr/bsj,bsk->bjk/dot_general | solution.py:76
  155.5 2.7 %fusion.79 = (f32[16,128,1,128]{3,1,0,2:T(8,128)S(1)}, f32[16,128,1,128]{3,1,0,2:T(8,128)S(1)}) fusion(f32[16,256,256]{2,1,0:T(8,128)} %fusion.78), kind=kLoop, calls=%fused_computation.32.clone.1 | loop fusion | flops 524288 | bytes 6291456 | tf_op jit(solution)/shard_map/while/body/eval_jaxpr/stack | solution.py:79
  158.4 0.8 copy.50
  159.2 16.6 %all-reduce.4.cloned.1.call-done = f32[128,2,128]{2,1,0:T(2,128)} async-done(((f32[128,2,128]{2,1,0:T(2,128)}), f32[128,2,128]{2,1,0:T(2,128)}) %all-reduce.4.cloned.1.call-update) | async-done | bytes 131088
  175.9 1.5 fusion.47
  (116 shorter events, 13.6 us)
Async XLA Ops:
  6.5 11.8 %copy-start = (bf16[8,4,2,128]{3,2,1,0:T(2,128)(2,1)S(1)}, bf16[8,4,2,128]{3,2,1,0:T(2,128)(2,1)}, u32[]{:S(2)}) copy-start(bf16[8,4,2,128]{3,2,1,0:T(2,128)(2,1)} %param.10) | copy-start | bytes 49156
  6.5 67.9 %all-gather.2.cloned.1.call-start = ((), (), s32[]{:S(2)}) async-start(), calls=%async_computation.3 | async-start | bytes 2228224 | tf_op jit(solution)/shard_map/all_gather | solution.py:21
  12.0 11.7 %all-to-all-start.1 = ((bf16[4,4,1]{1,2,0:T(2,128)(2,1)}), bf16[4,4,1]{1,2,0:T(2,128)(2,1)S(1)}, u32[]{:S(2)}, u32[]{:S(2)}) async-start(bf16[4,4,1]{1,2,0:T(2,128)(2,1)} %copy.43), calls=%async_computation.1 | async-start | bytes 4096 | tf_op jit(solution)/shard_map/all_to_all | solution.py:134
  23.7 9.4 %all-to-all-start = ((bf16[16,2,128]{2,1,0:T(2,128)(2,1)}), bf16[16,2,128]{2,1,0:T(2,128)(2,1)S(1)}, u32[]{:S(2)}, u32[]{:S(2)}) async-start(bf16[16,2,128]{2,1,0:T(2,128)(2,1)} %broadcast_select_fusion.1), calls=%async_computation | async-start | bytes 16384 | tf_op jit(solution)/shard_map/all_to_all | solution.py:133
  33.2 25.9 %all-to-all-start.2 = ((bf16[16,4,2,128]{3,2,1,0:T(2,128)(2,1)}), bf16[16,4,2,128]{3,2,1,0:T(2,128)(2,1)S(1)}, u32[]{:S(2)}, u32[]{:S(2)}) async-start(bf16[16,4,2,128]{3,2,1,0:T(2,128)(2,1)} %fusion.48), calls=%async_computation.2 | async-start | bytes 65536 | tf_op jit(solution)/shard_map/all_to_all | solution.py:132
  36.4 139.5 %all-reduce.4.cloned.1.call-start = ((), (), s32[]{:S(2)}) async-start(), calls=%async_computation.4 | async-start | bytes 262144
  82.4 4.4 %copy-start.1 = (bf16[16,65536]{1,0:T(8,128)(2,1)}, bf16[16,65536]{1,0:T(8,128)(2,1)S(1)}, u32[]{:S(2)}) copy-start(bf16[16,65536]{1,0:T(8,128)(2,1)S(1)} %get-tuple-element.285) | copy-start | bytes 6291460 | tf_op jit(solution)/shard_map/while
  98.5 2.9 %copy-start.2 = (bf16[16,65536]{1,0:T(8,128)(2,1)S(1)}, bf16[16,65536]{1,0:T(8,128)(2,1)}, u32[]{:S(2)}) copy-start(bf16[16,65536]{1,0:T(8,128)(2,1)} %copy-done.1) | copy-start | bytes 6291460 | tf_op jit(solution)/shard_map/while
  101.4 4.4 %copy-start.1 = (bf16[16,65536]{1,0:T(8,128)(2,1)}, bf16[16,65536]{1,0:T(8,128)(2,1)S(1)}, u32[]{:S(2)}) copy-start(bf16[16,65536]{1,0:T(8,128)(2,1)S(1)} %get-tuple-element.285) | copy-start | bytes 6291460 | tf_op jit(solution)/shard_map/while
  117.5 2.9 %copy-start.2 = (bf16[16,65536]{1,0:T(8,128)(2,1)S(1)}, bf16[16,65536]{1,0:T(8,128)(2,1)}, u32[]{:S(2)}) copy-start(bf16[16,65536]{1,0:T(8,128)(2,1)} %copy-done.1) | copy-start | bytes 6291460 | tf_op jit(solution)/shard_map/while
  120.4 4.4 %copy-start.1 = (bf16[16,65536]{1,0:T(8,128)(2,1)}, bf16[16,65536]{1,0:T(8,128)(2,1)S(1)}, u32[]{:S(2)}) copy-start(bf16[16,65536]{1,0:T(8,128)(2,1)S(1)} %get-tuple-element.285) | copy-start | bytes 6291460 | tf_op jit(solution)/shard_map/while
  136.5 2.9 %copy-start.2 = (bf16[16,65536]{1,0:T(8,128)(2,1)S(1)}, bf16[16,65536]{1,0:T(8,128)(2,1)}, u32[]{:S(2)}) copy-start(bf16[16,65536]{1,0:T(8,128)(2,1)} %copy-done.1) | copy-start | bytes 6291460 | tf_op jit(solution)/shard_map/while
  139.4 4.4 %copy-start.1 = (bf16[16,65536]{1,0:T(8,128)(2,1)}, bf16[16,65536]{1,0:T(8,128)(2,1)S(1)}, u32[]{:S(2)}) copy-start(bf16[16,65536]{1,0:T(8,128)(2,1)S(1)} %get-tuple-element.285) | copy-start | bytes 6291460 | tf_op jit(solution)/shard_map/while
  155.5 2.9 %copy-start.2 = (bf16[16,65536]{1,0:T(8,128)(2,1)S(1)}, bf16[16,65536]{1,0:T(8,128)(2,1)}, u32[]{:S(2)}) copy-start(bf16[16,65536]{1,0:T(8,128)(2,1)} %copy-done.1) | copy-start | bytes 6291460 | tf_op jit(solution)/shard_map/while
Sparse Core Ops, SparseCore 0:
  10.2 64.1 all-gather.1
  159.3 16.5 all-reduce.3
where the time goes:
time: 185 us; the launch traced here: 184 us
  other arithmetic  42 us (23%)
  matrix products  33.4 us (18%)
  waiting for transfers between devices  29.5 us (16%)
  blocking collectives  25.8 us (14%)
  local copies, waits for them, and re-layouts  24.7 us (13%)
  between operations  14.8 us (8%)
  starting transfers between devices  13.4 us (7%)
    dot_general x4, matrix products, block_grids(): jnp.einsum('bsj,bsk->bjk', weighted, spread_v, preferred_element_type=jnp...  22.1 us
    unnamed x3, waiting for transfers between devices  16.7 us
    another operation x4, other arithmetic  14.5 us
    another operation x4, other arithmetic, block_grids(): return jnp.stack([grid_real, grid_imag], axis=2)  10.7 us
    unnamed x1, blocking collectives  9.82 us
    all_gather x1, blocking collectives, body(): lax.all_gather(samples_in, 'facet', axis=0, tiled=True)  8.74 us
    dot_general x4, matrix products, block_grids(): jnp.einsum('bsj,bjk->bsk', profile(along_u, shifts[:, 0]), kernels[:, 0],...  8.27 us
    all_gather x1, blocking collectives, body(): lax.all_gather(place_in, 'facet', axis=0, tiled=True)  7.29 us
  transfers between devices with their start and end apart: 5, of which 4 were waited for; matrix products, arithmetic and copies ran while one was open for 7% of the time, Pallas kernels for 0%

commit v1 on v0

v1 whole, which is shorter than its diff:
```python
import functools
import math

import jax
import jax.numpy as jnp
from jax import lax
from jax.experimental import pallas as pl
from jax.experimental.pallas import tpu as pltpu
from jax.sharding import PartitionSpec as P

SU = 128
CH = 8
KERNEL_SPREAD = 1.5
ALPHA = math.sqrt(math.log2(math.e) / (2.0 * KERNEL_SPREAD * KERNEL_SPREAD))
UNROLL = 2
NT = (((1,), (1,)), ((), ()))


def cos_sin(turns):
    quarter = jnp.floor(4.0 * turns + 0.5)
    angle = (2.0 * math.pi) * (turns - 0.25 * quarter)
    sq = angle * angle
    sine = angle * (
        1.0 + sq * (-1.0 / 6 + sq * (1.0 / 120 + sq * (-1.0 / 5040 + sq * (1.0 / 362880))))
    )
    cosine = 1.0 + sq * (
        -0.5 + sq * (1.0 / 24 + sq * (-1.0 / 720 + sq * (1.0 / 40320 + sq * (-1.0 / 3628800))))
    )
    turn = quarter.astype(jnp.int32) & 3
    odd = (turn & 1) == 1
    cos_out = jnp.where(odd, sine, cosine)
    sin_out = jnp.where(odd, cosine, sine)
    cos_out = jnp.where((turn == 1) | (turn == 2), -cos_out, cos_out)
    sin_out = jnp.where(turn >= 2, -sin_out, sin_out)
    return cos_out, sin_out


def split_bf16(x):
    high = x.astype(jnp.bfloat16)
    low = (x - high.astype(jnp.float32)).astype(jnp.bfloat16)
    return high, low


def grid_kernel(sizes, norm, packed_ref, offsets_ref, centre_ref, gain_ref, *refs):
    facets, groups, held, chans, rows = sizes
    slots = 2 * facets
    table_refs = refs[:slots]
    mine_ref, other_ref = refs[slots : slots + 2]
    flat, meta_v, meta_s, order, grids, stacked, table_f, total, sem = refs[slots + 2 :]
    devices = facets * groups
    facet = lax.axis_index("facet")
    group = lax.axis_index("bl")
    chan = lax.axis_index("chan")
    place_row = held * chans * 2
    meta_row = place_row + 2 * held

    def widen(d, carry):
        at = pl.multiple_of(d * rows, rows)
        flat[pl.ds(at, rows), :] = packed_ref[pl.ds(at, rows), :].astype(jnp.float32)
        return carry

    lax.fori_loop(0, devices, widen, 0)
    meta_v[...] = flat[pl.ds(meta_row, devices, stride=rows), :].astype(jnp.int32)
    copy = pltpu.make_async_copy(meta_v, meta_s, sem)
    copy.start()
    grids[...] = jnp.zeros_like(grids)
    copy.wait()

    def pick(d, count):
        for i in range(held):
            plane = meta_s[d, i]
            of_group = meta_s[d, held + i]
            set_id = jnp.where(lax.rem(plane, groups) == group, 0, 1)
            shift = lax.rem(facet - lax.div(plane, groups) + facets, facets)
            order[count] = (d * held + i) * slots + set_id * facets + shift
            count = count + jnp.where(of_group == group, 1, 0)
        return count

    count = lax.fori_loop(0, devices, pick, 0)
    for i in range(UNROLL):
        order[count + i] = 0

    offset_u = offsets_ref[facet, group, 0].astype(jnp.float32)
    offset_v = offsets_ref[facet, group, 1].astype(jnp.float32)
    along_l = centre_ref[facet, 0]
    along_m = centre_ref[facet, 1]
    channel = (chan * chans + lax.broadcasted_iota(jnp.int32, (chans, SU), 0)).astype(jnp.float32)
    scale = 1.0 + 0.01 * (channel - 0.5 * (CH - 1))
    cells = ALPHA * lax.broadcasted_iota(jnp.int32, (SU, SU), 0).astype(jnp.float32)

    def profile(spot):
        apart = spot - cells
        return jnp.exp2(-(apart * apart)).astype(jnp.bfloat16)

    def tiled(row):
        return jnp.broadcast_to(row, (16, SU)).astype(jnp.bfloat16)[None]

    def one_block(at):
        code = order[at]
        block = lax.div(code, slots)
        slot = lax.rem(code, slots)
        d = lax.div(block, held)
        i = lax.rem(block, held)
        keep = jnp.where(at < count, 1.0, 0.0)
        base = pl.multiple_of(d * rows + i * 2 * chans, 2 * chans)
        real = flat[pl.ds(base, chans, stride=2), :] * keep
        imag = flat[pl.ds(base + 1, chans, stride=2), :] * keep
        at_place = d * rows + place_row + 2 * i
        along_u = flat[pl.ds(at_place, 1), :]
        along_v = flat[pl.ds(at_place + 1, 1), :]
        spot_u = ALPHA * (scale * along_u - offset_u)
        spot_v = ALPHA * (scale * along_v - offset_v)
        turns = (1.0 / SU) * (scale * (along_u * along_l + along_v * along_m))
        cosine, sine = cos_sin(turns)
        turned_real = real * cosine - imag * sine
        turned_imag = real * sine + imag * cosine
        lefts_real, lefts_imag, rights = [], [], []
        for c in range(chans):
            left = profile(spot_u[c : c + 1]).reshape(SU // 16, 16, SU)
            lefts_real.append((left * tiled(turned_real[c : c + 1])).reshape(SU, SU))
            lefts_imag.append((left * tiled(turned_imag[c : c + 1])).reshape(SU, SU))
            rights.append(profile(spot_v[c : c + 1]))
        left = jnp.concatenate(
            [jnp.concatenate(lefts_real, axis=1), jnp.concatenate(lefts_imag, axis=1)], axis=0
        )
        right = jnp.concatenate(rights, axis=1)
        grids[slot] += lax.dot_general(left, right, NT, preferred_element_type=jnp.float32)

    def step(k, carry):
        for i in range(UNROLL):
            one_block(k * UNROLL + i)
        return carry

    lax.fori_loop(0, lax.div(count + UNROLL - 1, UNROLL), step, 0)

    result = jnp.zeros((SU, 2 * SU), jnp.float32)
    for s in range(slots):
        table_f[...] = table_refs[s][0].astype(jnp.float32)
        u_real = table_f[pl.ds(0, SU, stride=2), :]
        u_imag = table_f[pl.ds(1, SU, stride=2), :]
        u_side = jnp.concatenate([u_real.T, u_imag.T], axis=1).astype(jnp.bfloat16)
        grid_real = grids[s, :SU, :]
        grid_imag = grids[s, SU:, :]
        inner = jnp.concatenate(
            [
                jnp.concatenate([grid_real, grid_imag], axis=1),
                jnp.concatenate([-grid_imag, grid_real], axis=1),
            ],
            axis=0,
        )
        high, low = split_bf16(inner)
        half = jnp.dot(u_side, high, preferred_element_type=jnp.float32) + jnp.dot(
            u_side, low, preferred_element_type=jnp.float32
        )
        table_f[...] = table_refs[s][1].astype(jnp.float32)
        v_real = table_f[pl.ds(0, SU, stride=2), :]
        v_imag = table_f[pl.ds(1, SU, stride=2), :]
        v_side = jnp.concatenate(
            [
                jnp.concatenate([v_real, v_imag], axis=1),
                jnp.concatenate([-v_imag, v_real], axis=1),
            ],
            axis=0,
        ).astype(jnp.bfloat16)
        high, low = split_bf16(half)
        result = (
            result
            + jnp.dot(high, v_side, preferred_element_type=jnp.float32)
            + jnp.dot(low, v_side, preferred_element_type=jnp.float32)
        )
    gain_u = jnp.broadcast_to(gain_ref[0, 0:1, :], (SU, SU)).T
    gains = gain_u * gain_ref[0, 1:2, :] * norm
    total[...] = result * jnp.concatenate([gains, gains], axis=1)
    half_rows = mine_ref.shape[0]
    mine_ref[...] = total[pl.ds(pl.multiple_of(chan * half_rows, half_rows), half_rows), :]
    other_ref[...] = total[pl.ds(pl.multiple_of((1 - chan) * half_rows, half_rows), half_rows), :]


def body(
    visibilities, coords, plane_index, block_group, offsets, facet_centre, tables, antenna_gain
):
    facets = lax.axis_size("facet")
    groups = lax.axis_size("bl")
    chan_count = lax.axis_size("chan")
    held, chans = visibilities.shape[:2]
    devices = facets * groups
    norm = SU / math.sqrt(visibilities.shape[3] * held * facets * CH)

    own_table = tables.reshape(2, 2 * SU, SU)
    slot_tables = []
    for set_id in range(2):
        for shift in range(facets):
            if set_id == 0 and shift == 0:
                slot_tables.append(own_table)
                continue
            perm = [
                (f * groups + g, (f + shift) % facets * groups + (g + set_id) % groups)
                for f in range(facets)
                for g in range(groups)
            ]
            slot_tables.append(lax.ppermute(own_table, ("facet", "bl"), perm))

    numbers = jnp.concatenate([plane_index, block_group[:, 0]]).astype(jnp.bfloat16)
    numbers = jnp.pad(numbers[None, :], ((0, 15), (0, SU - 2 * held)))
    packed = jnp.concatenate(
        [
            visibilities.reshape(held * chans * 2, SU),
            coords.reshape(held * 2, SU),
            numbers,
        ],
        axis=0,
    )
    rows = packed.shape[0]
    gathered = lax.all_gather(packed, ("facet", "bl"), axis=0, tiled=True)

    slots = 2 * facets
    half_rows = SU // chan_count
    vmem = pl.BlockSpec(memory_space=pltpu.VMEM)
    smem = pl.BlockSpec(memory_space=pltpu.SMEM)
    mine, other = pl.pallas_call(
        functools.partial(grid_kernel, (facets, groups, held, chans, rows), norm),
        out_shape=[jax.ShapeDtypeStruct((half_rows, 2 * SU), jnp.float32)] * 2,
        in_specs=[vmem, smem, smem, vmem] + [vmem] * slots,
        out_specs=[vmem, vmem],
        scratch_shapes=[
            pltpu.VMEM((devices * rows, SU), jnp.float32),
            pltpu.VMEM((devices, SU), jnp.int32),
            pltpu.SMEM((devices, SU), jnp.int32),
            pltpu.SMEM((devices * held + UNROLL,), jnp.int32),
            pltpu.VMEM((slots, 2 * SU, SU), jnp.float32),
            pltpu.VMEM((2 * SU, 2 * SU), jnp.float32),
            pltpu.VMEM((2 * SU, SU), jnp.float32),
            pltpu.VMEM((SU, 2 * SU), jnp.float32),
            pltpu.SemaphoreType.DMA,
        ],
        compiler_params=pltpu.CompilerParams(vmem_limit_bytes=40 * 1024 * 1024),
        cost_estimate=pl.CostEstimate(
            flops=4_000_000_000, bytes_accessed=2_000_000, transcendentals=4_000_000
        ),
        name="grid",
    )(gathered, offsets, facet_centre, antenna_gain, *slot_tables)
    arrived = lax.ppermute(other, "chan", [(c, 1 - c) for c in range(chan_count)])
    return (mine + arrived).reshape(1, 1, half_rows, 2, SU)


def solution(mesh):
    in_specs = (
        P(("facet", "bl"), "chan", None, None),
        P(("facet", "bl"), None, None),
        P(("facet", "bl")),
        P(("facet", "bl"), None),
        P(),
        P(),
        P(("facet", "bl"), None, None, None, None),
        P("bl", None, None),
    )
    out_specs = P("facet", "bl", "chan", None, None)
    return jax.shard_map(body, mesh=mesh, in_specs=in_specs, out_specs=out_specs, check_vma=False)
```

time: 185 us -> 71.1 us (0.38)
  other arithmetic: 42 us -> 0.1 us
  matrix products: 33.4 us -> 0 us
  waiting for transfers between devices: 29.5 us -> 1.73 us
  local copies, waits for them, and re-layouts: 24.7 us -> 2.26 us
  blocking collectives: 25.8 us -> 42.5 us
  between operations: 14.8 us -> 0.1 us
  Pallas kernels: 0 us -> 9.76 us
    dot_general x12 -> x0, matrix products: 33.4 us -> none  [the longest x4 22.1 us: block_grids(): jnp.einsum('bsj,bsk->bjk', weighted, spread_v, preferred_element_type=jnp...]
    all_gather x2 -> x1, blocking collectives: 16 us -> 42.5 us  [body(): gathered = lax.all_gather(packed, ('facet', 'bl'), axis=0, tiled=True)]
    another operation x8 -> x0, other arithmetic: 25.2 us -> none
    unnamed x3 -> x0, waiting for transfers between devices: 16.7 us -> none
    ppermute x0 -> x8, starting transfers between devices: none -> 14.3 us  [the longest x7 14.3 us: body(): slot_tables.append(lax.ppermute(own_table, ('facet', 'bl'), perm))]
    all_to_all x3 -> x0, starting transfers between devices: 13.4 us -> none  [the longest x1 6.32 us: body(): lax.all_to_all(planes_out, 'bl', split_axis=0, concat_axis=0, tiled=True)]
    unnamed x1 -> x0, blocking collectives: 9.82 us -> none
    pallas_call x0 -> x1, Pallas kernels: none -> 9.76 us  [body(): pl.pallas_call(functools.partial(grid_kernel, (facets, groups, held, chan...]
  transfers between devices with their start and end apart: 5 -> 8, of which waited for: 4 -> 2; matrix products, arithmetic and copies ran while one was open for 7% -> 2% of each run, Pallas kernels for 0% -> 0%
where the time goes in v1:
time: 71.1 us; the launch traced here: 70.7 us
  blocking collectives  42.5 us (60%)
  starting transfers between devices  14.3 us (20%)
  Pallas kernels  9.76 us (14%)
  local copies, waits for them, and re-layouts  2.26 us (3%)
  waiting for transfers between devices  1.73 us (2%)
    all_gather x1, blocking collectives, body(): gathered = lax.all_gather(packed, ('facet', 'bl'), axis=0, tiled=True)  42.5 us
    ppermute x7, starting transfers between devices, body(): slot_tables.append(lax.ppermute(own_table, ('facet', 'bl'), perm))  14.3 us
    pallas_call x1, Pallas kernels, body(): pl.pallas_call(functools.partial(grid_kernel, (facets, groups, held, chan...  9.76 us
    unnamed x14, local copies, waits for them, and re-layouts  1.6 us
  transfers between devices with their start and end apart: 8, of which 2 were waited for; matrix products, arithmetic and copies ran while one was open for 2% of the time, Pallas kernels for 0%

profile of v1, /device:TPU:0, one launch (start us, length us, event | category | flops | bytes accessed | tf_op | source)
XLA Modules:
  0.0 70.7 jit_solution(16326379316049821651)
XLA Ops:
  0.0 0.0 copy-start.4
  0.0 0.0 copy-start.5
  0.0 0.0 copy-start.2
  0.0 5.0 %collective-permute-start.6 = (bf16[2,256,128]{2,1,0:T(8,128)(2,1)}, bf16[2,256,128]{2,1,0:T(8,128)(2,1)S(1)}, u32[]{:S(2)}, u32[]{:S(2)}) collective-permute-start(bf16[2,256,128]{2,1,0:T(8,128)(2,1)} %bitcast.7), channel_id=1, source_target_pairs={{0,26},{2,28},{4,30},{6,24},{8,2},{10,4},{12,6},{14,0},{16,10},{18... | collective-permute-start | bytes 393224 | tf_op jit(solution)/shard_map/ppermute | solution.py:201
  5.0 1.5 %collective-permute-start.5 = (bf16[2,256,128]{2,1,0:T(8,128)(2,1)}, bf16[2,256,128]{2,1,0:T(8,128)(2,1)S(1)}, u32[]{:S(2)}, u32[]{:S(2)}) collective-permute-start(bf16[2,256,128]{2,1,0:T(8,128)(2,1)} %bitcast.8), channel_id=1, source_target_pairs={{0,18},{2,20},{4,22},{6,16},{8,26},{10,28},{12,30},{14,24},{16,2},... | collective-permute-start | bytes 393224 | tf_op jit(solution)/shard_map/ppermute | solution.py:201
  6.5 1.6 %collective-permute-start.4 = (bf16[2,256,128]{2,1,0:T(8,128)(2,1)}, bf16[2,256,128]{2,1,0:T(8,128)(2,1)S(1)}, u32[]{:S(2)}, u32[]{:S(2)}) collective-permute-start(bf16[2,256,128]{2,1,0:T(8,128)(2,1)} %bitcast.9), channel_id=1, source_target_pairs={{0,10},{2,12},{4,14},{6,8},{8,18},{10,20},{12,22},{14,16},{16,26},... | collective-permute-start | bytes 393224 | tf_op jit(solution)/shard_map/ppermute | solution.py:201
  8.1 0.2 collective-permute-start.3
  8.3 2.3 %collective-permute-start.2 = (bf16[2,256,128]{2,1,0:T(8,128)(2,1)}, bf16[2,256,128]{2,1,0:T(8,128)(2,1)S(1)}, u32[]{:S(2)}, u32[]{:S(2)}) collective-permute-start(bf16[2,256,128]{2,1,0:T(8,128)(2,1)} %bitcast.11), channel_id=1, source_target_pairs={{0,24},{2,26},{4,28},{6,30},{8,0},{10,2},{12,4},{14,6},{16,8},{18,... | collective-permute-start | bytes 393224 | tf_op jit(solution)/shard_map/ppermute | solution.py:201
  10.7 0.0 copy-done.4
  10.7 0.0 copy-done.5
  10.7 0.1 fusion.5
  10.8 0.8 %copy.10.centre_ref = f32[4,2]{1,0:T(4,128)S(1)} copy(f32[4,2]{0,1:T(2,128)} %param.13) | data formatting | bytes 64 | tf_op args[5]
  11.5 0.0 copy-start.3
  11.5 0.8 %copy.9.offsets_ref = s32[4,4,2]{2,1,0:T(4,128)S(1)} copy(s32[4,4,2]{1,2,0:T(2,128)} %param.12) | data formatting | bytes 256 | tf_op args[4]
  12.3 0.0 copy-done.2
  12.3 0.0 copy-done.3
  12.3 0.0 copy-start
  12.3 0.0 copy-start.1
  12.4 0.0 collective-permute-done.6.refs_7_
  12.4 1.6 %collective-permute-start.1 = (bf16[2,256,128]{2,1,0:T(8,128)(2,1)}, bf16[2,256,128]{2,1,0:T(8,128)(2,1)S(1)}, u32[]{:S(2)}, u32[]{:S(2)}) collective-permute-start(bf16[2,256,128]{2,1,0:T(8,128)(2,1)} %bitcast.12), channel_id=1, source_target_pairs={{0,16},{2,18},{4,20},{6,22},{8,24},{10,26},{12,28},{14,30},{16,0},... | collective-permute-start | bytes 393224 | tf_op jit(solution)/shard_map/ppermute | solution.py:201
  14.0 0.5 collective-permute-done.5.refs_6_
  14.4 2.0 %collective-permute-start = (bf16[2,256,128]{2,1,0:T(8,128)(2,1)}, bf16[2,256,128]{2,1,0:T(8,128)(2,1)S(1)}, u32[]{:S(2)}, u32[]{:S(2)}) collective-permute-start(bf16[2,256,128]{2,1,0:T(8,128)(2,1)} %bitcast.13), channel_id=1, source_target_pairs={{0,8},{2,10},{4,12},{6,14},{8,16},{10,18},{12,20},{14,22},{16,24},... | collective-permute-start | bytes 393224 | tf_op jit(solution)/shard_map/ppermute | solution.py:201
  16.5 42.5 %all_gather.3.packed_ref = bf16[1536,128]{1,0:T(8,128)(2,1)S(1)} all-gather(bf16[96,128]{1,0:T(8,128)(2,1)S(1)} %pad_maximum_fusion), channel_id=1, replica_groups=mesh['facet'=4,'bl'=4,'chan'=2] {'facet','bl'}, dimensions={0}, use_global_device_ids=true | all-gather | bytes 417792 | tf_op jit(solution)/shard_map/all_gather | solution.py:214
  58.9 0.0 collective-permute-done.4.refs_5_
  58.9 0.0 collective-permute-done.3.refs_4_
  58.9 0.0 collective-permute-done.2.refs_3_
  58.9 0.0 collective-permute-done.1.refs_2_
  58.9 0.0 collective-permute-done.refs_1_
  58.9 0.0 copy-done
  59.0 0.0 copy-done.1
  59.0 9.8 %grid.1 = (f32[64,256]{1,0:T(8,128)S(1)}, f32[64,256]{1,0:T(8,128)S(1)}) custom-call(bf16[1536,128]{1,0:T(8,128)(2,1)S(1)} %all_gather.3.packed_ref, s32[4,4,2]{2,1,0:T(4,128)S(1)} %copy.9.offsets_ref, f32[4,2]{1,0:T(4,128)S(1)} %copy.10.centre_ref, f32[1,2,128]{2,1,0:T(2,128)S(1)} %copy-done.1, bf16[2,256,128]{2,1,0:T(8,128)(2,1)S(1)} %bitcast.14, ...), custom_call_target="tpu_custom_call" | custom-call | flops 4000000000 | bytes 2000000 | tf_op jit(solution)/shard_map/grid/pallas_call | solution.py:220
  68.7 0.1 collective-permute-start.7
  68.8 1.2 %collective-permute-done.7 = f32[64,256]{1,0:T(8,128)S(1)} collective-permute-done((f32[64,256]{1,0:T(8,128)S(1)}, f32[64,256]{1,0:T(8,128)S(1)}, u32[]{:S(2)}, u32[]{:S(2)}) %collective-permute-start.7) | collective-permute-done | bytes 65568 | tf_op jit(solution)/shard_map/ppermute | solution.py:242
  70.1 0.7 reshape.47
  (4 shorter events, 0.0 us)
Async XLA Ops:
  0.0 10.7 %copy-start.4 = (s32[8]{0:T(128)S(1)}, s32[8]{0:T(128)}, u32[]{:S(2)}) copy-start(s32[8]{0:T(128)} %param.10) | copy-start | bytes 100
  0.0 10.7 %copy-start.5 = (s32[8,1]{0,1:T(1,128)S(1)}, s32[8,1]{0,1:T(1,128)}, u32[]{:S(2)}) copy-start(s32[8,1]{0,1:T(1,128)} %param.11) | copy-start | bytes 100
  0.0 12.3 %copy-start.2 = (bf16[8,4,2,128]{3,2,1,0:T(2,128)(2,1)S(1)}, bf16[8,4,2,128]{3,2,1,0:T(2,128)(2,1)}, u32[]{:S(2)}) copy-start(bf16[8,4,2,128]{3,2,1,0:T(2,128)(2,1)} %param.8) | copy-start | bytes 49156
  0.0 12.4 %collective-permute-start.6 = (bf16[2,256,128]{2,1,0:T(8,128)(2,1)}, bf16[2,256,128]{2,1,0:T(8,128)(2,1)S(1)}, u32[]{:S(2)}, u32[]{:S(2)}) collective-permute-start(bf16[2,256,128]{2,1,0:T(8,128)(2,1)} %bitcast.7), channel_id=1, source_target_pairs={{0,26},{2,28},{4,30},{6,24},{8,2},{10,4},{12,6},{14,0},{16,10},{18... | collective-permute-start | bytes 393224 | tf_op jit(solution)/shard_map/ppermute | solution.py:201
  5.0 9.5 %collective-permute-start.5 = (bf16[2,256,128]{2,1,0:T(8,128)(2,1)}, bf16[2,256,128]{2,1,0:T(8,128)(2,1)S(1)}, u32[]{:S(2)}, u32[]{:S(2)}) collective-permute-start(bf16[2,256,128]{2,1,0:T(8,128)(2,1)} %bitcast.8), channel_id=1, source_target_pairs={{0,18},{2,20},{4,22},{6,16},{8,26},{10,28},{12,30},{14,24},{16,2},... | collective-permute-start | bytes 393224 | tf_op jit(solution)/shard_map/ppermute | solution.py:201
  6.5 52.4 %collective-permute-start.4 = (bf16[2,256,128]{2,1,0:T(8,128)(2,1)}, bf16[2,256,128]{2,1,0:T(8,128)(2,1)S(1)}, u32[]{:S(2)}, u32[]{:S(2)}) collective-permute-start(bf16[2,256,128]{2,1,0:T(8,128)(2,1)} %bitcast.9), channel_id=1, source_target_pairs={{0,10},{2,12},{4,14},{6,8},{8,18},{10,20},{12,22},{14,16},{16,26},... | collective-permute-start | bytes 393224 | tf_op jit(solution)/shard_map/ppermute | solution.py:201
  8.1 50.8 %collective-permute-start.3 = (bf16[2,256,128]{2,1,0:T(8,128)(2,1)}, bf16[2,256,128]{2,1,0:T(8,128)(2,1)S(1)}, u32[]{:S(2)}, u32[]{:S(2)}) collective-permute-start(bf16[2,256,128]{2,1,0:T(8,128)(2,1)} %bitcast.10), channel_id=1, source_target_pairs={{0,2},{2,4},{4,6},{6,0},{8,10},{10,12},{12,14},{14,8},{16,18},{18,... | collective-permute-start | bytes 393224 | tf_op jit(solution)/shard_map/ppermute | solution.py:201
  8.3 50.6 %collective-permute-start.2 = (bf16[2,256,128]{2,1,0:T(8,128)(2,1)}, bf16[2,256,128]{2,1,0:T(8,128)(2,1)S(1)}, u32[]{:S(2)}, u32[]{:S(2)}) collective-permute-start(bf16[2,256,128]{2,1,0:T(8,128)(2,1)} %bitcast.11), channel_id=1, source_target_pairs={{0,24},{2,26},{4,28},{6,30},{8,0},{10,2},{12,4},{14,6},{16,8},{18,... | collective-permute-start | bytes 393224 | tf_op jit(solution)/shard_map/ppermute | solution.py:201
  11.5 0.8 %copy-start.3 = (bf16[8,2,128]{2,1,0:T(2,128)(2,1)S(1)}, bf16[8,2,128]{2,1,0:T(2,128)(2,1)}, u32[]{:S(2)}) copy-start(bf16[8,2,128]{2,1,0:T(2,128)(2,1)} %param.9) | copy-start | bytes 12292
  12.3 46.6 %copy-start = (bf16[1,2,128,2,128]{4,3,2,1,0:T(2,128)(2,1)S(1)}, bf16[1,2,128,2,128]{4,3,2,1,0:T(2,128)(2,1)}, u32[]{:S(2)}) copy-start(bf16[1,2,128,2,128]{4,3,2,1,0:T(2,128)(2,1)} %param.14) | copy-start | bytes 393220
  12.3 46.6 %copy-start.1 = (f32[1,2,128]{2,1,0:T(2,128)S(1)}, f32[1,2,128]{2,1,0:T(2,128)}, u32[]{:S(2)}) copy-start(f32[1,2,128]{2,1,0:T(2,128)} %gain_ref.1) | copy-start | bytes 3076
  12.4 46.6 %collective-permute-start.1 = (bf16[2,256,128]{2,1,0:T(8,128)(2,1)}, bf16[2,256,128]{2,1,0:T(8,128)(2,1)S(1)}, u32[]{:S(2)}, u32[]{:S(2)}) collective-permute-start(bf16[2,256,128]{2,1,0:T(8,128)(2,1)} %bitcast.12), channel_id=1, source_target_pairs={{0,16},{2,18},{4,20},{6,22},{8,24},{10,26},{12,28},{14,30},{16,0},... | collective-permute-start | bytes 393224 | tf_op jit(solution)/shard_map/ppermute | solution.py:201
  14.4 44.5 %collective-permute-start = (bf16[2,256,128]{2,1,0:T(8,128)(2,1)}, bf16[2,256,128]{2,1,0:T(8,128)(2,1)S(1)}, u32[]{:S(2)}, u32[]{:S(2)}) collective-permute-start(bf16[2,256,128]{2,1,0:T(8,128)(2,1)} %bitcast.13), channel_id=1, source_target_pairs={{0,8},{2,10},{4,12},{6,14},{8,16},{10,18},{12,20},{14,22},{16,24},... | collective-permute-start | bytes 393224 | tf_op jit(solution)/shard_map/ppermute | solution.py:201
  68.7 1.3 %collective-permute-start.7 = (f32[64,256]{1,0:T(8,128)S(1)}, f32[64,256]{1,0:T(8,128)S(1)}, u32[]{:S(2)}, u32[]{:S(2)}) collective-permute-start(f32[64,256]{1,0:T(8,128)S(1)} %get-tuple-element.8), channel_id=1, source_target_pairs={{0,1},{1,0},{2,3},{3,2},{4,5},{5,4},{6,7},{7,6},{8,9},{9,8},{10,11... | collective-permute-start | bytes 196616 | tf_op jit(solution)/shard_map/ppermute | solution.py:242

commit v2 on v1

--- a/solution.py
+++ b/solution.py
@@ -14,6 +14,9 @@
 ALPHA = math.sqrt(math.log2(math.e) / (2.0 * KERNEL_SPREAD * KERNEL_SPREAD))
 UNROLL = 2
 NT = (((1,), (1,)), ((), ()))
+VMEM = pl.BlockSpec(memory_space=pltpu.VMEM)
+SMEM = pl.BlockSpec(memory_space=pltpu.SMEM)
+PARAMS = pltpu.CompilerParams(vmem_limit_bytes=32 * 1024 * 1024)
 
 
 def cos_sin(turns):
@@ -41,49 +44,66 @@
     return high, low
 
 
-def grid_kernel(sizes, norm, packed_ref, offsets_ref, centre_ref, gain_ref, *refs):
-    facets, groups, held, chans, rows = sizes
+def sort_kernel(sizes, plane_ref, group_ref, samples_ref, place_ref, out_ref, samples, place, sorted_, filled):
+    facets, groups, held, chans, cap, rows = sizes
+    per = 2 * chans
+    samples[...] = samples_ref[...].astype(jnp.float32)
+    place[...] = place_ref[...].astype(jnp.float32)
+    sorted_[...] = jnp.zeros_like(sorted_)
+    for g in range(groups):
+        filled[g] = 0
+    lane = lax.broadcasted_iota(jnp.int32, (1, SU), 1)
+    for i in range(held):
+        g = group_ref[0, i]
+        k = filled[g]
+        filled[g] = k + 1
+        sorted_[g, pl.ds(pl.multiple_of(k * per, per), per), :] = samples[i * per : (i + 1) * per, :]
+        sorted_[g, pl.ds(cap * per + 2 * k, 2), :] = place[2 * i : 2 * i + 2, :]
+        sorted_[g, cap * (per + 2) : cap * (per + 2) + 1, :] += jnp.where(
+            lane == k, (plane_ref[0, i] + 1).astype(jnp.float32), 0.0
+        )
+    for g in range(groups):
+        mine = sorted_[g].astype(jnp.bfloat16)
+        for f in range(facets):
+            out_ref[f * groups + g] = mine
+
+
+def grid_kernel(sizes, packed_ref, offsets_ref, centre_ref, grids, flat, meta_v, meta_s, order, sem):
+    facets, groups, chans, cap, rows = sizes
+    per = 2 * chans
+    devices = facets * groups
     slots = 2 * facets
-    table_refs = refs[:slots]
-    mine_ref, other_ref = refs[slots : slots + 2]
-    flat, meta_v, meta_s, order, grids, stacked, table_f, total, sem = refs[slots + 2 :]
-    devices = facets * groups
     facet = lax.axis_index("facet")
     group = lax.axis_index("bl")
     chan = lax.axis_index("chan")
-    place_row = held * chans * 2
-    meta_row = place_row + 2 * held
 
     def widen(d, carry):
-        at = pl.multiple_of(d * rows, rows)
-        flat[pl.ds(at, rows), :] = packed_ref[pl.ds(at, rows), :].astype(jnp.float32)
+        flat[pl.ds(pl.multiple_of(d * rows, rows), rows), :] = packed_ref[d].astype(jnp.float32)
         return carry
 
     lax.fori_loop(0, devices, widen, 0)
-    meta_v[...] = flat[pl.ds(meta_row, devices, stride=rows), :].astype(jnp.int32)
+    meta_v[...] = flat[pl.ds(cap * (per + 2), devices, stride=rows), :].astype(jnp.int32)
     copy = pltpu.make_async_copy(meta_v, meta_s, sem)
     copy.start()
     grids[...] = jnp.zeros_like(grids)
     copy.wait()
 
     def pick(d, count):
-        for i in range(held):
-            plane = meta_s[d, i]
-            of_group = meta_s[d, held + i]
+        for k in range(cap):
+            plane = meta_s[d, k] - 1
             set_id = jnp.where(lax.rem(plane, groups) == group, 0, 1)
-            shift = lax.rem(facet - lax.div(plane, groups) + facets, facets)
-            order[count] = (d * held + i) * slots + set_id * facets + shift
-            count = count + jnp.where(of_group == group, 1, 0)
+            order[count] = (d * cap + k) * slots + 2 * lax.div(plane, groups) + set_id
+            count = count + jnp.where(plane >= 0, 1, 0)
         return count
 
     count = lax.fori_loop(0, devices, pick, 0)
     for i in range(UNROLL):
         order[count + i] = 0
 
-    offset_u = offsets_ref[facet, group, 0].astype(jnp.float32)
-    offset_v = offsets_ref[facet, group, 1].astype(jnp.float32)
-    along_l = centre_ref[facet, 0]
-    along_m = centre_ref[facet, 1]
+    offset_u = offsets_ref[facet, 0, group].astype(jnp.float32)
+    offset_v = offsets_ref[facet, 1, group].astype(jnp.float32)
+    along_l = centre_ref[0, facet]
+    along_m = centre_ref[1, facet]
     channel = (chan * chans + lax.broadcasted_iota(jnp.int32, (chans, SU), 0)).astype(jnp.float32)
     scale = 1.0 + 0.01 * (channel - 0.5 * (CH - 1))
     cells = ALPHA * lax.broadcasted_iota(jnp.int32, (SU, SU), 0).astype(jnp.float32)
@@ -99,13 +119,13 @@
         code = order[at]
         block = lax.div(code, slots)
         slot = lax.rem(code, slots)
-        d = lax.div(block, held)
-        i = lax.rem(block, held)
+        d = lax.div(block, cap)
+        k = lax.rem(block, cap)
         keep = jnp.where(at < count, 1.0, 0.0)
-        base = pl.multiple_of(d * rows + i * 2 * chans, 2 * chans)
+        base = pl.multiple_of(d * rows + k * per, per)
         real = flat[pl.ds(base, chans, stride=2), :] * keep
         imag = flat[pl.ds(base + 1, chans, stride=2), :] * keep
-        at_place = d * rows + place_row + 2 * i
+        at_place = d * rows + cap * per + 2 * k
         along_u = flat[pl.ds(at_place, 1), :]
         along_v = flat[pl.ds(at_place + 1, 1), :]
         spot_u = ALPHA * (scale * along_u - offset_u)
@@ -133,9 +153,12 @@
 
     lax.fori_loop(0, lax.div(count + UNROLL - 1, UNROLL), step, 0)
 
+
+def table_kernel(slots, norm, grids, tables, gain_ref, mine_ref, other_ref, table_f, total):
+    chan = lax.axis_index("chan")
     result = jnp.zeros((SU, 2 * SU), jnp.float32)
     for s in range(slots):
-        table_f[...] = table_refs[s][0].astype(jnp.float32)
+        table_f[...] = tables[s, 0].astype(jnp.float32)
         u_real = table_f[pl.ds(0, SU, stride=2), :]
         u_imag = table_f[pl.ds(1, SU, stride=2), :]
         u_side = jnp.concatenate([u_real.T, u_imag.T], axis=1).astype(jnp.bfloat16)
@@ -152,7 +175,7 @@
         half = jnp.dot(u_side, high, preferred_element_type=jnp.float32) + jnp.dot(
             u_side, low, preferred_element_type=jnp.float32
         )
-        table_f[...] = table_refs[s][1].astype(jnp.float32)
+        table_f[...] = tables[s, 1].astype(jnp.float32)
         v_real = table_f[pl.ds(0, SU, stride=2), :]
         v_imag = table_f[pl.ds(1, SU, stride=2), :]
         v_side = jnp.concatenate(
@@ -184,61 +207,74 @@
     chan_count = lax.axis_size("chan")
     held, chans = visibilities.shape[:2]
     devices = facets * groups
+    slots = 2 * facets
+    cap = max(2, 2 * held // groups)
+    per = 2 * chans
+    rows = -(-(cap * (per + 2) + 1) // 16) * 16
+    half_rows = SU // chan_count
     norm = SU / math.sqrt(visibilities.shape[3] * held * facets * CH)
 
-    own_table = tables.reshape(2, 2 * SU, SU)
-    slot_tables = []
-    for set_id in range(2):
-        for shift in range(facets):
-            if set_id == 0 and shift == 0:
-                slot_tables.append(own_table)
-                continue
-            perm = [
-                (f * groups + g, (f + shift) % facets * groups + (g + set_id) % groups)
-                for f in range(facets)
-                for g in range(groups)
-            ]
-            slot_tables.append(lax.ppermute(own_table, ("facet", "bl"), perm))
-
-    numbers = jnp.concatenate([plane_index, block_group[:, 0]]).astype(jnp.bfloat16)
-    numbers = jnp.pad(numbers[None, :], ((0, 15), (0, SU - 2 * held)))
-    packed = jnp.concatenate(
-        [
-            visibilities.reshape(held * chans * 2, SU),
-            coords.reshape(held * 2, SU),
-            numbers,
+    packed = pl.pallas_call(
+        functools.partial(sort_kernel, (facets, groups, held, chans, cap, rows)),
+        out_shape=jax.ShapeDtypeStruct((devices, rows, SU), jnp.bfloat16),
+        in_specs=[SMEM, SMEM, VMEM, VMEM],
+        out_specs=VMEM,
+        scratch_shapes=[
+            pltpu.VMEM((held * per, SU), jnp.float32),
+            pltpu.VMEM((held * 2, SU), jnp.float32),
+            pltpu.VMEM((groups, rows, SU), jnp.float32),
+            pltpu.SMEM((groups,), jnp.int32),
         ],
-        axis=0,
-    )
-    rows = packed.shape[0]
-    gathered = lax.all_gather(packed, ("facet", "bl"), axis=0, tiled=True)
-
-    slots = 2 * facets
-    half_rows = SU // chan_count
-    vmem = pl.BlockSpec(memory_space=pltpu.VMEM)
-    smem = pl.BlockSpec(memory_space=pltpu.SMEM)
-    mine, other = pl.pallas_call(
-        functools.partial(grid_kernel, (facets, groups, held, chans, rows), norm),
-        out_shape=[jax.ShapeDtypeStruct((half_rows, 2 * SU), jnp.float32)] * 2,
-        in_specs=[vmem, smem, smem, vmem] + [vmem] * slots,
-        out_specs=[vmem, vmem],
+        compiler_params=PARAMS,
+        cost_estimate=pl.CostEstimate(flops=100_000, bytes_accessed=300_000, transcendentals=0),
+        name="sort_blocks",
+    )(
+        plane_index.reshape(1, held),
+        block_group.T,
+        visibilities.reshape(held * per, SU),
+        coords.reshape(held * 2, SU),
+    )
+    gathered = lax.all_to_all(packed, ("facet", "bl"), split_axis=0, concat_axis=0, tiled=True)
+
+    own_table = tables.reshape(1, 2, 2 * SU, SU)
+    perm = [(g, (g + 1) % groups) for g in range(groups)]
+    both = jnp.concatenate([own_table, lax.ppermute(own_table, "bl", perm)], axis=0)
+    spread = jnp.broadcast_to(both[None], (facets,) + both.shape)
+    slot_tables = lax.all_to_all(spread, "facet", split_axis=0, concat_axis=0, tiled=True)
+
+    grids = pl.pallas_call(
+        functools.partial(grid_kernel, (facets, groups, chans, cap, rows)),
+        out_shape=jax.ShapeDtypeStruct((slots, 2 * SU, SU), jnp.float32),
+        in_specs=[VMEM, SMEM, SMEM],
+        out_specs=VMEM,
         scratch_shapes=[
             pltpu.VMEM((devices * rows, SU), jnp.float32),
             pltpu.VMEM((devices, SU), jnp.int32),
             pltpu.SMEM((devices, SU), jnp.int32),
-            pltpu.SMEM((devices * held + UNROLL,), jnp.int32),
-            pltpu.VMEM((slots, 2 * SU, SU), jnp.float32),
-            pltpu.VMEM((2 * SU, 2 * SU), jnp.float32),
-            pltpu.VMEM((2 * SU, SU), jnp.float32),
-            pltpu.VMEM((SU, 2 * SU), jnp.float32),
+            pltpu.SMEM((devices * cap + UNROLL,), jnp.int32),
             pltpu.SemaphoreType.DMA,
         ],
-        compiler_params=pltpu.CompilerParams(vmem_limit_bytes=40 * 1024 * 1024),
+        compiler_params=PARAMS,
         cost_estimate=pl.CostEstimate(
             flops=4_000_000_000, bytes_accessed=2_000_000, transcendentals=4_000_000
         ),
         name="grid",
-    )(gathered, offsets, facet_centre, antenna_gain, *slot_tables)
+    )(gathered, offsets.transpose(0, 2, 1), facet_centre.T)
+    mine, other = pl.pallas_call(
+        functools.partial(table_kernel, slots, norm),
+        out_shape=[jax.ShapeDtypeStruct((half_rows, 2 * SU), jnp.float32)] * 2,
+        in_specs=[VMEM, VMEM, VMEM],
+        out_specs=[VMEM, VMEM],
+        scratch_shapes=[
+            pltpu.VMEM((2 * SU, SU), jnp.float32),
+            pltpu.VMEM((SU, 2 * SU), jnp.float32),
+        ],
+        compiler_params=PARAMS,
+        cost_estimate=pl.CostEstimate(
+            flops=1_000_000_000, bytes_accessed=2_000_000, transcendentals=0
+        ),
+        name="apply_tables",
+    )(grids, slot_tables.reshape(slots, 2, 2 * SU, SU), antenna_gain)
     arrived = lax.ppermute(other, "chan", [(c, 1 - c) for c in range(chan_count)])
     return (mine + arrived).reshape(1, 1, half_rows, 2, SU)
 

time: 71.1 us -> 42.2 us (0.59)
  blocking collectives: 42.5 us -> 0 us
  waiting for transfers between devices: 1.73 us -> 13.4 us
  local copies, waits for them, and re-layouts: 2.26 us -> 3.94 us
    all_gather x1 -> x0, blocking collectives: 42.5 us -> none  [body(): gathered = lax.all_gather(packed, ('facet', 'bl'), axis=0, tiled=True)]
    ppermute x7 -> x1, starting transfers between devices: 14.3 us -> 1.97 us  [body(): lax.ppermute(own_table, 'bl', perm)]
    all_to_all x0 -> x2, starting transfers between devices: none -> 12.1 us  [the longest x1 8.44 us: body(): lax.all_to_all(packed, ('facet', 'bl'), split_axis=0, concat_axis=0, tile...]
    ppermute x7 -> x1, waiting for transfers between devices: 0.48 us -> 8.06 us  [body(): lax.ppermute(own_table, 'bl', perm)]
    all_to_all x0 -> x2, waiting for transfers between devices: none -> 4.09 us  [the longest x1 2.18 us: body(): lax.all_to_all(spread, 'facet', split_axis=0, concat_axis=0, tiled=True)]
    broadcast_in_dim x0 -> x1, local copies, waits for them, and re-layouts: none -> 1.19 us  [body(): spread = jnp.broadcast_to(both[None], (facets,) + both.shape)]
    unnamed x14 -> x16, local copies, waits for them, and re-layouts: 1.6 us -> 2.09 us
    pallas_call x1 -> x3, Pallas kernels: 9.76 us -> 10.2 us  [the longest x1 7.91 us: body(): pl.pallas_call(functools.partial(grid_kernel, (facets, groups, chans, cap...]
  transfers between devices with their start and end apart: 8 -> 4, of which waited for: 2 -> 4; matrix products, arithmetic and copies ran while one was open for 2% -> 0% of each run, Pallas kernels for 0% -> 19%
where the time goes in v2:
time: 42.2 us; the launch traced here: 41.8 us
  starting transfers between devices  14.1 us (33%)
  waiting for transfers between devices  13.4 us (32%)
  Pallas kernels  10.2 us (24%)
  local copies, waits for them, and re-layouts  3.94 us (9%)
    all_to_all x1, starting transfers between devices, body(): lax.all_to_all(packed, ('facet', 'bl'), split_axis=0, concat_axis=0, tile...  8.44 us
    ppermute x1, waiting for transfers between devices, body(): lax.ppermute(own_table, 'bl', perm)  8.06 us
    pallas_call x1, Pallas kernels, body(): pl.pallas_call(functools.partial(grid_kernel, (facets, groups, chans, cap...  7.91 us
    all_to_all x1, starting transfers between devices, body(): lax.all_to_all(spread, 'facet', split_axis=0, concat_axis=0, tiled=True)  3.65 us
    all_to_all x1, waiting for transfers between devices, body(): lax.all_to_all(spread, 'facet', split_axis=0, concat_axis=0, tiled=True)  2.18 us
    unnamed x16, local copies, waits for them, and re-layouts  2.09 us
    ppermute x1, starting transfers between devices, body(): lax.ppermute(own_table, 'bl', perm)  1.97 us
    all_to_all x1, waiting for transfers between devices, body(): lax.all_to_all(packed, ('facet', 'bl'), split_axis=0, concat_axis=0, tile...  1.91 us
  transfers between devices with their start and end apart: 4, of which 4 were waited for; matrix products, arithmetic and copies ran while one was open for 0% of the time, Pallas kernels for 19%

profile of v2, /device:TPU:0, one launch (start us, length us, event | category | flops | bytes accessed | tf_op | source)
XLA Modules:
  0.0 41.8 jit_solution(8330668922549521687)
XLA Ops:
  0.0 0.0 copy-start.1
  0.0 0.0 copy-start.2
  0.0 0.0 copy-start.3
  0.0 0.7 %copy-done.1 = bf16[8,2,128]{2,1,0:T(2,128)(2,1)S(1)} copy-done((bf16[8,2,128]{2,1,0:T(2,128)(2,1)S(1)}, bf16[8,2,128]{2,1,0:T(2,128)(2,1)}, u32[]{:S(2)}) %copy-start.1) | copy-done | bytes 4120
  0.7 0.0 copy-done.2
  0.7 0.0 copy-done.3
  0.7 0.0 copy-start
  0.7 0.7 %copy-done = bf16[8,4,2,128]{3,2,1,0:T(2,128)(2,1)S(1)} copy-done((bf16[8,4,2,128]{3,2,1,0:T(2,128)(2,1)S(1)}, bf16[8,4,2,128]{3,2,1,0:T(2,128)(2,1)}, u32[]{:S(2)}) %copy-start) | copy-done | bytes 16408
  1.4 1.3 %sort_blocks.1 = bf16[16,48,128]{2,1,0:T(8,128)(2,1)} custom-call(s32[1,8]{1,0:T(1,128)S(1)} %bitcast.11, s32[1,8]{1,0:T(1,128)S(1)} %bitcast.12, bf16[64,128]{1,0:T(8,128)(2,1)S(1)} %bitcast.9, bf16[16,128]{1,0:T(8,128)(2,1)S(1)} %bitcast.10), custom_call_target="tpu_custom_call" | custom-call | flops 100000 | bytes 300000 | tf_op jit(solution)/shard_map/sort_blocks/pallas_call | solution.py:217
  2.7 0.0 copy-start.7
  2.7 8.4 %all-to-all-start = ((bf16[16,48,128]{2,1,0:T(8,128)(2,1)}), bf16[16,48,128]{2,1,0:T(8,128)(2,1)S(1)}, u32[]{:S(2)}, u32[]{:S(2)}) async-start(bf16[16,48,128]{2,1,0:T(8,128)(2,1)} %sort_blocks.1), calls=%async_computation | async-start | bytes 393216 | tf_op jit(solution)/shard_map/all_to_all | solution.py:237
  11.2 0.0 copy-done.7
  11.2 2.0 %collective-permute-start = (bf16[1,2,256,128]{3,2,1,0:T(8,128)(2,1)S(1)}, bf16[1,2,256,128]{3,2,1,0:T(8,128)(2,1)S(1)}, u32[]{:S(2)}, u32[]{:S(2)}) collective-permute-start(bf16[1,2,256,128]{3,2,1,0:T(8,128)(2,1)S(1)} %bitcast.15), channel_id=1, source_target_pairs={{0,2},{2,4},{4,6},{6,0},{1,3},{3,5},{5,7},{7,1},{8,10},{10,12},{12... | collective-permute-start | bytes 393224 | tf_op jit(solution)/shard_map/ppermute | solution.py:241
  13.2 8.1 %collective-permute-done = bf16[1,2,256,128]{3,2,1,0:T(8,128)(2,1)S(1)} collective-permute-done((bf16[1,2,256,128]{3,2,1,0:T(8,128)(2,1)S(1)}, bf16[1,2,256,128]{3,2,1,0:T(8,128)(2,1)S(1)}, u32[]{:S(2)}, u32[]{:S(2)}) %collective-permute-start) | collective-permute-done | bytes 131104 | tf_op jit(solution)/shard_map/ppermute | solution.py:241
  21.2 1.9 %all-to-all-done.packed_ref = bf16[16,48,128]{2,1,0:T(8,128)(2,1)S(1)} async-done(((bf16[16,48,128]{2,1,0:T(8,128)(2,1)}), bf16[16,48,128]{2,1,0:T(8,128)(2,1)S(1)}, u32[]{:S(2)}, u32[]{:S(2)}) %all-to-all-start) | async-done | bytes 196640 | tf_op jit(solution)/shard_map/all_to_all | solution.py:237
  23.1 1.2 %broadcast_in_dim.2 = bf16[4,2,2,256,128]{4,3,2,1,0:T(8,128)(2,1)} broadcast(bf16[2,2,256,128]{3,2,1,0:T(8,128)(2,1)S(1)} %pad_maximum_fusion), dimensions={1,2,3,4} | broadcast | bytes 1310720 | tf_op jit(solution)/shard_map/broadcast_in_dim | solution.py:242
  24.3 0.0 copy-start.4
  24.3 3.6 %all-to-all-start.1 = ((bf16[4,2,2,256,128]{4,3,2,1,0:T(8,128)(2,1)}), bf16[4,2,2,256,128]{4,3,2,1,0:T(8,128)(2,1)S(1)}, u32[]{:S(2)}, u32[]{:S(2)}) async-start(bf16[4,2,2,256,128]{4,3,2,1,0:T(8,128)(2,1)} %broadcast_in_dim.2), calls=%async_computation.1 | async-start | bytes 2097152 | tf_op jit(solution)/shard_map/all_to_all | solution.py:243
  28.0 0.0 copy-start.5
  28.0 0.0 copy-done.4
  28.0 0.7 %copy-done.5 = f32[4,2]{0,1:T(2,128)S(1)} copy-done((f32[4,2]{0,1:T(2,128)S(1)}, f32[4,2]{0,1:T(2,128)}, u32[]{:S(2)}) %copy-start.5) | copy-done | bytes 56
  28.7 7.9 %grid.1.grids = f32[8,256,128]{2,1,0:T(8,128)S(1)} custom-call(bf16[16,48,128]{2,1,0:T(8,128)(2,1)S(1)} %all-to-all-done.packed_ref, s32[4,2,4]{2,1,0:T(2,128)S(1)} %bitcast.13, f32[2,4]{1,0:T(2,128)S(1)} %bitcast.14), custom_call_target="tpu_custom_call" | custom-call | flops 4000000000 | bytes 2000000 | tf_op jit(solution)/shard_map/grid/pallas_call | solution.py:245
  36.6 0.0 copy-start.6
  36.6 2.2 %all-to-all-done.1 = bf16[4,2,2,256,128]{4,3,2,1,0:T(8,128)(2,1)S(1)} async-done(((bf16[4,2,2,256,128]{4,3,2,1,0:T(8,128)(2,1)}), bf16[4,2,2,256,128]{4,3,2,1,0:T(8,128)(2,1)S(1)}, u32[]{:S(2)}, u32[]{:S(2)}) %all-to-all-start.1) | async-done | bytes 1048608 | tf_op jit(solution)/shard_map/all_to_all | solution.py:243
  38.8 0.0 copy-done.6
  38.8 1.0 %apply_tables.1 = (f32[64,256]{1,0:T(8,128)S(1)}, f32[64,256]{1,0:T(8,128)S(1)}) custom-call(f32[8,256,128]{2,1,0:T(8,128)S(1)} %grid.1.grids, bf16[8,2,256,128]{3,2,1,0:T(8,128)(2,1)S(1)} %bitcast.8, f32[1,2,128]{2,1,0:T(2,128)S(1)} %copy-done.6), custom_call_target="tpu_custom_call" | custom-call | flops 1000000000 | bytes 2000000 | tf_op jit(solution)/shard_map/apply_tables/pallas_call | solution.py:263
  39.8 0.1 collective-permute-start.1
  39.9 1.2 %collective-permute-done.1 = f32[64,256]{1,0:T(8,128)S(1)} collective-permute-done((f32[64,256]{1,0:T(8,128)S(1)}, f32[64,256]{1,0:T(8,128)S(1)}, u32[]{:S(2)}, u32[]{:S(2)}) %collective-permute-start.1) | collective-permute-done | bytes 65568 | tf_op jit(solution)/shard_map/ppermute | solution.py:278
  41.2 0.7 %reshape.24 = f32[1,1,64,2,128]{4,3,2,1,0:T(2,128)} reshape(f32[64,256]{1,0:T(8,128)S(1)} %add.3) | data formatting | bytes 131072 | tf_op jit(solution)/shard_map/reshape | solution.py:279
  (2 shorter events, 0.0 us)
Async XLA Ops:
  0.0 0.7 %copy-start.1 = (bf16[8,2,128]{2,1,0:T(2,128)(2,1)S(1)}, bf16[8,2,128]{2,1,0:T(2,128)(2,1)}, u32[]{:S(2)}) copy-start(bf16[8,2,128]{2,1,0:T(2,128)(2,1)} %param.9) | copy-start | bytes 12292
  0.0 0.7 %copy-start.2 = (s32[8]{0:T(128)S(1)}, s32[8]{0:T(128)}, u32[]{:S(2)}) copy-start(s32[8]{0:T(128)} %param.10) | copy-start | bytes 100
  0.0 0.7 %copy-start.3 = (s32[8,1]{0,1:T(1,128)S(1)}, s32[8,1]{0,1:T(1,128)}, u32[]{:S(2)}) copy-start(s32[8,1]{0,1:T(1,128)} %param.11) | copy-start | bytes 100
  0.7 0.7 %copy-start = (bf16[8,4,2,128]{3,2,1,0:T(2,128)(2,1)S(1)}, bf16[8,4,2,128]{3,2,1,0:T(2,128)(2,1)}, u32[]{:S(2)}) copy-start(bf16[8,4,2,128]{3,2,1,0:T(2,128)(2,1)} %param.8) | copy-start | bytes 49156
  2.7 8.5 %copy-start.7 = (bf16[1,2,128,2,128]{4,3,2,1,0:T(2,128)(2,1)S(1)}, bf16[1,2,128,2,128]{4,3,2,1,0:T(2,128)(2,1)}, u32[]{:S(2)}) copy-start(bf16[1,2,128,2,128]{4,3,2,1,0:T(2,128)(2,1)} %param.14) | copy-start | bytes 393220
  2.7 20.4 %all-to-all-start = ((bf16[16,48,128]{2,1,0:T(8,128)(2,1)}), bf16[16,48,128]{2,1,0:T(8,128)(2,1)S(1)}, u32[]{:S(2)}, u32[]{:S(2)}) async-start(bf16[16,48,128]{2,1,0:T(8,128)(2,1)} %sort_blocks.1), calls=%async_computation | async-start | bytes 393216 | tf_op jit(solution)/shard_map/all_to_all | solution.py:237
  11.2 10.0 %collective-permute-start = (bf16[1,2,256,128]{3,2,1,0:T(8,128)(2,1)S(1)}, bf16[1,2,256,128]{3,2,1,0:T(8,128)(2,1)S(1)}, u32[]{:S(2)}, u32[]{:S(2)}) collective-permute-start(bf16[1,2,256,128]{3,2,1,0:T(8,128)(2,1)S(1)} %bitcast.15), channel_id=1, source_target_pairs={{0,2},{2,4},{4,6},{6,0},{1,3},{3,5},{5,7},{7,1},{8,10},{10,12},{12... | collective-permute-start | bytes 393224 | tf_op jit(solution)/shard_map/ppermute | solution.py:241
  24.3 3.7 %copy-start.4 = (s32[4,4,2]{1,2,0:T(2,128)S(1)}, s32[4,4,2]{1,2,0:T(2,128)}, u32[]{:S(2)}) copy-start(s32[4,4,2]{1,2,0:T(2,128)} %param.12) | copy-start | bytes 388
  24.3 14.4 %all-to-all-start.1 = ((bf16[4,2,2,256,128]{4,3,2,1,0:T(8,128)(2,1)}), bf16[4,2,2,256,128]{4,3,2,1,0:T(8,128)(2,1)S(1)}, u32[]{:S(2)}, u32[]{:S(2)}) async-start(bf16[4,2,2,256,128]{4,3,2,1,0:T(8,128)(2,1)} %broadcast_in_dim.2), calls=%async_computation.1 | async-start | bytes 2097152 | tf_op jit(solution)/shard_map/all_to_all | solution.py:243
  28.0 0.7 %copy-start.5 = (f32[4,2]{0,1:T(2,128)S(1)}, f32[4,2]{0,1:T(2,128)}, u32[]{:S(2)}) copy-start(f32[4,2]{0,1:T(2,128)} %param.13) | copy-start | bytes 100
  36.6 2.2 %copy-start.6 = (f32[1,2,128]{2,1,0:T(2,128)S(1)}, f32[1,2,128]{2,1,0:T(2,128)}, u32[]{:S(2)}) copy-start(f32[1,2,128]{2,1,0:T(2,128)} %gain_ref.1) | copy-start | bytes 3076
  39.8 1.3 %collective-permute-start.1 = (f32[64,256]{1,0:T(8,128)S(1)}, f32[64,256]{1,0:T(8,128)S(1)}, u32[]{:S(2)}, u32[]{:S(2)}) collective-permute-start(f32[64,256]{1,0:T(8,128)S(1)} %get-tuple-element.8), channel_id=1, source_target_pairs={{0,1},{1,0},{2,3},{3,2},{4,5},{5,4},{6,7},{7,6},{8,9},{9,8},{10,11... | collective-permute-start | bytes 196616 | tf_op jit(solution)/shard_map/ppermute | solution.py:278

commit v3 on v2

--- a/solution.py
+++ b/solution.py
@@ -12,11 +12,13 @@
 CH = 8
 KERNEL_SPREAD = 1.5
 ALPHA = math.sqrt(math.log2(math.e) / (2.0 * KERNEL_SPREAD * KERNEL_SPREAD))
-UNROLL = 2
+UNROLL = 4
 NT = (((1,), (1,)), ((), ()))
 VMEM = pl.BlockSpec(memory_space=pltpu.VMEM)
 SMEM = pl.BlockSpec(memory_space=pltpu.SMEM)
+HBM = pl.BlockSpec(memory_space=pltpu.HBM)
 PARAMS = pltpu.CompilerParams(vmem_limit_bytes=32 * 1024 * 1024)
+ALONE = pltpu.CompilerParams(vmem_limit_bytes=60 * 1024 * 1024)
 
 
 def cos_sin(turns):
@@ -44,48 +46,93 @@
     return high, low
 
 
-def sort_kernel(sizes, plane_ref, group_ref, samples_ref, place_ref, out_ref, samples, place, sorted_, filled):
-    facets, groups, held, chans, cap, rows = sizes
-    per = 2 * chans
-    samples[...] = samples_ref[...].astype(jnp.float32)
-    place[...] = place_ref[...].astype(jnp.float32)
+def sort_kernel(sizes, plane_hbm, group_hbm, samples_hbm, place_hbm, out_ref, *scratch):
+    groups, held, chans, cap, rows = sizes
+    plane_ref, group_ref, samples_b, place_b, samples, place, sorted_, filled, sems = scratch
+    sources = (plane_hbm, group_hbm, samples_hbm, place_hbm)
+    targets = (plane_ref, group_ref, samples_b, place_b)
+    copies = [
+        pltpu.make_async_copy(source, target, sems.at[n])
+        for n, (source, target) in enumerate(zip(sources, targets))
+    ]
+    for copy in copies:
+        copy.start()
     sorted_[...] = jnp.zeros_like(sorted_)
     for g in range(groups):
         filled[g] = 0
+    for copy in copies:
+        copy.wait()
+    samples[...] = samples_b[...].astype(jnp.float32)
+    place[...] = place_b[...].astype(jnp.float32)
     lane = lax.broadcasted_iota(jnp.int32, (1, SU), 1)
     for i in range(held):
         g = group_ref[0, i]
         k = filled[g]
         filled[g] = k + 1
-        sorted_[g, pl.ds(pl.multiple_of(k * per, per), per), :] = samples[i * per : (i + 1) * per, :]
-        sorted_[g, pl.ds(cap * per + 2 * k, 2), :] = place[2 * i : 2 * i + 2, :]
-        sorted_[g, cap * (per + 2) : cap * (per + 2) + 1, :] += jnp.where(
+        for part in range(2):
+            at = part * cap * chans + k * chans
+            sorted_[g, pl.ds(at, chans), :] = samples[pl.ds(2 * chans * i + part, chans, stride=2), :]
+            at = 2 * cap * chans + part * cap + k
+            sorted_[g, pl.ds(at, 1), :] = place[2 * i + part : 2 * i + part + 1, :]
+        meta = 2 * cap * (chans + 1)
+        sorted_[g, meta : meta + 1, :] += jnp.where(
             lane == k, (plane_ref[0, i] + 1).astype(jnp.float32), 0.0
         )
-    for g in range(groups):
-        mine = sorted_[g].astype(jnp.bfloat16)
-        for f in range(facets):
-            out_ref[f * groups + g] = mine
-
-
-def grid_kernel(sizes, packed_ref, offsets_ref, centre_ref, grids, flat, meta_v, meta_s, order, sem):
+    out_ref[...] = sorted_[...].astype(jnp.bfloat16)
+
+
+def grid_kernel(sizes, offsets_ref, centre_ref, *refs):
     facets, groups, chans, cap, rows = sizes
-    per = 2 * chans
+    packed_refs = refs[:facets]
+    grids = refs[facets]
+    meta_v, meta_s, order, spots_u, spots_v, turns_real, turns_imag, sem = refs[facets + 1 :]
     devices = facets * groups
     slots = 2 * facets
+    lines = cap * chans
     facet = lax.axis_index("facet")
     group = lax.axis_index("bl")
     chan = lax.axis_index("chan")
 
-    def widen(d, carry):
-        flat[pl.ds(pl.multiple_of(d * rows, rows), rows), :] = packed_ref[d].astype(jnp.float32)
-        return carry
-
-    lax.fori_loop(0, devices, widen, 0)
-    meta_v[...] = flat[pl.ds(cap * (per + 2), devices, stride=rows), :].astype(jnp.int32)
+    for f in range(facets):
+        for g in range(groups):
+            meta = packed_refs[f][g, rows - 16 : rows, :].astype(jnp.float32)
+            at = 2 * (lines + cap) - (rows - 16)
+            meta_v[f * groups + g : f * groups + g + 1, :] = meta[at : at + 1].astype(jnp.int32)
     copy = pltpu.make_async_copy(meta_v, meta_s, sem)
     copy.start()
     grids[...] = jnp.zeros_like(grids)
+
+    offset_u = offsets_ref[facet, 0, group].astype(jnp.float32)
+    offset_v = offsets_ref[facet, 1, group].astype(jnp.float32)
+    along_l = centre_ref[0, facet]
+    along_m = centre_ref[1, facet]
+    line = lax.broadcasted_iota(jnp.int32, (lines, SU), 0)
+    channel = (chan * chans + lax.rem(line, chans)).astype(jnp.float32)
+    scale = 1.0 + 0.01 * (channel - 0.5 * (CH - 1))
+
+    def spread_lines(place):
+        return jnp.concatenate(
+            [jnp.broadcast_to(place[k : k + 1], (chans, SU)) for k in range(cap)], axis=0
+        )
+
+    for f in range(facets):
+        for g in range(groups):
+            at = (f * groups + g) * lines
+            wide = packed_refs[f][g].astype(jnp.float32)
+            real = wide[:lines]
+            imag = wide[lines : 2 * lines]
+            along_u = spread_lines(wide[2 * lines : 2 * lines + cap])
+            along_v = spread_lines(wide[2 * lines + cap : 2 * (lines + cap)])
+            cosine, sine = cos_sin(
+                (1.0 / SU) * (scale * (along_u * along_l + along_v * along_m))
+            )
+            spots_u[at : at + lines, :] = ALPHA * (scale * along_u - offset_u)
+            spots_v[at : at + lines, :] = ALPHA * (scale * along_v - offset_v)
+            turns_real[at : at + lines, :] = real * cosine - imag * sine
+            turns_imag[at : at + lines, :] = real * sine + imag * cosine
+    last = devices * lines
+    for ref in (spots_u, spots_v, turns_real, turns_imag):
+        ref[last : last + 8, :] = jnp.zeros((8, SU), jnp.float32)
     copy.wait()
 
     def pick(d, count):
@@ -98,14 +145,8 @@
 
     count = lax.fori_loop(0, devices, pick, 0)
     for i in range(UNROLL):
-        order[count + i] = 0
-
-    offset_u = offsets_ref[facet, 0, group].astype(jnp.float32)
-    offset_v = offsets_ref[facet, 1, group].astype(jnp.float32)
-    along_l = centre_ref[0, facet]
-    along_m = centre_ref[1, facet]
-    channel = (chan * chans + lax.broadcasted_iota(jnp.int32, (chans, SU), 0)).astype(jnp.float32)
-    scale = 1.0 + 0.01 * (channel - 0.5 * (CH - 1))
+        order[count + i] = devices * cap * slots
+
     cells = ALPHA * lax.broadcasted_iota(jnp.int32, (SU, SU), 0).astype(jnp.float32)
 
     def profile(spot):
@@ -117,38 +158,24 @@
 
     def one_block(at):
         code = order[at]
-        block = lax.div(code, slots)
         slot = lax.rem(code, slots)
-        d = lax.div(block, cap)
-        k = lax.rem(block, cap)
-        keep = jnp.where(at < count, 1.0, 0.0)
-        base = pl.multiple_of(d * rows + k * per, per)
-        real = flat[pl.ds(base, chans, stride=2), :] * keep
-        imag = flat[pl.ds(base + 1, chans, stride=2), :] * keep
-        at_place = d * rows + cap * per + 2 * k
-        along_u = flat[pl.ds(at_place, 1), :]
-        along_v = flat[pl.ds(at_place + 1, 1), :]
-        spot_u = ALPHA * (scale * along_u - offset_u)
-        spot_v = ALPHA * (scale * along_v - offset_v)
-        turns = (1.0 / SU) * (scale * (along_u * along_l + along_v * along_m))
-        cosine, sine = cos_sin(turns)
-        turned_real = real * cosine - imag * sine
-        turned_imag = real * sine + imag * cosine
+        base = lax.div(code, slots) * chans
         lefts_real, lefts_imag, rights = [], [], []
         for c in range(chans):
-            left = profile(spot_u[c : c + 1]).reshape(SU // 16, 16, SU)
-            lefts_real.append((left * tiled(turned_real[c : c + 1])).reshape(SU, SU))
-            lefts_imag.append((left * tiled(turned_imag[c : c + 1])).reshape(SU, SU))
-            rights.append(profile(spot_v[c : c + 1]))
+            here = pl.ds(base + c, 1)
+            left = profile(spots_u[here, :]).reshape(SU // 16, 16, SU)
+            lefts_real.append((left * tiled(turns_real[here, :])).reshape(SU, SU))
+            lefts_imag.append((left * tiled(turns_imag[here, :])).reshape(SU, SU))
+            rights.append(profile(spots_v[here, :]))
         left = jnp.concatenate(
             [jnp.concatenate(lefts_real, axis=1), jnp.concatenate(lefts_imag, axis=1)], axis=0
         )
         right = jnp.concatenate(rights, axis=1)
-        grids[slot] += lax.dot_general(left, right, NT, preferred_element_type=jnp.float32)
+        return slot, lax.dot_general(left, right, NT, preferred_element_type=jnp.float32)
 
     def step(k, carry):
-        for i in range(UNROLL):
-            one_block(k * UNROLL + i)
+        for slot, part in [one_block(k * UNROLL + i) for i in range(UNROLL)]:
+            grids[slot] += part
         return carry
 
     lax.fori_loop(0, lax.div(count + UNROLL - 1, UNROLL), step, 0)
@@ -209,32 +236,40 @@
     devices = facets * groups
     slots = 2 * facets
     cap = max(2, 2 * held // groups)
-    per = 2 * chans
-    rows = -(-(cap * (per + 2) + 1) // 16) * 16
+    rows = -(-(2 * cap * (chans + 1) + 1) // 16) * 16
     half_rows = SU // chan_count
     norm = SU / math.sqrt(visibilities.shape[3] * held * facets * CH)
 
     packed = pl.pallas_call(
-        functools.partial(sort_kernel, (facets, groups, held, chans, cap, rows)),
-        out_shape=jax.ShapeDtypeStruct((devices, rows, SU), jnp.bfloat16),
-        in_specs=[SMEM, SMEM, VMEM, VMEM],
+        functools.partial(sort_kernel, (groups, held, chans, cap, rows)),
+        out_shape=jax.ShapeDtypeStruct((groups, rows, SU), jnp.bfloat16),
+        in_specs=[HBM] * 4,
         out_specs=VMEM,
         scratch_shapes=[
-            pltpu.VMEM((held * per, SU), jnp.float32),
+            pltpu.SMEM((1, held), jnp.int32),
+            pltpu.SMEM((1, held), jnp.int32),
+            pltpu.VMEM((held * 2 * chans, SU), jnp.bfloat16),
+            pltpu.VMEM((held * 2, SU), jnp.bfloat16),
+            pltpu.VMEM((held * 2 * chans, SU), jnp.float32),
             pltpu.VMEM((held * 2, SU), jnp.float32),
             pltpu.VMEM((groups, rows, SU), jnp.float32),
             pltpu.SMEM((groups,), jnp.int32),
+            pltpu.SemaphoreType.DMA((4,)),
         ],
-        compiler_params=PARAMS,
-        cost_estimate=pl.CostEstimate(flops=100_000, bytes_accessed=300_000, transcendentals=0),
+        compiler_params=ALONE,
+        cost_estimate=pl.CostEstimate(flops=100_000, bytes_accessed=100_000, transcendentals=0),
         name="sort_blocks",
     )(
         plane_index.reshape(1, held),
         block_group.T,
-        visibilities.reshape(held * per, SU),
+        visibilities.reshape(held * 2 * chans, SU),
         coords.reshape(held * 2, SU),
     )
-    gathered = lax.all_to_all(packed, ("facet", "bl"), split_axis=0, concat_axis=0, tiled=True)
+    here = lax.all_to_all(packed, "bl", split_axis=0, concat_axis=0, tiled=True)
+    blocks = [here] + [
+        lax.ppermute(here, "facet", [(f, (f + shift) % facets) for f in range(facets)])
+        for shift in range(1, facets)
+    ]
 
     own_table = tables.reshape(1, 2, 2 * SU, SU)
     perm = [(g, (g + 1) % groups) for g in range(groups)]
@@ -245,21 +280,21 @@
     grids = pl.pallas_call(
         functools.partial(grid_kernel, (facets, groups, chans, cap, rows)),
         out_shape=jax.ShapeDtypeStruct((slots, 2 * SU, SU), jnp.float32),
-        in_specs=[VMEM, SMEM, SMEM],
+        in_specs=[SMEM, SMEM] + [VMEM] * facets,
         out_specs=VMEM,
         scratch_shapes=[
-            pltpu.VMEM((devices * rows, SU), jnp.float32),
             pltpu.VMEM((devices, SU), jnp.int32),
             pltpu.SMEM((devices, SU), jnp.int32),
             pltpu.SMEM((devices * cap + UNROLL,), jnp.int32),
-            pltpu.SemaphoreType.DMA,
-        ],
+        ]
+        + [pltpu.VMEM((devices * cap * chans + 8, SU), jnp.float32)] * 4
+        + [pltpu.SemaphoreType.DMA],
         compiler_params=PARAMS,
         cost_estimate=pl.CostEstimate(
             flops=4_000_000_000, bytes_accessed=2_000_000, transcendentals=4_000_000
         ),
         name="grid",
-    )(gathered, offsets.transpose(0, 2, 1), facet_centre.T)
+    )(offsets.transpose(0, 2, 1), facet_centre.T, *blocks)
     mine, other = pl.pallas_call(
         functools.partial(table_kernel, slots, norm),
         out_shape=[jax.ShapeDtypeStruct((half_rows, 2 * SU), jnp.float32)] * 2,

time: 42.2 us -> 45.9 us (1.088)
  waiting for transfers between devices: 13.4 us -> 17.9 us
  starting transfers between devices: 14.1 us -> 14.9 us
  local copies, waits for them, and re-layouts: 3.94 us -> 3.19 us
  Pallas kernels: 10.2 us -> 9.54 us
    ppermute x0 -> x3, waiting for transfers between devices: none -> 11 us  [body(): lax.ppermute(here, 'facet', [(f, (f + shift) % facets) for f in range(fac...]
    ppermute x1, waiting for transfers between devices: 8.06 us -> 0.48 us  [body(): lax.ppermute(own_table, 'bl', perm)]
    all_to_all x1, starting transfers between devices: 8.44 us -> 3.87 us  [body(): here = lax.all_to_all(packed, 'bl', split_axis=0, concat_axis=0, tiled=True)]
    ppermute x0 -> x3, starting transfers between devices: none -> 4.05 us  [body(): lax.ppermute(here, 'facet', [(f, (f + shift) % facets) for f in range(fac...]
    all_to_all x1, waiting for transfers between devices: 1.91 us -> 5.19 us  [body(): here = lax.all_to_all(packed, 'bl', split_axis=0, concat_axis=0, tiled=True)]
    all_to_all x1, waiting for transfers between devices: 2.18 us -> 0.01 us  [body(): lax.all_to_all(spread, 'facet', split_axis=0, concat_axis=0, tiled=True)]
    ppermute x1, starting transfers between devices: 1.97 us -> 3.02 us  [body(): lax.ppermute(own_table, 'bl', perm)]
    pallas_call x1, Pallas kernels: 7.91 us -> 7.06 us  [body(): pl.pallas_call(functools.partial(grid_kernel, (facets, groups, chans, cap...]
  transfers between devices with their start and end apart: 4 -> 7, of which waited for: 4 -> 5; matrix products, arithmetic and copies ran while one was open for 0% -> 0% of each run, Pallas kernels for 19% -> 19%
where the time goes in v3:
time: 45.9 us; the launch traced here: 45.6 us
  waiting for transfers between devices  17.9 us (39%)
  starting transfers between devices  14.9 us (32%)
  Pallas kernels  9.54 us (21%)
  local copies, waits for them, and re-layouts  3.19 us (7%)
    ppermute x3, waiting for transfers between devices, body(): lax.ppermute(here, 'facet', [(f, (f + shift) % facets) for f in range(fac...  11 us
    pallas_call x1, Pallas kernels, body(): pl.pallas_call(functools.partial(grid_kernel, (facets, groups, chans, cap...  7.06 us
    all_to_all x1, waiting for transfers between devices, body(): here = lax.all_to_all(packed, 'bl', split_axis=0, concat_axis=0, tiled=True)  5.19 us
    ppermute x3, starting transfers between devices, body(): lax.ppermute(here, 'facet', [(f, (f + shift) % facets) for f in range(fac...  4.05 us
    all_to_all x1, starting transfers between devices, body(): here = lax.all_to_all(packed, 'bl', split_axis=0, concat_axis=0, tiled=True)  3.87 us
    all_to_all x1, starting transfers between devices, body(): lax.all_to_all(spread, 'facet', split_axis=0, concat_axis=0, tiled=True)  3.84 us
    ppermute x1, starting transfers between devices, body(): lax.ppermute(own_table, 'bl', perm)  3.02 us
    pallas_call x1, Pallas kernels, body(): pl.pallas_call(functools.partial(sort_kernel, (groups, held, chans, cap,...  1.44 us
  transfers between devices with their start and end apart: 7, of which 5 were waited for; matrix products, arithmetic and copies ran while one was open for 0% of the time, Pallas kernels for 19%

profile of v3, /device:TPU:0, one launch (start us, length us, event | category | flops | bytes accessed | tf_op | source)
XLA Modules:
  0.0 45.6 jit_solution(15836468838872145782)
XLA Ops:
  0.0 0.0 copy-start.3
  0.0 3.0 %collective-permute-start.3 = (bf16[1,2,256,128]{3,2,1,0:T(8,128)(2,1)}, bf16[1,2,256,128]{3,2,1,0:T(8,128)(2,1)S(1)}, u32[]{:S(2)}, u32[]{:S(2)}) collective-permute-start(bf16[1,2,256,128]{3,2,1,0:T(8,128)(2,1)} %bitcast.11), channel_id=1, source_target_pairs={{0,2},{2,4},{4,6},{6,0},{1,3},{3,5},{5,7},{7,1},{8,10},{10,12},{12... | collective-permute-start | bytes 393224 | tf_op jit(solution)/shard_map/ppermute | solution.py:276
  3.0 1.4 %sort_blocks.1 = bf16[4,48,128]{2,1,0:T(8,128)(2,1)} custom-call(s32[1,8]{1,0:T(1,128)} %bitcast.15, s32[1,8]{1,0:T(1,128)} %bitcast.16, bf16[64,128]{1,0:T(8,128)(2,1)} %bitcast.13, bf16[16,128]{1,0:T(8,128)(2,1)} %bitcast.14), custom_call_target="tpu_custom_call" | custom-call | flops 100000 | bytes 100000 | tf_op jit(solution)/shard_map/sort_blocks/pallas_call | solution.py:243
  4.5 3.9 %all-to-all-start = ((bf16[4,48,128]{2,1,0:T(8,128)(2,1)}), bf16[4,48,128]{2,1,0:T(8,128)(2,1)S(1)}, u32[]{:S(2)}, u32[]{:S(2)}) async-start(bf16[4,48,128]{2,1,0:T(8,128)(2,1)} %sort_blocks.1), calls=%async_computation | async-start | bytes 98304 | tf_op jit(solution)/shard_map/all_to_all | solution.py:268
  8.3 0.5 %collective-permute-done.3 = bf16[1,2,256,128]{3,2,1,0:T(8,128)(2,1)S(1)} collective-permute-done((bf16[1,2,256,128]{3,2,1,0:T(8,128)(2,1)}, bf16[1,2,256,128]{3,2,1,0:T(8,128)(2,1)S(1)}, u32[]{:S(2)}, u32[]{:S(2)}) %collective-permute-start.3) | collective-permute-done | bytes 131104 | tf_op jit(solution)/shard_map/ppermute | solution.py:276
  8.8 0.0 copy-done.3
  8.9 5.2 %all-to-all-done.refs_0_ = bf16[4,48,128]{2,1,0:T(8,128)(2,1)S(1)} async-done(((bf16[4,48,128]{2,1,0:T(8,128)(2,1)}), bf16[4,48,128]{2,1,0:T(8,128)(2,1)S(1)}, u32[]{:S(2)}, u32[]{:S(2)}) %all-to-all-start) | async-done | bytes 49184 | tf_op jit(solution)/shard_map/all_to_all | solution.py:268
  14.0 1.2 %broadcast_in_dim.2 = bf16[4,2,2,256,128]{4,3,2,1,0:T(8,128)(2,1)} broadcast(bf16[2,2,256,128]{3,2,1,0:T(8,128)(2,1)S(1)} %pad_maximum_fusion), dimensions={1,2,3,4} | broadcast | bytes 1310720 | tf_op jit(solution)/shard_map/broadcast_in_dim | solution.py:277
  15.2 0.0 copy-start
  15.2 3.8 %all-to-all-start.1 = ((bf16[4,2,2,256,128]{4,3,2,1,0:T(8,128)(2,1)}), bf16[4,2,2,256,128]{4,3,2,1,0:T(8,128)(2,1)S(1)}, u32[]{:S(2)}, u32[]{:S(2)}) async-start(bf16[4,2,2,256,128]{4,3,2,1,0:T(8,128)(2,1)} %broadcast_in_dim.2), calls=%async_computation.1 | async-start | bytes 2097152 | tf_op jit(solution)/shard_map/all_to_all | solution.py:278
  19.1 2.9 %collective-permute-start.2 = (bf16[4,48,128]{2,1,0:T(8,128)(2,1)S(1)}, bf16[4,48,128]{2,1,0:T(8,128)(2,1)S(1)}, u32[]{:S(2)}, u32[]{:S(2)}) collective-permute-start(bf16[4,48,128]{2,1,0:T(8,128)(2,1)S(1)} %all-to-all-done.refs_0_), channel_id=1, source_target_pairs={{0,24},{8,0},{16,8},{24,16},{1,25},{9,1},{17,9},{25,17},{2,26},{10... | collective-permute-start | bytes 147464 | tf_op jit(solution)/shard_map/ppermute | solution.py:270
  22.0 0.6 %collective-permute-start.1 = (bf16[4,48,128]{2,1,0:T(8,128)(2,1)S(1)}, bf16[4,48,128]{2,1,0:T(8,128)(2,1)S(1)}, u32[]{:S(2)}, u32[]{:S(2)}) collective-permute-start(bf16[4,48,128]{2,1,0:T(8,128)(2,1)S(1)} %all-to-all-done.refs_0_), channel_id=1, source_target_pairs={{0,16},{8,24},{16,0},{24,8},{1,17},{9,25},{17,1},{25,9},{2,18},{10... | collective-permute-start | bytes 147464 | tf_op jit(solution)/shard_map/ppermute | solution.py:270
  22.6 0.6 %collective-permute-start = (bf16[4,48,128]{2,1,0:T(8,128)(2,1)S(1)}, bf16[4,48,128]{2,1,0:T(8,128)(2,1)S(1)}, u32[]{:S(2)}, u32[]{:S(2)}) collective-permute-start(bf16[4,48,128]{2,1,0:T(8,128)(2,1)S(1)} %all-to-all-done.refs_0_), channel_id=1, source_target_pairs={{0,8},{8,16},{16,24},{24,0},{1,9},{9,17},{17,25},{25,1},{2,10},{10... | collective-permute-start | bytes 147464 | tf_op jit(solution)/shard_map/ppermute | solution.py:270
  23.1 9.5 %collective-permute-done.2.refs_3_ = bf16[4,48,128]{2,1,0:T(8,128)(2,1)S(1)} collective-permute-done((bf16[4,48,128]{2,1,0:T(8,128)(2,1)S(1)}, bf16[4,48,128]{2,1,0:T(8,128)(2,1)S(1)}, u32[]{:S(2)}, u32[]{:S(2)}) %collective-permute-start.2) | collective-permute-done | bytes 49184 | tf_op jit(solution)/shard_map/ppermute | solution.py:270
  32.7 0.0 collective-permute-done.1.refs_2_
  32.7 1.4 %collective-permute-done.refs_1_ = bf16[4,48,128]{2,1,0:T(8,128)(2,1)S(1)} collective-permute-done((bf16[4,48,128]{2,1,0:T(8,128)(2,1)S(1)}, bf16[4,48,128]{2,1,0:T(8,128)(2,1)S(1)}, u32[]{:S(2)}, u32[]{:S(2)}) %collective-permute-start) | collective-permute-done | bytes 49184 | tf_op jit(solution)/shard_map/ppermute | solution.py:270
  34.1 0.0 copy-start.1
  34.1 0.0 copy-done
  34.1 0.7 %copy-done.1 = f32[4,2]{0,1:T(2,128)S(1)} copy-done((f32[4,2]{0,1:T(2,128)S(1)}, f32[4,2]{0,1:T(2,128)}, u32[]{:S(2)}) %copy-start.1) | copy-done | bytes 56
  34.8 7.1 %grid.1.grids = f32[8,256,128]{2,1,0:T(8,128)S(1)} custom-call(s32[4,2,4]{2,1,0:T(2,128)S(1)} %bitcast.9, f32[2,4]{1,0:T(2,128)S(1)} %bitcast.10, bf16[4,48,128]{2,1,0:T(8,128)(2,1)S(1)} %all-to-all-done.refs_0_, bf16[4,48,128]{2,1,0:T(8,128)(2,1)S(1)} %collective-permute-done.refs_1_, bf16[4,48,128]{2,1,0:T(8,128)(2,1)S(1)} %collective-permute-done.1.refs_2_, ...), custom_call_target="tpu_custom_call" | custom-call | flops 4000000000 | bytes 2000000 | tf_op jit(solution)/shard_map/grid/pallas_call | solution.py:280
  41.8 0.0 copy-start.2
  41.9 0.0 all-to-all-done.1
  41.9 0.7 %copy-done.2 = f32[1,2,128]{2,1,0:T(2,128)S(1)} copy-done((f32[1,2,128]{2,1,0:T(2,128)S(1)}, f32[1,2,128]{2,1,0:T(2,128)}, u32[]{:S(2)}) %copy-start.2) | copy-done | bytes 1048
  42.5 1.0 %apply_tables.1 = (f32[64,256]{1,0:T(8,128)S(1)}, f32[64,256]{1,0:T(8,128)S(1)}) custom-call(f32[8,256,128]{2,1,0:T(8,128)S(1)} %grid.1.grids, bf16[8,2,256,128]{3,2,1,0:T(8,128)(2,1)S(1)} %bitcast.8, f32[1,2,128]{2,1,0:T(2,128)S(1)} %copy-done.2), custom_call_target="tpu_custom_call" | custom-call | flops 1000000000 | bytes 2000000 | tf_op jit(solution)/shard_map/apply_tables/pallas_call | solution.py:298
  43.6 0.1 collective-permute-start.4
  43.6 1.2 %collective-permute-done.4 = f32[64,256]{1,0:T(8,128)S(1)} collective-permute-done((f32[64,256]{1,0:T(8,128)S(1)}, f32[64,256]{1,0:T(8,128)S(1)}, u32[]{:S(2)}, u32[]{:S(2)}) %collective-permute-start.4) | collective-permute-done | bytes 65568 | tf_op jit(solution)/shard_map/ppermute | solution.py:313
  44.9 0.7 %reshape.24 = f32[1,1,64,2,128]{4,3,2,1,0:T(2,128)} reshape(f32[64,256]{1,0:T(8,128)S(1)} %add.3) | data formatting | bytes 131072 | tf_op jit(solution)/shard_map/reshape | solution.py:314
  (2 shorter events, 0.0 us)
Async XLA Ops:
  0.0 8.8 %copy-start.3 = (bf16[1,2,128,2,128]{4,3,2,1,0:T(2,128)(2,1)S(1)}, bf16[1,2,128,2,128]{4,3,2,1,0:T(2,128)(2,1)}, u32[]{:S(2)}) copy-start(bf16[1,2,128,2,128]{4,3,2,1,0:T(2,128)(2,1)} %param.14) | copy-start | bytes 393220
  0.0 8.8 %collective-permute-start.3 = (bf16[1,2,256,128]{3,2,1,0:T(8,128)(2,1)}, bf16[1,2,256,128]{3,2,1,0:T(8,128)(2,1)S(1)}, u32[]{:S(2)}, u32[]{:S(2)}) collective-permute-start(bf16[1,2,256,128]{3,2,1,0:T(8,128)(2,1)} %bitcast.11), channel_id=1, source_target_pairs={{0,2},{2,4},{4,6},{6,0},{1,3},{3,5},{5,7},{7,1},{8,10},{10,12},{12... | collective-permute-start | bytes 393224 | tf_op jit(solution)/shard_map/ppermute | solution.py:276
  4.5 9.6 %all-to-all-start = ((bf16[4,48,128]{2,1,0:T(8,128)(2,1)}), bf16[4,48,128]{2,1,0:T(8,128)(2,1)S(1)}, u32[]{:S(2)}, u32[]{:S(2)}) async-start(bf16[4,48,128]{2,1,0:T(8,128)(2,1)} %sort_blocks.1), calls=%async_computation | async-start | bytes 98304 | tf_op jit(solution)/shard_map/all_to_all | solution.py:268
  15.2 18.9 %copy-start = (s32[4,4,2]{1,2,0:T(2,128)S(1)}, s32[4,4,2]{1,2,0:T(2,128)}, u32[]{:S(2)}) copy-start(s32[4,4,2]{1,2,0:T(2,128)} %param.12) | copy-start | bytes 388
  15.2 26.6 %all-to-all-start.1 = ((bf16[4,2,2,256,128]{4,3,2,1,0:T(8,128)(2,1)}), bf16[4,2,2,256,128]{4,3,2,1,0:T(8,128)(2,1)S(1)}, u32[]{:S(2)}, u32[]{:S(2)}) async-start(bf16[4,2,2,256,128]{4,3,2,1,0:T(8,128)(2,1)} %broadcast_in_dim.2), calls=%async_computation.1 | async-start | bytes 2097152 | tf_op jit(solution)/shard_map/all_to_all | solution.py:278
  19.1 13.6 %collective-permute-start.2 = (bf16[4,48,128]{2,1,0:T(8,128)(2,1)S(1)}, bf16[4,48,128]{2,1,0:T(8,128)(2,1)S(1)}, u32[]{:S(2)}, u32[]{:S(2)}) collective-permute-start(bf16[4,48,128]{2,1,0:T(8,128)(2,1)S(1)} %all-to-all-done.refs_0_), channel_id=1, source_target_pairs={{0,24},{8,0},{16,8},{24,16},{1,25},{9,1},{17,9},{25,17},{2,26},{10... | collective-permute-start | bytes 147464 | tf_op jit(solution)/shard_map/ppermute | solution.py:270
  22.0 10.7 %collective-permute-start.1 = (bf16[4,48,128]{2,1,0:T(8,128)(2,1)S(1)}, bf16[4,48,128]{2,1,0:T(8,128)(2,1)S(1)}, u32[]{:S(2)}, u32[]{:S(2)}) collective-permute-start(bf16[4,48,128]{2,1,0:T(8,128)(2,1)S(1)} %all-to-all-done.refs_0_), channel_id=1, source_target_pairs={{0,16},{8,24},{16,0},{24,8},{1,17},{9,25},{17,1},{25,9},{2,18},{10... | collective-permute-start | bytes 147464 | tf_op jit(solution)/shard_map/ppermute | solution.py:270
  22.6 11.5 %collective-permute-start = (bf16[4,48,128]{2,1,0:T(8,128)(2,1)S(1)}, bf16[4,48,128]{2,1,0:T(8,128)(2,1)S(1)}, u32[]{:S(2)}, u32[]{:S(2)}) collective-permute-start(bf16[4,48,128]{2,1,0:T(8,128)(2,1)S(1)} %all-to-all-done.refs_0_), channel_id=1, source_target_pairs={{0,8},{8,16},{16,24},{24,0},{1,9},{9,17},{17,25},{25,1},{2,10},{10... | collective-permute-start | bytes 147464 | tf_op jit(solution)/shard_map/ppermute | solution.py:270
  34.1 0.7 %copy-start.1 = (f32[4,2]{0,1:T(2,128)S(1)}, f32[4,2]{0,1:T(2,128)}, u32[]{:S(2)}) copy-start(f32[4,2]{0,1:T(2,128)} %param.13) | copy-start | bytes 100
  41.8 0.7 %copy-start.2 = (f32[1,2,128]{2,1,0:T(2,128)S(1)}, f32[1,2,128]{2,1,0:T(2,128)}, u32[]{:S(2)}) copy-start(f32[1,2,128]{2,1,0:T(2,128)} %gain_ref.1) | copy-start | bytes 3076
  43.6 1.3 %collective-permute-start.4 = (f32[64,256]{1,0:T(8,128)S(1)}, f32[64,256]{1,0:T(8,128)S(1)}, u32[]{:S(2)}, u32[]{:S(2)}) collective-permute-start(f32[64,256]{1,0:T(8,128)S(1)} %get-tuple-element.8), channel_id=1, source_target_pairs={{0,1},{1,0},{2,3},{3,2},{4,5},{5,4},{6,7},{7,6},{8,9},{9,8},{10,11... | collective-permute-start | bytes 196616 | tf_op jit(solution)/shard_map/ppermute | solution.py:313

commit v4 on v3

--- a/solution.py
+++ b/solution.py
@@ -15,7 +15,6 @@
 UNROLL = 4
 NT = (((1,), (1,)), ((), ()))
 VMEM = pl.BlockSpec(memory_space=pltpu.VMEM)
-SMEM = pl.BlockSpec(memory_space=pltpu.SMEM)
 HBM = pl.BlockSpec(memory_space=pltpu.HBM)
 PARAMS = pltpu.CompilerParams(vmem_limit_bytes=32 * 1024 * 1024)
 ALONE = pltpu.CompilerParams(vmem_limit_bytes=60 * 1024 * 1024)
@@ -46,14 +45,24 @@
     return high, low
 
 
-def sort_kernel(sizes, plane_hbm, group_hbm, samples_hbm, place_hbm, out_ref, *scratch):
+def three_parts(x):
+    parts = []
+    for _ in range(3):
+        part = x.astype(jnp.bfloat16)
+        x = x - part.astype(jnp.float32)
+        parts.append(part.astype(jnp.float32))
+    return parts
+
+
+def sort_kernel(sizes, *refs):
     groups, held, chans, cap, rows = sizes
-    plane_ref, group_ref, samples_b, place_b, samples, place, sorted_, filled, sems = scratch
-    sources = (plane_hbm, group_hbm, samples_hbm, place_hbm)
-    targets = (plane_ref, group_ref, samples_b, place_b)
+    out_ref = refs[7]
+    plane_ref, group_ref, samples_b, place_b, offsets_ref, centre_ref, gain_ref = refs[8:15]
+    samples, place, sorted_, filled, sems = refs[15:]
+    facet = lax.axis_index("facet")
     copies = [
         pltpu.make_async_copy(source, target, sems.at[n])
-        for n, (source, target) in enumerate(zip(sources, targets))
+        for n, (source, target) in enumerate(zip(refs[:7], refs[8:15]))
     ]
     for copy in copies:
         copy.start()
@@ -65,6 +74,23 @@
     samples[...] = samples_b[...].astype(jnp.float32)
     place[...] = place_b[...].astype(jnp.float32)
     lane = lax.broadcasted_iota(jnp.int32, (1, SU), 1)
+    meta = 2 * cap * (chans + 1)
+    centre = [
+        part
+        for axis in range(2)
+        for part in three_parts(jnp.full((1, SU), centre_ref[axis, facet], jnp.float32))
+    ]
+    gains = three_parts(gain_ref[0])
+    for g in range(groups):
+        numbers = jnp.zeros((1, SU), jnp.float32)
+        for axis in range(2):
+            offset = offsets_ref[facet, axis, g].astype(jnp.float32)
+            numbers = jnp.where(lane == axis, offset, numbers)
+        for n, part in enumerate(centre):
+            numbers = jnp.where(lane == 2 + n, part, numbers)
+        sorted_[g, meta + 1 : meta + 2, :] = numbers
+        for n, part in enumerate(gains):
+            sorted_[g, meta + 2 + 2 * n : meta + 4 + 2 * n, :] = part
     for i in range(held):
         g = group_ref[0, i]
         k = filled[g]
@@ -74,14 +100,13 @@
             sorted_[g, pl.ds(at, chans), :] = samples[pl.ds(2 * chans * i + part, chans, stride=2), :]
             at = 2 * cap * chans + part * cap + k
             sorted_[g, pl.ds(at, 1), :] = place[2 * i + part : 2 * i + part + 1, :]
-        meta = 2 * cap * (chans + 1)
         sorted_[g, meta : meta + 1, :] += jnp.where(
             lane == k, (plane_ref[0, i] + 1).astype(jnp.float32), 0.0
         )
     out_ref[...] = sorted_[...].astype(jnp.bfloat16)
 
 
-def grid_kernel(sizes, offsets_ref, centre_ref, *refs):
+def grid_kernel(sizes, *refs):
     facets, groups, chans, cap, rows = sizes
     packed_refs = refs[:facets]
     grids = refs[facets]
@@ -89,23 +114,30 @@
     devices = facets * groups
     slots = 2 * facets
     lines = cap * chans
-    facet = lax.axis_index("facet")
+    meta_row = 2 * (lines + cap)
+    tail = meta_row // 16 * 16
     group = lax.axis_index("bl")
     chan = lax.axis_index("chan")
 
     for f in range(facets):
         for g in range(groups):
-            meta = packed_refs[f][g, rows - 16 : rows, :].astype(jnp.float32)
-            at = 2 * (lines + cap) - (rows - 16)
-            meta_v[f * groups + g : f * groups + g + 1, :] = meta[at : at + 1].astype(jnp.int32)
+            meta = packed_refs[f][g, tail : tail + 16, :].astype(jnp.float32)
+            meta_v[f * groups + g : f * groups + g + 1, :] = meta[
+                meta_row - tail : meta_row - tail + 1
+            ].astype(jnp.int32)
+            if f == 0 and g == 0:
+                numbers = meta[meta_row - tail + 1 : meta_row - tail + 2]
     copy = pltpu.make_async_copy(meta_v, meta_s, sem)
     copy.start()
     grids[...] = jnp.zeros_like(grids)
 
-    offset_u = offsets_ref[facet, 0, group].astype(jnp.float32)
-    offset_v = offsets_ref[facet, 1, group].astype(jnp.float32)
-    along_l = centre_ref[0, facet]
-    along_m = centre_ref[1, facet]
+    def number(n):
+        return jnp.broadcast_to(numbers[:, n : n + 1], (lines, SU))
+
+    offset_u = number(0)
+    offset_v = number(1)
+    along_l = number(2) + number(3) + number(4)
+    along_m = number(5) + number(6) + number(7)
     line = lax.broadcasted_iota(jnp.int32, (lines, SU), 0)
     channel = (chan * chans + lax.rem(line, chans)).astype(jnp.float32)
     scale = 1.0 + 0.01 * (channel - 0.5 * (CH - 1))
@@ -150,8 +182,8 @@
     cells = ALPHA * lax.broadcasted_iota(jnp.int32, (SU, SU), 0).astype(jnp.float32)
 
     def profile(spot):
-        apart = spot - cells
-        return jnp.exp2(-(apart * apart)).astype(jnp.bfloat16)
+        apart = (spot - cells).astype(jnp.bfloat16)
+        return jnp.exp2(-(apart * apart))
 
     def tiled(row):
         return jnp.broadcast_to(row, (16, SU)).astype(jnp.bfloat16)[None]
@@ -181,13 +213,29 @@
     lax.fori_loop(0, lax.div(count + UNROLL - 1, UNROLL), step, 0)
 
 
-def table_kernel(slots, norm, grids, tables, gain_ref, mine_ref, other_ref, table_f, total):
+def spread_kernel(own, shifted, out_ref):
     chan = lax.axis_index("chan")
+    for n, ref in enumerate((own, shifted)):
+        table = ref[chan]
+        for f in range(out_ref.shape[0]):
+            out_ref[f, n] = table
+
+
+def table_kernel(sizes, norm, grids, own, swapped, packed, mine_ref, other_ref, table_f, total):
+    slots, meta_row = sizes
+    chan = lax.axis_index("chan")
+    group = lax.axis_index("bl")
+    first = chan == 0
+
+    def parts(table):
+        table_f[...] = table
+        return table_f[pl.ds(0, SU, stride=2), :], table_f[pl.ds(1, SU, stride=2), :]
+
     result = jnp.zeros((SU, 2 * SU), jnp.float32)
     for s in range(slots):
-        table_f[...] = tables[s, 0].astype(jnp.float32)
-        u_real = table_f[pl.ds(0, SU, stride=2), :]
-        u_imag = table_f[pl.ds(1, SU, stride=2), :]
+        ours = own[s].astype(jnp.float32)
+        theirs = swapped[s].astype(jnp.float32)
+        u_real, u_imag = parts(jnp.where(first, ours, theirs))
         u_side = jnp.concatenate([u_real.T, u_imag.T], axis=1).astype(jnp.bfloat16)
         grid_real = grids[s, :SU, :]
         grid_imag = grids[s, SU:, :]
@@ -202,9 +250,7 @@
         half = jnp.dot(u_side, high, preferred_element_type=jnp.float32) + jnp.dot(
             u_side, low, preferred_element_type=jnp.float32
         )
-        table_f[...] = tables[s, 1].astype(jnp.float32)
-        v_real = table_f[pl.ds(0, SU, stride=2), :]
-        v_imag = table_f[pl.ds(1, SU, stride=2), :]
+        v_real, v_imag = parts(jnp.where(first, theirs, ours))
         v_side = jnp.concatenate(
             [
                 jnp.concatenate([v_real, v_imag], axis=1),
@@ -218,8 +264,12 @@
             + jnp.dot(high, v_side, preferred_element_type=jnp.float32)
             + jnp.dot(low, v_side, preferred_element_type=jnp.float32)
         )
-    gain_u = jnp.broadcast_to(gain_ref[0, 0:1, :], (SU, SU)).T
-    gains = gain_u * gain_ref[0, 1:2, :] * norm
+    tail = meta_row // 16 * 16
+    wide = packed[group, tail : tail + 16, :].astype(jnp.float32)
+    at = meta_row - tail + 2
+    gain = (wide[at : at + 2] + wide[at + 2 : at + 4]) + wide[at + 4 : at + 6]
+    gain_u = jnp.broadcast_to(gain[0:1], (SU, SU)).T
+    gains = gain_u * gain[1:2] * norm
     total[...] = result * jnp.concatenate([gains, gains], axis=1)
     half_rows = mine_ref.shape[0]
     mine_ref[...] = total[pl.ds(pl.multiple_of(chan * half_rows, half_rows), half_rows), :]
@@ -236,25 +286,29 @@
     devices = facets * groups
     slots = 2 * facets
     cap = max(2, 2 * held // groups)
-    rows = -(-(2 * cap * (chans + 1) + 1) // 16) * 16
+    meta_row = 2 * cap * (chans + 1)
+    rows = -(-(meta_row + 8) // 16) * 16
     half_rows = SU // chan_count
     norm = SU / math.sqrt(visibilities.shape[3] * held * facets * CH)
 
     packed = pl.pallas_call(
         functools.partial(sort_kernel, (groups, held, chans, cap, rows)),
         out_shape=jax.ShapeDtypeStruct((groups, rows, SU), jnp.bfloat16),
-        in_specs=[HBM] * 4,
+        in_specs=[HBM] * 7,
         out_specs=VMEM,
         scratch_shapes=[
             pltpu.SMEM((1, held), jnp.int32),
             pltpu.SMEM((1, held), jnp.int32),
             pltpu.VMEM((held * 2 * chans, SU), jnp.bfloat16),
             pltpu.VMEM((held * 2, SU), jnp.bfloat16),
+            pltpu.SMEM((facets, 2, groups), jnp.int32),
+            pltpu.SMEM((2, facets), jnp.float32),
+            pltpu.VMEM((1, 2, SU), jnp.float32),
             pltpu.VMEM((held * 2 * chans, SU), jnp.float32),
             pltpu.VMEM((held * 2, SU), jnp.float32),
             pltpu.VMEM((groups, rows, SU), jnp.float32),
             pltpu.SMEM((groups,), jnp.int32),
-            pltpu.SemaphoreType.DMA((4,)),
+            pltpu.SemaphoreType.DMA((7,)),
         ],
         compiler_params=ALONE,
         cost_estimate=pl.CostEstimate(flops=100_000, bytes_accessed=100_000, transcendentals=0),
@@ -264,6 +318,9 @@
         block_group.T,
         visibilities.reshape(held * 2 * chans, SU),
         coords.reshape(held * 2, SU),
+        offsets.transpose(0, 2, 1),
+        facet_centre.T,
+        antenna_gain,
     )
     here = lax.all_to_all(packed, "bl", split_axis=0, concat_axis=0, tiled=True)
     blocks = [here] + [
@@ -271,16 +328,26 @@
         for shift in range(1, facets)
     ]
 
-    own_table = tables.reshape(1, 2, 2 * SU, SU)
-    perm = [(g, (g + 1) % groups) for g in range(groups)]
-    both = jnp.concatenate([own_table, lax.ppermute(own_table, "bl", perm)], axis=0)
-    spread = jnp.broadcast_to(both[None], (facets,) + both.shape)
+    swap = [(c, 1 - c) for c in range(chan_count)]
+    own_table = tables.reshape(2, 2 * SU, SU)
+    shifted = lax.ppermute(own_table, "bl", [(g, (g + 1) % groups) for g in range(groups)])
+    spread = pl.pallas_call(
+        spread_kernel,
+        out_shape=jax.ShapeDtypeStruct((facets, 2, 2 * SU, SU), jnp.bfloat16),
+        in_specs=[VMEM, VMEM],
+        out_specs=VMEM,
+        compiler_params=PARAMS,
+        cost_estimate=pl.CostEstimate(flops=0, bytes_accessed=1_000_000, transcendentals=0),
+        name="spread_tables",
+    )(own_table, shifted)
     slot_tables = lax.all_to_all(spread, "facet", split_axis=0, concat_axis=0, tiled=True)
+    slot_tables = slot_tables.reshape(slots, 2 * SU, SU)
+    swapped_tables = lax.ppermute(slot_tables, "chan", swap)
 
     grids = pl.pallas_call(
         functools.partial(grid_kernel, (facets, groups, chans, cap, rows)),
         out_shape=jax.ShapeDtypeStruct((slots, 2 * SU, SU), jnp.float32),
-        in_specs=[SMEM, SMEM] + [VMEM] * facets,
+        in_specs=[VMEM] * facets,
         out_specs=VMEM,
         scratch_shapes=[
             pltpu.VMEM((devices, SU), jnp.int32),
@@ -294,11 +361,11 @@
             flops=4_000_000_000, bytes_accessed=2_000_000, transcendentals=4_000_000
         ),
         name="grid",
-    )(offsets.transpose(0, 2, 1), facet_centre.T, *blocks)
+    )(*blocks)
     mine, other = pl.pallas_call(
-        functools.partial(table_kernel, slots, norm),
+        functools.partial(table_kernel, (slots, meta_row), norm),
         out_shape=[jax.ShapeDtypeStruct((half_rows, 2 * SU), jnp.float32)] * 2,
-        in_specs=[VMEM, VMEM, VMEM],
+        in_specs=[VMEM] * 4,
         out_specs=[VMEM, VMEM],
         scratch_shapes=[
             pltpu.VMEM((2 * SU, SU), jnp.float32),
@@ -309,8 +376,8 @@
             flops=1_000_000_000, bytes_accessed=2_000_000, transcendentals=0
         ),
         name="apply_tables",
-    )(grids, slot_tables.reshape(slots, 2, 2 * SU, SU), antenna_gain)
-    arrived = lax.ppermute(other, "chan", [(c, 1 - c) for c in range(chan_count)])
+    )(grids, slot_tables, swapped_tables, here)
+    arrived = lax.ppermute(other, "chan", swap)
     return (mine + arrived).reshape(1, 1, half_rows, 2, SU)
 
 

time: 45.9 us -> 46.5 us (1.013)
  blocking collectives: 0 us -> 20.2 us
  waiting for transfers between devices: 17.9 us -> 8.72 us
  starting transfers between devices: 14.9 us -> 6.93 us
  local copies, waits for them, and re-layouts: 3.19 us -> 1.57 us
  Pallas kernels: 9.54 us -> 8.72 us
    all_to_all x0 -> x2, blocking collectives: none -> 20.2 us  [the longest x1 11.2 us: body(): lax.all_to_all(spread, 'facet', split_axis=0, concat_axis=0, tiled=True)]
    ppermute x3, waiting for transfers between devices: 11 us -> 1.75 us  [body(): lax.ppermute(here, 'facet', [(f, (f + shift) % facets) for f in range(fac...]
    all_to_all x2 -> x0, starting transfers between devices: 7.72 us -> none  [the longest x1 3.87 us: body(): here = lax.all_to_all(packed, 'bl', split_axis=0, concat_axis=0, tiled=True)]
    ppermute x2 -> x3, waiting for transfers between devices: 1.72 us -> 6.97 us  [the longest x1 5.73 us: body(): lax.ppermute(own_table, 'bl', [(g, (g + 1) % groups) for g in range(group...]
    all_to_all x2 -> x0, waiting for transfers between devices: 5.19 us -> none  [the longest x1 5.19 us: body(): here = lax.all_to_all(packed, 'bl', split_axis=0, concat_axis=0, tiled=True)]
    broadcast_in_dim x1 -> x0, local copies, waits for them, and re-layouts: 1.18 us -> none  [body(): spread = jnp.broadcast_to(both[None], (facets,) + both.shape)]
    pallas_call x1, Pallas kernels: 7.06 us -> 5.89 us  [body(): pl.pallas_call(functools.partial(grid_kernel, (facets, groups, chans, cap...]
    unnamed x8 -> x2, local copies, waits for them, and re-layouts: 1.35 us -> 0.9 us
  transfers between devices with their start and end apart: 7 -> 6, of which waited for: 5 -> 5; matrix products, arithmetic and copies ran while one was open for 0% -> 0% of each run, Pallas kernels for 19% -> 16%
where the time goes in v4:
time: 46.5 us; the launch traced here: 46.2 us
  blocking collectives  20.2 us (43%)
  waiting for transfers between devices  8.72 us (19%)
  Pallas kernels  8.72 us (19%)
  starting transfers between devices  6.93 us (15%)
  local copies, waits for them, and re-layouts  1.57 us (3%)
    all_to_all x1, blocking collectives, body(): lax.all_to_all(spread, 'facet', split_axis=0, concat_axis=0, tiled=True)  11.2 us
    all_to_all x1, blocking collectives, body(): here = lax.all_to_all(packed, 'bl', split_axis=0, concat_axis=0, tiled=True)  8.95 us
    pallas_call x1, Pallas kernels, body(): pl.pallas_call(functools.partial(grid_kernel, (facets, groups, chans, cap...  5.89 us
    ppermute x1, waiting for transfers between devices, body(): lax.ppermute(own_table, 'bl', [(g, (g + 1) % groups) for g in range(group...  5.73 us
    ppermute x3, starting transfers between devices, body(): lax.ppermute(here, 'facet', [(f, (f + shift) % facets) for f in range(fac...  3.84 us
    ppermute x1, starting transfers between devices, body(): lax.ppermute(own_table, 'bl', [(g, (g + 1) % groups) for g in range(group...  3.02 us
    ppermute x3, waiting for transfers between devices, body(): lax.ppermute(here, 'facet', [(f, (f + shift) % facets) for f in range(fac...  1.75 us
    pallas_call x1, Pallas kernels, body(): pl.pallas_call(functools.partial(sort_kernel, (groups, held, chans, cap,...  1.66 us
  transfers between devices with their start and end apart: 6, of which 5 were waited for; matrix products, arithmetic and copies ran while one was open for 0% of the time, Pallas kernels for 16%

profile of v4, /device:TPU:0, one launch (start us, length us, event | category | flops | bytes accessed | tf_op | source)
XLA Modules:
  0.0 46.2 jit_solution(10539972886668405772)
XLA Ops:
  0.0 3.0 %collective-permute-start.3 = (bf16[2,256,128]{2,1,0:T(8,128)(2,1)}, bf16[2,256,128]{2,1,0:T(8,128)(2,1)S(1)}, u32[]{:S(2)}, u32[]{:S(2)}) collective-permute-start(bf16[2,256,128]{2,1,0:T(8,128)(2,1)} %bitcast.10), channel_id=1, source_target_pairs={{0,2},{2,4},{4,6},{6,0},{1,3},{3,5},{5,7},{7,1},{8,10},{10,12},{12... | collective-permute-start | bytes 393224 | tf_op jit(solution)/shard_map/ppermute | solution.py:333
  3.0 5.7 %collective-permute-done.3.shifted = bf16[2,256,128]{2,1,0:T(8,128)(2,1)S(1)} collective-permute-done((bf16[2,256,128]{2,1,0:T(8,128)(2,1)}, bf16[2,256,128]{2,1,0:T(8,128)(2,1)S(1)}, u32[]{:S(2)}, u32[]{:S(2)}) %collective-permute-start.3) | collective-permute-done | bytes 131104 | tf_op jit(solution)/shard_map/ppermute | solution.py:333
  8.8 0.0 copy-start
  8.8 0.9 %copy-done = bf16[1,2,128,2,128]{4,3,2,1,0:T(2,128)(2,1)S(1)} copy-done((bf16[1,2,128,2,128]{4,3,2,1,0:T(2,128)(2,1)S(1)}, bf16[1,2,128,2,128]{4,3,2,1,0:T(2,128)(2,1)}, u32[]{:S(2)}) %copy-start) | copy-done | bytes 131096
  9.7 0.1 spread_tables.1
  9.7 11.2 %all_to_all.10 = bf16[4,2,256,128]{3,2,1,0:T(8,128)(2,1)S(1)} all-to-all(bf16[4,2,256,128]{3,2,1,0:T(8,128)(2,1)S(1)} %spread_tables.1), channel_id=1, replica_groups=mesh['facet'=4,'bl'=4,'chan'=2] {'facet'}, dimensions={0} | all-to-all | bytes 1048576 | tf_op jit(solution)/shard_map/all_to_all | solution.py:343
  21.0 0.0 collective-permute-start.4
  21.0 1.7 %sort_blocks.1 = bf16[4,48,128]{2,1,0:T(8,128)(2,1)} custom-call(s32[1,8]{1,0:T(1,128)} %bitcast.16, s32[1,8]{1,0:T(1,128)} %bitcast.17, bf16[64,128]{1,0:T(8,128)(2,1)} %bitcast.12, bf16[16,128]{1,0:T(8,128)(2,1)} %bitcast.13, s32[4,2,4]{2,1,0:T(2,128)} %bitcast.14, f32[2,4]{1,0:T(2,128)} %bitcast.15, f32[1,2,128]{2,1,0:T(2,128)} %refs_6_.1), custom_call_target="tpu_custom_call" | custom-call | flops 100000 | bytes 100000 | tf_op jit(solution)/shard_map/sort_blocks/pallas_call | solution.py:294
  22.6 9.0 %all_to_all.11.refs_0_.packed = bf16[4,48,128]{2,1,0:T(8,128)(2,1)S(1)} all-to-all(bf16[4,48,128]{2,1,0:T(8,128)(2,1)} %sort_blocks.1), channel_id=1, replica_groups=mesh['facet'=4,'bl'=4,'chan'=2] {'bl'}, dimensions={0} | all-to-all | bytes 98304 | tf_op jit(solution)/shard_map/all_to_all | solution.py:325
  31.6 0.9 %collective-permute-start = (bf16[4,48,128]{2,1,0:T(8,128)(2,1)S(1)}, bf16[4,48,128]{2,1,0:T(8,128)(2,1)S(1)}, u32[]{:S(2)}, u32[]{:S(2)}) collective-permute-start(bf16[4,48,128]{2,1,0:T(8,128)(2,1)S(1)} %all_to_all.11.refs_0_.packed), channel_id=1, source_target_pairs={{0,8},{8,16},{16,24},{24,0},{1,9},{9,17},{17,25},{25,1},{2,10},{10... | collective-permute-start | bytes 147464 | tf_op jit(solution)/shard_map/ppermute | solution.py:327
  32.5 0.6 %collective-permute-start.1 = (bf16[4,48,128]{2,1,0:T(8,128)(2,1)S(1)}, bf16[4,48,128]{2,1,0:T(8,128)(2,1)S(1)}, u32[]{:S(2)}, u32[]{:S(2)}) collective-permute-start(bf16[4,48,128]{2,1,0:T(8,128)(2,1)S(1)} %all_to_all.11.refs_0_.packed), channel_id=1, source_target_pairs={{0,16},{8,24},{16,0},{24,8},{1,17},{9,25},{17,1},{25,9},{2,18},{10... | collective-permute-start | bytes 147464 | tf_op jit(solution)/shard_map/ppermute | solution.py:327
  33.1 2.4 %collective-permute-start.2 = (bf16[4,48,128]{2,1,0:T(8,128)(2,1)S(1)}, bf16[4,48,128]{2,1,0:T(8,128)(2,1)S(1)}, u32[]{:S(2)}, u32[]{:S(2)}) collective-permute-start(bf16[4,48,128]{2,1,0:T(8,128)(2,1)S(1)} %all_to_all.11.refs_0_.packed), channel_id=1, source_target_pairs={{0,24},{8,0},{16,8},{24,16},{1,25},{9,1},{17,9},{25,17},{2,26},{10... | collective-permute-start | bytes 147464 | tf_op jit(solution)/shard_map/ppermute | solution.py:327
  35.4 1.2 %collective-permute-done.refs_1_ = bf16[4,48,128]{2,1,0:T(8,128)(2,1)S(1)} collective-permute-done((bf16[4,48,128]{2,1,0:T(8,128)(2,1)S(1)}, bf16[4,48,128]{2,1,0:T(8,128)(2,1)S(1)}, u32[]{:S(2)}, u32[]{:S(2)}) %collective-permute-start) | collective-permute-done | bytes 49184 | tf_op jit(solution)/shard_map/ppermute | solution.py:327
  36.6 0.5 %collective-permute-done.1.refs_2_ = bf16[4,48,128]{2,1,0:T(8,128)(2,1)S(1)} collective-permute-done((bf16[4,48,128]{2,1,0:T(8,128)(2,1)S(1)}, bf16[4,48,128]{2,1,0:T(8,128)(2,1)S(1)}, u32[]{:S(2)}, u32[]{:S(2)}) %collective-permute-start.1) | collective-permute-done | bytes 49184 | tf_op jit(solution)/shard_map/ppermute | solution.py:327
  37.1 0.1 collective-permute-done.2.refs_3_
  37.2 5.9 %grid.1.grids = f32[8,256,128]{2,1,0:T(8,128)S(1)} custom-call(bf16[4,48,128]{2,1,0:T(8,128)(2,1)S(1)} %all_to_all.11.refs_0_.packed, bf16[4,48,128]{2,1,0:T(8,128)(2,1)S(1)} %collective-permute-done.refs_1_, bf16[4,48,128]{2,1,0:T(8,128)(2,1)S(1)} %collective-permute-done.1.refs_2_, bf16[4,48,128]{2,1,0:T(8,128)(2,1)S(1)} %collective-permute-done.2.refs_3_), custom_call_target="tpu_custom_call" | custom-call | flops 4000000000 | bytes 2000000 | tf_op jit(solution)/shard_map/grid/pallas_call | solution.py:347
  43.1 0.0 collective-permute-done.4.swapped
  43.1 1.1 %apply_tables.1 = (f32[64,256]{1,0:T(8,128)S(1)}, f32[64,256]{1,0:T(8,128)S(1)}) custom-call(f32[8,256,128]{2,1,0:T(8,128)S(1)} %grid.1.grids, bf16[8,256,128]{2,1,0:T(8,128)(2,1)S(1)} %bitcast.9, bf16[8,256,128]{2,1,0:T(8,128)(2,1)S(1)} %collective-permute-done.4.swapped, bf16[4,48,128]{2,1,0:T(8,128)(2,1)S(1)} %all_to_all.11.refs_0_.packed), custom_call_target="tpu_custom_call" | custom-call | flops 1000000000 | bytes 2000000 | tf_op jit(solution)/shard_map/apply_tables/pallas_call | solution.py:365
  44.2 0.1 collective-permute-start.5
  44.3 1.2 %collective-permute-done.5 = f32[64,256]{1,0:T(8,128)S(1)} collective-permute-done((f32[64,256]{1,0:T(8,128)S(1)}, f32[64,256]{1,0:T(8,128)S(1)}, u32[]{:S(2)}, u32[]{:S(2)}) %collective-permute-start.5) | collective-permute-done | bytes 65568 | tf_op jit(solution)/shard_map/ppermute | solution.py:380
  45.5 0.7 %reshape.23 = f32[1,1,64,2,128]{4,3,2,1,0:T(2,128)} reshape(f32[64,256]{1,0:T(8,128)S(1)} %add.3) | data formatting | bytes 131072 | tf_op jit(solution)/shard_map/reshape | solution.py:381
  (1 shorter events, 0.0 us)
Async XLA Ops:
  0.0 8.8 %collective-permute-start.3 = (bf16[2,256,128]{2,1,0:T(8,128)(2,1)}, bf16[2,256,128]{2,1,0:T(8,128)(2,1)S(1)}, u32[]{:S(2)}, u32[]{:S(2)}) collective-permute-start(bf16[2,256,128]{2,1,0:T(8,128)(2,1)} %bitcast.10), channel_id=1, source_target_pairs={{0,2},{2,4},{4,6},{6,0},{1,3},{3,5},{5,7},{7,1},{8,10},{10,12},{12... | collective-permute-start | bytes 393224 | tf_op jit(solution)/shard_map/ppermute | solution.py:333
  8.8 0.9 %copy-start = (bf16[1,2,128,2,128]{4,3,2,1,0:T(2,128)(2,1)S(1)}, bf16[1,2,128,2,128]{4,3,2,1,0:T(2,128)(2,1)}, u32[]{:S(2)}) copy-start(bf16[1,2,128,2,128]{4,3,2,1,0:T(2,128)(2,1)} %param.14) | copy-start | bytes 393220
  21.0 22.1 %collective-permute-start.4 = (bf16[8,256,128]{2,1,0:T(8,128)(2,1)S(1)}, bf16[8,256,128]{2,1,0:T(8,128)(2,1)S(1)}, u32[]{:S(2)}, u32[]{:S(2)}) collective-permute-start(bf16[8,256,128]{2,1,0:T(8,128)(2,1)S(1)} %bitcast.8), channel_id=1, source_target_pairs={{0,1},{1,0},{2,3},{3,2},{4,5},{5,4},{6,7},{7,6},{8,9},{9,8},{10,11... | collective-permute-start | bytes 1572872 | tf_op jit(solution)/shard_map/ppermute | solution.py:345
  31.6 5.0 %collective-permute-start = (bf16[4,48,128]{2,1,0:T(8,128)(2,1)S(1)}, bf16[4,48,128]{2,1,0:T(8,128)(2,1)S(1)}, u32[]{:S(2)}, u32[]{:S(2)}) collective-permute-start(bf16[4,48,128]{2,1,0:T(8,128)(2,1)S(1)} %all_to_all.11.refs_0_.packed), channel_id=1, source_target_pairs={{0,8},{8,16},{16,24},{24,0},{1,9},{9,17},{17,25},{25,1},{2,10},{10... | collective-permute-start | bytes 147464 | tf_op jit(solution)/shard_map/ppermute | solution.py:327
  32.5 4.6 %collective-permute-start.1 = (bf16[4,48,128]{2,1,0:T(8,128)(2,1)S(1)}, bf16[4,48,128]{2,1,0:T(8,128)(2,1)S(1)}, u32[]{:S(2)}, u32[]{:S(2)}) collective-permute-start(bf16[4,48,128]{2,1,0:T(8,128)(2,1)S(1)} %all_to_all.11.refs_0_.packed), channel_id=1, source_target_pairs={{0,16},{8,24},{16,0},{24,8},{1,17},{9,25},{17,1},{25,9},{2,18},{10... | collective-permute-start | bytes 147464 | tf_op jit(solution)/shard_map/ppermute | solution.py:327
  33.1 4.1 %collective-permute-start.2 = (bf16[4,48,128]{2,1,0:T(8,128)(2,1)S(1)}, bf16[4,48,128]{2,1,0:T(8,128)(2,1)S(1)}, u32[]{:S(2)}, u32[]{:S(2)}) collective-permute-start(bf16[4,48,128]{2,1,0:T(8,128)(2,1)S(1)} %all_to_all.11.refs_0_.packed), channel_id=1, source_target_pairs={{0,24},{8,0},{16,8},{24,16},{1,25},{9,1},{17,9},{25,17},{2,26},{10... | collective-permute-start | bytes 147464 | tf_op jit(solution)/shard_map/ppermute | solution.py:327
  44.2 1.3 %collective-permute-start.5 = (f32[64,256]{1,0:T(8,128)S(1)}, f32[64,256]{1,0:T(8,128)S(1)}, u32[]{:S(2)}, u32[]{:S(2)}) collective-permute-start(f32[64,256]{1,0:T(8,128)S(1)} %get-tuple-element.8), channel_id=1, source_target_pairs={{0,1},{1,0},{2,3},{3,2},{4,5},{5,4},{6,7},{7,6},{8,9},{9,8},{10,11... | collective-permute-start | bytes 196616 | tf_op jit(solution)/shard_map/ppermute | solution.py:380

commit v5 on v4

--- a/solution.py
+++ b/solution.py
@@ -16,6 +16,7 @@
 NT = (((1,), (1,)), ((), ()))
 VMEM = pl.BlockSpec(memory_space=pltpu.VMEM)
 HBM = pl.BlockSpec(memory_space=pltpu.HBM)
+ANY = pl.BlockSpec(memory_space=pl.ANY)
 PARAMS = pltpu.CompilerParams(vmem_limit_bytes=32 * 1024 * 1024)
 ALONE = pltpu.CompilerParams(vmem_limit_bytes=60 * 1024 * 1024)
 
@@ -56,15 +57,17 @@
 
 def sort_kernel(sizes, *refs):
     groups, held, chans, cap, rows = sizes
-    out_ref = refs[7]
-    plane_ref, group_ref, samples_b, place_b, offsets_ref, centre_ref, gain_ref = refs[8:15]
-    samples, place, sorted_, filled, sems = refs[15:]
+    table_hbm, out_refs, half_hbm = refs[7], refs[8 : 8 + groups], refs[8 + groups]
+    targets = refs[9 + groups : 16 + groups]
+    plane_ref, group_ref, samples_b, place_b, offsets_ref, centre_ref, gain_ref = targets
+    samples, place, sorted_, filled, sems = refs[16 + groups :]
     facet = lax.axis_index("facet")
     copies = [
         pltpu.make_async_copy(source, target, sems.at[n])
-        for n, (source, target) in enumerate(zip(refs[:7], refs[8:15]))
+        for n, (source, target) in enumerate(zip(refs[:7], targets))
     ]
-    for copy in copies:
+    half = pltpu.make_async_copy(table_hbm.at[lax.axis_index("chan")], half_hbm, sems.at[7])
+    for copy in copies + [half]:
         copy.start()
     sorted_[...] = jnp.zeros_like(sorted_)
     for g in range(groups):
@@ -103,7 +106,10 @@
         sorted_[g, meta : meta + 1, :] += jnp.where(
             lane == k, (plane_ref[0, i] + 1).astype(jnp.float32), 0.0
         )
-    out_ref[...] = sorted_[...].astype(jnp.bfloat16)
+    for shift, out_ref in enumerate(out_refs):
+        g = lax.rem(lax.axis_index("bl") + shift, groups)
+        out_ref[...] = sorted_[g].astype(jnp.bfloat16)
+    half.wait()
 
 
 def grid_kernel(sizes, *refs):
@@ -116,15 +122,20 @@
     lines = cap * chans
     meta_row = 2 * (lines + cap)
     tail = meta_row // 16 * 16
+    facet = lax.axis_index("facet")
     group = lax.axis_index("bl")
     chan = lax.axis_index("chan")
 
+    lane = lax.broadcasted_iota(jnp.int32, (1, SU), 1)
     for f in range(facets):
         for g in range(groups):
             meta = packed_refs[f][g, tail : tail + 16, :].astype(jnp.float32)
-            meta_v[f * groups + g : f * groups + g + 1, :] = meta[
-                meta_row - tail : meta_row - tail + 1
-            ].astype(jnp.int32)
+            d = f * groups + g
+            plane = meta[meta_row - tail : meta_row - tail + 1].astype(jnp.int32) - 1
+            set_id = jnp.where(lax.rem(plane, groups) == group, 0, 1)
+            shift = lax.rem(facet - lax.div(plane, groups) + facets, facets)
+            code = (d * cap + lane) * slots + 2 * shift + set_id
+            meta_v[d : d + 1, :] = jnp.where(plane >= 0, code, -1)
             if f == 0 and g == 0:
                 numbers = meta[meta_row - tail + 1 : meta_row - tail + 2]
     copy = pltpu.make_async_copy(meta_v, meta_s, sem)
@@ -167,23 +178,20 @@
         ref[last : last + 8, :] = jnp.zeros((8, SU), jnp.float32)
     copy.wait()
 
-    def pick(d, count):
+    count = jnp.int32(0)
+    for d in range(devices):
         for k in range(cap):
-            plane = meta_s[d, k] - 1
-            set_id = jnp.where(lax.rem(plane, groups) == group, 0, 1)
-            order[count] = (d * cap + k) * slots + 2 * lax.div(plane, groups) + set_id
-            count = count + jnp.where(plane >= 0, 1, 0)
-        return count
-
-    count = lax.fori_loop(0, devices, pick, 0)
+            code = meta_s[d, k]
+            order[count] = code
+            count = count + jnp.where(code >= 0, 1, 0)
     for i in range(UNROLL):
         order[count + i] = devices * cap * slots
 
     cells = ALPHA * lax.broadcasted_iota(jnp.int32, (SU, SU), 0).astype(jnp.float32)
 
     def profile(spot):
-        apart = (spot - cells).astype(jnp.bfloat16)
-        return jnp.exp2(-(apart * apart))
+        apart = spot - cells
+        return jnp.exp2(-(apart * apart)).astype(jnp.bfloat16)
 
     def tiled(row):
         return jnp.broadcast_to(row, (16, SU)).astype(jnp.bfloat16)[None]
@@ -213,18 +221,34 @@
     lax.fori_loop(0, lax.div(count + UNROLL - 1, UNROLL), step, 0)
 
 
-def spread_kernel(own, shifted, out_ref):
+def copy_kernel(*refs):
+    for source, target in zip(refs[: len(refs) // 2], refs[len(refs) // 2 :]):
+        target[...] = source[...]
+
+
+def stack_kernel(count, *refs):
+    for n in range(count):
+        refs[-1][n] = refs[n][...]
+
+
+def local(kernel, operands, shapes, name, after=()):
+    return pl.pallas_call(
+        kernel,
+        out_shape=[jax.ShapeDtypeStruct(shape, jnp.bfloat16) for shape in shapes],
+        in_specs=[VMEM] * len(operands) + [ANY] * len(after),
+        out_specs=[VMEM] * len(shapes),
+        compiler_params=PARAMS,
+        cost_estimate=pl.CostEstimate(flops=0, bytes_accessed=400_000, transcendentals=0),
+        name=name,
+    )(*operands, *after)
+
+
+def table_kernel(sizes, norm, grids, packed, *refs):
+    facets, meta_row = sizes
+    slots = 2 * facets
+    ours, theirs = refs[:facets], refs[facets:slots]
+    mine_ref, other_ref, table_f, total = refs[slots:]
     chan = lax.axis_index("chan")
-    for n, ref in enumerate((own, shifted)):
-        table = ref[chan]
-        for f in range(out_ref.shape[0]):
-            out_ref[f, n] = table
-
-
-def table_kernel(sizes, norm, grids, own, swapped, packed, mine_ref, other_ref, table_f, total):
-    slots, meta_row = sizes
-    chan = lax.axis_index("chan")
-    group = lax.axis_index("bl")
     first = chan == 0
 
     def parts(table):
@@ -233,9 +257,12 @@
 
     result = jnp.zeros((SU, 2 * SU), jnp.float32)
     for s in range(slots):
-        ours = own[s].astype(jnp.float32)
-        theirs = swapped[s].astype(jnp.float32)
-        u_real, u_imag = parts(jnp.where(first, ours, theirs))
+        shift, set_id = divmod(s, 2)
+        fetched = ours[shift][set_id].astype(jnp.float32)
+        swapped = theirs[shift][set_id].astype(jnp.float32)
+        u_table = jnp.where(first, fetched, swapped)
+        v_table = jnp.where(first, swapped, fetched)
+        u_real, u_imag = parts(u_table)
         u_side = jnp.concatenate([u_real.T, u_imag.T], axis=1).astype(jnp.bfloat16)
         grid_real = grids[s, :SU, :]
         grid_imag = grids[s, SU:, :]
@@ -250,7 +277,7 @@
         half = jnp.dot(u_side, high, preferred_element_type=jnp.float32) + jnp.dot(
             u_side, low, preferred_element_type=jnp.float32
         )
-        v_real, v_imag = parts(jnp.where(first, theirs, ours))
+        v_real, v_imag = parts(v_table)
         v_side = jnp.concatenate(
             [
                 jnp.concatenate([v_real, v_imag], axis=1),
@@ -265,7 +292,7 @@
             + jnp.dot(low, v_side, preferred_element_type=jnp.float32)
         )
     tail = meta_row // 16 * 16
-    wide = packed[group, tail : tail + 16, :].astype(jnp.float32)
+    wide = packed[0, tail : tail + 16, :].astype(jnp.float32)
     at = meta_row - tail + 2
     gain = (wide[at : at + 2] + wide[at + 2 : at + 4]) + wide[at + 4 : at + 6]
     gain_u = jnp.broadcast_to(gain[0:1], (SU, SU)).T
@@ -274,6 +301,10 @@
     half_rows = mine_ref.shape[0]
     mine_ref[...] = total[pl.ds(pl.multiple_of(chan * half_rows, half_rows), half_rows), :]
     other_ref[...] = total[pl.ds(pl.multiple_of((1 - chan) * half_rows, half_rows), half_rows), :]
+
+
+def ring(size, shift):
+    return [(n, (n + shift) % size) for n in range(size)]
 
 
 def body(
@@ -291,11 +322,13 @@
     half_rows = SU // chan_count
     norm = SU / math.sqrt(visibilities.shape[3] * held * facets * CH)
 
-    packed = pl.pallas_call(
+    own_table = tables.reshape(2, 2 * SU, SU)
+    *pieces, own_half = pl.pallas_call(
         functools.partial(sort_kernel, (groups, held, chans, cap, rows)),
-        out_shape=jax.ShapeDtypeStruct((groups, rows, SU), jnp.bfloat16),
-        in_specs=[HBM] * 7,
-        out_specs=VMEM,
+        out_shape=[jax.ShapeDtypeStruct((rows, SU), jnp.bfloat16)] * groups
+        + [jax.ShapeDtypeStruct((2 * SU, SU), jnp.bfloat16)],
+        in_specs=[HBM] * 8,
+        out_specs=[VMEM] * groups + [HBM],
         scratch_shapes=[
             pltpu.SMEM((1, held), jnp.int32),
             pltpu.SMEM((1, held), jnp.int32),
@@ -308,7 +341,7 @@
             pltpu.VMEM((held * 2, SU), jnp.float32),
             pltpu.VMEM((groups, rows, SU), jnp.float32),
             pltpu.SMEM((groups,), jnp.int32),
-            pltpu.SemaphoreType.DMA((7,)),
+            pltpu.SemaphoreType.DMA((8,)),
         ],
         compiler_params=ALONE,
         cost_estimate=pl.CostEstimate(flops=100_000, bytes_accessed=100_000, transcendentals=0),
@@ -321,28 +354,28 @@
         offsets.transpose(0, 2, 1),
         facet_centre.T,
         antenna_gain,
-    )
-    here = lax.all_to_all(packed, "bl", split_axis=0, concat_axis=0, tiled=True)
-    blocks = [here] + [
-        lax.ppermute(here, "facet", [(f, (f + shift) % facets) for f in range(facets)])
-        for shift in range(1, facets)
+        own_table,
+    )
+    arrived = [
+        lax.ppermute(pieces[shift], "bl", ring(groups, shift)) for shift in range(1, groups)
     ]
-
-    swap = [(c, 1 - c) for c in range(chan_count)]
-    own_table = tables.reshape(2, 2 * SU, SU)
-    shifted = lax.ppermute(own_table, "bl", [(g, (g + 1) % groups) for g in range(groups)])
-    spread = pl.pallas_call(
-        spread_kernel,
-        out_shape=jax.ShapeDtypeStruct((facets, 2, 2 * SU, SU), jnp.bfloat16),
-        in_specs=[VMEM, VMEM],
-        out_specs=VMEM,
-        compiler_params=PARAMS,
-        cost_estimate=pl.CostEstimate(flops=0, bytes_accessed=1_000_000, transcendentals=0),
-        name="spread_tables",
-    )(own_table, shifted)
-    slot_tables = lax.all_to_all(spread, "facet", split_axis=0, concat_axis=0, tiled=True)
-    slot_tables = slot_tables.reshape(slots, 2 * SU, SU)
-    swapped_tables = lax.ppermute(slot_tables, "chan", swap)
+    shifted_half = lax.ppermute(own_half, "bl", ring(groups, 1))
+    kept, kept_half = local(
+        copy_kernel, [pieces[0], own_half], [(rows, SU), (2 * SU, SU)], "keep_own"
+    )
+    (here,) = local(
+        functools.partial(stack_kernel, groups), [kept, *arrived], [(groups, rows, SU)], "join"
+    )
+    shifts = range(1, facets)
+    blocks = [here] + [lax.ppermute(here, "facet", ring(facets, shift)) for shift in shifts]
+    (halves,) = local(
+        functools.partial(stack_kernel, 2),
+        [kept_half, shifted_half],
+        [(2, 2 * SU, SU)],
+        "stack_halves",
+        after=blocks[1:2],
+    )
+    fetched = [lax.ppermute(halves, "facet", ring(facets, shift)) for shift in shifts]
 
     grids = pl.pallas_call(
         functools.partial(grid_kernel, (facets, groups, chans, cap, rows)),
@@ -362,10 +395,14 @@
         ),
         name="grid",
     )(*blocks)
+    grids, halves, fetched = lax.optimization_barrier((grids, halves, fetched))
+    swap = ring(chan_count, 1)
+    ours = [halves, *fetched]
+    theirs = [lax.ppermute(table, "chan", swap) for table in ours]
     mine, other = pl.pallas_call(
-        functools.partial(table_kernel, (slots, meta_row), norm),
+        functools.partial(table_kernel, (facets, meta_row), norm),
         out_shape=[jax.ShapeDtypeStruct((half_rows, 2 * SU), jnp.float32)] * 2,
-        in_specs=[VMEM] * 4,
+        in_specs=[VMEM] * (2 + 2 * facets),
         out_specs=[VMEM, VMEM],
         scratch_shapes=[
             pltpu.VMEM((2 * SU, SU), jnp.float32),
@@ -376,9 +413,9 @@
             flops=1_000_000_000, bytes_accessed=2_000_000, transcendentals=0
         ),
         name="apply_tables",
-    )(grids, slot_tables, swapped_tables, here)
-    arrived = lax.ppermute(other, "chan", swap)
-    return (mine + arrived).reshape(1, 1, half_rows, 2, SU)
+    )(grids, here, *ours, *theirs)
+    summand = lax.ppermute(other, "chan", swap)
+    return (mine + summand).reshape(1, 1, half_rows, 2, SU)
 
 
 def solution(mesh):

time: 46.5 us -> 34.4 us (0.74)
  blocking collectives: 20.2 us -> 0 us
  starting transfers between devices: 6.93 us -> 18.1 us
  waiting for transfers between devices: 8.72 us -> 2.56 us
  Pallas kernels: 8.72 us -> 11.1 us
  local copies, waits for them, and re-layouts: 1.57 us -> 2.21 us
    all_to_all x2 -> x0, blocking collectives: 20.2 us -> none  [the longest x1 11.2 us: body(): lax.all_to_all(spread, 'facet', split_axis=0, concat_axis=0, tiled=True)]
    ppermute x6 -> x15, starting transfers between devices: 6.93 us -> 18.1 us  [the longest x3 5.51 us: body(): lax.ppermute(pieces[shift], 'bl', ring(groups, shift))]
    ppermute x6 -> x15, waiting for transfers between devices: 8.72 us -> 2.56 us  [the longest x4 1.02 us: body(): theirs = [lax.ppermute(table, 'chan', swap) for table in ours]]
    pallas_call x1, Pallas kernels: 1.66 us -> 3.79 us  [body(): pl.pallas_call(functools.partial(sort_kernel, (groups, held, chans, cap,...]
    unnamed x2 -> x4, local copies, waits for them, and re-layouts: 0.9 us -> 1.55 us
    pallas_call x2 -> x4, Pallas kernels: 1.17 us -> 1.12 us  [the longest x1 1.1 us: body(): pl.pallas_call(functools.partial(table_kernel, (facets, meta_row), norm),...]
  transfers between devices with their start and end apart: 6 -> 15, of which waited for: 5 -> 6; matrix products, arithmetic and copies ran while one was open for 0% -> 0% of each run, Pallas kernels for 16% -> 18%
where the time goes in v5:
time: 34.4 us; the launch traced here: 34.1 us
  starting transfers between devices  18.1 us (53%)
  Pallas kernels  11.1 us (32%)
  waiting for transfers between devices  2.56 us (7%)
  local copies, waits for them, and re-layouts  2.21 us (6%)
    pallas_call x1, Pallas kernels, body(): pl.pallas_call(functools.partial(grid_kernel, (facets, groups, chans, cap...  6.23 us
    ppermute x3, starting transfers between devices, body(): lax.ppermute(pieces[shift], 'bl', ring(groups, shift))  5.51 us
    ppermute x3, starting transfers between devices, body(): lax.ppermute(here, 'facet', ring(facets, shift))  4.47 us
    pallas_call x1, Pallas kernels, body(): pl.pallas_call(functools.partial(sort_kernel, (groups, held, chans, cap,...  3.79 us
    ppermute x3, starting transfers between devices, body(): lax.ppermute(halves, 'facet', ring(facets, shift))  3.6 us
    ppermute x1, starting transfers between devices, body(): shifted_half = lax.ppermute(own_half, 'bl', ring(groups, 1))  3.08 us
    unnamed x4, local copies, waits for them, and re-layouts  1.55 us
    pallas_call x1, Pallas kernels, body(): pl.pallas_call(functools.partial(table_kernel, (facets, meta_row), norm),...  1.1 us
  transfers between devices with their start and end apart: 15, of which 6 were waited for; matrix products, arithmetic and copies ran while one was open for 0% of the time, Pallas kernels for 18%

profile of v5, /device:TPU:0, one launch (start us, length us, event | category | flops | bytes accessed | tf_op | source)
XLA Modules:
  0.0 34.1 jit_solution(1892032267330610925)
XLA Ops:
  0.0 3.8 %sort_blocks.1 = (bf16[48,128]{1,0:T(8,128)(2,1)}, bf16[48,128]{1,0:T(8,128)(2,1)}, bf16[48,128]{1,0:T(8,128)(2,1)}, bf16[48,128]{1,0:T(8,128)(2,1)}, bf16[256,128]{1,0:T(8,128)(2,1)}) custom-call(s32[1,8]{1,0:T(1,128)} %bitcast.12, s32[1,8]{1,0:T(1,128)} %bitcast.13, bf16[64,128]{1,0:T(8,128)(2,1)} %bitcast.8, bf16[16,128]{1,0:T(8,128)(2,1)} %bitcast.9, ...), custom_call_target="tpu_custom_call" | custom-call | flops 100000 | bytes 100000 | tf_op jit(solution)/shard_map/sort_blocks/pallas_call | solution.py:326
  3.8 3.1 %collective-permute-start.6 = (bf16[256,128]{1,0:T(8,128)(2,1)}, bf16[256,128]{1,0:T(8,128)(2,1)S(1)}, u32[]{:S(2)}, u32[]{:S(2)}) collective-permute-start(bf16[256,128]{1,0:T(8,128)(2,1)} %get-tuple-element.20.refs_1_), channel_id=1, source_target_pairs={{0,2},{2,4},{4,6},{6,0},{1,3},{3,5},{5,7},{7,1},{8,10},{10,12},{12... | collective-permute-start | bytes 196616 | tf_op jit(solution)/shard_map/ppermute | solution.py:362
  6.9 1.6 %collective-permute-start = (bf16[48,128]{1,0:T(8,128)(2,1)}, bf16[48,128]{1,0:T(8,128)(2,1)S(1)}, u32[]{:S(2)}, u32[]{:S(2)}) collective-permute-start(bf16[48,128]{1,0:T(8,128)(2,1)} %get-tuple-element.22), channel_id=1, source_target_pairs={{0,2},{2,4},{4,6},{6,0},{1,3},{3,5},{5,7},{7,1},{8,10},{10,12},{12... | collective-permute-start | bytes 36872 | tf_op jit(solution)/shard_map/ppermute | solution.py:360
  8.5 1.1 %collective-permute-start.1 = (bf16[48,128]{1,0:T(8,128)(2,1)}, bf16[48,128]{1,0:T(8,128)(2,1)S(1)}, u32[]{:S(2)}, u32[]{:S(2)}) collective-permute-start(bf16[48,128]{1,0:T(8,128)(2,1)} %get-tuple-element.23), channel_id=1, source_target_pairs={{0,4},{2,6},{4,0},{6,2},{1,5},{3,7},{5,1},{7,3},{8,12},{10,14},{12... | collective-permute-start | bytes 36872 | tf_op jit(solution)/shard_map/ppermute | solution.py:360
  9.5 2.9 %collective-permute-start.2 = (bf16[48,128]{1,0:T(8,128)(2,1)}, bf16[48,128]{1,0:T(8,128)(2,1)S(1)}, u32[]{:S(2)}, u32[]{:S(2)}) collective-permute-start(bf16[48,128]{1,0:T(8,128)(2,1)} %get-tuple-element.24), channel_id=1, source_target_pairs={{0,6},{2,0},{4,2},{6,4},{1,7},{3,1},{5,3},{7,5},{8,14},{10,8},{12,... | collective-permute-start | bytes 36872 | tf_op jit(solution)/shard_map/ppermute | solution.py:360
  12.4 0.0 copy-start
  12.4 0.8 %copy-done = bf16[256,128]{1,0:T(8,128)(2,1)S(1)} copy-done((bf16[256,128]{1,0:T(8,128)(2,1)S(1)}, bf16[256,128]{1,0:T(8,128)(2,1)}, u32[]{:S(2)}) %copy-start) | copy-done | bytes 65560
  13.2 0.0 copy-start.1
  13.2 0.7 %copy-done.1 = bf16[48,128]{1,0:T(8,128)(2,1)S(1)} copy-done((bf16[48,128]{1,0:T(8,128)(2,1)S(1)}, bf16[48,128]{1,0:T(8,128)(2,1)}, u32[]{:S(2)}) %copy-start.1) | copy-done | bytes 12312
  13.9 0.0 collective-permute-done.refs_1_
  14.0 0.0 collective-permute-done.1.refs_2_
  14.0 0.0 collective-permute-done.2.refs_3_
  14.0 1.5 %collective-permute-start.3 = (bf16[4,48,128]{2,1,0:T(8,128)(2,1)S(1)}, bf16[4,48,128]{2,1,0:T(8,128)(2,1)S(1)}, u32[]{:S(2)}, u32[]{:S(2)}) collective-permute-start(bf16[4,48,128]{2,1,0:T(8,128)(2,1)S(1)} %join.1.refs_0_.packed), channel_id=1, source_target_pairs={{0,8},{8,16},{16,24},{24,0},{1,9},{9,17},{17,25},{25,1},{2,10},{10... | collective-permute-start | bytes 147464 | tf_op jit(solution)/shard_map/ppermute | solution.py:370
  15.5 1.4 %collective-permute-start.5 = (bf16[4,48,128]{2,1,0:T(8,128)(2,1)S(1)}, bf16[4,48,128]{2,1,0:T(8,128)(2,1)S(1)}, u32[]{:S(2)}, u32[]{:S(2)}) collective-permute-start(bf16[4,48,128]{2,1,0:T(8,128)(2,1)S(1)} %join.1.refs_0_.packed), channel_id=1, source_target_pairs={{0,24},{8,0},{16,8},{24,16},{1,25},{9,1},{17,9},{25,17},{2,26},{10... | collective-permute-start | bytes 147464 | tf_op jit(solution)/shard_map/ppermute | solution.py:370
  17.0 1.5 %collective-permute-start.4 = (bf16[4,48,128]{2,1,0:T(8,128)(2,1)S(1)}, bf16[4,48,128]{2,1,0:T(8,128)(2,1)S(1)}, u32[]{:S(2)}, u32[]{:S(2)}) collective-permute-start(bf16[4,48,128]{2,1,0:T(8,128)(2,1)S(1)} %join.1.refs_0_.packed), channel_id=1, source_target_pairs={{0,16},{8,24},{16,0},{24,8},{1,17},{9,25},{17,1},{25,9},{2,18},{10... | collective-permute-start | bytes 147464 | tf_op jit(solution)/shard_map/ppermute | solution.py:370
  18.5 0.5 %collective-permute-done.3.refs_1_.refs_2_ = bf16[4,48,128]{2,1,0:T(8,128)(2,1)S(1)} collective-permute-done((bf16[4,48,128]{2,1,0:T(8,128)(2,1)S(1)}, bf16[4,48,128]{2,1,0:T(8,128)(2,1)S(1)}, u32[]{:S(2)}, u32[]{:S(2)}) %collective-permute-start.3) | collective-permute-done | bytes 49184 | tf_op jit(solution)/shard_map/ppermute | solution.py:370
  19.0 0.0 collective-permute-done.6.refs_1_
  19.0 1.6 %collective-permute-start.9 = (bf16[2,256,128]{2,1,0:T(8,128)(2,1)S(1)}, bf16[2,256,128]{2,1,0:T(8,128)(2,1)S(1)}, u32[]{:S(2)}, u32[]{:S(2)}) collective-permute-start(bf16[2,256,128]{2,1,0:T(8,128)(2,1)S(1)} %stack_halves.1.refs_0_), channel_id=1, source_target_pairs={{0,24},{8,0},{16,8},{24,16},{1,25},{9,1},{17,9},{25,17},{2,26},{10... | collective-permute-start | bytes 393224 | tf_op jit(solution)/shard_map/ppermute | solution.py:378
  20.6 0.5 %collective-permute-start.8 = (bf16[2,256,128]{2,1,0:T(8,128)(2,1)S(1)}, bf16[2,256,128]{2,1,0:T(8,128)(2,1)S(1)}, u32[]{:S(2)}, u32[]{:S(2)}) collective-permute-start(bf16[2,256,128]{2,1,0:T(8,128)(2,1)S(1)} %stack_halves.1.refs_0_), channel_id=1, source_target_pairs={{0,16},{8,24},{16,0},{24,8},{1,17},{9,25},{17,1},{25,9},{2,18},{10... | collective-permute-start | bytes 393224 | tf_op jit(solution)/shard_map/ppermute | solution.py:378
  21.2 1.5 %collective-permute-start.7 = (bf16[2,256,128]{2,1,0:T(8,128)(2,1)S(1)}, bf16[2,256,128]{2,1,0:T(8,128)(2,1)S(1)}, u32[]{:S(2)}, u32[]{:S(2)}) collective-permute-start(bf16[2,256,128]{2,1,0:T(8,128)(2,1)S(1)} %stack_halves.1.refs_0_), channel_id=1, source_target_pairs={{0,8},{8,16},{16,24},{24,0},{1,9},{9,17},{17,25},{25,1},{2,10},{10... | collective-permute-start | bytes 393224 | tf_op jit(solution)/shard_map/ppermute | solution.py:378
  22.6 0.0 collective-permute-done.5.refs_3_
  22.6 0.0 collective-permute-done.4.refs_2_
  22.6 6.2 %grid.1.grids = f32[8,256,128]{2,1,0:T(8,128)S(1)} custom-call(bf16[4,48,128]{2,1,0:T(8,128)(2,1)S(1)} %join.1.refs_0_.packed, bf16[4,48,128]{2,1,0:T(8,128)(2,1)S(1)} %collective-permute-done.3.refs_1_.refs_2_, bf16[4,48,128]{2,1,0:T(8,128)(2,1)S(1)} %collective-permute-done.4.refs_2_, bf16[4,48,128]{2,1,0:T(8,128)(2,1)S(1)} %collective-permute-done.5.refs_3_), custom_call_target="tpu_custom_call" | custom-call | flops 4000000000 | bytes 2000000 | tf_op jit(solution)/shard_map/grid/pallas_call | solution.py:380
  28.9 0.0 collective-permute-done.9.refs_3_
  28.9 0.0 collective-permute-done.8.refs_2_
  28.9 0.0 collective-permute-done.7.refs_1_
  28.9 0.1 collective-permute-start.10
  29.0 0.5 %collective-permute-start.11 = (bf16[2,256,128]{2,1,0:T(8,128)(2,1)S(1)}, bf16[2,256,128]{2,1,0:T(8,128)(2,1)S(1)}, u32[]{:S(2)}, u32[]{:S(2)}) collective-permute-start(bf16[2,256,128]{2,1,0:T(8,128)(2,1)S(1)} %collective-permute-done.7.refs_1_), channel_id=1, source_target_pairs={{0,1},{1,0},{2,3},{3,2},{4,5},{5,4},{6,7},{7,6},{8,9},{9,8},{10,11... | collective-permute-start | bytes 393224 | tf_op jit(solution)/shard_map/ppermute | solution.py:401
  29.5 0.1 collective-permute-start.12
  29.6 0.4 %collective-permute-start.13 = (bf16[2,256,128]{2,1,0:T(8,128)(2,1)S(1)}, bf16[2,256,128]{2,1,0:T(8,128)(2,1)S(1)}, u32[]{:S(2)}, u32[]{:S(2)}) collective-permute-start(bf16[2,256,128]{2,1,0:T(8,128)(2,1)S(1)} %collective-permute-done.9.refs_3_), channel_id=1, source_target_pairs={{0,1},{1,0},{2,3},{3,2},{4,5},{5,4},{6,7},{7,6},{8,9},{9,8},{10,11... | collective-permute-start | bytes 393224 | tf_op jit(solution)/shard_map/ppermute | solution.py:401
  30.0 0.3 collective-permute-done.10.refs_4_
  30.3 0.2 collective-permute-done.11.refs_5_
  30.5 0.3 collective-permute-done.12.refs_6_
  30.8 0.2 collective-permute-done.13.refs_7_
  31.0 1.1 %apply_tables.1 = (f32[64,256]{1,0:T(8,128)S(1)}, f32[64,256]{1,0:T(8,128)S(1)}) custom-call(f32[8,256,128]{2,1,0:T(8,128)S(1)} %grid.1.grids, bf16[4,48,128]{2,1,0:T(8,128)(2,1)S(1)} %join.1.refs_0_.packed, bf16[2,256,128]{2,1,0:T(8,128)(2,1)S(1)} %stack_halves.1.refs_0_, bf16[2,256,128]{2,1,0:T(8,128)(2,1)S(1)} %collective-permute-done.7.refs_1_, ...), custom_call_target="tpu_custom_call" | custom-call | flops 1000000000 | bytes 2000000 | tf_op jit(solution)/shard_map/apply_tables/pallas_call | solution.py:402
  32.1 0.4 %collective-permute-start.14 = (f32[64,256]{1,0:T(8,128)S(1)}, f32[64,256]{1,0:T(8,128)S(1)}, u32[]{:S(2)}, u32[]{:S(2)}) collective-permute-start(f32[64,256]{1,0:T(8,128)S(1)} %get-tuple-element.32), channel_id=1, source_target_pairs={{0,1},{1,0},{2,3},{3,2},{4,5},{5,4},{6,7},{7,6},{8,9},{9,8},{10,11... | collective-permute-start | bytes 196616 | tf_op jit(solution)/shard_map/ppermute | solution.py:417
  32.5 0.9 %collective-permute-done.14 = f32[64,256]{1,0:T(8,128)S(1)} collective-permute-done((f32[64,256]{1,0:T(8,128)S(1)}, f32[64,256]{1,0:T(8,128)S(1)}, u32[]{:S(2)}, u32[]{:S(2)}) %collective-permute-start.14) | collective-permute-done | bytes 65568 | tf_op jit(solution)/shard_map/ppermute | solution.py:417
  33.5 0.7 %reshape.19 = f32[1,1,64,2,128]{4,3,2,1,0:T(2,128)} reshape(f32[64,256]{1,0:T(8,128)S(1)} %add.3) | data formatting | bytes 131072 | tf_op jit(solution)/shard_map/reshape | solution.py:418
  (4 shorter events, 0.0 us)
Async XLA Ops:
  3.8 15.2 %collective-permute-start.6 = (bf16[256,128]{1,0:T(8,128)(2,1)}, bf16[256,128]{1,0:T(8,128)(2,1)S(1)}, u32[]{:S(2)}, u32[]{:S(2)}) collective-permute-start(bf16[256,128]{1,0:T(8,128)(2,1)} %get-tuple-element.20.refs_1_), channel_id=1, source_target_pairs={{0,2},{2,4},{4,6},{6,0},{1,3},{3,5},{5,7},{7,1},{8,10},{10,12},{12... | collective-permute-start | bytes 196616 | tf_op jit(solution)/shard_map/ppermute | solution.py:362
  6.9 7.1 %collective-permute-start = (bf16[48,128]{1,0:T(8,128)(2,1)}, bf16[48,128]{1,0:T(8,128)(2,1)S(1)}, u32[]{:S(2)}, u32[]{:S(2)}) collective-permute-start(bf16[48,128]{1,0:T(8,128)(2,1)} %get-tuple-element.22), channel_id=1, source_target_pairs={{0,2},{2,4},{4,6},{6,0},{1,3},{3,5},{5,7},{7,1},{8,10},{10,12},{12... | collective-permute-start | bytes 36872 | tf_op jit(solution)/shard_map/ppermute | solution.py:360
  8.5 5.5 %collective-permute-start.1 = (bf16[48,128]{1,0:T(8,128)(2,1)}, bf16[48,128]{1,0:T(8,128)(2,1)S(1)}, u32[]{:S(2)}, u32[]{:S(2)}) collective-permute-start(bf16[48,128]{1,0:T(8,128)(2,1)} %get-tuple-element.23), channel_id=1, source_target_pairs={{0,4},{2,6},{4,0},{6,2},{1,5},{3,7},{5,1},{7,3},{8,12},{10,14},{12... | collective-permute-start | bytes 36872 | tf_op jit(solution)/shard_map/ppermute | solution.py:360
  9.5 4.5 %collective-permute-start.2 = (bf16[48,128]{1,0:T(8,128)(2,1)}, bf16[48,128]{1,0:T(8,128)(2,1)S(1)}, u32[]{:S(2)}, u32[]{:S(2)}) collective-permute-start(bf16[48,128]{1,0:T(8,128)(2,1)} %get-tuple-element.24), channel_id=1, source_target_pairs={{0,6},{2,0},{4,2},{6,4},{1,7},{3,1},{5,3},{7,5},{8,14},{10,8},{12,... | collective-permute-start | bytes 36872 | tf_op jit(solution)/shard_map/ppermute | solution.py:360
  12.4 0.8 %copy-start = (bf16[256,128]{1,0:T(8,128)(2,1)S(1)}, bf16[256,128]{1,0:T(8,128)(2,1)}, u32[]{:S(2)}) copy-start(bf16[256,128]{1,0:T(8,128)(2,1)} %get-tuple-element.20.refs_1_) | copy-start | bytes 196612
  13.2 0.7 %copy-start.1 = (bf16[48,128]{1,0:T(8,128)(2,1)S(1)}, bf16[48,128]{1,0:T(8,128)(2,1)}, u32[]{:S(2)}) copy-start(bf16[48,128]{1,0:T(8,128)(2,1)} %get-tuple-element.19.refs_0_) | copy-start | bytes 36868
  14.0 5.0 %collective-permute-start.3 = (bf16[4,48,128]{2,1,0:T(8,128)(2,1)S(1)}, bf16[4,48,128]{2,1,0:T(8,128)(2,1)S(1)}, u32[]{:S(2)}, u32[]{:S(2)}) collective-permute-start(bf16[4,48,128]{2,1,0:T(8,128)(2,1)S(1)} %join.1.refs_0_.packed), channel_id=1, source_target_pairs={{0,8},{8,16},{16,24},{24,0},{1,9},{9,17},{17,25},{25,1},{2,10},{10... | collective-permute-start | bytes 147464 | tf_op jit(solution)/shard_map/ppermute | solution.py:370
  15.5 7.1 %collective-permute-start.5 = (bf16[4,48,128]{2,1,0:T(8,128)(2,1)S(1)}, bf16[4,48,128]{2,1,0:T(8,128)(2,1)S(1)}, u32[]{:S(2)}, u32[]{:S(2)}) collective-permute-start(bf16[4,48,128]{2,1,0:T(8,128)(2,1)S(1)} %join.1.refs_0_.packed), channel_id=1, source_target_pairs={{0,24},{8,0},{16,8},{24,16},{1,25},{9,1},{17,9},{25,17},{2,26},{10... | collective-permute-start | bytes 147464 | tf_op jit(solution)/shard_map/ppermute | solution.py:370
  17.0 5.7 %collective-permute-start.4 = (bf16[4,48,128]{2,1,0:T(8,128)(2,1)S(1)}, bf16[4,48,128]{2,1,0:T(8,128)(2,1)S(1)}, u32[]{:S(2)}, u32[]{:S(2)}) collective-permute-start(bf16[4,48,128]{2,1,0:T(8,128)(2,1)S(1)} %join.1.refs_0_.packed), channel_id=1, source_target_pairs={{0,16},{8,24},{16,0},{24,8},{1,17},{9,25},{17,1},{25,9},{2,18},{10... | collective-permute-start | bytes 147464 | tf_op jit(solution)/shard_map/ppermute | solution.py:370
  19.0 9.8 %collective-permute-start.9 = (bf16[2,256,128]{2,1,0:T(8,128)(2,1)S(1)}, bf16[2,256,128]{2,1,0:T(8,128)(2,1)S(1)}, u32[]{:S(2)}, u32[]{:S(2)}) collective-permute-start(bf16[2,256,128]{2,1,0:T(8,128)(2,1)S(1)} %stack_halves.1.refs_0_), channel_id=1, source_target_pairs={{0,24},{8,0},{16,8},{24,16},{1,25},{9,1},{17,9},{25,17},{2,26},{10... | collective-permute-start | bytes 393224 | tf_op jit(solution)/shard_map/ppermute | solution.py:378
  20.6 8.3 %collective-permute-start.8 = (bf16[2,256,128]{2,1,0:T(8,128)(2,1)S(1)}, bf16[2,256,128]{2,1,0:T(8,128)(2,1)S(1)}, u32[]{:S(2)}, u32[]{:S(2)}) collective-permute-start(bf16[2,256,128]{2,1,0:T(8,128)(2,1)S(1)} %stack_halves.1.refs_0_), channel_id=1, source_target_pairs={{0,16},{8,24},{16,0},{24,8},{1,17},{9,25},{17,1},{25,9},{2,18},{10... | collective-permute-start | bytes 393224 | tf_op jit(solution)/shard_map/ppermute | solution.py:378
  21.2 7.8 %collective-permute-start.7 = (bf16[2,256,128]{2,1,0:T(8,128)(2,1)S(1)}, bf16[2,256,128]{2,1,0:T(8,128)(2,1)S(1)}, u32[]{:S(2)}, u32[]{:S(2)}) collective-permute-start(bf16[2,256,128]{2,1,0:T(8,128)(2,1)S(1)} %stack_halves.1.refs_0_), channel_id=1, source_target_pairs={{0,8},{8,16},{16,24},{24,0},{1,9},{9,17},{17,25},{25,1},{2,10},{10... | collective-permute-start | bytes 393224 | tf_op jit(solution)/shard_map/ppermute | solution.py:378
  28.9 1.4 %collective-permute-start.10 = (bf16[2,256,128]{2,1,0:T(8,128)(2,1)S(1)}, bf16[2,256,128]{2,1,0:T(8,128)(2,1)S(1)}, u32[]{:S(2)}, u32[]{:S(2)}) collective-permute-start(bf16[2,256,128]{2,1,0:T(8,128)(2,1)S(1)} %stack_halves.1.refs_0_), channel_id=1, source_target_pairs={{0,1},{1,0},{2,3},{3,2},{4,5},{5,4},{6,7},{7,6},{8,9},{9,8},{10,11... | collective-permute-start | bytes 393224 | tf_op jit(solution)/shard_map/ppermute | solution.py:401
  29.0 1.5 %collective-permute-start.11 = (bf16[2,256,128]{2,1,0:T(8,128)(2,1)S(1)}, bf16[2,256,128]{2,1,0:T(8,128)(2,1)S(1)}, u32[]{:S(2)}, u32[]{:S(2)}) collective-permute-start(bf16[2,256,128]{2,1,0:T(8,128)(2,1)S(1)} %collective-permute-done.7.refs_1_), channel_id=1, source_target_pairs={{0,1},{1,0},{2,3},{3,2},{4,5},{5,4},{6,7},{7,6},{8,9},{9,8},{10,11... | collective-permute-start | bytes 393224 | tf_op jit(solution)/shard_map/ppermute | solution.py:401
  29.5 1.3 %collective-permute-start.12 = (bf16[2,256,128]{2,1,0:T(8,128)(2,1)S(1)}, bf16[2,256,128]{2,1,0:T(8,128)(2,1)S(1)}, u32[]{:S(2)}, u32[]{:S(2)}) collective-permute-start(bf16[2,256,128]{2,1,0:T(8,128)(2,1)S(1)} %collective-permute-done.8.refs_2_), channel_id=1, source_target_pairs={{0,1},{1,0},{2,3},{3,2},{4,5},{5,4},{6,7},{7,6},{8,9},{9,8},{10,11... | collective-permute-start | bytes 393224 | tf_op jit(solution)/shard_map/ppermute | solution.py:401
  29.6 1.5 %collective-permute-start.13 = (bf16[2,256,128]{2,1,0:T(8,128)(2,1)S(1)}, bf16[2,256,128]{2,1,0:T(8,128)(2,1)S(1)}, u32[]{:S(2)}, u32[]{:S(2)}) collective-permute-start(bf16[2,256,128]{2,1,0:T(8,128)(2,1)S(1)} %collective-permute-done.9.refs_3_), channel_id=1, source_target_pairs={{0,1},{1,0},{2,3},{3,2},{4,5},{5,4},{6,7},{7,6},{8,9},{9,8},{10,11... | collective-permute-start | bytes 393224 | tf_op jit(solution)/shard_map/ppermute | solution.py:401
  32.1 1.3 %collective-permute-start.14 = (f32[64,256]{1,0:T(8,128)S(1)}, f32[64,256]{1,0:T(8,128)S(1)}, u32[]{:S(2)}, u32[]{:S(2)}) collective-permute-start(f32[64,256]{1,0:T(8,128)S(1)} %get-tuple-element.32), channel_id=1, source_target_pairs={{0,1},{1,0},{2,3},{3,2},{4,5},{5,4},{6,7},{7,6},{8,9},{9,8},{10,11... | collective-permute-start | bytes 196616 | tf_op jit(solution)/shard_map/ppermute | solution.py:417

commit v6 on v5

--- a/solution.py
+++ b/solution.py
@@ -21,6 +21,18 @@
 ALONE = pltpu.CompilerParams(vmem_limit_bytes=60 * 1024 * 1024)
 
 
+def partner(index, shift, size):
+    if size & (size - 1) == 0:
+        return index ^ shift
+    return lax.rem(index + shift, size) if isinstance(index, jax.Array) else (index + shift) % size
+
+
+def source(index, origin, size):
+    if size & (size - 1) == 0:
+        return index ^ origin
+    return lax.rem(index - origin + size, size)
+
+
 def cos_sin(turns):
     quarter = jnp.floor(4.0 * turns + 0.5)
     angle = (2.0 * math.pi) * (turns - 0.25 * quarter)
@@ -57,17 +69,16 @@
 
 def sort_kernel(sizes, *refs):
     groups, held, chans, cap, rows = sizes
-    table_hbm, out_refs, half_hbm = refs[7], refs[8 : 8 + groups], refs[8 + groups]
-    targets = refs[9 + groups : 16 + groups]
+    out_refs = refs[7 : 7 + groups]
+    targets = refs[7 + groups : 14 + groups]
     plane_ref, group_ref, samples_b, place_b, offsets_ref, centre_ref, gain_ref = targets
-    samples, place, sorted_, filled, sems = refs[16 + groups :]
+    samples, place, sorted_, filled, sems = refs[14 + groups :]
     facet = lax.axis_index("facet")
     copies = [
         pltpu.make_async_copy(source, target, sems.at[n])
         for n, (source, target) in enumerate(zip(refs[:7], targets))
     ]
-    half = pltpu.make_async_copy(table_hbm.at[lax.axis_index("chan")], half_hbm, sems.at[7])
-    for copy in copies + [half]:
+    for copy in copies:
         copy.start()
     sorted_[...] = jnp.zeros_like(sorted_)
     for g in range(groups):
@@ -106,10 +117,9 @@
         sorted_[g, meta : meta + 1, :] += jnp.where(
             lane == k, (plane_ref[0, i] + 1).astype(jnp.float32), 0.0
         )
+    here = lax.axis_index("bl")
     for shift, out_ref in enumerate(out_refs):
-        g = lax.rem(lax.axis_index("bl") + shift, groups)
-        out_ref[...] = sorted_[g].astype(jnp.bfloat16)
-    half.wait()
+        out_ref[...] = sorted_[partner(here, shift, groups)].astype(jnp.bfloat16)
 
 
 def grid_kernel(sizes, *refs):
@@ -133,7 +143,7 @@
             d = f * groups + g
             plane = meta[meta_row - tail : meta_row - tail + 1].astype(jnp.int32) - 1
             set_id = jnp.where(lax.rem(plane, groups) == group, 0, 1)
-            shift = lax.rem(facet - lax.div(plane, groups) + facets, facets)
+            shift = source(facet, lax.div(plane, groups), facets)
             code = (d * cap + lane) * slots + 2 * shift + set_id
             meta_v[d : d + 1, :] = jnp.where(plane >= 0, code, -1)
             if f == 0 and g == 0:
@@ -246,8 +256,8 @@
 def table_kernel(sizes, norm, grids, packed, *refs):
     facets, meta_row = sizes
     slots = 2 * facets
-    ours, theirs = refs[:facets], refs[facets:slots]
-    mine_ref, other_ref, table_f, total = refs[slots:]
+    own, ours, theirs = refs[0], refs[1 : 2 + facets - 1], refs[1 + facets : 1 + 2 * facets]
+    mine_ref, other_ref, table_f, total = refs[1 + 2 * facets :]
     chan = lax.axis_index("chan")
     first = chan == 0
 
@@ -258,11 +268,17 @@
     result = jnp.zeros((SU, 2 * SU), jnp.float32)
     for s in range(slots):
         shift, set_id = divmod(s, 2)
-        fetched = ours[shift][set_id].astype(jnp.float32)
-        swapped = theirs[shift][set_id].astype(jnp.float32)
-        u_table = jnp.where(first, fetched, swapped)
-        v_table = jnp.where(first, swapped, fetched)
-        u_real, u_imag = parts(u_table)
+
+        def table(kind):
+            if s == 0:
+                return own[kind].astype(jnp.float32)
+            if s == 1:
+                fetched, given = ours[0][kind], theirs[0][kind]
+            else:
+                fetched, given = ours[shift][set_id, kind], theirs[shift][set_id, kind]
+            return jnp.where(first, given.astype(jnp.float32), fetched.astype(jnp.float32))
+
+        u_real, u_imag = parts(table(0))
         u_side = jnp.concatenate([u_real.T, u_imag.T], axis=1).astype(jnp.bfloat16)
         grid_real = grids[s, :SU, :]
         grid_imag = grids[s, SU:, :]
@@ -277,7 +293,7 @@
         half = jnp.dot(u_side, high, preferred_element_type=jnp.float32) + jnp.dot(
             u_side, low, preferred_element_type=jnp.float32
         )
-        v_real, v_imag = parts(v_table)
+        v_real, v_imag = parts(table(1))
         v_side = jnp.concatenate(
             [
                 jnp.concatenate([v_real, v_imag], axis=1),
@@ -303,8 +319,8 @@
     other_ref[...] = total[pl.ds(pl.multiple_of((1 - chan) * half_rows, half_rows), half_rows), :]
 
 
-def ring(size, shift):
-    return [(n, (n + shift) % size) for n in range(size)]
+def pairs(size, shift):
+    return [(n, partner(n, shift, size)) for n in range(size)]
 
 
 def body(
@@ -323,12 +339,11 @@
     norm = SU / math.sqrt(visibilities.shape[3] * held * facets * CH)
 
     own_table = tables.reshape(2, 2 * SU, SU)
-    *pieces, own_half = pl.pallas_call(
+    pieces = pl.pallas_call(
         functools.partial(sort_kernel, (groups, held, chans, cap, rows)),
-        out_shape=[jax.ShapeDtypeStruct((rows, SU), jnp.bfloat16)] * groups
-        + [jax.ShapeDtypeStruct((2 * SU, SU), jnp.bfloat16)],
-        in_specs=[HBM] * 8,
-        out_specs=[VMEM] * groups + [HBM],
+        out_shape=[jax.ShapeDtypeStruct((rows, SU), jnp.bfloat16)] * groups,
+        in_specs=[HBM] * 7,
+        out_specs=[VMEM] * groups,
         scratch_shapes=[
             pltpu.SMEM((1, held), jnp.int32),
             pltpu.SMEM((1, held), jnp.int32),
@@ -341,7 +356,7 @@
             pltpu.VMEM((held * 2, SU), jnp.float32),
             pltpu.VMEM((groups, rows, SU), jnp.float32),
             pltpu.SMEM((groups,), jnp.int32),
-            pltpu.SemaphoreType.DMA((8,)),
+            pltpu.SemaphoreType.DMA((7,)),
         ],
         compiler_params=ALONE,
         cost_estimate=pl.CostEstimate(flops=100_000, bytes_accessed=100_000, transcendentals=0),
@@ -354,28 +369,39 @@
         offsets.transpose(0, 2, 1),
         facet_centre.T,
         antenna_gain,
+    )
+    last = chan_count - 1
+    shifted = lax.ppermute(
         own_table,
+        ("bl", "chan"),
+        [(g * chan_count + last, (g + 1) % groups * chan_count + last) for g in range(groups)],
     )
     arrived = [
-        lax.ppermute(pieces[shift], "bl", ring(groups, shift)) for shift in range(1, groups)
+        lax.ppermute(pieces[shift], "bl", pairs(groups, shift)) for shift in range(1, groups)
     ]
-    shifted_half = lax.ppermute(own_half, "bl", ring(groups, 1))
-    kept, kept_half = local(
-        copy_kernel, [pieces[0], own_half], [(rows, SU), (2 * SU, SU)], "keep_own"
+    kept, kept_table = local(
+        copy_kernel, [pieces[0], own_table], [(rows, SU), (2, 2 * SU, SU)], "keep_own"
     )
     (here,) = local(
         functools.partial(stack_kernel, groups), [kept, *arrived], [(groups, rows, SU)], "join"
     )
     shifts = range(1, facets)
-    blocks = [here] + [lax.ppermute(here, "facet", ring(facets, shift)) for shift in shifts]
-    (halves,) = local(
+    blocks = [here] + [lax.ppermute(here, "facet", pairs(facets, shift)) for shift in shifts]
+    (both,) = local(
         functools.partial(stack_kernel, 2),
-        [kept_half, shifted_half],
-        [(2, 2 * SU, SU)],
-        "stack_halves",
+        [kept_table, shifted],
+        [(2, 2, 2 * SU, SU)],
+        "stack_tables",
         after=blocks[1:2],
     )
-    fetched = [lax.ppermute(halves, "facet", ring(facets, shift)) for shift in shifts]
+    fetched = [
+        lax.ppermute(
+            both,
+            ("facet", "chan"),
+            [(f * chan_count + last, t * chan_count + last) for f, t in pairs(facets, shift)],
+        )
+        for shift in shifts
+    ]
 
     grids = pl.pallas_call(
         functools.partial(grid_kernel, (facets, groups, chans, cap, rows)),
@@ -395,14 +421,15 @@
         ),
         name="grid",
     )(*blocks)
-    grids, halves, fetched = lax.optimization_barrier((grids, halves, fetched))
-    swap = ring(chan_count, 1)
-    ours = [halves, *fetched]
-    theirs = [lax.ppermute(table, "chan", swap) for table in ours]
+    grids, fetched = lax.optimization_barrier((grids, fetched))
+    ours = [kept_table, shifted, *fetched]
+    theirs = [
+        lax.ppermute(table, "chan", [(last, c) for c in range(last)][:1]) for table in ours[1:]
+    ]
     mine, other = pl.pallas_call(
         functools.partial(table_kernel, (facets, meta_row), norm),
         out_shape=[jax.ShapeDtypeStruct((half_rows, 2 * SU), jnp.float32)] * 2,
-        in_specs=[VMEM] * (2 + 2 * facets),
+        in_specs=[VMEM] * (3 + 2 * facets),
         out_specs=[VMEM, VMEM],
         scratch_shapes=[
             pltpu.VMEM((2 * SU, SU), jnp.float32),
@@ -414,7 +441,7 @@
         ),
         name="apply_tables",
     )(grids, here, *ours, *theirs)
-    summand = lax.ppermute(other, "chan", swap)
+    summand = lax.ppermute(other, "chan", pairs(chan_count, 1))
     return (mine + summand).reshape(1, 1, half_rows, 2, SU)
 
 

time: 34.4 us -> 39.7 us (1.15)
  waiting for transfers between devices: 2.56 us -> 11.3 us
  Pallas kernels: 11.1 us -> 8.38 us
  starting transfers between devices: 18.1 us -> 17.2 us
    ppermute x15, waiting for transfers between devices: 2.56 us -> 11.3 us  [the longest x4 4.62 us: body(): lax.ppermute(table, 'chan', [(last, c) for c in range(last)][:1])]
    pallas_call x1, Pallas kernels: 3.79 us -> 1.65 us  [body(): pl.pallas_call(functools.partial(sort_kernel, (groups, held, chans, cap,...]
    ppermute x15, starting transfers between devices: 18.1 us -> 17.2 us  [the longest x3 5.68 us: body(): lax.ppermute(pieces[shift], 'bl', pairs(groups, shift))]
    pallas_call x1, Pallas kernels: 6.23 us -> 5.62 us  [body(): pl.pallas_call(functools.partial(grid_kernel, (facets, groups, chans, cap...]
  transfers between devices with their start and end apart: 15 -> 15, of which waited for: 6 -> 7; matrix products, arithmetic and copies ran while one was open for 0% -> 0% of each run, Pallas kernels for 18% -> 19%
where the time goes in v6:
time: 39.7 us; the launch traced here: 39.3 us
  starting transfers between devices  17.2 us (43%)
  waiting for transfers between devices  11.3 us (28%)
  Pallas kernels  8.38 us (21%)
  local copies, waits for them, and re-layouts  2.27 us (6%)
    ppermute x3, starting transfers between devices, body(): lax.ppermute(pieces[shift], 'bl', pairs(groups, shift))  5.68 us
    pallas_call x1, Pallas kernels, body(): pl.pallas_call(functools.partial(grid_kernel, (facets, groups, chans, cap...  5.62 us
    ppermute x4, starting transfers between devices, body(): lax.ppermute(table, 'chan', [(last, c) for c in range(last)][:1])  5.17 us
    ppermute x4, waiting for transfers between devices, body(): lax.ppermute(table, 'chan', [(last, c) for c in range(last)][:1])  4.62 us
    ppermute x3, waiting for transfers between devices, body(): lax.ppermute(pieces[shift], 'bl', pairs(groups, shift))  4.07 us
    ppermute x3, starting transfers between devices, body(): lax.ppermute(here, 'facet', pairs(facets, shift))  3.49 us
    ppermute x3, starting transfers between devices, body(): lax.ppermute(both, ('facet', 'chan'), [(f * chan_count + last, t * chan_c...  2.03 us
    pallas_call x1, Pallas kernels, body(): pl.pallas_call(functools.partial(sort_kernel, (groups, held, chans, cap,...  1.65 us
  transfers between devices with their start and end apart: 15, of which 7 were waited for; matrix products, arithmetic and copies ran while one was open for 0% of the time, Pallas kernels for 19%

profile of v6, /device:TPU:0, one launch (start us, length us, event | category | flops | bytes accessed | tf_op | source)
XLA Modules:
  0.0 39.3 jit_solution(8441647884426213619)
XLA Ops:
  0.0 0.7 %collective-permute-start.6 = (bf16[2,256,128]{2,1,0:T(8,128)(2,1)}, bf16[2,256,128]{2,1,0:T(8,128)(2,1)S(1)}, u32[]{:S(2)}, u32[]{:S(2)}) collective-permute-start(bf16[2,256,128]{2,1,0:T(8,128)(2,1)} %bitcast.7), channel_id=1, source_target_pairs={{1,3},{3,5},{5,7},{7,1},{9,11},{11,13},{13,15},{15,9},{17,19},{19,... | collective-permute-start | bytes 393224 | tf_op jit(solution)/shard_map/ppermute | solution.py:374
  0.7 1.6 %sort_blocks.1 = (bf16[48,128]{1,0:T(8,128)(2,1)}, bf16[48,128]{1,0:T(8,128)(2,1)}, bf16[48,128]{1,0:T(8,128)(2,1)}, bf16[48,128]{1,0:T(8,128)(2,1)}) custom-call(s32[1,8]{1,0:T(1,128)} %bitcast.13, s32[1,8]{1,0:T(1,128)} %bitcast.14, bf16[64,128]{1,0:T(8,128)(2,1)} %bitcast.9, bf16[16,128]{1,0:T(8,128)(2,1)} %bitcast.10, s32[4,2,4]{2,1,0:T(2,128)} %bitcast.11, ...), custom_call_target="tpu_custom_call" | custom-call | flops 100000 | bytes 100000 | tf_op jit(solution)/shard_map/sort_blocks/pallas_call | solution.py:342
  2.3 3.1 %collective-permute-start = (bf16[48,128]{1,0:T(8,128)(2,1)}, bf16[48,128]{1,0:T(8,128)(2,1)S(1)}, u32[]{:S(2)}, u32[]{:S(2)}) collective-permute-start(bf16[48,128]{1,0:T(8,128)(2,1)} %get-tuple-element.19), channel_id=1, source_target_pairs={{0,2},{2,0},{4,6},{6,4},{1,3},{3,1},{5,7},{7,5},{8,10},{10,8},{12,... | collective-permute-start | bytes 36872 | tf_op jit(solution)/shard_map/ppermute | solution.py:380
  5.4 2.6 %collective-permute-start.1 = (bf16[48,128]{1,0:T(8,128)(2,1)}, bf16[48,128]{1,0:T(8,128)(2,1)S(1)}, u32[]{:S(2)}, u32[]{:S(2)}) collective-permute-start(bf16[48,128]{1,0:T(8,128)(2,1)} %get-tuple-element.20), channel_id=1, source_target_pairs={{0,4},{2,6},{4,0},{6,2},{1,5},{3,7},{5,1},{7,3},{8,12},{10,14},{12... | collective-permute-start | bytes 36872 | tf_op jit(solution)/shard_map/ppermute | solution.py:380
  8.0 0.0 collective-permute-start.2
  8.0 0.0 copy-start
  8.0 0.9 %copy-done = bf16[1,2,128,2,128]{4,3,2,1,0:T(2,128)(2,1)S(1)} copy-done((bf16[1,2,128,2,128]{4,3,2,1,0:T(2,128)(2,1)S(1)}, bf16[1,2,128,2,128]{4,3,2,1,0:T(2,128)(2,1)}, u32[]{:S(2)}) %copy-start) | copy-done | bytes 131096
  8.9 0.0 copy-start.1
  8.9 0.7 %copy-done.1 = bf16[48,128]{1,0:T(8,128)(2,1)S(1)} copy-done((bf16[48,128]{1,0:T(8,128)(2,1)S(1)}, bf16[48,128]{1,0:T(8,128)(2,1)}, u32[]{:S(2)}) %copy-start.1) | copy-done | bytes 12312
  9.6 0.0 collective-permute-done.refs_1_
  9.6 0.6 %collective-permute-done.1.refs_2_ = bf16[48,128]{1,0:T(8,128)(2,1)S(1)} collective-permute-done((bf16[48,128]{1,0:T(8,128)(2,1)}, bf16[48,128]{1,0:T(8,128)(2,1)S(1)}, u32[]{:S(2)}, u32[]{:S(2)}) %collective-permute-start.1) | collective-permute-done | bytes 12320 | tf_op jit(solution)/shard_map/ppermute | solution.py:380
  10.2 3.5 %collective-permute-done.2.refs_3_ = bf16[48,128]{1,0:T(8,128)(2,1)S(1)} collective-permute-done((bf16[48,128]{1,0:T(8,128)(2,1)}, bf16[48,128]{1,0:T(8,128)(2,1)S(1)}, u32[]{:S(2)}, u32[]{:S(2)}) %collective-permute-start.2) | collective-permute-done | bytes 12320 | tf_op jit(solution)/shard_map/ppermute | solution.py:380
  13.7 1.5 %collective-permute-start.3 = (bf16[4,48,128]{2,1,0:T(8,128)(2,1)S(1)}, bf16[4,48,128]{2,1,0:T(8,128)(2,1)S(1)}, u32[]{:S(2)}, u32[]{:S(2)}) collective-permute-start(bf16[4,48,128]{2,1,0:T(8,128)(2,1)S(1)} %join.1.refs_0_.packed), channel_id=1, source_target_pairs={{0,8},{8,0},{16,24},{24,16},{1,9},{9,1},{17,25},{25,17},{2,10},{10... | collective-permute-start | bytes 147464 | tf_op jit(solution)/shard_map/ppermute | solution.py:389
  15.2 1.5 %collective-permute-start.5 = (bf16[4,48,128]{2,1,0:T(8,128)(2,1)S(1)}, bf16[4,48,128]{2,1,0:T(8,128)(2,1)S(1)}, u32[]{:S(2)}, u32[]{:S(2)}) collective-permute-start(bf16[4,48,128]{2,1,0:T(8,128)(2,1)S(1)} %join.1.refs_0_.packed), channel_id=1, source_target_pairs={{0,24},{8,16},{16,8},{24,0},{1,25},{9,17},{17,9},{25,1},{2,26},{10... | collective-permute-start | bytes 147464 | tf_op jit(solution)/shard_map/ppermute | solution.py:389
  16.7 0.5 %collective-permute-start.4 = (bf16[4,48,128]{2,1,0:T(8,128)(2,1)S(1)}, bf16[4,48,128]{2,1,0:T(8,128)(2,1)S(1)}, u32[]{:S(2)}, u32[]{:S(2)}) collective-permute-start(bf16[4,48,128]{2,1,0:T(8,128)(2,1)S(1)} %join.1.refs_0_.packed), channel_id=1, source_target_pairs={{0,16},{8,24},{16,0},{24,8},{1,17},{9,25},{17,1},{25,9},{2,18},{10... | collective-permute-start | bytes 147464 | tf_op jit(solution)/shard_map/ppermute | solution.py:389
  17.2 0.6 %collective-permute-done.3.refs_1_.refs_2_ = bf16[4,48,128]{2,1,0:T(8,128)(2,1)S(1)} collective-permute-done((bf16[4,48,128]{2,1,0:T(8,128)(2,1)S(1)}, bf16[4,48,128]{2,1,0:T(8,128)(2,1)S(1)}, u32[]{:S(2)}, u32[]{:S(2)}) %collective-permute-start.3) | collective-permute-done | bytes 49184 | tf_op jit(solution)/shard_map/ppermute | solution.py:389
  17.8 0.0 collective-permute-done.6.refs_1_
  17.8 0.7 %collective-permute-start.9 = (bf16[2,2,256,128]{3,2,1,0:T(8,128)(2,1)S(1)}, bf16[2,2,256,128]{3,2,1,0:T(8,128)(2,1)S(1)}, u32[]{:S(2)}, u32[]{:S(2)}) collective-permute-start(bf16[2,2,256,128]{3,2,1,0:T(8,128)(2,1)S(1)} %stack_tables.1), channel_id=1, source_target_pairs={{1,25},{9,17},{17,9},{25,1},{3,27},{11,19},{19,11},{27,3},{5,29},{... | collective-permute-start | bytes 786440 | tf_op jit(solution)/shard_map/ppermute | solution.py:398
  18.5 0.7 %collective-permute-start.8 = (bf16[2,2,256,128]{3,2,1,0:T(8,128)(2,1)S(1)}, bf16[2,2,256,128]{3,2,1,0:T(8,128)(2,1)S(1)}, u32[]{:S(2)}, u32[]{:S(2)}) collective-permute-start(bf16[2,2,256,128]{3,2,1,0:T(8,128)(2,1)S(1)} %stack_tables.1), channel_id=1, source_target_pairs={{1,17},{9,25},{17,1},{25,9},{3,19},{11,27},{19,3},{27,11},{5,21},{... | collective-permute-start | bytes 786440 | tf_op jit(solution)/shard_map/ppermute | solution.py:398
  19.2 0.7 %collective-permute-start.7 = (bf16[2,2,256,128]{3,2,1,0:T(8,128)(2,1)S(1)}, bf16[2,2,256,128]{3,2,1,0:T(8,128)(2,1)S(1)}, u32[]{:S(2)}, u32[]{:S(2)}) collective-permute-start(bf16[2,2,256,128]{3,2,1,0:T(8,128)(2,1)S(1)} %stack_tables.1), channel_id=1, source_target_pairs={{1,9},{9,1},{17,25},{25,17},{3,11},{11,3},{19,27},{27,19},{5,13},{... | collective-permute-start | bytes 786440 | tf_op jit(solution)/shard_map/ppermute | solution.py:398
  19.9 0.3 collective-permute-done.5.refs_3_
  20.2 0.6 %collective-permute-done.4.refs_2_ = bf16[4,48,128]{2,1,0:T(8,128)(2,1)S(1)} collective-permute-done((bf16[4,48,128]{2,1,0:T(8,128)(2,1)S(1)}, bf16[4,48,128]{2,1,0:T(8,128)(2,1)S(1)}, u32[]{:S(2)}, u32[]{:S(2)}) %collective-permute-start.4) | collective-permute-done | bytes 49184 | tf_op jit(solution)/shard_map/ppermute | solution.py:389
  20.8 5.6 %grid.1.grids = f32[8,256,128]{2,1,0:T(8,128)S(1)} custom-call(bf16[4,48,128]{2,1,0:T(8,128)(2,1)S(1)} %join.1.refs_0_.packed, bf16[4,48,128]{2,1,0:T(8,128)(2,1)S(1)} %collective-permute-done.3.refs_1_.refs_2_, bf16[4,48,128]{2,1,0:T(8,128)(2,1)S(1)} %collective-permute-done.4.refs_2_, bf16[4,48,128]{2,1,0:T(8,128)(2,1)S(1)} %collective-permute-done.5.refs_3_), custom_call_target="tpu_custom_call" | custom-call | flops 4000000000 | bytes 2000000 | tf_op jit(solution)/shard_map/grid/pallas_call | solution.py:406
  26.4 0.0 collective-permute-done.9.refs_4_
  26.4 0.0 collective-permute-done.8.refs_3_
  26.4 0.0 collective-permute-done.7.refs_2_
  26.4 1.3 %collective-permute-start.11 = (bf16[2,2,256,128]{3,2,1,0:T(8,128)(2,1)S(1)}, bf16[2,2,256,128]{3,2,1,0:T(8,128)(2,1)S(1)}, u32[]{:S(2)}, u32[]{:S(2)}) collective-permute-start(bf16[2,2,256,128]{3,2,1,0:T(8,128)(2,1)S(1)} %collective-permute-done.7.refs_2_), channel_id=1, source_target_pairs={{1,0},{3,2},{5,4},{7,6},{9,8},{11,10},{13,12},{15,14},{17,16},{19,... | collective-permute-start | bytes 786440 | tf_op jit(solution)/shard_map/ppermute | solution.py:427
  27.7 1.3 %collective-permute-start.12 = (bf16[2,2,256,128]{3,2,1,0:T(8,128)(2,1)S(1)}, bf16[2,2,256,128]{3,2,1,0:T(8,128)(2,1)S(1)}, u32[]{:S(2)}, u32[]{:S(2)}) collective-permute-start(bf16[2,2,256,128]{3,2,1,0:T(8,128)(2,1)S(1)} %collective-permute-done.8.refs_3_), channel_id=1, source_target_pairs={{1,0},{3,2},{5,4},{7,6},{9,8},{11,10},{13,12},{15,14},{17,16},{19,... | collective-permute-start | bytes 786440 | tf_op jit(solution)/shard_map/ppermute | solution.py:427
  29.0 1.3 %collective-permute-start.13 = (bf16[2,2,256,128]{3,2,1,0:T(8,128)(2,1)S(1)}, bf16[2,2,256,128]{3,2,1,0:T(8,128)(2,1)S(1)}, u32[]{:S(2)}, u32[]{:S(2)}) collective-permute-start(bf16[2,2,256,128]{3,2,1,0:T(8,128)(2,1)S(1)} %collective-permute-done.9.refs_4_), channel_id=1, source_target_pairs={{1,0},{3,2},{5,4},{7,6},{9,8},{11,10},{13,12},{15,14},{17,16},{19,... | collective-permute-start | bytes 786440 | tf_op jit(solution)/shard_map/ppermute | solution.py:427
  30.3 1.3 %collective-permute-start.10 = (bf16[2,256,128]{2,1,0:T(8,128)(2,1)S(1)}, bf16[2,256,128]{2,1,0:T(8,128)(2,1)S(1)}, u32[]{:S(2)}, u32[]{:S(2)}) collective-permute-start(bf16[2,256,128]{2,1,0:T(8,128)(2,1)S(1)} %collective-permute-done.6.refs_1_), channel_id=1, source_target_pairs={{1,0},{3,2},{5,4},{7,6},{9,8},{11,10},{13,12},{15,14},{17,16},{19,... | collective-permute-start | bytes 393224 | tf_op jit(solution)/shard_map/ppermute | solution.py:427
  31.6 4.6 %collective-permute-done.10.refs_5_ = bf16[2,256,128]{2,1,0:T(8,128)(2,1)S(1)} collective-permute-done((bf16[2,256,128]{2,1,0:T(8,128)(2,1)S(1)}, bf16[2,256,128]{2,1,0:T(8,128)(2,1)S(1)}, u32[]{:S(2)}, u32[]{:S(2)}) %collective-permute-start.10) | collective-permute-done | bytes 131104 | tf_op jit(solution)/shard_map/ppermute | solution.py:427
  36.3 0.0 collective-permute-done.11.refs_6_
  36.3 0.0 collective-permute-done.12.refs_7_
  36.3 0.0 collective-permute-done.13.refs_8_
  36.3 1.1 %apply_tables.1 = (f32[64,256]{1,0:T(8,128)S(1)}, f32[64,256]{1,0:T(8,128)S(1)}) custom-call(f32[8,256,128]{2,1,0:T(8,128)S(1)} %grid.1.grids, bf16[4,48,128]{2,1,0:T(8,128)(2,1)S(1)} %join.1.refs_0_.packed, bf16[2,256,128]{2,1,0:T(8,128)(2,1)S(1)} %get-tuple-element.22.refs_0_, bf16[2,256,128]{2,1,0:T(8,128)(2,1)S(1)} %collective-permute-done.6.refs_1_, ...), custom_call_target="tpu_custom_call" | custom-call | flops 1000000000 | bytes 2000000 | tf_op jit(solution)/shard_map/apply_tables/pallas_call | solution.py:429
  37.3 0.2 collective-permute-start.14
  37.6 1.1 %collective-permute-done.14 = f32[64,256]{1,0:T(8,128)S(1)} collective-permute-done((f32[64,256]{1,0:T(8,128)S(1)}, f32[64,256]{1,0:T(8,128)S(1)}, u32[]{:S(2)}, u32[]{:S(2)}) %collective-permute-start.14) | collective-permute-done | bytes 65568 | tf_op jit(solution)/shard_map/ppermute | solution.py:444
  38.7 0.7 %reshape.19 = f32[1,1,64,2,128]{4,3,2,1,0:T(2,128)} reshape(f32[64,256]{1,0:T(8,128)S(1)} %add.3) | data formatting | bytes 131072 | tf_op jit(solution)/shard_map/reshape | solution.py:445
  (4 shorter events, 0.0 us)
Async XLA Ops:
  0.0 17.8 %collective-permute-start.6 = (bf16[2,256,128]{2,1,0:T(8,128)(2,1)}, bf16[2,256,128]{2,1,0:T(8,128)(2,1)S(1)}, u32[]{:S(2)}, u32[]{:S(2)}) collective-permute-start(bf16[2,256,128]{2,1,0:T(8,128)(2,1)} %bitcast.7), channel_id=1, source_target_pairs={{1,3},{3,5},{5,7},{7,1},{9,11},{11,13},{13,15},{15,9},{17,19},{19,... | collective-permute-start | bytes 393224 | tf_op jit(solution)/shard_map/ppermute | solution.py:374
  2.3 7.3 %collective-permute-start = (bf16[48,128]{1,0:T(8,128)(2,1)}, bf16[48,128]{1,0:T(8,128)(2,1)S(1)}, u32[]{:S(2)}, u32[]{:S(2)}) collective-permute-start(bf16[48,128]{1,0:T(8,128)(2,1)} %get-tuple-element.19), channel_id=1, source_target_pairs={{0,2},{2,0},{4,6},{6,4},{1,3},{3,1},{5,7},{7,5},{8,10},{10,8},{12,... | collective-permute-start | bytes 36872 | tf_op jit(solution)/shard_map/ppermute | solution.py:380
  5.4 4.8 %collective-permute-start.1 = (bf16[48,128]{1,0:T(8,128)(2,1)}, bf16[48,128]{1,0:T(8,128)(2,1)S(1)}, u32[]{:S(2)}, u32[]{:S(2)}) collective-permute-start(bf16[48,128]{1,0:T(8,128)(2,1)} %get-tuple-element.20), channel_id=1, source_target_pairs={{0,4},{2,6},{4,0},{6,2},{1,5},{3,7},{5,1},{7,3},{8,12},{10,14},{12... | collective-permute-start | bytes 36872 | tf_op jit(solution)/shard_map/ppermute | solution.py:380
  8.0 5.7 %collective-permute-start.2 = (bf16[48,128]{1,0:T(8,128)(2,1)}, bf16[48,128]{1,0:T(8,128)(2,1)S(1)}, u32[]{:S(2)}, u32[]{:S(2)}) collective-permute-start(bf16[48,128]{1,0:T(8,128)(2,1)} %get-tuple-element.21), channel_id=1, source_target_pairs={{0,6},{2,4},{4,2},{6,0},{1,7},{3,5},{5,3},{7,1},{8,14},{10,12},{12... | collective-permute-start | bytes 36872 | tf_op jit(solution)/shard_map/ppermute | solution.py:380
  8.0 0.9 %copy-start = (bf16[1,2,128,2,128]{4,3,2,1,0:T(2,128)(2,1)S(1)}, bf16[1,2,128,2,128]{4,3,2,1,0:T(2,128)(2,1)}, u32[]{:S(2)}) copy-start(bf16[1,2,128,2,128]{4,3,2,1,0:T(2,128)(2,1)} %param.14) | copy-start | bytes 393220
  8.9 0.7 %copy-start.1 = (bf16[48,128]{1,0:T(8,128)(2,1)S(1)}, bf16[48,128]{1,0:T(8,128)(2,1)}, u32[]{:S(2)}) copy-start(bf16[48,128]{1,0:T(8,128)(2,1)} %get-tuple-element.17.refs_0_) | copy-start | bytes 36868
  13.7 4.1 %collective-permute-start.3 = (bf16[4,48,128]{2,1,0:T(8,128)(2,1)S(1)}, bf16[4,48,128]{2,1,0:T(8,128)(2,1)S(1)}, u32[]{:S(2)}, u32[]{:S(2)}) collective-permute-start(bf16[4,48,128]{2,1,0:T(8,128)(2,1)S(1)} %join.1.refs_0_.packed), channel_id=1, source_target_pairs={{0,8},{8,0},{16,24},{24,16},{1,9},{9,1},{17,25},{25,17},{2,10},{10... | collective-permute-start | bytes 147464 | tf_op jit(solution)/shard_map/ppermute | solution.py:389
  15.2 5.0 %collective-permute-start.5 = (bf16[4,48,128]{2,1,0:T(8,128)(2,1)S(1)}, bf16[4,48,128]{2,1,0:T(8,128)(2,1)S(1)}, u32[]{:S(2)}, u32[]{:S(2)}) collective-permute-start(bf16[4,48,128]{2,1,0:T(8,128)(2,1)S(1)} %join.1.refs_0_.packed), channel_id=1, source_target_pairs={{0,24},{8,16},{16,8},{24,0},{1,25},{9,17},{17,9},{25,1},{2,26},{10... | collective-permute-start | bytes 147464 | tf_op jit(solution)/shard_map/ppermute | solution.py:389
  16.7 4.1 %collective-permute-start.4 = (bf16[4,48,128]{2,1,0:T(8,128)(2,1)S(1)}, bf16[4,48,128]{2,1,0:T(8,128)(2,1)S(1)}, u32[]{:S(2)}, u32[]{:S(2)}) collective-permute-start(bf16[4,48,128]{2,1,0:T(8,128)(2,1)S(1)} %join.1.refs_0_.packed), channel_id=1, source_target_pairs={{0,16},{8,24},{16,0},{24,8},{1,17},{9,25},{17,1},{25,9},{2,18},{10... | collective-permute-start | bytes 147464 | tf_op jit(solution)/shard_map/ppermute | solution.py:389
  17.8 8.6 %collective-permute-start.9 = (bf16[2,2,256,128]{3,2,1,0:T(8,128)(2,1)S(1)}, bf16[2,2,256,128]{3,2,1,0:T(8,128)(2,1)S(1)}, u32[]{:S(2)}, u32[]{:S(2)}) collective-permute-start(bf16[2,2,256,128]{3,2,1,0:T(8,128)(2,1)S(1)} %stack_tables.1), channel_id=1, source_target_pairs={{1,25},{9,17},{17,9},{25,1},{3,27},{11,19},{19,11},{27,3},{5,29},{... | collective-permute-start | bytes 786440 | tf_op jit(solution)/shard_map/ppermute | solution.py:398
  18.5 7.9 %collective-permute-start.8 = (bf16[2,2,256,128]{3,2,1,0:T(8,128)(2,1)S(1)}, bf16[2,2,256,128]{3,2,1,0:T(8,128)(2,1)S(1)}, u32[]{:S(2)}, u32[]{:S(2)}) collective-permute-start(bf16[2,2,256,128]{3,2,1,0:T(8,128)(2,1)S(1)} %stack_tables.1), channel_id=1, source_target_pairs={{1,17},{9,25},{17,1},{25,9},{3,19},{11,27},{19,3},{27,11},{5,21},{... | collective-permute-start | bytes 786440 | tf_op jit(solution)/shard_map/ppermute | solution.py:398
  19.2 7.2 %collective-permute-start.7 = (bf16[2,2,256,128]{3,2,1,0:T(8,128)(2,1)S(1)}, bf16[2,2,256,128]{3,2,1,0:T(8,128)(2,1)S(1)}, u32[]{:S(2)}, u32[]{:S(2)}) collective-permute-start(bf16[2,2,256,128]{3,2,1,0:T(8,128)(2,1)S(1)} %stack_tables.1), channel_id=1, source_target_pairs={{1,9},{9,1},{17,25},{25,17},{3,11},{11,3},{19,27},{27,19},{5,13},{... | collective-permute-start | bytes 786440 | tf_op jit(solution)/shard_map/ppermute | solution.py:398
  26.4 9.8 %collective-permute-start.11 = (bf16[2,2,256,128]{3,2,1,0:T(8,128)(2,1)S(1)}, bf16[2,2,256,128]{3,2,1,0:T(8,128)(2,1)S(1)}, u32[]{:S(2)}, u32[]{:S(2)}) collective-permute-start(bf16[2,2,256,128]{3,2,1,0:T(8,128)(2,1)S(1)} %collective-permute-done.7.refs_2_), channel_id=1, source_target_pairs={{1,0},{3,2},{5,4},{7,6},{9,8},{11,10},{13,12},{15,14},{17,16},{19,... | collective-permute-start | bytes 786440 | tf_op jit(solution)/shard_map/ppermute | solution.py:427
  27.7 8.5 %collective-permute-start.12 = (bf16[2,2,256,128]{3,2,1,0:T(8,128)(2,1)S(1)}, bf16[2,2,256,128]{3,2,1,0:T(8,128)(2,1)S(1)}, u32[]{:S(2)}, u32[]{:S(2)}) collective-permute-start(bf16[2,2,256,128]{3,2,1,0:T(8,128)(2,1)S(1)} %collective-permute-done.8.refs_3_), channel_id=1, source_target_pairs={{1,0},{3,2},{5,4},{7,6},{9,8},{11,10},{13,12},{15,14},{17,16},{19,... | collective-permute-start | bytes 786440 | tf_op jit(solution)/shard_map/ppermute | solution.py:427
  29.0 7.2 %collective-permute-start.13 = (bf16[2,2,256,128]{3,2,1,0:T(8,128)(2,1)S(1)}, bf16[2,2,256,128]{3,2,1,0:T(8,128)(2,1)S(1)}, u32[]{:S(2)}, u32[]{:S(2)}) collective-permute-start(bf16[2,2,256,128]{3,2,1,0:T(8,128)(2,1)S(1)} %collective-permute-done.9.refs_4_), channel_id=1, source_target_pairs={{1,0},{3,2},{5,4},{7,6},{9,8},{11,10},{13,12},{15,14},{17,16},{19,... | collective-permute-start | bytes 786440 | tf_op jit(solution)/shard_map/ppermute | solution.py:427
  30.3 5.9 %collective-permute-start.10 = (bf16[2,256,128]{2,1,0:T(8,128)(2,1)S(1)}, bf16[2,256,128]{2,1,0:T(8,128)(2,1)S(1)}, u32[]{:S(2)}, u32[]{:S(2)}) collective-permute-start(bf16[2,256,128]{2,1,0:T(8,128)(2,1)S(1)} %collective-permute-done.6.refs_1_), channel_id=1, source_target_pairs={{1,0},{3,2},{5,4},{7,6},{9,8},{11,10},{13,12},{15,14},{17,16},{19,... | collective-permute-start | bytes 393224 | tf_op jit(solution)/shard_map/ppermute | solution.py:427
  37.3 1.3 %collective-permute-start.14 = (f32[64,256]{1,0:T(8,128)S(1)}, f32[64,256]{1,0:T(8,128)S(1)}, u32[]{:S(2)}, u32[]{:S(2)}) collective-permute-start(f32[64,256]{1,0:T(8,128)S(1)} %get-tuple-element.28), channel_id=1, source_target_pairs={{0,1},{1,0},{2,3},{3,2},{4,5},{5,4},{6,7},{7,6},{8,9},{9,8},{10,11... | collective-permute-start | bytes 196616 | tf_op jit(solution)/shard_map/ppermute | solution.py:444

commit v7 on v6

--- a/solution.py
+++ b/solution.py
@@ -231,9 +231,9 @@
     lax.fori_loop(0, lax.div(count + UNROLL - 1, UNROLL), step, 0)
 
 
-def copy_kernel(*refs):
-    for source, target in zip(refs[: len(refs) // 2], refs[len(refs) // 2 :]):
-        target[...] = source[...]
+def keep_kernel(piece, table, kept, half):
+    kept[...] = piece[...]
+    half[...] = table[lax.axis_index("chan")]
 
 
 def stack_kernel(count, *refs):
@@ -256,8 +256,8 @@
 def table_kernel(sizes, norm, grids, packed, *refs):
     facets, meta_row = sizes
     slots = 2 * facets
-    own, ours, theirs = refs[0], refs[1 : 2 + facets - 1], refs[1 + facets : 1 + 2 * facets]
-    mine_ref, other_ref, table_f, total = refs[1 + 2 * facets :]
+    ours, theirs = refs[:facets], refs[facets:slots]
+    mine_ref, other_ref, table_f, total = refs[slots:]
     chan = lax.axis_index("chan")
     first = chan == 0
 
@@ -268,17 +268,9 @@
     result = jnp.zeros((SU, 2 * SU), jnp.float32)
     for s in range(slots):
         shift, set_id = divmod(s, 2)
-
-        def table(kind):
-            if s == 0:
-                return own[kind].astype(jnp.float32)
-            if s == 1:
-                fetched, given = ours[0][kind], theirs[0][kind]
-            else:
-                fetched, given = ours[shift][set_id, kind], theirs[shift][set_id, kind]
-            return jnp.where(first, given.astype(jnp.float32), fetched.astype(jnp.float32))
-
-        u_real, u_imag = parts(table(0))
+        fetched = ours[shift][set_id].astype(jnp.float32)
+        swapped = theirs[shift][set_id].astype(jnp.float32)
+        u_real, u_imag = parts(jnp.where(first, fetched, swapped))
         u_side = jnp.concatenate([u_real.T, u_imag.T], axis=1).astype(jnp.bfloat16)
         grid_real = grids[s, :SU, :]
         grid_imag = grids[s, SU:, :]
@@ -293,7 +285,7 @@
         half = jnp.dot(u_side, high, preferred_element_type=jnp.float32) + jnp.dot(
             u_side, low, preferred_element_type=jnp.float32
         )
-        v_real, v_imag = parts(table(1))
+        v_real, v_imag = parts(jnp.where(first, swapped, fetched))
         v_side = jnp.concatenate(
             [
                 jnp.concatenate([v_real, v_imag], axis=1),
@@ -370,38 +362,26 @@
         facet_centre.T,
         antenna_gain,
     )
-    last = chan_count - 1
-    shifted = lax.ppermute(
-        own_table,
-        ("bl", "chan"),
-        [(g * chan_count + last, (g + 1) % groups * chan_count + last) for g in range(groups)],
-    )
     arrived = [
         lax.ppermute(pieces[shift], "bl", pairs(groups, shift)) for shift in range(1, groups)
     ]
-    kept, kept_table = local(
-        copy_kernel, [pieces[0], own_table], [(rows, SU), (2, 2 * SU, SU)], "keep_own"
-    )
+    kept, kept_half = local(
+        keep_kernel, [pieces[0], own_table], [(rows, SU), (2 * SU, SU)], "keep_own"
+    )
+    shifted_half = lax.ppermute(kept_half, "bl", [(g, (g + 1) % groups) for g in range(groups)])
     (here,) = local(
         functools.partial(stack_kernel, groups), [kept, *arrived], [(groups, rows, SU)], "join"
     )
     shifts = range(1, facets)
     blocks = [here] + [lax.ppermute(here, "facet", pairs(facets, shift)) for shift in shifts]
-    (both,) = local(
+    (halves,) = local(
         functools.partial(stack_kernel, 2),
-        [kept_table, shifted],
-        [(2, 2, 2 * SU, SU)],
-        "stack_tables",
+        [kept_half, shifted_half],
+        [(2, 2 * SU, SU)],
+        "stack_halves",
         after=blocks[1:2],
     )
-    fetched = [
-        lax.ppermute(
-            both,
-            ("facet", "chan"),
-            [(f * chan_count + last, t * chan_count + last) for f, t in pairs(facets, shift)],
-        )
-        for shift in shifts
-    ]
+    fetched = [lax.ppermute(halves, "facet", pairs(facets, shift)) for shift in shifts]
 
     grids = pl.pallas_call(
         functools.partial(grid_kernel, (facets, groups, chans, cap, rows)),
@@ -421,15 +401,14 @@
         ),
         name="grid",
     )(*blocks)
+    swap = pairs(chan_count, 1)
     grids, fetched = lax.optimization_barrier((grids, fetched))
-    ours = [kept_table, shifted, *fetched]
-    theirs = [
-        lax.ppermute(table, "chan", [(last, c) for c in range(last)][:1]) for table in ours[1:]
-    ]
+    ours = [halves, *fetched]
+    theirs = [lax.ppermute(table, "chan", swap) for table in ours]
     mine, other = pl.pallas_call(
         functools.partial(table_kernel, (facets, meta_row), norm),
         out_shape=[jax.ShapeDtypeStruct((half_rows, 2 * SU), jnp.float32)] * 2,
-        in_specs=[VMEM] * (3 + 2 * facets),
+        in_specs=[VMEM] * (2 + 2 * facets),
         out_specs=[VMEM, VMEM],
         scratch_shapes=[
             pltpu.VMEM((2 * SU, SU), jnp.float32),
@@ -441,7 +420,7 @@
         ),
         name="apply_tables",
     )(grids, here, *ours, *theirs)
-    summand = lax.ppermute(other, "chan", pairs(chan_count, 1))
+    summand = lax.ppermute(other, "chan", swap)
     return (mine + summand).reshape(1, 1, half_rows, 2, SU)
 
 

time: 39.7 us -> 34.6 us (0.87); the launches traced: 39.3 us -> 35.3 us
  waiting for transfers between devices: 11.3 us -> 7.3 us
  starting transfers between devices: 17.2 us -> 16 us
  Pallas kernels: 8.38 us -> 9.55 us
    ppermute x9, waiting for transfers between devices: 5.74 us -> 1.96 us  [the longest x4 1.02 us: body(): theirs = [lax.ppermute(table, 'chan', swap) for table in ours]]
    ppermute x3, starting transfers between devices: 5.68 us -> 4.39 us  [body(): lax.ppermute(pieces[shift], 'bl', pairs(groups, shift))]
    pallas_call x1, Pallas kernels: 5.62 us -> 6.79 us  [body(): pl.pallas_call(functools.partial(grid_kernel, (facets, groups, chans, cap...]
    ppermute x3, waiting for transfers between devices: 1.5 us -> 1.01 us  [body(): lax.ppermute(here, 'facet', pairs(facets, shift))]
    unnamed x4 -> x10, local copies, waits for them, and re-layouts: 1.61 us -> 1.62 us
  transfers between devices with their start and end apart: 15 -> 15, of which waited for: 7 -> 10; matrix products, arithmetic and copies ran while one was open for 0% -> 0% of each run, Pallas kernels for 19% -> 19%
where the time goes in v7:
time: 34.6 us; the launch traced here: 35.3 us
  starting transfers between devices  16 us (46%)
  Pallas kernels  9.55 us (28%)
  waiting for transfers between devices  7.3 us (21%)
  local copies, waits for them, and re-layouts  2.28 us (7%)
    pallas_call x1, Pallas kernels, body(): pl.pallas_call(functools.partial(grid_kernel, (facets, groups, chans, cap...  6.79 us
    ppermute x3, starting transfers between devices, body(): lax.ppermute(pieces[shift], 'bl', pairs(groups, shift))  4.39 us
    ppermute x3, waiting for transfers between devices, body(): lax.ppermute(pieces[shift], 'bl', pairs(groups, shift))  4.32 us
    ppermute x3, starting transfers between devices, body(): lax.ppermute(halves, 'facet', pairs(facets, shift))  3.56 us
    ppermute x3, starting transfers between devices, body(): lax.ppermute(here, 'facet', pairs(facets, shift))  3.49 us
    ppermute x1, starting transfers between devices, body(): lax.ppermute(kept_half, 'bl', [(g, (g + 1) % groups) for g in range(group...  3.08 us
    pallas_call x1, Pallas kernels, body(): pl.pallas_call(functools.partial(sort_kernel, (groups, held, chans, cap,...  1.65 us
    unnamed x10, local copies, waits for them, and re-layouts  1.62 us
  transfers between devices with their start and end apart: 15, of which 10 were waited for; matrix products, arithmetic and copies ran while one was open for 0% of the time, Pallas kernels for 19%

profile of v7, /device:TPU:0, one launch (start us, length us, event | category | flops | bytes accessed | tf_op | source)
XLA Modules:
  0.0 35.3 jit_solution(12164413639066283686)
XLA Ops:
  0.0 1.6 %sort_blocks.1 = (bf16[48,128]{1,0:T(8,128)(2,1)}, bf16[48,128]{1,0:T(8,128)(2,1)}, bf16[48,128]{1,0:T(8,128)(2,1)}, bf16[48,128]{1,0:T(8,128)(2,1)}) custom-call(s32[1,8]{1,0:T(1,128)} %bitcast.12, s32[1,8]{1,0:T(1,128)} %bitcast.13, bf16[64,128]{1,0:T(8,128)(2,1)} %bitcast.8, bf16[16,128]{1,0:T(8,128)(2,1)} %bitcast.9, s32[4,2,4]{2,1,0:T(2,128)} %bitcast.10, ...), custom_call_target="tpu_custom_call" | custom-call | flops 100000 | bytes 100000 | tf_op jit(solution)/shard_map/sort_blocks/pallas_call | solution.py:334
  1.7 0.0 copy-start
  1.7 0.9 %copy-done = bf16[1,2,128,2,128]{4,3,2,1,0:T(2,128)(2,1)S(1)} copy-done((bf16[1,2,128,2,128]{4,3,2,1,0:T(2,128)(2,1)S(1)}, bf16[1,2,128,2,128]{4,3,2,1,0:T(2,128)(2,1)}, u32[]{:S(2)}) %copy-start) | copy-done | bytes 131096
  2.6 0.0 copy-start.1
  2.6 0.7 %copy-done.1 = bf16[48,128]{1,0:T(8,128)(2,1)S(1)} copy-done((bf16[48,128]{1,0:T(8,128)(2,1)S(1)}, bf16[48,128]{1,0:T(8,128)(2,1)}, u32[]{:S(2)}) %copy-start.1) | copy-done | bytes 12312
  3.3 0.0 copy-start.4
  3.3 0.0 copy-start.3
  3.3 0.0 copy-start.2
  3.3 3.1 %collective-permute-start.6 = (bf16[256,128]{1,0:T(8,128)(2,1)S(1)}, bf16[256,128]{1,0:T(8,128)(2,1)S(1)}, u32[]{:S(2)}, u32[]{:S(2)}) collective-permute-start(bf16[256,128]{1,0:T(8,128)(2,1)S(1)} %get-tuple-element.22.refs_0_), channel_id=1, source_target_pairs={{0,2},{2,4},{4,6},{6,0},{1,3},{3,5},{5,7},{7,1},{8,10},{10,12},{12... | collective-permute-start | bytes 196616 | tf_op jit(solution)/shard_map/ppermute | solution.py:371
  6.4 0.0 copy-done.4
  6.4 1.6 %collective-permute-start = (bf16[48,128]{1,0:T(8,128)(2,1)S(1)}, bf16[48,128]{1,0:T(8,128)(2,1)S(1)}, u32[]{:S(2)}, u32[]{:S(2)}) collective-permute-start(bf16[48,128]{1,0:T(8,128)(2,1)S(1)} %copy-done.4), channel_id=1, source_target_pairs={{0,2},{2,0},{4,6},{6,4},{1,3},{3,1},{5,7},{7,5},{8,10},{10,8},{12,... | collective-permute-start | bytes 36872 | tf_op jit(solution)/shard_map/ppermute | solution.py:366
  7.9 0.0 copy-done.3
  7.9 1.6 %collective-permute-start.1 = (bf16[48,128]{1,0:T(8,128)(2,1)S(1)}, bf16[48,128]{1,0:T(8,128)(2,1)S(1)}, u32[]{:S(2)}, u32[]{:S(2)}) collective-permute-start(bf16[48,128]{1,0:T(8,128)(2,1)S(1)} %copy-done.3), channel_id=1, source_target_pairs={{0,4},{2,6},{4,0},{6,2},{1,5},{3,7},{5,1},{7,3},{8,12},{10,14},{12... | collective-permute-start | bytes 36872 | tf_op jit(solution)/shard_map/ppermute | solution.py:366
  9.6 0.0 copy-done.2
  9.6 1.2 %collective-permute-start.2 = (bf16[48,128]{1,0:T(8,128)(2,1)S(1)}, bf16[48,128]{1,0:T(8,128)(2,1)S(1)}, u32[]{:S(2)}, u32[]{:S(2)}) collective-permute-start(bf16[48,128]{1,0:T(8,128)(2,1)S(1)} %copy-done.2), channel_id=1, source_target_pairs={{0,6},{2,4},{4,2},{6,0},{1,7},{3,5},{5,3},{7,1},{8,14},{10,12},{12... | collective-permute-start | bytes 36872 | tf_op jit(solution)/shard_map/ppermute | solution.py:366
  10.8 0.1 collective-permute-done.refs_1_
  10.9 1.7 %collective-permute-done.1.refs_2_ = bf16[48,128]{1,0:T(8,128)(2,1)S(1)} collective-permute-done((bf16[48,128]{1,0:T(8,128)(2,1)S(1)}, bf16[48,128]{1,0:T(8,128)(2,1)S(1)}, u32[]{:S(2)}, u32[]{:S(2)}) %collective-permute-start.1) | collective-permute-done | bytes 12320 | tf_op jit(solution)/shard_map/ppermute | solution.py:366
  12.6 2.5 %collective-permute-done.2.refs_3_ = bf16[48,128]{1,0:T(8,128)(2,1)S(1)} collective-permute-done((bf16[48,128]{1,0:T(8,128)(2,1)S(1)}, bf16[48,128]{1,0:T(8,128)(2,1)S(1)}, u32[]{:S(2)}, u32[]{:S(2)}) %collective-permute-start.2) | collective-permute-done | bytes 12320 | tf_op jit(solution)/shard_map/ppermute | solution.py:366
  15.1 1.5 %collective-permute-start.3 = (bf16[4,48,128]{2,1,0:T(8,128)(2,1)S(1)}, bf16[4,48,128]{2,1,0:T(8,128)(2,1)S(1)}, u32[]{:S(2)}, u32[]{:S(2)}) collective-permute-start(bf16[4,48,128]{2,1,0:T(8,128)(2,1)S(1)} %join.1.refs_0_.packed), channel_id=1, source_target_pairs={{0,8},{8,0},{16,24},{24,16},{1,9},{9,1},{17,25},{25,17},{2,10},{10... | collective-permute-start | bytes 147464 | tf_op jit(solution)/shard_map/ppermute | solution.py:376
  16.6 1.5 %collective-permute-start.5 = (bf16[4,48,128]{2,1,0:T(8,128)(2,1)S(1)}, bf16[4,48,128]{2,1,0:T(8,128)(2,1)S(1)}, u32[]{:S(2)}, u32[]{:S(2)}) collective-permute-start(bf16[4,48,128]{2,1,0:T(8,128)(2,1)S(1)} %join.1.refs_0_.packed), channel_id=1, source_target_pairs={{0,24},{8,16},{16,8},{24,0},{1,25},{9,17},{17,9},{25,1},{2,26},{10... | collective-permute-start | bytes 147464 | tf_op jit(solution)/shard_map/ppermute | solution.py:376
  18.1 0.5 %collective-permute-start.4 = (bf16[4,48,128]{2,1,0:T(8,128)(2,1)S(1)}, bf16[4,48,128]{2,1,0:T(8,128)(2,1)S(1)}, u32[]{:S(2)}, u32[]{:S(2)}) collective-permute-start(bf16[4,48,128]{2,1,0:T(8,128)(2,1)S(1)} %join.1.refs_0_.packed), channel_id=1, source_target_pairs={{0,16},{8,24},{16,0},{24,8},{1,17},{9,25},{17,1},{25,9},{2,18},{10... | collective-permute-start | bytes 147464 | tf_op jit(solution)/shard_map/ppermute | solution.py:376
  18.6 0.6 %collective-permute-done.3.refs_1_.refs_2_ = bf16[4,48,128]{2,1,0:T(8,128)(2,1)S(1)} collective-permute-done((bf16[4,48,128]{2,1,0:T(8,128)(2,1)S(1)}, bf16[4,48,128]{2,1,0:T(8,128)(2,1)S(1)}, u32[]{:S(2)}, u32[]{:S(2)}) %collective-permute-start.3) | collective-permute-done | bytes 49184 | tf_op jit(solution)/shard_map/ppermute | solution.py:376
  19.2 0.0 collective-permute-done.6.refs_1_
  19.2 2.9 %collective-permute-start.9 = (bf16[2,256,128]{2,1,0:T(8,128)(2,1)S(1)}, bf16[2,256,128]{2,1,0:T(8,128)(2,1)S(1)}, u32[]{:S(2)}, u32[]{:S(2)}) collective-permute-start(bf16[2,256,128]{2,1,0:T(8,128)(2,1)S(1)} %stack_halves.1.refs_0_), channel_id=1, source_target_pairs={{0,24},{8,16},{16,8},{24,0},{1,25},{9,17},{17,9},{25,1},{2,26},{10... | collective-permute-start | bytes 393224 | tf_op jit(solution)/shard_map/ppermute | solution.py:384
  22.1 0.1 collective-permute-start.8
  22.2 0.5 %collective-permute-start.7 = (bf16[2,256,128]{2,1,0:T(8,128)(2,1)S(1)}, bf16[2,256,128]{2,1,0:T(8,128)(2,1)S(1)}, u32[]{:S(2)}, u32[]{:S(2)}) collective-permute-start(bf16[2,256,128]{2,1,0:T(8,128)(2,1)S(1)} %stack_halves.1.refs_0_), channel_id=1, source_target_pairs={{0,8},{8,0},{16,24},{24,16},{1,9},{9,1},{17,25},{25,17},{2,10},{10... | collective-permute-start | bytes 393224 | tf_op jit(solution)/shard_map/ppermute | solution.py:384
  22.8 0.0 collective-permute-done.5.refs_3_
  22.8 0.4 %collective-permute-done.4.refs_2_ = bf16[4,48,128]{2,1,0:T(8,128)(2,1)S(1)} collective-permute-done((bf16[4,48,128]{2,1,0:T(8,128)(2,1)S(1)}, bf16[4,48,128]{2,1,0:T(8,128)(2,1)S(1)}, u32[]{:S(2)}, u32[]{:S(2)}) %collective-permute-start.4) | collective-permute-done | bytes 49184 | tf_op jit(solution)/shard_map/ppermute | solution.py:376
  23.2 6.8 %grid.1.grids = f32[8,256,128]{2,1,0:T(8,128)S(1)} custom-call(bf16[4,48,128]{2,1,0:T(8,128)(2,1)S(1)} %join.1.refs_0_.packed, bf16[4,48,128]{2,1,0:T(8,128)(2,1)S(1)} %collective-permute-done.3.refs_1_.refs_2_, bf16[4,48,128]{2,1,0:T(8,128)(2,1)S(1)} %collective-permute-done.4.refs_2_, bf16[4,48,128]{2,1,0:T(8,128)(2,1)S(1)} %collective-permute-done.5.refs_3_), custom_call_target="tpu_custom_call" | custom-call | flops 4000000000 | bytes 2000000 | tf_op jit(solution)/shard_map/grid/pallas_call | solution.py:386
  30.0 0.1 collective-permute-start.10
  30.1 0.0 collective-permute-done.9.refs_3_
  30.1 0.0 collective-permute-done.8.refs_2_
  30.1 0.0 collective-permute-done.7.refs_1_
  30.1 0.5 %collective-permute-start.11 = (bf16[2,256,128]{2,1,0:T(8,128)(2,1)S(1)}, bf16[2,256,128]{2,1,0:T(8,128)(2,1)S(1)}, u32[]{:S(2)}, u32[]{:S(2)}) collective-permute-start(bf16[2,256,128]{2,1,0:T(8,128)(2,1)S(1)} %collective-permute-done.7.refs_1_), channel_id=1, source_target_pairs={{0,1},{1,0},{2,3},{3,2},{4,5},{5,4},{6,7},{7,6},{8,9},{9,8},{10,11... | collective-permute-start | bytes 393224 | tf_op jit(solution)/shard_map/ppermute | solution.py:407
  30.6 0.1 collective-permute-start.12
  30.7 0.4 %collective-permute-start.13 = (bf16[2,256,128]{2,1,0:T(8,128)(2,1)S(1)}, bf16[2,256,128]{2,1,0:T(8,128)(2,1)S(1)}, u32[]{:S(2)}, u32[]{:S(2)}) collective-permute-start(bf16[2,256,128]{2,1,0:T(8,128)(2,1)S(1)} %collective-permute-done.9.refs_3_), channel_id=1, source_target_pairs={{0,1},{1,0},{2,3},{3,2},{4,5},{5,4},{6,7},{7,6},{8,9},{9,8},{10,11... | collective-permute-start | bytes 393224 | tf_op jit(solution)/shard_map/ppermute | solution.py:407
  31.1 0.2 collective-permute-done.10.refs_4_
  31.4 0.2 collective-permute-done.11.refs_5_
  31.6 0.4 %collective-permute-done.12.refs_6_ = bf16[2,256,128]{2,1,0:T(8,128)(2,1)S(1)} collective-permute-done((bf16[2,256,128]{2,1,0:T(8,128)(2,1)S(1)}, bf16[2,256,128]{2,1,0:T(8,128)(2,1)S(1)}, u32[]{:S(2)}, u32[]{:S(2)}) %collective-permute-start.12) | collective-permute-done | bytes 131104 | tf_op jit(solution)/shard_map/ppermute | solution.py:407
  32.0 0.2 collective-permute-done.13.refs_7_
  32.2 1.1 %apply_tables.1 = (f32[64,256]{1,0:T(8,128)S(1)}, f32[64,256]{1,0:T(8,128)S(1)}) custom-call(f32[8,256,128]{2,1,0:T(8,128)S(1)} %grid.1.grids, bf16[4,48,128]{2,1,0:T(8,128)(2,1)S(1)} %join.1.refs_0_.packed, bf16[2,256,128]{2,1,0:T(8,128)(2,1)S(1)} %stack_halves.1.refs_0_, bf16[2,256,128]{2,1,0:T(8,128)(2,1)S(1)} %collective-permute-done.7.refs_1_, ...), custom_call_target="tpu_custom_call" | custom-call | flops 1000000000 | bytes 2000000 | tf_op jit(solution)/shard_map/apply_tables/pallas_call | solution.py:408
  33.3 0.4 %collective-permute-start.14 = (f32[64,256]{1,0:T(8,128)S(1)}, f32[64,256]{1,0:T(8,128)S(1)}, u32[]{:S(2)}, u32[]{:S(2)}) collective-permute-start(f32[64,256]{1,0:T(8,128)S(1)} %get-tuple-element.28), channel_id=1, source_target_pairs={{0,1},{1,0},{2,3},{3,2},{4,5},{5,4},{6,7},{7,6},{8,9},{9,8},{10,11... | collective-permute-start | bytes 196616 | tf_op jit(solution)/shard_map/ppermute | solution.py:423
  33.6 0.9 %collective-permute-done.14 = f32[64,256]{1,0:T(8,128)S(1)} collective-permute-done((f32[64,256]{1,0:T(8,128)S(1)}, f32[64,256]{1,0:T(8,128)S(1)}, u32[]{:S(2)}, u32[]{:S(2)}) %collective-permute-start.14) | collective-permute-done | bytes 65568 | tf_op jit(solution)/shard_map/ppermute | solution.py:423
  34.6 0.7 %reshape.19 = f32[1,1,64,2,128]{4,3,2,1,0:T(2,128)} reshape(f32[64,256]{1,0:T(8,128)S(1)} %add.3) | data formatting | bytes 131072 | tf_op jit(solution)/shard_map/reshape | solution.py:424
  (4 shorter events, 0.0 us)
Async XLA Ops:
  1.7 0.9 %copy-start = (bf16[1,2,128,2,128]{4,3,2,1,0:T(2,128)(2,1)S(1)}, bf16[1,2,128,2,128]{4,3,2,1,0:T(2,128)(2,1)}, u32[]{:S(2)}) copy-start(bf16[1,2,128,2,128]{4,3,2,1,0:T(2,128)(2,1)} %param.14) | copy-start | bytes 393220
  2.6 0.7 %copy-start.1 = (bf16[48,128]{1,0:T(8,128)(2,1)S(1)}, bf16[48,128]{1,0:T(8,128)(2,1)}, u32[]{:S(2)}) copy-start(bf16[48,128]{1,0:T(8,128)(2,1)} %get-tuple-element.17.piece) | copy-start | bytes 36868
  3.3 3.1 %copy-start.4 = (bf16[48,128]{1,0:T(8,128)(2,1)S(1)}, bf16[48,128]{1,0:T(8,128)(2,1)}, u32[]{:S(2)}) copy-start(bf16[48,128]{1,0:T(8,128)(2,1)} %get-tuple-element.19) | copy-start | bytes 36868
  3.3 4.7 %copy-start.3 = (bf16[48,128]{1,0:T(8,128)(2,1)S(1)}, bf16[48,128]{1,0:T(8,128)(2,1)}, u32[]{:S(2)}) copy-start(bf16[48,128]{1,0:T(8,128)(2,1)} %get-tuple-element.20) | copy-start | bytes 36868
  3.3 6.3 %copy-start.2 = (bf16[48,128]{1,0:T(8,128)(2,1)S(1)}, bf16[48,128]{1,0:T(8,128)(2,1)}, u32[]{:S(2)}) copy-start(bf16[48,128]{1,0:T(8,128)(2,1)} %get-tuple-element.21) | copy-start | bytes 36868
  3.3 15.9 %collective-permute-start.6 = (bf16[256,128]{1,0:T(8,128)(2,1)S(1)}, bf16[256,128]{1,0:T(8,128)(2,1)S(1)}, u32[]{:S(2)}, u32[]{:S(2)}) collective-permute-start(bf16[256,128]{1,0:T(8,128)(2,1)S(1)} %get-tuple-element.22.refs_0_), channel_id=1, source_target_pairs={{0,2},{2,4},{4,6},{6,0},{1,3},{3,5},{5,7},{7,1},{8,10},{10,12},{12... | collective-permute-start | bytes 196616 | tf_op jit(solution)/shard_map/ppermute | solution.py:371
  6.4 4.5 %collective-permute-start = (bf16[48,128]{1,0:T(8,128)(2,1)S(1)}, bf16[48,128]{1,0:T(8,128)(2,1)S(1)}, u32[]{:S(2)}, u32[]{:S(2)}) collective-permute-start(bf16[48,128]{1,0:T(8,128)(2,1)S(1)} %copy-done.4), channel_id=1, source_target_pairs={{0,2},{2,0},{4,6},{6,4},{1,3},{3,1},{5,7},{7,5},{8,10},{10,8},{12,... | collective-permute-start | bytes 36872 | tf_op jit(solution)/shard_map/ppermute | solution.py:366
  7.9 4.6 %collective-permute-start.1 = (bf16[48,128]{1,0:T(8,128)(2,1)S(1)}, bf16[48,128]{1,0:T(8,128)(2,1)S(1)}, u32[]{:S(2)}, u32[]{:S(2)}) collective-permute-start(bf16[48,128]{1,0:T(8,128)(2,1)S(1)} %copy-done.3), channel_id=1, source_target_pairs={{0,4},{2,6},{4,0},{6,2},{1,5},{3,7},{5,1},{7,3},{8,12},{10,14},{12... | collective-permute-start | bytes 36872 | tf_op jit(solution)/shard_map/ppermute | solution.py:366
  9.6 5.5 %collective-permute-start.2 = (bf16[48,128]{1,0:T(8,128)(2,1)S(1)}, bf16[48,128]{1,0:T(8,128)(2,1)S(1)}, u32[]{:S(2)}, u32[]{:S(2)}) collective-permute-start(bf16[48,128]{1,0:T(8,128)(2,1)S(1)} %copy-done.2), channel_id=1, source_target_pairs={{0,6},{2,4},{4,2},{6,0},{1,7},{3,5},{5,3},{7,1},{8,14},{10,12},{12... | collective-permute-start | bytes 36872 | tf_op jit(solution)/shard_map/ppermute | solution.py:366
  15.1 4.1 %collective-permute-start.3 = (bf16[4,48,128]{2,1,0:T(8,128)(2,1)S(1)}, bf16[4,48,128]{2,1,0:T(8,128)(2,1)S(1)}, u32[]{:S(2)}, u32[]{:S(2)}) collective-permute-start(bf16[4,48,128]{2,1,0:T(8,128)(2,1)S(1)} %join.1.refs_0_.packed), channel_id=1, source_target_pairs={{0,8},{8,0},{16,24},{24,16},{1,9},{9,1},{17,25},{25,17},{2,10},{10... | collective-permute-start | bytes 147464 | tf_op jit(solution)/shard_map/ppermute | solution.py:376
  16.6 6.2 %collective-permute-start.5 = (bf16[4,48,128]{2,1,0:T(8,128)(2,1)S(1)}, bf16[4,48,128]{2,1,0:T(8,128)(2,1)S(1)}, u32[]{:S(2)}, u32[]{:S(2)}) collective-permute-start(bf16[4,48,128]{2,1,0:T(8,128)(2,1)S(1)} %join.1.refs_0_.packed), channel_id=1, source_target_pairs={{0,24},{8,16},{16,8},{24,0},{1,25},{9,17},{17,9},{25,1},{2,26},{10... | collective-permute-start | bytes 147464 | tf_op jit(solution)/shard_map/ppermute | solution.py:376
  18.1 5.1 %collective-permute-start.4 = (bf16[4,48,128]{2,1,0:T(8,128)(2,1)S(1)}, bf16[4,48,128]{2,1,0:T(8,128)(2,1)S(1)}, u32[]{:S(2)}, u32[]{:S(2)}) collective-permute-start(bf16[4,48,128]{2,1,0:T(8,128)(2,1)S(1)} %join.1.refs_0_.packed), channel_id=1, source_target_pairs={{0,16},{8,24},{16,0},{24,8},{1,17},{9,25},{17,1},{25,9},{2,18},{10... | collective-permute-start | bytes 147464 | tf_op jit(solution)/shard_map/ppermute | solution.py:376
  19.2 10.9 %collective-permute-start.9 = (bf16[2,256,128]{2,1,0:T(8,128)(2,1)S(1)}, bf16[2,256,128]{2,1,0:T(8,128)(2,1)S(1)}, u32[]{:S(2)}, u32[]{:S(2)}) collective-permute-start(bf16[2,256,128]{2,1,0:T(8,128)(2,1)S(1)} %stack_halves.1.refs_0_), channel_id=1, source_target_pairs={{0,24},{8,16},{16,8},{24,0},{1,25},{9,17},{17,9},{25,1},{2,26},{10... | collective-permute-start | bytes 393224 | tf_op jit(solution)/shard_map/ppermute | solution.py:384
  22.1 7.9 %collective-permute-start.8 = (bf16[2,256,128]{2,1,0:T(8,128)(2,1)S(1)}, bf16[2,256,128]{2,1,0:T(8,128)(2,1)S(1)}, u32[]{:S(2)}, u32[]{:S(2)}) collective-permute-start(bf16[2,256,128]{2,1,0:T(8,128)(2,1)S(1)} %stack_halves.1.refs_0_), channel_id=1, source_target_pairs={{0,16},{8,24},{16,0},{24,8},{1,17},{9,25},{17,1},{25,9},{2,18},{10... | collective-permute-start | bytes 393224 | tf_op jit(solution)/shard_map/ppermute | solution.py:384
  22.2 7.9 %collective-permute-start.7 = (bf16[2,256,128]{2,1,0:T(8,128)(2,1)S(1)}, bf16[2,256,128]{2,1,0:T(8,128)(2,1)S(1)}, u32[]{:S(2)}, u32[]{:S(2)}) collective-permute-start(bf16[2,256,128]{2,1,0:T(8,128)(2,1)S(1)} %stack_halves.1.refs_0_), channel_id=1, source_target_pairs={{0,8},{8,0},{16,24},{24,16},{1,9},{9,1},{17,25},{25,17},{2,10},{10... | collective-permute-start | bytes 393224 | tf_op jit(solution)/shard_map/ppermute | solution.py:384
  30.0 1.4 %collective-permute-start.10 = (bf16[2,256,128]{2,1,0:T(8,128)(2,1)S(1)}, bf16[2,256,128]{2,1,0:T(8,128)(2,1)S(1)}, u32[]{:S(2)}, u32[]{:S(2)}) collective-permute-start(bf16[2,256,128]{2,1,0:T(8,128)(2,1)S(1)} %stack_halves.1.refs_0_), channel_id=1, source_target_pairs={{0,1},{1,0},{2,3},{3,2},{4,5},{5,4},{6,7},{7,6},{8,9},{9,8},{10,11... | collective-permute-start | bytes 393224 | tf_op jit(solution)/shard_map/ppermute | solution.py:407
  30.1 1.5 %collective-permute-start.11 = (bf16[2,256,128]{2,1,0:T(8,128)(2,1)S(1)}, bf16[2,256,128]{2,1,0:T(8,128)(2,1)S(1)}, u32[]{:S(2)}, u32[]{:S(2)}) collective-permute-start(bf16[2,256,128]{2,1,0:T(8,128)(2,1)S(1)} %collective-permute-done.7.refs_1_), channel_id=1, source_target_pairs={{0,1},{1,0},{2,3},{3,2},{4,5},{5,4},{6,7},{7,6},{8,9},{9,8},{10,11... | collective-permute-start | bytes 393224 | tf_op jit(solution)/shard_map/ppermute | solution.py:407
  30.6 1.3 %collective-permute-start.12 = (bf16[2,256,128]{2,1,0:T(8,128)(2,1)S(1)}, bf16[2,256,128]{2,1,0:T(8,128)(2,1)S(1)}, u32[]{:S(2)}, u32[]{:S(2)}) collective-permute-start(bf16[2,256,128]{2,1,0:T(8,128)(2,1)S(1)} %collective-permute-done.8.refs_2_), channel_id=1, source_target_pairs={{0,1},{1,0},{2,3},{3,2},{4,5},{5,4},{6,7},{7,6},{8,9},{9,8},{10,11... | collective-permute-start | bytes 393224 | tf_op jit(solution)/shard_map/ppermute | solution.py:407
  30.7 1.5 %collective-permute-start.13 = (bf16[2,256,128]{2,1,0:T(8,128)(2,1)S(1)}, bf16[2,256,128]{2,1,0:T(8,128)(2,1)S(1)}, u32[]{:S(2)}, u32[]{:S(2)}) collective-permute-start(bf16[2,256,128]{2,1,0:T(8,128)(2,1)S(1)} %collective-permute-done.9.refs_3_), channel_id=1, source_target_pairs={{0,1},{1,0},{2,3},{3,2},{4,5},{5,4},{6,7},{7,6},{8,9},{9,8},{10,11... | collective-permute-start | bytes 393224 | tf_op jit(solution)/shard_map/ppermute | solution.py:407
  33.3 1.3 %collective-permute-start.14 = (f32[64,256]{1,0:T(8,128)S(1)}, f32[64,256]{1,0:T(8,128)S(1)}, u32[]{:S(2)}, u32[]{:S(2)}) collective-permute-start(f32[64,256]{1,0:T(8,128)S(1)} %get-tuple-element.28), channel_id=1, source_target_pairs={{0,1},{1,0},{2,3},{3,2},{4,5},{5,4},{6,7},{7,6},{8,9},{9,8},{10,11... | collective-permute-start | bytes 196616 | tf_op jit(solution)/shard_map/ppermute | solution.py:423

commit v8 on v4

--- a/solution.py
+++ b/solution.py
@@ -55,14 +55,15 @@
 
 
 def sort_kernel(sizes, *refs):
-    groups, held, chans, cap, rows = sizes
+    facets, groups, held, chans, cap, rows = sizes
     out_ref = refs[7]
-    plane_ref, group_ref, samples_b, place_b, offsets_ref, centre_ref, gain_ref = refs[8:15]
+    targets = refs[8:15]
+    plane_ref, group_ref, samples_b, place_b, offsets_ref, centre_ref, gain_ref = targets
     samples, place, sorted_, filled, sems = refs[15:]
     facet = lax.axis_index("facet")
     copies = [
         pltpu.make_async_copy(source, target, sems.at[n])
-        for n, (source, target) in enumerate(zip(refs[:7], refs[8:15]))
+        for n, (source, target) in enumerate(zip(refs[:7], targets))
     ]
     for copy in copies:
         copy.start()
@@ -103,30 +104,34 @@
         sorted_[g, meta : meta + 1, :] += jnp.where(
             lane == k, (plane_ref[0, i] + 1).astype(jnp.float32), 0.0
         )
-    out_ref[...] = sorted_[...].astype(jnp.bfloat16)
+    for g in range(groups):
+        rows_of = sorted_[g].astype(jnp.bfloat16)
+        for f in range(facets):
+            out_ref[f * groups + g] = rows_of
 
 
 def grid_kernel(sizes, *refs):
     facets, groups, chans, cap, rows = sizes
-    packed_refs = refs[:facets]
-    grids = refs[facets]
-    meta_v, meta_s, order, spots_u, spots_v, turns_real, turns_imag, sem = refs[facets + 1 :]
+    packed, grids = refs[:2]
+    meta_v, meta_s, order, spots_u, spots_v, turns_real, turns_imag, sem = refs[2:]
     devices = facets * groups
     slots = 2 * facets
     lines = cap * chans
     meta_row = 2 * (lines + cap)
     tail = meta_row // 16 * 16
+    facet = lax.axis_index("facet")
     group = lax.axis_index("bl")
     chan = lax.axis_index("chan")
 
-    for f in range(facets):
-        for g in range(groups):
-            meta = packed_refs[f][g, tail : tail + 16, :].astype(jnp.float32)
-            meta_v[f * groups + g : f * groups + g + 1, :] = meta[
-                meta_row - tail : meta_row - tail + 1
-            ].astype(jnp.int32)
-            if f == 0 and g == 0:
-                numbers = meta[meta_row - tail + 1 : meta_row - tail + 2]
+    lane = lax.broadcasted_iota(jnp.int32, (1, SU), 1)
+    own = packed[facet * groups + group, tail : tail + 16, :].astype(jnp.float32)
+    numbers = own[meta_row - tail + 1 : meta_row - tail + 2]
+    for d in range(devices):
+        meta = packed[d, tail : tail + 16, :].astype(jnp.float32)
+        plane = meta[meta_row - tail : meta_row - tail + 1].astype(jnp.int32) - 1
+        set_id = jnp.where(lax.rem(plane, groups) == group, 0, 1)
+        code = (d * cap + lane) * slots + 2 * lax.div(plane, groups) + set_id
+        meta_v[d : d + 1, :] = jnp.where(plane >= 0, code, -1)
     copy = pltpu.make_async_copy(meta_v, meta_s, sem)
     copy.start()
     grids[...] = jnp.zeros_like(grids)
@@ -147,43 +152,37 @@
             [jnp.broadcast_to(place[k : k + 1], (chans, SU)) for k in range(cap)], axis=0
         )
 
-    for f in range(facets):
-        for g in range(groups):
-            at = (f * groups + g) * lines
-            wide = packed_refs[f][g].astype(jnp.float32)
-            real = wide[:lines]
-            imag = wide[lines : 2 * lines]
-            along_u = spread_lines(wide[2 * lines : 2 * lines + cap])
-            along_v = spread_lines(wide[2 * lines + cap : 2 * (lines + cap)])
-            cosine, sine = cos_sin(
-                (1.0 / SU) * (scale * (along_u * along_l + along_v * along_m))
-            )
-            spots_u[at : at + lines, :] = ALPHA * (scale * along_u - offset_u)
-            spots_v[at : at + lines, :] = ALPHA * (scale * along_v - offset_v)
-            turns_real[at : at + lines, :] = real * cosine - imag * sine
-            turns_imag[at : at + lines, :] = real * sine + imag * cosine
+    for d in range(devices):
+        at = d * lines
+        wide = packed[d].astype(jnp.float32)
+        real = wide[:lines]
+        imag = wide[lines : 2 * lines]
+        along_u = spread_lines(wide[2 * lines : 2 * lines + cap])
+        along_v = spread_lines(wide[2 * lines + cap : 2 * (lines + cap)])
+        cosine, sine = cos_sin((1.0 / SU) * (scale * (along_u * along_l + along_v * along_m)))
+        spots_u[at : at + lines, :] = ALPHA * (scale * along_u - offset_u)
+        spots_v[at : at + lines, :] = ALPHA * (scale * along_v - offset_v)
+        turns_real[at : at + lines, :] = real * cosine - imag * sine
+        turns_imag[at : at + lines, :] = real * sine + imag * cosine
     last = devices * lines
     for ref in (spots_u, spots_v, turns_real, turns_imag):
         ref[last : last + 8, :] = jnp.zeros((8, SU), jnp.float32)
     copy.wait()
 
-    def pick(d, count):
+    count = jnp.int32(0)
+    for d in range(devices):
         for k in range(cap):
-            plane = meta_s[d, k] - 1
-            set_id = jnp.where(lax.rem(plane, groups) == group, 0, 1)
-            order[count] = (d * cap + k) * slots + 2 * lax.div(plane, groups) + set_id
-            count = count + jnp.where(plane >= 0, 1, 0)
-        return count
-
-    count = lax.fori_loop(0, devices, pick, 0)
+            code = meta_s[d, k]
+            order[count] = code
+            count = count + jnp.where(code >= 0, 1, 0)
     for i in range(UNROLL):
         order[count + i] = devices * cap * slots
 
     cells = ALPHA * lax.broadcasted_iota(jnp.int32, (SU, SU), 0).astype(jnp.float32)
 
     def profile(spot):
-        apart = (spot - cells).astype(jnp.bfloat16)
-        return jnp.exp2(-(apart * apart))
+        apart = spot - cells
+        return jnp.exp2(-(apart * apart)).astype(jnp.bfloat16)
 
     def tiled(row):
         return jnp.broadcast_to(row, (16, SU)).astype(jnp.bfloat16)[None]
@@ -221,11 +220,11 @@
             out_ref[f, n] = table
 
 
-def table_kernel(sizes, norm, grids, own, swapped, packed, mine_ref, other_ref, table_f, total):
+def table_kernel(sizes, norm, grids, packed, ours, theirs, mine_ref, other_ref, table_f, total):
     slots, meta_row = sizes
     chan = lax.axis_index("chan")
-    group = lax.axis_index("bl")
     first = chan == 0
+    own = lax.axis_index("facet") * lax.axis_size("bl") + lax.axis_index("bl")
 
     def parts(table):
         table_f[...] = table
@@ -233,9 +232,10 @@
 
     result = jnp.zeros((SU, 2 * SU), jnp.float32)
     for s in range(slots):
-        ours = own[s].astype(jnp.float32)
-        theirs = swapped[s].astype(jnp.float32)
-        u_real, u_imag = parts(jnp.where(first, ours, theirs))
+        origin, set_id = divmod(s, 2)
+        fetched = ours[origin, set_id].astype(jnp.float32)
+        swapped = theirs[origin, set_id].astype(jnp.float32)
+        u_real, u_imag = parts(jnp.where(first, fetched, swapped))
         u_side = jnp.concatenate([u_real.T, u_imag.T], axis=1).astype(jnp.bfloat16)
         grid_real = grids[s, :SU, :]
         grid_imag = grids[s, SU:, :]
@@ -250,7 +250,7 @@
         half = jnp.dot(u_side, high, preferred_element_type=jnp.float32) + jnp.dot(
             u_side, low, preferred_element_type=jnp.float32
         )
-        v_real, v_imag = parts(jnp.where(first, theirs, ours))
+        v_real, v_imag = parts(jnp.where(first, swapped, fetched))
         v_side = jnp.concatenate(
             [
                 jnp.concatenate([v_real, v_imag], axis=1),
@@ -265,7 +265,7 @@
             + jnp.dot(low, v_side, preferred_element_type=jnp.float32)
         )
     tail = meta_row // 16 * 16
-    wide = packed[group, tail : tail + 16, :].astype(jnp.float32)
+    wide = packed[own, tail : tail + 16, :].astype(jnp.float32)
     at = meta_row - tail + 2
     gain = (wide[at : at + 2] + wide[at + 2 : at + 4]) + wide[at + 4 : at + 6]
     gain_u = jnp.broadcast_to(gain[0:1], (SU, SU)).T
@@ -291,9 +291,10 @@
     half_rows = SU // chan_count
     norm = SU / math.sqrt(visibilities.shape[3] * held * facets * CH)
 
+    own_table = tables.reshape(2, 2 * SU, SU)
     packed = pl.pallas_call(
-        functools.partial(sort_kernel, (groups, held, chans, cap, rows)),
-        out_shape=jax.ShapeDtypeStruct((groups, rows, SU), jnp.bfloat16),
+        functools.partial(sort_kernel, (facets, groups, held, chans, cap, rows)),
+        out_shape=jax.ShapeDtypeStruct((devices, rows, SU), jnp.bfloat16),
         in_specs=[HBM] * 7,
         out_specs=VMEM,
         scratch_shapes=[
@@ -322,32 +323,24 @@
         facet_centre.T,
         antenna_gain,
     )
-    here = lax.all_to_all(packed, "bl", split_axis=0, concat_axis=0, tiled=True)
-    blocks = [here] + [
-        lax.ppermute(here, "facet", [(f, (f + shift) % facets) for f in range(facets)])
-        for shift in range(1, facets)
-    ]
-
-    swap = [(c, 1 - c) for c in range(chan_count)]
-    own_table = tables.reshape(2, 2 * SU, SU)
+    blocks = lax.all_to_all(packed, ("facet", "bl"), split_axis=0, concat_axis=0, tiled=True)
     shifted = lax.ppermute(own_table, "bl", [(g, (g + 1) % groups) for g in range(groups)])
+    own_table, packed = lax.optimization_barrier((own_table, packed))
     spread = pl.pallas_call(
         spread_kernel,
         out_shape=jax.ShapeDtypeStruct((facets, 2, 2 * SU, SU), jnp.bfloat16),
         in_specs=[VMEM, VMEM],
         out_specs=VMEM,
         compiler_params=PARAMS,
-        cost_estimate=pl.CostEstimate(flops=0, bytes_accessed=1_000_000, transcendentals=0),
+        cost_estimate=pl.CostEstimate(flops=0, bytes_accessed=800_000, transcendentals=0),
         name="spread_tables",
     )(own_table, shifted)
-    slot_tables = lax.all_to_all(spread, "facet", split_axis=0, concat_axis=0, tiled=True)
-    slot_tables = slot_tables.reshape(slots, 2 * SU, SU)
-    swapped_tables = lax.ppermute(slot_tables, "chan", swap)
+    fetched = lax.all_to_all(spread, "facet", split_axis=0, concat_axis=0, tiled=True)
 
     grids = pl.pallas_call(
         functools.partial(grid_kernel, (facets, groups, chans, cap, rows)),
         out_shape=jax.ShapeDtypeStruct((slots, 2 * SU, SU), jnp.float32),
-        in_specs=[VMEM] * facets,
+        in_specs=[VMEM],
         out_specs=VMEM,
         scratch_shapes=[
             pltpu.VMEM((devices, SU), jnp.int32),
@@ -361,7 +354,10 @@
             flops=4_000_000_000, bytes_accessed=2_000_000, transcendentals=4_000_000
         ),
         name="grid",
-    )(*blocks)
+    )(blocks)
+    swap = [(c, 1 - c) for c in range(chan_count)]
+    grids, fetched = lax.optimization_barrier((grids, fetched))
+    swapped = lax.ppermute(fetched, "chan", swap)
     mine, other = pl.pallas_call(
         functools.partial(table_kernel, (slots, meta_row), norm),
         out_shape=[jax.ShapeDtypeStruct((half_rows, 2 * SU), jnp.float32)] * 2,
@@ -376,9 +372,9 @@
             flops=1_000_000_000, bytes_accessed=2_000_000, transcendentals=0
         ),
         name="apply_tables",
-    )(grids, slot_tables, swapped_tables, here)
-    arrived = lax.ppermute(other, "chan", swap)
-    return (mine + arrived).reshape(1, 1, half_rows, 2, SU)
+    )(grids, blocks, fetched, swapped)
+    summand = lax.ppermute(other, "chan", swap)
+    return (mine + summand).reshape(1, 1, half_rows, 2, SU)
 
 
 def solution(mesh):

time: 46.5 us -> 37.5 us (0.81)
  blocking collectives: 20.2 us -> 0 us
  starting transfers between devices: 6.93 us -> 14.1 us
  waiting for transfers between devices: 8.72 us -> 13.1 us
  local copies, waits for them, and re-layouts: 1.57 us -> 0.67 us
  Pallas kernels: 8.72 us -> 9.29 us
    all_to_all x2 -> x0, blocking collectives: 20.2 us -> none  [the longest x1 11.2 us: body(): lax.all_to_all(spread, 'facet', split_axis=0, concat_axis=0, tiled=True)]
    all_to_all x0 -> x2, starting transfers between devices: none -> 11.9 us  [the longest x1 8.45 us: body(): lax.all_to_all(packed, ('facet', 'bl'), split_axis=0, concat_axis=0, tile...]
    ppermute x5 -> x2, starting transfers between devices: 3.91 us -> 0.21 us  [the longest x1 0.2 us: body(): summand = lax.ppermute(other, 'chan', swap)]
    ppermute x1, waiting for transfers between devices: 5.73 us -> 8.06 us  [body(): lax.ppermute(own_table, 'bl', [(g, (g + 1) % groups) for g in range(group...]
    all_to_all x0 -> x2, waiting for transfers between devices: none -> 2 us  [the longest x1 1.06 us: body(): lax.all_to_all(packed, ('facet', 'bl'), split_axis=0, concat_axis=0, tile...]
    ppermute x1, starting transfers between devices: 3.02 us -> 1.97 us  [body(): lax.ppermute(own_table, 'bl', [(g, (g + 1) % groups) for g in range(group...]
    unnamed x2, local copies, waits for them, and re-layouts: 0.9 us -> 0.01 us
    pallas_call x1, Pallas kernels: 0.07 us -> 0.87 us  [body(): pl.pallas_call(spread_kernel, out_shape=jax.ShapeDtypeStruct((facets, 2,...]
  transfers between devices with their start and end apart: 6 -> 5, of which waited for: 5 -> 5; matrix products, arithmetic and copies ran while one was open for 0% -> 0% of each run, Pallas kernels for 16% -> 17%
where the time goes in v8:
time: 37.5 us; the launch traced here: 37.2 us
  starting transfers between devices  14.1 us (38%)
  waiting for transfers between devices  13.1 us (35%)
  Pallas kernels  9.29 us (25%)
  local copies, waits for them, and re-layouts  0.67 us (2%)
    all_to_all x1, starting transfers between devices, body(): lax.all_to_all(packed, ('facet', 'bl'), split_axis=0, concat_axis=0, tile...  8.45 us
    ppermute x1, waiting for transfers between devices, body(): lax.ppermute(own_table, 'bl', [(g, (g + 1) % groups) for g in range(group...  8.06 us
    pallas_call x1, Pallas kernels, body(): pl.pallas_call(functools.partial(grid_kernel, (facets, groups, chans, cap...  5.6 us
    all_to_all x1, starting transfers between devices, body(): lax.all_to_all(spread, 'facet', split_axis=0, concat_axis=0, tiled=True)  3.47 us
    ppermute x1, starting transfers between devices, body(): lax.ppermute(own_table, 'bl', [(g, (g + 1) % groups) for g in range(group...  1.97 us
    ppermute x1, waiting for transfers between devices, body(): swapped = lax.ppermute(fetched, 'chan', swap)  1.91 us
    pallas_call x1, Pallas kernels, body(): pl.pallas_call(functools.partial(sort_kernel, (facets, groups, held, chan...  1.72 us
    ppermute x1, waiting for transfers between devices, body(): summand = lax.ppermute(other, 'chan', swap)  1.12 us
  transfers between devices with their start and end apart: 5, of which 5 were waited for; matrix products, arithmetic and copies ran while one was open for 0% of the time, Pallas kernels for 17%

profile of v8, /device:TPU:0, one launch (start us, length us, event | category | flops | bytes accessed | tf_op | source)
XLA Modules:
  0.0 37.2 jit_solution(68847389619951395)
XLA Ops:
  0.0 1.7 %sort_blocks.1 = bf16[16,48,128]{2,1,0:T(8,128)(2,1)} custom-call(s32[1,8]{1,0:T(1,128)} %bitcast.13, s32[1,8]{1,0:T(1,128)} %bitcast.14, bf16[64,128]{1,0:T(8,128)(2,1)} %bitcast.9, bf16[16,128]{1,0:T(8,128)(2,1)} %bitcast.10, s32[4,2,4]{2,1,0:T(2,128)} %bitcast.11, f32[2,4]{1,0:T(2,128)} %bitcast.12, f32[1,2,128]{2,1,0:T(2,128)} %refs_6_.1), custom_call_target="tpu_custom_call" | custom-call | flops 100000 | bytes 100000 | tf_op jit(solution)/shard_map/sort_blocks/pallas_call | solution.py:295
  1.7 0.0 copy-start
  1.7 8.5 %all-to-all-start = ((bf16[16,48,128]{2,1,0:T(8,128)(2,1)}), bf16[16,48,128]{2,1,0:T(8,128)(2,1)S(1)}, u32[]{:S(2)}, u32[]{:S(2)}) async-start(bf16[16,48,128]{2,1,0:T(8,128)(2,1)} %sort_blocks.1), calls=%async_computation | async-start | bytes 393216 | tf_op jit(solution)/shard_map/all_to_all | solution.py:326
  10.2 0.0 copy-done
  10.2 2.0 %collective-permute-start = (bf16[2,256,128]{2,1,0:T(8,128)(2,1)S(1)}, bf16[2,256,128]{2,1,0:T(8,128)(2,1)S(1)}, u32[]{:S(2)}, u32[]{:S(2)}) collective-permute-start(bf16[2,256,128]{2,1,0:T(8,128)(2,1)S(1)} %bitcast.7), channel_id=1, source_target_pairs={{0,2},{2,4},{4,6},{6,0},{1,3},{3,5},{5,7},{7,1},{8,10},{10,12},{12... | collective-permute-start | bytes 393224 | tf_op jit(solution)/shard_map/ppermute | solution.py:327
  12.2 8.1 %collective-permute-done.shifted = bf16[2,256,128]{2,1,0:T(8,128)(2,1)S(1)} collective-permute-done((bf16[2,256,128]{2,1,0:T(8,128)(2,1)S(1)}, bf16[2,256,128]{2,1,0:T(8,128)(2,1)S(1)}, u32[]{:S(2)}, u32[]{:S(2)}) %collective-permute-start) | collective-permute-done | bytes 131104 | tf_op jit(solution)/shard_map/ppermute | solution.py:327
  20.2 0.9 %spread_tables.1 = bf16[4,2,256,128]{3,2,1,0:T(8,128)(2,1)} custom-call(bf16[2,256,128]{2,1,0:T(8,128)(2,1)S(1)} %bitcast.8, bf16[2,256,128]{2,1,0:T(8,128)(2,1)S(1)} %collective-permute-done.shifted), custom_call_target="tpu_custom_call" | custom-call | bytes 800000 | tf_op jit(solution)/shard_map/spread_tables/pallas_call | solution.py:329
  21.1 1.1 %all-to-all-done.refs_0_.packed = bf16[16,48,128]{2,1,0:T(8,128)(2,1)S(1)} async-done(((bf16[16,48,128]{2,1,0:T(8,128)(2,1)}), bf16[16,48,128]{2,1,0:T(8,128)(2,1)S(1)}, u32[]{:S(2)}, u32[]{:S(2)}) %all-to-all-start) | async-done | bytes 196640 | tf_op jit(solution)/shard_map/all_to_all | solution.py:326
  22.2 3.5 %all-to-all-start.1 = ((bf16[4,2,256,128]{3,2,1,0:T(8,128)(2,1)}), bf16[4,2,256,128]{3,2,1,0:T(8,128)(2,1)S(1)}, u32[]{:S(2)}, u32[]{:S(2)}) async-start(bf16[4,2,256,128]{3,2,1,0:T(8,128)(2,1)} %spread_tables.1), calls=%async_computation.1 | async-start | bytes 1048576 | tf_op jit(solution)/shard_map/all_to_all | solution.py:338
  25.7 5.6 %grid.1.grids = f32[8,256,128]{2,1,0:T(8,128)S(1)} custom-call(bf16[16,48,128]{2,1,0:T(8,128)(2,1)S(1)} %all-to-all-done.refs_0_.packed), custom_call_target="tpu_custom_call" | custom-call | flops 4000000000 | bytes 2000000 | tf_op jit(solution)/shard_map/grid/pallas_call | solution.py:340
  31.3 0.9 %all-to-all-done.1.ours = bf16[4,2,256,128]{3,2,1,0:T(8,128)(2,1)S(1)} async-done(((bf16[4,2,256,128]{3,2,1,0:T(8,128)(2,1)}), bf16[4,2,256,128]{3,2,1,0:T(8,128)(2,1)S(1)}, u32[]{:S(2)}, u32[]{:S(2)}) %all-to-all-start.1) | async-done | bytes 524320 | tf_op jit(solution)/shard_map/all_to_all | solution.py:338
  32.2 0.0 collective-permute-start.1
  32.2 1.9 %collective-permute-done.1.theirs = bf16[4,2,256,128]{3,2,1,0:T(8,128)(2,1)S(1)} collective-permute-done((bf16[4,2,256,128]{3,2,1,0:T(8,128)(2,1)S(1)}, bf16[4,2,256,128]{3,2,1,0:T(8,128)(2,1)S(1)}, u32[]{:S(2)}, u32[]{:S(2)}) %collective-permute-start.1) | collective-permute-done | bytes 524320 | tf_op jit(solution)/shard_map/ppermute | solution.py:360
  34.1 1.1 %apply_tables.1 = (f32[64,256]{1,0:T(8,128)S(1)}, f32[64,256]{1,0:T(8,128)S(1)}) custom-call(f32[8,256,128]{2,1,0:T(8,128)S(1)} %grid.1.grids, bf16[16,48,128]{2,1,0:T(8,128)(2,1)S(1)} %all-to-all-done.refs_0_.packed, bf16[4,2,256,128]{3,2,1,0:T(8,128)(2,1)S(1)} %all-to-all-done.1.ours, bf16[4,2,256,128]{3,2,1,0:T(8,128)(2,1)S(1)} %collective-permute-done.1.theirs), custom_call_target="tpu_custom_call" | custom-call | flops 1000000000 | bytes 2000000 | tf_op jit(solution)/shard_map/apply_tables/pallas_call | solution.py:361
  35.2 0.2 collective-permute-start.2
  35.4 1.1 %collective-permute-done.2 = f32[64,256]{1,0:T(8,128)S(1)} collective-permute-done((f32[64,256]{1,0:T(8,128)S(1)}, f32[64,256]{1,0:T(8,128)S(1)}, u32[]{:S(2)}, u32[]{:S(2)}) %collective-permute-start.2) | collective-permute-done | bytes 65568 | tf_op jit(solution)/shard_map/ppermute | solution.py:376
  36.5 0.7 %reshape.19 = f32[1,1,64,2,128]{4,3,2,1,0:T(2,128)} reshape(f32[64,256]{1,0:T(8,128)S(1)} %add.3) | data formatting | bytes 131072 | tf_op jit(solution)/shard_map/reshape | solution.py:377
  (1 shorter events, 0.0 us)
Async XLA Ops:
  1.7 8.5 %copy-start = (bf16[1,2,128,2,128]{4,3,2,1,0:T(2,128)(2,1)S(1)}, bf16[1,2,128,2,128]{4,3,2,1,0:T(2,128)(2,1)}, u32[]{:S(2)}) copy-start(bf16[1,2,128,2,128]{4,3,2,1,0:T(2,128)(2,1)} %param.14) | copy-start | bytes 393220
  1.7 20.4 %all-to-all-start = ((bf16[16,48,128]{2,1,0:T(8,128)(2,1)}), bf16[16,48,128]{2,1,0:T(8,128)(2,1)S(1)}, u32[]{:S(2)}, u32[]{:S(2)}) async-start(bf16[16,48,128]{2,1,0:T(8,128)(2,1)} %sort_blocks.1), calls=%async_computation | async-start | bytes 393216 | tf_op jit(solution)/shard_map/all_to_all | solution.py:326
  10.2 10.0 %collective-permute-start = (bf16[2,256,128]{2,1,0:T(8,128)(2,1)S(1)}, bf16[2,256,128]{2,1,0:T(8,128)(2,1)S(1)}, u32[]{:S(2)}, u32[]{:S(2)}) collective-permute-start(bf16[2,256,128]{2,1,0:T(8,128)(2,1)S(1)} %bitcast.7), channel_id=1, source_target_pairs={{0,2},{2,4},{4,6},{6,0},{1,3},{3,5},{5,7},{7,1},{8,10},{10,12},{12... | collective-permute-start | bytes 393224 | tf_op jit(solution)/shard_map/ppermute | solution.py:327
  22.2 10.0 %all-to-all-start.1 = ((bf16[4,2,256,128]{3,2,1,0:T(8,128)(2,1)}), bf16[4,2,256,128]{3,2,1,0:T(8,128)(2,1)S(1)}, u32[]{:S(2)}, u32[]{:S(2)}) async-start(bf16[4,2,256,128]{3,2,1,0:T(8,128)(2,1)} %spread_tables.1), calls=%async_computation.1 | async-start | bytes 1048576 | tf_op jit(solution)/shard_map/all_to_all | solution.py:338
  32.2 1.9 %collective-permute-start.1 = (bf16[4,2,256,128]{3,2,1,0:T(8,128)(2,1)S(1)}, bf16[4,2,256,128]{3,2,1,0:T(8,128)(2,1)S(1)}, u32[]{:S(2)}, u32[]{:S(2)}) collective-permute-start(bf16[4,2,256,128]{3,2,1,0:T(8,128)(2,1)S(1)} %all-to-all-done.1.ours), channel_id=1, source_target_pairs={{0,1},{1,0},{2,3},{3,2},{4,5},{5,4},{6,7},{7,6},{8,9},{9,8},{10,11... | collective-permute-start | bytes 1572872 | tf_op jit(solution)/shard_map/ppermute | solution.py:360
  35.2 1.3 %collective-permute-start.2 = (f32[64,256]{1,0:T(8,128)S(1)}, f32[64,256]{1,0:T(8,128)S(1)}, u32[]{:S(2)}, u32[]{:S(2)}) collective-permute-start(f32[64,256]{1,0:T(8,128)S(1)} %get-tuple-element.14), channel_id=1, source_target_pairs={{0,1},{1,0},{2,3},{3,2},{4,5},{5,4},{6,7},{7,6},{8,9},{9,8},{10,11... | collective-permute-start | bytes 196616 | tf_op jit(solution)/shard_map/ppermute | solution.py:376

commit v9 on v8

--- a/solution.py
+++ b/solution.py
@@ -12,7 +12,8 @@
 CH = 8
 KERNEL_SPREAD = 1.5
 ALPHA = math.sqrt(math.log2(math.e) / (2.0 * KERNEL_SPREAD * KERNEL_SPREAD))
-UNROLL = 4
+UNROLL = 8
+REST = 2
 NT = (((1,), (1,)), ((), ()))
 VMEM = pl.BlockSpec(memory_space=pltpu.VMEM)
 HBM = pl.BlockSpec(memory_space=pltpu.HBM)
@@ -175,7 +176,7 @@
             code = meta_s[d, k]
             order[count] = code
             count = count + jnp.where(code >= 0, 1, 0)
-    for i in range(UNROLL):
+    for i in range(REST):
         order[count + i] = devices * cap * slots
 
     cells = ALPHA * lax.broadcasted_iota(jnp.int32, (SU, SU), 0).astype(jnp.float32)
@@ -204,24 +205,29 @@
         right = jnp.concatenate(rights, axis=1)
         return slot, lax.dot_general(left, right, NT, preferred_element_type=jnp.float32)
 
-    def step(k, carry):
-        for slot, part in [one_block(k * UNROLL + i) for i in range(UNROLL)]:
-            grids[slot] += part
-        return carry
-
-    lax.fori_loop(0, lax.div(count + UNROLL - 1, UNROLL), step, 0)
-
-
-def spread_kernel(own, shifted, out_ref):
-    chan = lax.axis_index("chan")
-    for n, ref in enumerate((own, shifted)):
-        table = ref[chan]
-        for f in range(out_ref.shape[0]):
-            out_ref[f, n] = table
-
-
-def table_kernel(sizes, norm, grids, packed, ours, theirs, mine_ref, other_ref, table_f, total):
+    def steps(first, blocks, number):
+        def step(k, carry):
+            for slot, part in [one_block(first + k * blocks + i) for i in range(blocks)]:
+                grids[slot] += part
+            return carry
+
+        lax.fori_loop(0, number, step, 0)
+
+    whole = lax.div(count, UNROLL)
+    steps(0, UNROLL, whole)
+    steps(whole * UNROLL, REST, lax.div(lax.rem(count, UNROLL) + REST - 1, REST))
+
+
+def spread_kernel(own, out_ref):
+    table = own[lax.axis_index("chan")]
+    for f in range(out_ref.shape[0]):
+        out_ref[f] = table
+
+
+def table_kernel(sizes, norm, grids, packed, *refs):
     slots, meta_row = sizes
+    ours, theirs = refs[:2], refs[2:4]
+    mine_ref, other_ref, table_f, total = refs[4:]
     chan = lax.axis_index("chan")
     first = chan == 0
     own = lax.axis_index("facet") * lax.axis_size("bl") + lax.axis_index("bl")
@@ -233,8 +239,8 @@
     result = jnp.zeros((SU, 2 * SU), jnp.float32)
     for s in range(slots):
         origin, set_id = divmod(s, 2)
-        fetched = ours[origin, set_id].astype(jnp.float32)
-        swapped = theirs[origin, set_id].astype(jnp.float32)
+        fetched = ours[set_id][origin].astype(jnp.float32)
+        swapped = theirs[set_id][origin].astype(jnp.float32)
         u_real, u_imag = parts(jnp.where(first, fetched, swapped))
         u_side = jnp.concatenate([u_real.T, u_imag.T], axis=1).astype(jnp.bfloat16)
         grid_real = grids[s, :SU, :]
@@ -324,18 +330,20 @@
         antenna_gain,
     )
     blocks = lax.all_to_all(packed, ("facet", "bl"), split_axis=0, concat_axis=0, tiled=True)
-    shifted = lax.ppermute(own_table, "bl", [(g, (g + 1) % groups) for g in range(groups)])
     own_table, packed = lax.optimization_barrier((own_table, packed))
     spread = pl.pallas_call(
         spread_kernel,
-        out_shape=jax.ShapeDtypeStruct((facets, 2, 2 * SU, SU), jnp.bfloat16),
-        in_specs=[VMEM, VMEM],
+        out_shape=jax.ShapeDtypeStruct((facets, 2 * SU, SU), jnp.bfloat16),
+        in_specs=[VMEM],
         out_specs=VMEM,
         compiler_params=PARAMS,
-        cost_estimate=pl.CostEstimate(flops=0, bytes_accessed=800_000, transcendentals=0),
+        cost_estimate=pl.CostEstimate(flops=0, bytes_accessed=400_000, transcendentals=0),
         name="spread_tables",
-    )(own_table, shifted)
+    )(own_table)
+    swap = [(c, 1 - c) for c in range(chan_count)]
     fetched = lax.all_to_all(spread, "facet", split_axis=0, concat_axis=0, tiled=True)
+    fetched_swapped = lax.ppermute(fetched, "chan", swap)
+    shifted = lax.ppermute(fetched, "bl", [(g, (g + 1) % groups) for g in range(groups)])
 
     grids = pl.pallas_call(
         functools.partial(grid_kernel, (facets, groups, chans, cap, rows)),
@@ -345,7 +353,7 @@
         scratch_shapes=[
             pltpu.VMEM((devices, SU), jnp.int32),
             pltpu.SMEM((devices, SU), jnp.int32),
-            pltpu.SMEM((devices * cap + UNROLL,), jnp.int32),
+            pltpu.SMEM((devices * cap + REST,), jnp.int32),
         ]
         + [pltpu.VMEM((devices * cap * chans + 8, SU), jnp.float32)] * 4
         + [pltpu.SemaphoreType.DMA],
@@ -355,13 +363,12 @@
         ),
         name="grid",
     )(blocks)
-    swap = [(c, 1 - c) for c in range(chan_count)]
-    grids, fetched = lax.optimization_barrier((grids, fetched))
-    swapped = lax.ppermute(fetched, "chan", swap)
+    grids, shifted = lax.optimization_barrier((grids, shifted))
+    shifted_swapped = lax.ppermute(shifted, "chan", swap)
     mine, other = pl.pallas_call(
         functools.partial(table_kernel, (slots, meta_row), norm),
         out_shape=[jax.ShapeDtypeStruct((half_rows, 2 * SU), jnp.float32)] * 2,
-        in_specs=[VMEM] * 4,
+        in_specs=[VMEM] * 6,
         out_specs=[VMEM, VMEM],
         scratch_shapes=[
             pltpu.VMEM((2 * SU, SU), jnp.float32),
@@ -372,7 +379,7 @@
             flops=1_000_000_000, bytes_accessed=2_000_000, transcendentals=0
         ),
         name="apply_tables",
-    )(grids, blocks, fetched, swapped)
+    )(grids, blocks, fetched, shifted, fetched_swapped, shifted_swapped)
     summand = lax.ppermute(other, "chan", swap)
     return (mine + summand).reshape(1, 1, half_rows, 2, SU)
 

time: 37.5 us -> 37.6 us (level); the launches traced: 37.2 us -> 37.8 us
  blocking collectives: 0 us -> 10.7 us
  starting transfers between devices: 14.1 us -> 7.58 us
  waiting for transfers between devices: 13.1 us -> 9.69 us
    all_to_all x0 -> x1, blocking collectives: none -> 10.7 us  [body(): lax.all_to_all(spread, 'facet', split_axis=0, concat_axis=0, tiled=True)]
    ppermute x2 -> x3, waiting for transfers between devices: 9.96 us -> 1.52 us  [the longest x1 1.51 us: body(): shifted_swapped = lax.ppermute(shifted, 'chan', swap)]
    all_to_all x1, waiting for transfers between devices: 1.06 us -> 7.06 us  [body(): lax.all_to_all(packed, ('facet', 'bl'), split_axis=0, concat_axis=0, tile...]
    all_to_all x1 -> x0, starting transfers between devices: 3.47 us -> none  [body(): lax.all_to_all(spread, 'facet', split_axis=0, concat_axis=0, tiled=True)]
    all_to_all x1, starting transfers between devices: 8.45 us -> 5.33 us  [body(): lax.all_to_all(packed, ('facet', 'bl'), split_axis=0, concat_axis=0, tile...]
    all_to_all x1 -> x0, waiting for transfers between devices: 0.94 us -> none  [body(): lax.all_to_all(spread, 'facet', split_axis=0, concat_axis=0, tiled=True)]
    pallas_call x1, Pallas kernels: 0.87 us -> 0.04 us  [body(): pl.pallas_call(spread_kernel, out_shape=jax.ShapeDtypeStruct((facets, 2 *...]
    pallas_call x1, Pallas kernels: 5.6 us -> 6.25 us  [body(): pl.pallas_call(functools.partial(grid_kernel, (facets, groups, chans, cap...]
  transfers between devices with their start and end apart: 5 -> 5, of which waited for: 5 -> 3; matrix products, arithmetic and copies ran while one was open for 0% -> 0% of each run, Pallas kernels for 17% -> 17%
where the time goes in v9:
time: 37.6 us; the launch traced here: 37.8 us
  blocking collectives  10.7 us (28%)
  waiting for transfers between devices  9.69 us (26%)
  Pallas kernels  9.11 us (24%)
  starting transfers between devices  7.58 us (20%)
  local copies, waits for them, and re-layouts  0.67 us (2%)
    all_to_all x1, blocking collectives, body(): lax.all_to_all(spread, 'facet', split_axis=0, concat_axis=0, tiled=True)  10.7 us
    all_to_all x1, waiting for transfers between devices, body(): lax.all_to_all(packed, ('facet', 'bl'), split_axis=0, concat_axis=0, tile...  7.06 us
    pallas_call x1, Pallas kernels, body(): pl.pallas_call(functools.partial(grid_kernel, (facets, groups, chans, cap...  6.25 us
    all_to_all x1, starting transfers between devices, body(): lax.all_to_all(packed, ('facet', 'bl'), split_axis=0, concat_axis=0, tile...  5.33 us
    ppermute x1, starting transfers between devices, body(): lax.ppermute(fetched, 'bl', [(g, (g + 1) % groups) for g in range(groups)])  1.91 us
    pallas_call x1, Pallas kernels, body(): pl.pallas_call(functools.partial(sort_kernel, (facets, groups, held, chan...  1.72 us
    ppermute x1, waiting for transfers between devices, body(): shifted_swapped = lax.ppermute(shifted, 'chan', swap)  1.51 us
    ppermute x1, waiting for transfers between devices, body(): summand = lax.ppermute(other, 'chan', swap)  1.12 us
  transfers between devices with their start and end apart: 5, of which 3 were waited for; matrix products, arithmetic and copies ran while one was open for 0% of the time, Pallas kernels for 17%

profile of v9, /device:TPU:0, one launch (start us, length us, event | category | flops | bytes accessed | tf_op | source)
XLA Modules:
  0.0 37.8 jit_solution(5624564925285013330)
XLA Ops:
  0.0 0.0 copy-start
  0.0 1.7 %sort_blocks.1 = bf16[16,48,128]{2,1,0:T(8,128)(2,1)} custom-call(s32[1,8]{1,0:T(1,128)} %bitcast.12, s32[1,8]{1,0:T(1,128)} %bitcast.13, bf16[64,128]{1,0:T(8,128)(2,1)} %bitcast.8, bf16[16,128]{1,0:T(8,128)(2,1)} %bitcast.9, s32[4,2,4]{2,1,0:T(2,128)} %bitcast.10, f32[2,4]{1,0:T(2,128)} %bitcast.11, f32[1,2,128]{2,1,0:T(2,128)} %refs_6_.1), custom_call_target="tpu_custom_call" | custom-call | flops 100000 | bytes 100000 | tf_op jit(solution)/shard_map/sort_blocks/pallas_call | solution.py:301
  1.7 0.0 copy-done
  1.8 10.7 %all_to_all.10.refs_0_ = bf16[4,256,128]{2,1,0:T(8,128)(2,1)S(1)} all-to-all(bf16[4,256,128]{2,1,0:T(8,128)(2,1)S(1)} %spread_tables.1), channel_id=1, replica_groups=mesh['facet'=4,'bl'=4,'chan'=2] {'facet'}, dimensions={0} | all-to-all | bytes 524288 | tf_op jit(solution)/shard_map/all_to_all | solution.py:344
  12.5 5.3 %all-to-all-start = ((bf16[16,48,128]{2,1,0:T(8,128)(2,1)}), bf16[16,48,128]{2,1,0:T(8,128)(2,1)S(1)}, u32[]{:S(2)}, u32[]{:S(2)}) async-start(bf16[16,48,128]{2,1,0:T(8,128)(2,1)} %sort_blocks.1), calls=%async_computation | async-start | bytes 393216 | tf_op jit(solution)/shard_map/all_to_all | solution.py:332
  17.8 0.1 collective-permute-start.1
  17.9 1.9 %collective-permute-start = (bf16[4,256,128]{2,1,0:T(8,128)(2,1)S(1)}, bf16[4,256,128]{2,1,0:T(8,128)(2,1)S(1)}, u32[]{:S(2)}, u32[]{:S(2)}) collective-permute-start(bf16[4,256,128]{2,1,0:T(8,128)(2,1)S(1)} %all_to_all.10.refs_0_), channel_id=1, source_target_pairs={{0,2},{2,4},{4,6},{6,0},{1,3},{3,5},{5,7},{7,1},{8,10},{10,12},{12... | collective-permute-start | bytes 786440 | tf_op jit(solution)/shard_map/ppermute | solution.py:346
  19.8 7.1 %all-to-all-done.refs_0_.packed = bf16[16,48,128]{2,1,0:T(8,128)(2,1)S(1)} async-done(((bf16[16,48,128]{2,1,0:T(8,128)(2,1)}), bf16[16,48,128]{2,1,0:T(8,128)(2,1)S(1)}, u32[]{:S(2)}, u32[]{:S(2)}) %all-to-all-start) | async-done | bytes 196640 | tf_op jit(solution)/shard_map/all_to_all | solution.py:332
  26.9 6.3 %grid.1.grids = f32[8,256,128]{2,1,0:T(8,128)S(1)} custom-call(bf16[16,48,128]{2,1,0:T(8,128)(2,1)S(1)} %all-to-all-done.refs_0_.packed), custom_call_target="tpu_custom_call" | custom-call | flops 4000000000 | bytes 2000000 | tf_op jit(solution)/shard_map/grid/pallas_call | solution.py:348
  33.1 0.0 collective-permute-done.refs_1_
  33.1 0.1 collective-permute-start.2
  33.2 0.0 collective-permute-done.1.refs_2_
  33.2 1.5 %collective-permute-done.2.refs_3_ = bf16[4,256,128]{2,1,0:T(8,128)(2,1)S(1)} collective-permute-done((bf16[4,256,128]{2,1,0:T(8,128)(2,1)S(1)}, bf16[4,256,128]{2,1,0:T(8,128)(2,1)S(1)}, u32[]{:S(2)}, u32[]{:S(2)}) %collective-permute-start.2) | collective-permute-done | bytes 262176 | tf_op jit(solution)/shard_map/ppermute | solution.py:367
  34.7 1.1 %apply_tables.1 = (f32[64,256]{1,0:T(8,128)S(1)}, f32[64,256]{1,0:T(8,128)S(1)}) custom-call(f32[8,256,128]{2,1,0:T(8,128)S(1)} %grid.1.grids, bf16[16,48,128]{2,1,0:T(8,128)(2,1)S(1)} %all-to-all-done.refs_0_.packed, bf16[4,256,128]{2,1,0:T(8,128)(2,1)S(1)} %all_to_all.10.refs_0_, bf16[4,256,128]{2,1,0:T(8,128)(2,1)S(1)} %collective-permute-done.refs_1_, ...), custom_call_target="tpu_custom_call" | custom-call | flops 1000000000 | bytes 2000000 | tf_op jit(solution)/shard_map/apply_tables/pallas_call | solution.py:368
  35.8 0.2 collective-permute-start.3
  36.0 1.1 %collective-permute-done.3 = f32[64,256]{1,0:T(8,128)S(1)} collective-permute-done((f32[64,256]{1,0:T(8,128)S(1)}, f32[64,256]{1,0:T(8,128)S(1)}, u32[]{:S(2)}, u32[]{:S(2)}) %collective-permute-start.3) | collective-permute-done | bytes 65568 | tf_op jit(solution)/shard_map/ppermute | solution.py:383
  37.2 0.7 %reshape.19 = f32[1,1,64,2,128]{4,3,2,1,0:T(2,128)} reshape(f32[64,256]{1,0:T(8,128)S(1)} %add.3) | data formatting | bytes 131072 | tf_op jit(solution)/shard_map/reshape | solution.py:384
  (2 shorter events, 0.1 us)
Async XLA Ops:
  0.0 1.7 %copy-start = (bf16[1,2,128,2,128]{4,3,2,1,0:T(2,128)(2,1)S(1)}, bf16[1,2,128,2,128]{4,3,2,1,0:T(2,128)(2,1)}, u32[]{:S(2)}) copy-start(bf16[1,2,128,2,128]{4,3,2,1,0:T(2,128)(2,1)} %param.14) | copy-start | bytes 393220
  12.5 14.4 %all-to-all-start = ((bf16[16,48,128]{2,1,0:T(8,128)(2,1)}), bf16[16,48,128]{2,1,0:T(8,128)(2,1)S(1)}, u32[]{:S(2)}, u32[]{:S(2)}) async-start(bf16[16,48,128]{2,1,0:T(8,128)(2,1)} %sort_blocks.1), calls=%async_computation | async-start | bytes 393216 | tf_op jit(solution)/shard_map/all_to_all | solution.py:332
  17.8 15.4 %collective-permute-start.1 = (bf16[4,256,128]{2,1,0:T(8,128)(2,1)S(1)}, bf16[4,256,128]{2,1,0:T(8,128)(2,1)S(1)}, u32[]{:S(2)}, u32[]{:S(2)}) collective-permute-start(bf16[4,256,128]{2,1,0:T(8,128)(2,1)S(1)} %all_to_all.10.refs_0_), channel_id=1, source_target_pairs={{0,1},{1,0},{2,3},{3,2},{4,5},{5,4},{6,7},{7,6},{8,9},{9,8},{10,11... | collective-permute-start | bytes 786440 | tf_op jit(solution)/shard_map/ppermute | solution.py:345
  17.9 15.2 %collective-permute-start = (bf16[4,256,128]{2,1,0:T(8,128)(2,1)S(1)}, bf16[4,256,128]{2,1,0:T(8,128)(2,1)S(1)}, u32[]{:S(2)}, u32[]{:S(2)}) collective-permute-start(bf16[4,256,128]{2,1,0:T(8,128)(2,1)S(1)} %all_to_all.10.refs_0_), channel_id=1, source_target_pairs={{0,2},{2,4},{4,6},{6,0},{1,3},{3,5},{5,7},{7,1},{8,10},{10,12},{12... | collective-permute-start | bytes 786440 | tf_op jit(solution)/shard_map/ppermute | solution.py:346
  33.1 1.6 %collective-permute-start.2 = (bf16[4,256,128]{2,1,0:T(8,128)(2,1)S(1)}, bf16[4,256,128]{2,1,0:T(8,128)(2,1)S(1)}, u32[]{:S(2)}, u32[]{:S(2)}) collective-permute-start(bf16[4,256,128]{2,1,0:T(8,128)(2,1)S(1)} %collective-permute-done.refs_1_), channel_id=1, source_target_pairs={{0,1},{1,0},{2,3},{3,2},{4,5},{5,4},{6,7},{7,6},{8,9},{9,8},{10,11... | collective-permute-start | bytes 786440 | tf_op jit(solution)/shard_map/ppermute | solution.py:367
  35.8 1.3 %collective-permute-start.3 = (f32[64,256]{1,0:T(8,128)S(1)}, f32[64,256]{1,0:T(8,128)S(1)}, u32[]{:S(2)}, u32[]{:S(2)}) collective-permute-start(f32[64,256]{1,0:T(8,128)S(1)} %get-tuple-element.14), channel_id=1, source_target_pairs={{0,1},{1,0},{2,3},{3,2},{4,5},{5,4},{6,7},{7,6},{8,9},{9,8},{10,11... | collective-permute-start | bytes 196616 | tf_op jit(solution)/shard_map/ppermute | solution.py:383

commit v10 on v9

--- a/solution.py
+++ b/solution.py
@@ -18,7 +18,6 @@
 VMEM = pl.BlockSpec(memory_space=pltpu.VMEM)
 HBM = pl.BlockSpec(memory_space=pltpu.HBM)
 PARAMS = pltpu.CompilerParams(vmem_limit_bytes=32 * 1024 * 1024)
-ALONE = pltpu.CompilerParams(vmem_limit_bytes=60 * 1024 * 1024)
 
 
 def cos_sin(turns):
@@ -56,17 +55,18 @@
 
 
 def sort_kernel(sizes, *refs):
-    facets, groups, held, chans, cap, rows = sizes
-    out_ref = refs[7]
-    targets = refs[8:15]
+    groups, held, chans, cap, rows = sizes
+    table_hbm, send, keep, half = refs[7:11]
+    targets = refs[11:18]
     plane_ref, group_ref, samples_b, place_b, offsets_ref, centre_ref, gain_ref = targets
-    samples, place, sorted_, filled, sems = refs[15:]
+    samples, place, sorted_, filled, sems = refs[18:]
     facet = lax.axis_index("facet")
     copies = [
         pltpu.make_async_copy(source, target, sems.at[n])
         for n, (source, target) in enumerate(zip(refs[:7], targets))
     ]
-    for copy in copies:
+    table = pltpu.make_async_copy(table_hbm.at[lax.axis_index("chan")], half, sems.at[7])
+    for copy in copies + [table]:
         copy.start()
     sorted_[...] = jnp.zeros_like(sorted_)
     for g in range(groups):
@@ -105,16 +105,26 @@
         sorted_[g, meta : meta + 1, :] += jnp.where(
             lane == k, (plane_ref[0, i] + 1).astype(jnp.float32), 0.0
         )
-    for g in range(groups):
-        rows_of = sorted_[g].astype(jnp.bfloat16)
-        for f in range(facets):
-            out_ref[f * groups + g] = rows_of
+    here = lax.axis_index("bl")
+    for step in range(groups):
+        target = (keep, send)[step % 2]
+        target[step // 2, 0] = sorted_[here ^ step].astype(jnp.bfloat16)
+    table.wait()
+
+
+def fold_kernel(keep, arrived, *refs):
+    count = keep.shape[1]
+    for n in range(keep.shape[0]):
+        target = refs[n % 2]
+        target[n // 2, :count] = keep[n]
+        target[n // 2, count:] = arrived[n]
 
 
 def grid_kernel(sizes, *refs):
     facets, groups, chans, cap, rows = sizes
-    packed, grids = refs[:2]
-    meta_v, meta_s, order, spots_u, spots_v, turns_real, turns_imag, sem = refs[2:]
+    halves, grids = refs[:2], refs[2]
+    meta_v, meta_s, order, spots_u, spots_v, turns_real, turns_imag, sem = refs[3:]
+    pieces = [ref.at[n] for ref in halves for n in range(ref.shape[0])]
     devices = facets * groups
     slots = 2 * facets
     lines = cap * chans
@@ -125,13 +135,13 @@
     chan = lax.axis_index("chan")
 
     lane = lax.broadcasted_iota(jnp.int32, (1, SU), 1)
-    own = packed[facet * groups + group, tail : tail + 16, :].astype(jnp.float32)
+    own = pieces[0][tail : tail + 16, :].astype(jnp.float32)
     numbers = own[meta_row - tail + 1 : meta_row - tail + 2]
     for d in range(devices):
-        meta = packed[d, tail : tail + 16, :].astype(jnp.float32)
+        meta = pieces[d][tail : tail + 16, :].astype(jnp.float32)
         plane = meta[meta_row - tail : meta_row - tail + 1].astype(jnp.int32) - 1
         set_id = jnp.where(lax.rem(plane, groups) == group, 0, 1)
-        code = (d * cap + lane) * slots + 2 * lax.div(plane, groups) + set_id
+        code = (d * cap + lane) * slots + 2 * (lax.div(plane, groups) ^ facet) + set_id
         meta_v[d : d + 1, :] = jnp.where(plane >= 0, code, -1)
     copy = pltpu.make_async_copy(meta_v, meta_s, sem)
     copy.start()
@@ -155,7 +165,7 @@
 
     for d in range(devices):
         at = d * lines
-        wide = packed[d].astype(jnp.float32)
+        wide = pieces[d][...].astype(jnp.float32)
         real = wide[:lines]
         imag = wide[lines : 2 * lines]
         along_u = spread_lines(wide[2 * lines : 2 * lines + cap])
@@ -218,10 +228,36 @@
     steps(whole * UNROLL, REST, lax.div(lax.rem(count, UNROLL) + REST - 1, REST))
 
 
-def spread_kernel(own, out_ref):
-    table = own[lax.axis_index("chan")]
-    for f in range(out_ref.shape[0]):
-        out_ref[f] = table
+def fold(keep, arrived):
+    parts, count = keep.shape[:2]
+    shape = (max(parts // 2, 1), 2 * count) + keep.shape[2:]
+    outs = min(parts, 2)
+    return pl.pallas_call(
+        fold_kernel,
+        out_shape=[jax.ShapeDtypeStruct(shape, keep.dtype)] * outs,
+        in_specs=[VMEM] * 2,
+        out_specs=[VMEM] * outs,
+        compiler_params=PARAMS,
+        cost_estimate=pl.CostEstimate(flops=0, bytes_accessed=200_000, transcendentals=0),
+        name="fold",
+    )(keep, arrived)
+
+
+def exchange(value, axis, bit):
+    return lax.ppermute(value, axis, [(n, n ^ bit) for n in range(lax.axis_size(axis))])
+
+
+def gather(value, axis, whole=False):
+    bit = 1
+    while True:
+        arrived = exchange(value, axis, bit)
+        bit *= 2
+        if bit == lax.axis_size(axis) and not whole:
+            return [value, arrived]
+        (value,) = fold(value[None], arrived[None])
+        value = value[0]
+        if bit == lax.axis_size(axis):
+            return value
 
 
 def table_kernel(sizes, norm, grids, packed, *refs):
@@ -230,7 +266,6 @@
     mine_ref, other_ref, table_f, total = refs[4:]
     chan = lax.axis_index("chan")
     first = chan == 0
-    own = lax.axis_index("facet") * lax.axis_size("bl") + lax.axis_index("bl")
 
     def parts(table):
         table_f[...] = table
@@ -271,7 +306,7 @@
             + jnp.dot(low, v_side, preferred_element_type=jnp.float32)
         )
     tail = meta_row // 16 * 16
-    wide = packed[own, tail : tail + 16, :].astype(jnp.float32)
+    wide = packed[0, tail : tail + 16, :].astype(jnp.float32)
     at = meta_row - tail + 2
     gain = (wide[at : at + 2] + wide[at + 2 : at + 4]) + wide[at + 4 : at + 6]
     gain_u = jnp.broadcast_to(gain[0:1], (SU, SU)).T
@@ -298,11 +333,12 @@
     norm = SU / math.sqrt(visibilities.shape[3] * held * facets * CH)
 
     own_table = tables.reshape(2, 2 * SU, SU)
-    packed = pl.pallas_call(
-        functools.partial(sort_kernel, (facets, groups, held, chans, cap, rows)),
-        out_shape=jax.ShapeDtypeStruct((devices, rows, SU), jnp.bfloat16),
-        in_specs=[HBM] * 7,
-        out_specs=VMEM,
+    send, keep, half = pl.pallas_call(
+        functools.partial(sort_kernel, (groups, held, chans, cap, rows)),
+        out_shape=[jax.ShapeDtypeStruct((groups // 2, 1, rows, SU), jnp.bfloat16)] * 2
+        + [jax.ShapeDtypeStruct((2 * SU, SU), jnp.bfloat16)],
+        in_specs=[HBM] * 8,
+        out_specs=[VMEM] * 3,
         scratch_shapes=[
             pltpu.SMEM((1, held), jnp.int32),
             pltpu.SMEM((1, held), jnp.int32),
@@ -315,40 +351,42 @@
             pltpu.VMEM((held * 2, SU), jnp.float32),
             pltpu.VMEM((groups, rows, SU), jnp.float32),
             pltpu.SMEM((groups,), jnp.int32),
-            pltpu.SemaphoreType.DMA((7,)),
+            pltpu.SemaphoreType.DMA((8,)),
         ],
-        compiler_params=ALONE,
+        compiler_params=PARAMS,
         cost_estimate=pl.CostEstimate(flops=100_000, bytes_accessed=100_000, transcendentals=0),
         name="sort_blocks",
     )(
-        plane_index.reshape(1, held),
-        block_group.T,
-        visibilities.reshape(held * 2 * chans, SU),
-        coords.reshape(held * 2, SU),
-        offsets.transpose(0, 2, 1),
-        facet_centre.T,
-        antenna_gain,
+        *(
+            pltpu.with_memory_space_constraint(operand, pltpu.HBM)
+            for operand in (
+                plane_index.reshape(1, held),
+                block_group.T,
+                visibilities.reshape(held * 2 * chans, SU),
+                coords.reshape(held * 2, SU),
+                offsets.transpose(0, 2, 1),
+                facet_centre.T,
+                antenna_gain,
+                own_table,
+            )
+        )
     )
-    blocks = lax.all_to_all(packed, ("facet", "bl"), split_axis=0, concat_axis=0, tiled=True)
-    own_table, packed = lax.optimization_barrier((own_table, packed))
-    spread = pl.pallas_call(
-        spread_kernel,
-        out_shape=jax.ShapeDtypeStruct((facets, 2 * SU, SU), jnp.bfloat16),
-        in_specs=[VMEM],
-        out_specs=VMEM,
-        compiler_params=PARAMS,
-        cost_estimate=pl.CostEstimate(flops=0, bytes_accessed=400_000, transcendentals=0),
-        name="spread_tables",
-    )(own_table)
+    bit = 1
+    while bit < groups:
+        arrived = exchange(send, "bl", bit)
+        keep, *send = fold(keep, arrived)
+        send = send[0] if send else None
+        bit *= 2
+    blocks = gather(keep[0], "facet")
+    fetched = gather(half[None], "facet", True)
     swap = [(c, 1 - c) for c in range(chan_count)]
-    fetched = lax.all_to_all(spread, "facet", split_axis=0, concat_axis=0, tiled=True)
     fetched_swapped = lax.ppermute(fetched, "chan", swap)
     shifted = lax.ppermute(fetched, "bl", [(g, (g + 1) % groups) for g in range(groups)])
 
     grids = pl.pallas_call(
         functools.partial(grid_kernel, (facets, groups, chans, cap, rows)),
         out_shape=jax.ShapeDtypeStruct((slots, 2 * SU, SU), jnp.float32),
-        in_specs=[VMEM],
+        in_specs=[VMEM] * 2,
         out_specs=VMEM,
         scratch_shapes=[
             pltpu.VMEM((devices, SU), jnp.int32),
@@ -362,7 +400,7 @@
             flops=4_000_000_000, bytes_accessed=2_000_000, transcendentals=4_000_000
         ),
         name="grid",
-    )(blocks)
+    )(*blocks)
     grids, shifted = lax.optimization_barrier((grids, shifted))
     shifted_swapped = lax.ppermute(shifted, "chan", swap)
     mine, other = pl.pallas_call(
@@ -379,7 +417,7 @@
             flops=1_000_000_000, bytes_accessed=2_000_000, transcendentals=0
         ),
         name="apply_tables",
-    )(grids, blocks, fetched, shifted, fetched_swapped, shifted_swapped)
+    )(grids, blocks[0], fetched, shifted, fetched_swapped, shifted_swapped)
     summand = lax.ppermute(other, "chan", swap)
     return (mine + summand).reshape(1, 1, half_rows, 2, SU)
 

time: 37.6 us -> 33.3 us (0.89); the launches traced: 37.8 us -> 33.1 us
  blocking collectives: 10.7 us -> 0 us
  starting transfers between devices: 7.58 us -> 14.8 us
  Pallas kernels: 9.11 us -> 7.39 us
  waiting for transfers between devices: 9.69 us -> 10.2 us
    ppermute x0 -> x6, starting transfers between devices: none -> 12.9 us  [exchange(): lax.ppermute(value, axis, [(n, n ^ bit) for n in range(lax.axis_size(axis...]
    all_to_all x1 -> x0, blocking collectives: 10.7 us -> none  [body(): lax.all_to_all(spread, 'facet', split_axis=0, concat_axis=0, tiled=True)]
    all_to_all x1 -> x0, waiting for transfers between devices: 7.06 us -> none  [body(): lax.all_to_all(packed, ('facet', 'bl'), split_axis=0, concat_axis=0, tile...]
    all_to_all x1 -> x0, starting transfers between devices: 5.33 us -> none  [body(): lax.all_to_all(packed, ('facet', 'bl'), split_axis=0, concat_axis=0, tile...]
    ppermute x0 -> x6, waiting for transfers between devices: none -> 3.83 us  [exchange(): lax.ppermute(value, axis, [(n, n ^ bit) for n in range(lax.axis_size(axis...]
    ppermute x1, waiting for transfers between devices: 0.01 us -> 3.7 us  [body(): lax.ppermute(fetched, 'bl', [(g, (g + 1) % groups) for g in range(groups)])]
    pallas_call x1, Pallas kernels: 6.25 us -> 5.2 us  [body(): pl.pallas_call(functools.partial(grid_kernel, (facets, groups, chans, cap...]
    pallas_call x2 -> x6, Pallas kernels: 1.76 us -> 1.09 us  [the longest x1 1.05 us: body(): pl.pallas_call(functools.partial(sort_kernel, (groups, held, chans, cap,...]
  transfers between devices with their start and end apart: 5 -> 10, of which waited for: 3 -> 8; matrix products, arithmetic and copies ran while one was open for 0% -> 0% of each run, Pallas kernels for 17% -> 16%
where the time goes in v10:
time: 33.3 us; the launch traced here: 33.1 us
  starting transfers between devices  14.8 us (44%)
  waiting for transfers between devices  10.2 us (31%)
  Pallas kernels  7.39 us (22%)
  local copies, waits for them, and re-layouts  0.66 us (2%)
    ppermute x6, starting transfers between devices, exchange(): lax.ppermute(value, axis, [(n, n ^ bit) for n in range(lax.axis_size(axis...  12.9 us
    pallas_call x1, Pallas kernels, body(): pl.pallas_call(functools.partial(grid_kernel, (facets, groups, chans, cap...  5.2 us
    ppermute x6, waiting for transfers between devices, exchange(): lax.ppermute(value, axis, [(n, n ^ bit) for n in range(lax.axis_size(axis...  3.83 us
    ppermute x1, waiting for transfers between devices, body(): lax.ppermute(fetched, 'bl', [(g, (g + 1) % groups) for g in range(groups)])  3.7 us
    ppermute x1, starting transfers between devices, body(): lax.ppermute(fetched, 'bl', [(g, (g + 1) % groups) for g in range(groups)])  1.63 us
    ppermute x1, waiting for transfers between devices, body(): shifted_swapped = lax.ppermute(shifted, 'chan', swap)  1.53 us
    ppermute x1, waiting for transfers between devices, body(): summand = lax.ppermute(other, 'chan', swap)  1.12 us
    pallas_call x1, Pallas kernels, body(): pl.pallas_call(functools.partial(table_kernel, (slots, meta_row), norm),...  1.09 us
  transfers between devices with their start and end apart: 10, of which 8 were waited for; matrix products, arithmetic and copies ran while one was open for 0% of the time, Pallas kernels for 16%

profile of v10, /device:TPU:0, one launch (start us, length us, event | category | flops | bytes accessed | tf_op | source)
XLA Modules:
  0.0 33.1 jit_solution(4138269459369660298)
XLA Ops:
  0.0 1.0 %sort_blocks.1 = (bf16[2,1,48,128]{3,2,1,0:T(8,128)(2,1)S(1)}, bf16[2,1,48,128]{3,2,1,0:T(8,128)(2,1)S(1)}, bf16[256,128]{1,0:T(8,128)(2,1)S(1)}) custom-call(s32[1,8]{1,0:T(1,128)} %bitcast.34, s32[1,8]{1,0:T(1,128)} %bitcast.35, bf16[64,128]{1,0:T(8,128)(2,1)} %bitcast.30, bf16[16,128]{1,0:T(8,128)(2,1)} %bitcast.31, s32[4,2,4]{2,1,0:T(2,128)} %bitcast.32, ...), custom_call_target="tpu_custom_call" | custom-call | flops 100000 | bytes 100000 | tf_op jit(solution)/shard_map/sort_blocks/pallas_call | solution.py:336
  1.1 3.1 %collective-permute-start = (bf16[2,1,48,128]{3,2,1,0:T(8,128)(2,1)S(1)}, bf16[2,1,48,128]{3,2,1,0:T(8,128)(2,1)S(1)}, u32[]{:S(2)}, u32[]{:S(2)}) collective-permute-start(bf16[2,1,48,128]{3,2,1,0:T(8,128)(2,1)S(1)} %get-tuple-element.15), channel_id=1, source_target_pairs={{0,2},{2,0},{4,6},{6,4},{1,3},{3,1},{5,7},{7,5},{8,10},{10,8},{12,... | collective-permute-start | bytes 73736 | tf_op jit(solution)/shard_map/ppermute | solution.py:247
  4.2 1.5 %collective-permute-start.4 = (bf16[1,256,128]{2,1,0:T(8,128)(2,1)S(1)}, bf16[1,256,128]{2,1,0:T(8,128)(2,1)S(1)}, u32[]{:S(2)}, u32[]{:S(2)}) collective-permute-start(bf16[1,256,128]{2,1,0:T(8,128)(2,1)S(1)} %bitcast.25), channel_id=1, source_target_pairs={{0,8},{8,0},{16,24},{24,16},{1,9},{9,1},{17,25},{25,17},{2,10},{10... | collective-permute-start | bytes 196616 | tf_op jit(solution)/shard_map/ppermute | solution.py:247
  5.6 0.3 collective-permute-done.arrived
  6.0 3.0 %collective-permute-start.1 = (bf16[1,2,48,128]{3,2,1,0:T(8,128)(2,1)S(1)}, bf16[1,2,48,128]{3,2,1,0:T(8,128)(2,1)S(1)}, u32[]{:S(2)}, u32[]{:S(2)}) collective-permute-start(bf16[1,2,48,128]{3,2,1,0:T(8,128)(2,1)S(1)} %get-tuple-element.17), channel_id=1, source_target_pairs={{0,4},{2,6},{4,0},{6,2},{1,5},{3,7},{5,1},{7,3},{8,12},{10,14},{12... | collective-permute-start | bytes 73736 | tf_op jit(solution)/shard_map/ppermute | solution.py:247
  9.0 1.8 %collective-permute-done.1.arrived = bf16[1,2,48,128]{3,2,1,0:T(8,128)(2,1)S(1)} collective-permute-done((bf16[1,2,48,128]{3,2,1,0:T(8,128)(2,1)S(1)}, bf16[1,2,48,128]{3,2,1,0:T(8,128)(2,1)S(1)}, u32[]{:S(2)}, u32[]{:S(2)}) %collective-permute-start.1) | collective-permute-done | bytes 24608 | tf_op jit(solution)/shard_map/ppermute | solution.py:247
  10.8 1.8 %collective-permute-start.2 = (bf16[4,48,128]{2,1,0:T(8,128)(2,1)S(1)}, bf16[4,48,128]{2,1,0:T(8,128)(2,1)S(1)}, u32[]{:S(2)}, u32[]{:S(2)}) collective-permute-start(bf16[4,48,128]{2,1,0:T(8,128)(2,1)S(1)} %bitcast.20), channel_id=1, source_target_pairs={{0,8},{8,0},{16,24},{24,16},{1,9},{9,1},{17,25},{25,17},{2,10},{10... | collective-permute-start | bytes 147464 | tf_op jit(solution)/shard_map/ppermute | solution.py:247
  12.6 0.0 collective-permute-done.4
  12.6 1.6 %collective-permute-start.5 = (bf16[2,256,128]{2,1,0:T(8,128)(2,1)S(1)}, bf16[2,256,128]{2,1,0:T(8,128)(2,1)S(1)}, u32[]{:S(2)}, u32[]{:S(2)}) collective-permute-start(bf16[2,256,128]{2,1,0:T(8,128)(2,1)S(1)} %bitcast.16), channel_id=1, source_target_pairs={{0,16},{8,24},{16,0},{24,8},{1,17},{9,25},{17,1},{25,9},{2,18},{10... | collective-permute-start | bytes 393224 | tf_op jit(solution)/shard_map/ppermute | solution.py:247
  14.2 0.7 %collective-permute-done.2 = bf16[4,48,128]{2,1,0:T(8,128)(2,1)S(1)} collective-permute-done((bf16[4,48,128]{2,1,0:T(8,128)(2,1)S(1)}, bf16[4,48,128]{2,1,0:T(8,128)(2,1)S(1)}, u32[]{:S(2)}, u32[]{:S(2)}) %collective-permute-start.2) | collective-permute-done | bytes 49184 | tf_op jit(solution)/shard_map/ppermute | solution.py:247
  14.9 1.9 %collective-permute-start.3 = (bf16[8,48,128]{2,1,0:T(8,128)(2,1)S(1)}, bf16[8,48,128]{2,1,0:T(8,128)(2,1)S(1)}, u32[]{:S(2)}, u32[]{:S(2)}) collective-permute-start(bf16[8,48,128]{2,1,0:T(8,128)(2,1)S(1)} %bitcast.22), channel_id=1, source_target_pairs={{0,16},{8,24},{16,0},{24,8},{1,17},{9,25},{17,1},{25,9},{2,18},{10... | collective-permute-start | bytes 294920 | tf_op jit(solution)/shard_map/ppermute | solution.py:247
  16.8 0.9 %collective-permute-done.5 = bf16[2,256,128]{2,1,0:T(8,128)(2,1)S(1)} collective-permute-done((bf16[2,256,128]{2,1,0:T(8,128)(2,1)S(1)}, bf16[2,256,128]{2,1,0:T(8,128)(2,1)S(1)}, u32[]{:S(2)}, u32[]{:S(2)}) %collective-permute-start.5) | collective-permute-done | bytes 131104 | tf_op jit(solution)/shard_map/ppermute | solution.py:247
  17.7 0.1 collective-permute-start.7
  17.8 1.6 %collective-permute-start.6 = (bf16[4,256,128]{2,1,0:T(8,128)(2,1)S(1)}, bf16[4,256,128]{2,1,0:T(8,128)(2,1)S(1)}, u32[]{:S(2)}, u32[]{:S(2)}) collective-permute-start(bf16[4,256,128]{2,1,0:T(8,128)(2,1)S(1)} %bitcast.18), channel_id=1, source_target_pairs={{0,2},{2,4},{4,6},{6,0},{1,3},{3,5},{5,7},{7,1},{8,10},{10,12},{12... | collective-permute-start | bytes 786440 | tf_op jit(solution)/shard_map/ppermute | solution.py:384
  19.4 0.2 collective-permute-done.3.refs_1_
  19.6 5.2 %grid.1.grids = f32[8,256,128]{2,1,0:T(8,128)S(1)} custom-call(bf16[8,48,128]{2,1,0:T(8,128)(2,1)S(1)} %bitcast.23, bf16[8,48,128]{2,1,0:T(8,128)(2,1)S(1)} %collective-permute-done.3.refs_1_), custom_call_target="tpu_custom_call" | custom-call | flops 4000000000 | bytes 2000000 | tf_op jit(solution)/shard_map/grid/pallas_call | solution.py:386
  24.8 3.7 %collective-permute-done.6.refs_1_ = bf16[4,256,128]{2,1,0:T(8,128)(2,1)S(1)} collective-permute-done((bf16[4,256,128]{2,1,0:T(8,128)(2,1)S(1)}, bf16[4,256,128]{2,1,0:T(8,128)(2,1)S(1)}, u32[]{:S(2)}, u32[]{:S(2)}) %collective-permute-start.6) | collective-permute-done | bytes 262176 | tf_op jit(solution)/shard_map/ppermute | solution.py:384
  28.5 0.0 collective-permute-start.8
  28.5 0.0 collective-permute-done.7.refs_2_
  28.5 1.5 %collective-permute-done.8.refs_3_ = bf16[4,256,128]{2,1,0:T(8,128)(2,1)S(1)} collective-permute-done((bf16[4,256,128]{2,1,0:T(8,128)(2,1)S(1)}, bf16[4,256,128]{2,1,0:T(8,128)(2,1)S(1)}, u32[]{:S(2)}, u32[]{:S(2)}) %collective-permute-start.8) | collective-permute-done | bytes 262176 | tf_op jit(solution)/shard_map/ppermute | solution.py:405
  30.0 1.1 %apply_tables.1 = (f32[64,256]{1,0:T(8,128)S(1)}, f32[64,256]{1,0:T(8,128)S(1)}) custom-call(f32[8,256,128]{2,1,0:T(8,128)S(1)} %grid.1.grids, bf16[8,48,128]{2,1,0:T(8,128)(2,1)S(1)} %bitcast.24, bf16[4,256,128]{2,1,0:T(8,128)(2,1)S(1)} %bitcast.19, bf16[4,256,128]{2,1,0:T(8,128)(2,1)S(1)} %collective-permute-done.6.refs_1_, ...), custom_call_target="tpu_custom_call" | custom-call | flops 1000000000 | bytes 2000000 | tf_op jit(solution)/shard_map/apply_tables/pallas_call | solution.py:406
  31.1 0.2 collective-permute-start.9
  31.3 1.1 %collective-permute-done.9 = f32[64,256]{1,0:T(8,128)S(1)} collective-permute-done((f32[64,256]{1,0:T(8,128)S(1)}, f32[64,256]{1,0:T(8,128)S(1)}, u32[]{:S(2)}, u32[]{:S(2)}) %collective-permute-start.9) | collective-permute-done | bytes 65568 | tf_op jit(solution)/shard_map/ppermute | solution.py:421
  32.5 0.7 %reshape.19 = f32[1,1,64,2,128]{4,3,2,1,0:T(2,128)} reshape(f32[64,256]{1,0:T(8,128)S(1)} %add.3) | data formatting | bytes 131072 | tf_op jit(solution)/shard_map/reshape | solution.py:422
  (6 shorter events, 0.1 us)
Async XLA Ops:
  1.1 4.9 %collective-permute-start = (bf16[2,1,48,128]{3,2,1,0:T(8,128)(2,1)S(1)}, bf16[2,1,48,128]{3,2,1,0:T(8,128)(2,1)S(1)}, u32[]{:S(2)}, u32[]{:S(2)}) collective-permute-start(bf16[2,1,48,128]{3,2,1,0:T(8,128)(2,1)S(1)} %get-tuple-element.15), channel_id=1, source_target_pairs={{0,2},{2,0},{4,6},{6,4},{1,3},{3,1},{5,7},{7,5},{8,10},{10,8},{12,... | collective-permute-start | bytes 73736 | tf_op jit(solution)/shard_map/ppermute | solution.py:247
  4.2 8.5 %collective-permute-start.4 = (bf16[1,256,128]{2,1,0:T(8,128)(2,1)S(1)}, bf16[1,256,128]{2,1,0:T(8,128)(2,1)S(1)}, u32[]{:S(2)}, u32[]{:S(2)}) collective-permute-start(bf16[1,256,128]{2,1,0:T(8,128)(2,1)S(1)} %bitcast.25), channel_id=1, source_target_pairs={{0,8},{8,0},{16,24},{24,16},{1,9},{9,1},{17,25},{25,17},{2,10},{10... | collective-permute-start | bytes 196616 | tf_op jit(solution)/shard_map/ppermute | solution.py:247
  6.0 4.8 %collective-permute-start.1 = (bf16[1,2,48,128]{3,2,1,0:T(8,128)(2,1)S(1)}, bf16[1,2,48,128]{3,2,1,0:T(8,128)(2,1)S(1)}, u32[]{:S(2)}, u32[]{:S(2)}) collective-permute-start(bf16[1,2,48,128]{3,2,1,0:T(8,128)(2,1)S(1)} %get-tuple-element.17), channel_id=1, source_target_pairs={{0,4},{2,6},{4,0},{6,2},{1,5},{3,7},{5,1},{7,3},{8,12},{10,14},{12... | collective-permute-start | bytes 73736 | tf_op jit(solution)/shard_map/ppermute | solution.py:247
  10.8 4.1 %collective-permute-start.2 = (bf16[4,48,128]{2,1,0:T(8,128)(2,1)S(1)}, bf16[4,48,128]{2,1,0:T(8,128)(2,1)S(1)}, u32[]{:S(2)}, u32[]{:S(2)}) collective-permute-start(bf16[4,48,128]{2,1,0:T(8,128)(2,1)S(1)} %bitcast.20), channel_id=1, source_target_pairs={{0,8},{8,0},{16,24},{24,16},{1,9},{9,1},{17,25},{25,17},{2,10},{10... | collective-permute-start | bytes 147464 | tf_op jit(solution)/shard_map/ppermute | solution.py:247
  12.6 5.0 %collective-permute-start.5 = (bf16[2,256,128]{2,1,0:T(8,128)(2,1)S(1)}, bf16[2,256,128]{2,1,0:T(8,128)(2,1)S(1)}, u32[]{:S(2)}, u32[]{:S(2)}) collective-permute-start(bf16[2,256,128]{2,1,0:T(8,128)(2,1)S(1)} %bitcast.16), channel_id=1, source_target_pairs={{0,16},{8,24},{16,0},{24,8},{1,17},{9,25},{17,1},{25,9},{2,18},{10... | collective-permute-start | bytes 393224 | tf_op jit(solution)/shard_map/ppermute | solution.py:247
  14.9 4.7 %collective-permute-start.3 = (bf16[8,48,128]{2,1,0:T(8,128)(2,1)S(1)}, bf16[8,48,128]{2,1,0:T(8,128)(2,1)S(1)}, u32[]{:S(2)}, u32[]{:S(2)}) collective-permute-start(bf16[8,48,128]{2,1,0:T(8,128)(2,1)S(1)} %bitcast.22), channel_id=1, source_target_pairs={{0,16},{8,24},{16,0},{24,8},{1,17},{9,25},{17,1},{25,9},{2,18},{10... | collective-permute-start | bytes 294920 | tf_op jit(solution)/shard_map/ppermute | solution.py:247
  17.7 10.8 %collective-permute-start.7 = (bf16[4,256,128]{2,1,0:T(8,128)(2,1)S(1)}, bf16[4,256,128]{2,1,0:T(8,128)(2,1)S(1)}, u32[]{:S(2)}, u32[]{:S(2)}) collective-permute-start(bf16[4,256,128]{2,1,0:T(8,128)(2,1)S(1)} %bitcast.17), channel_id=1, source_target_pairs={{0,1},{1,0},{2,3},{3,2},{4,5},{5,4},{6,7},{7,6},{8,9},{9,8},{10,11... | collective-permute-start | bytes 786440 | tf_op jit(solution)/shard_map/ppermute | solution.py:383
  17.8 10.7 %collective-permute-start.6 = (bf16[4,256,128]{2,1,0:T(8,128)(2,1)S(1)}, bf16[4,256,128]{2,1,0:T(8,128)(2,1)S(1)}, u32[]{:S(2)}, u32[]{:S(2)}) collective-permute-start(bf16[4,256,128]{2,1,0:T(8,128)(2,1)S(1)} %bitcast.18), channel_id=1, source_target_pairs={{0,2},{2,4},{4,6},{6,0},{1,3},{3,5},{5,7},{7,1},{8,10},{10,12},{12... | collective-permute-start | bytes 786440 | tf_op jit(solution)/shard_map/ppermute | solution.py:384
  28.5 1.5 %collective-permute-start.8 = (bf16[4,256,128]{2,1,0:T(8,128)(2,1)S(1)}, bf16[4,256,128]{2,1,0:T(8,128)(2,1)S(1)}, u32[]{:S(2)}, u32[]{:S(2)}) collective-permute-start(bf16[4,256,128]{2,1,0:T(8,128)(2,1)S(1)} %collective-permute-done.6.refs_1_), channel_id=1, source_target_pairs={{0,1},{1,0},{2,3},{3,2},{4,5},{5,4},{6,7},{7,6},{8,9},{9,8},{10,11... | collective-permute-start | bytes 786440 | tf_op jit(solution)/shard_map/ppermute | solution.py:405
  31.1 1.3 %collective-permute-start.9 = (f32[64,256]{1,0:T(8,128)S(1)}, f32[64,256]{1,0:T(8,128)S(1)}, u32[]{:S(2)}, u32[]{:S(2)}) collective-permute-start(f32[64,256]{1,0:T(8,128)S(1)} %get-tuple-element.22), channel_id=1, source_target_pairs={{0,1},{1,0},{2,3},{3,2},{4,5},{5,4},{6,7},{7,6},{8,9},{9,8},{10,11... | collective-permute-start | bytes 196616 | tf_op jit(solution)/shard_map/ppermute | solution.py:421

commit v11 on v10

--- a/solution.py
+++ b/solution.py
@@ -56,10 +56,10 @@
 
 def sort_kernel(sizes, *refs):
     groups, held, chans, cap, rows = sizes
-    table_hbm, send, keep, half = refs[7:11]
-    targets = refs[11:18]
+    table_hbm, outs, half = refs[7], refs[8 : 8 + groups], refs[8 + groups]
+    targets = refs[9 + groups : 16 + groups]
     plane_ref, group_ref, samples_b, place_b, offsets_ref, centre_ref, gain_ref = targets
-    samples, place, sorted_, filled, sems = refs[18:]
+    samples, place, sorted_, filled, sems = refs[16 + groups :]
     facet = lax.axis_index("facet")
     copies = [
         pltpu.make_async_copy(source, target, sems.at[n])
@@ -105,26 +105,35 @@
         sorted_[g, meta : meta + 1, :] += jnp.where(
             lane == k, (plane_ref[0, i] + 1).astype(jnp.float32), 0.0
         )
-    here = lax.axis_index("bl")
-    for step in range(groups):
-        target = (keep, send)[step % 2]
-        target[step // 2, 0] = sorted_[here ^ step].astype(jnp.bfloat16)
+    for shift, out_ref in enumerate(outs):
+        g = lax.rem(lax.axis_index("bl") + shift, groups)
+        out_ref[:rows, :] = sorted_[g].astype(jnp.bfloat16)
     table.wait()
-
-
-def fold_kernel(keep, arrived, *refs):
-    count = keep.shape[1]
-    for n in range(keep.shape[0]):
-        target = refs[n % 2]
-        target[n // 2, :count] = keep[n]
-        target[n // 2, count:] = arrived[n]
+    outs[1][rows:, :] = half[...]
+
+
+def join_kernel(rows, half, *refs):
+    *pieces, here, joined = refs
+    for n, ref in enumerate(pieces):
+        piece = ref[:rows, :]
+        here[n * rows : (n + 1) * rows, :] = piece
+        joined[n * rows : (n + 1) * rows, :] = piece
+    at = len(pieces) * rows
+    joined[at : at + 2 * SU, :] = half[...]
+    joined[at + 2 * SU :, :] = pieces[1][rows:, :]
+
+
+def stack_kernel(skip, own, arrived, out_ref):
+    count = own.shape[0] - skip
+    out_ref[:count, :] = own[skip:, :]
+    out_ref[count:, :] = arrived[skip:, :]
 
 
 def grid_kernel(sizes, *refs):
     facets, groups, chans, cap, rows = sizes
-    halves, grids = refs[:2], refs[2]
-    meta_v, meta_s, order, spots_u, spots_v, turns_real, turns_imag, sem = refs[3:]
-    pieces = [ref.at[n] for ref in halves for n in range(ref.shape[0])]
+    grids = refs[facets]
+    meta_v, meta_s, order, spots_u, spots_v, turns_real, turns_imag, sem = refs[facets + 1 :]
+    pieces = [ref.at[pl.ds(n * rows, rows)] for ref in refs[:facets] for n in range(groups)]
     devices = facets * groups
     slots = 2 * facets
     lines = cap * chans
@@ -228,36 +237,20 @@
     steps(whole * UNROLL, REST, lax.div(lax.rem(count, UNROLL) + REST - 1, REST))
 
 
-def fold(keep, arrived):
-    parts, count = keep.shape[:2]
-    shape = (max(parts // 2, 1), 2 * count) + keep.shape[2:]
-    outs = min(parts, 2)
+def local(kernel, operands, shapes, name):
     return pl.pallas_call(
-        fold_kernel,
-        out_shape=[jax.ShapeDtypeStruct(shape, keep.dtype)] * outs,
-        in_specs=[VMEM] * 2,
-        out_specs=[VMEM] * outs,
+        kernel,
+        out_shape=[jax.ShapeDtypeStruct(shape, jnp.bfloat16) for shape in shapes],
+        in_specs=[VMEM] * len(operands),
+        out_specs=[VMEM] * len(shapes),
         compiler_params=PARAMS,
-        cost_estimate=pl.CostEstimate(flops=0, bytes_accessed=200_000, transcendentals=0),
-        name="fold",
-    )(keep, arrived)
-
-
-def exchange(value, axis, bit):
-    return lax.ppermute(value, axis, [(n, n ^ bit) for n in range(lax.axis_size(axis))])
-
-
-def gather(value, axis, whole=False):
-    bit = 1
-    while True:
-        arrived = exchange(value, axis, bit)
-        bit *= 2
-        if bit == lax.axis_size(axis) and not whole:
-            return [value, arrived]
-        (value,) = fold(value[None], arrived[None])
-        value = value[0]
-        if bit == lax.axis_size(axis):
-            return value
+        cost_estimate=pl.CostEstimate(flops=0, bytes_accessed=400_000, transcendentals=0),
+        name=name,
+    )(*operands)
+
+
+def exchange(value, axis, shift):
+    return lax.ppermute(value, axis, [(n, n ^ shift) for n in range(lax.axis_size(axis))])
 
 
 def table_kernel(sizes, norm, grids, packed, *refs):
@@ -273,9 +266,9 @@
 
     result = jnp.zeros((SU, 2 * SU), jnp.float32)
     for s in range(slots):
-        origin, set_id = divmod(s, 2)
-        fetched = ours[set_id][origin].astype(jnp.float32)
-        swapped = theirs[set_id][origin].astype(jnp.float32)
+        half, at = divmod(2 * SU * s, ours[0].shape[0])
+        fetched = ours[half][at : at + 2 * SU, :].astype(jnp.float32)
+        swapped = theirs[half][at : at + 2 * SU, :].astype(jnp.float32)
         u_real, u_imag = parts(jnp.where(first, fetched, swapped))
         u_side = jnp.concatenate([u_real.T, u_imag.T], axis=1).astype(jnp.bfloat16)
         grid_real = grids[s, :SU, :]
@@ -306,7 +299,7 @@
             + jnp.dot(low, v_side, preferred_element_type=jnp.float32)
         )
     tail = meta_row // 16 * 16
-    wide = packed[0, tail : tail + 16, :].astype(jnp.float32)
+    wide = packed[tail : tail + 16, :].astype(jnp.float32)
     at = meta_row - tail + 2
     gain = (wide[at : at + 2] + wide[at + 2 : at + 4]) + wide[at + 4 : at + 6]
     gain_u = jnp.broadcast_to(gain[0:1], (SU, SU)).T
@@ -333,12 +326,15 @@
     norm = SU / math.sqrt(visibilities.shape[3] * held * facets * CH)
 
     own_table = tables.reshape(2, 2 * SU, SU)
-    send, keep, half = pl.pallas_call(
+    *pieces, half = pl.pallas_call(
         functools.partial(sort_kernel, (groups, held, chans, cap, rows)),
-        out_shape=[jax.ShapeDtypeStruct((groups // 2, 1, rows, SU), jnp.bfloat16)] * 2
+        out_shape=[
+            jax.ShapeDtypeStruct((rows + (2 * SU if shift == 1 else 0), SU), jnp.bfloat16)
+            for shift in range(groups)
+        ]
         + [jax.ShapeDtypeStruct((2 * SU, SU), jnp.bfloat16)],
         in_specs=[HBM] * 8,
-        out_specs=[VMEM] * 3,
+        out_specs=[VMEM] * (groups + 1),
         scratch_shapes=[
             pltpu.SMEM((1, held), jnp.int32),
             pltpu.SMEM((1, held), jnp.int32),
@@ -371,22 +367,39 @@
             )
         )
     )
-    bit = 1
-    while bit < groups:
-        arrived = exchange(send, "bl", bit)
-        keep, *send = fold(keep, arrived)
-        send = send[0] if send else None
+    arrived = [
+        lax.ppermute(pieces[shift], "bl", [(g, (g + shift) % groups) for g in range(groups)])
+        for shift in range(1, groups)
+    ]
+    vis_rows = groups * rows
+    here, joined = local(
+        functools.partial(join_kernel, rows),
+        [half, pieces[0], *arrived],
+        [(vis_rows, SU), (vis_rows + 4 * SU, SU)],
+        "join",
+    )
+    blocks = [here] + [
+        exchange(joined if shift == 1 else here, "facet", shift) for shift in range(1, facets)
+    ]
+    (near,) = local(
+        functools.partial(stack_kernel, vis_rows), [joined, blocks[1]], [(8 * SU, SU)], "stack"
+    )
+    bit = 2
+    while True:
+        far = exchange(near, "facet", bit)
         bit *= 2
-    blocks = gather(keep[0], "facet")
-    fetched = gather(half[None], "facet", True)
+        if bit == facets:
+            break
+        (near,) = local(
+            functools.partial(stack_kernel, 0), [near, far], [(2 * near.shape[0], SU)], "stack"
+        )
     swap = [(c, 1 - c) for c in range(chan_count)]
-    fetched_swapped = lax.ppermute(fetched, "chan", swap)
-    shifted = lax.ppermute(fetched, "bl", [(g, (g + 1) % groups) for g in range(groups)])
+    near_swapped = lax.ppermute(near, "chan", swap)
 
     grids = pl.pallas_call(
         functools.partial(grid_kernel, (facets, groups, chans, cap, rows)),
         out_shape=jax.ShapeDtypeStruct((slots, 2 * SU, SU), jnp.float32),
-        in_specs=[VMEM] * 2,
+        in_specs=[VMEM] * facets,
         out_specs=VMEM,
         scratch_shapes=[
             pltpu.VMEM((devices, SU), jnp.int32),
@@ -401,8 +414,8 @@
         ),
         name="grid",
     )(*blocks)
-    grids, shifted = lax.optimization_barrier((grids, shifted))
-    shifted_swapped = lax.ppermute(shifted, "chan", swap)
+    grids, far = lax.optimization_barrier((grids, far))
+    far_swapped = lax.ppermute(far, "chan", swap)
     mine, other = pl.pallas_call(
         functools.partial(table_kernel, (slots, meta_row), norm),
         out_shape=[jax.ShapeDtypeStruct((half_rows, 2 * SU), jnp.float32)] * 2,
@@ -417,7 +430,7 @@
             flops=1_000_000_000, bytes_accessed=2_000_000, transcendentals=0
         ),
         name="apply_tables",
-    )(grids, blocks[0], fetched, shifted, fetched_swapped, shifted_swapped)
+    )(grids, here, near, far, near_swapped, far_swapped)
     summand = lax.ppermute(other, "chan", swap)
     return (mine + summand).reshape(1, 1, half_rows, 2, SU)
 

time: 33.3 us -> 30.2 us (0.907)
  starting transfers between devices: 14.8 us -> 12.2 us
  waiting for transfers between devices: 10.2 us -> 8.59 us
  Pallas kernels: 7.39 us -> 8.45 us
    ppermute x9, starting transfers between devices: 14.6 us -> 12 us  [the longest x3 7.01 us: body(): lax.ppermute(pieces[shift], 'bl', [(g, (g + shift) % groups) for g in ran...]
    ppermute x9, waiting for transfers between devices: 9.05 us -> 7.48 us  [the longest x4 3.6 us: exchange(): lax.ppermute(value, axis, [(n, n ^ shift) for n in range(lax.axis_size(ax...]
    pallas_call x1, Pallas kernels: 5.2 us -> 6.25 us  [body(): pl.pallas_call(functools.partial(grid_kernel, (facets, groups, chans, cap...]
  transfers between devices with their start and end apart: 10 -> 10, of which waited for: 8 -> 7; matrix products, arithmetic and copies ran while one was open for 0% -> 0% of each run, Pallas kernels for 16% -> 21%
where the time goes in v11:
time: 30.2 us; the launch traced here: 30 us
  starting transfers between devices  12.2 us (40%)
  waiting for transfers between devices  8.59 us (28%)
  Pallas kernels  8.45 us (28%)
  local copies, waits for them, and re-layouts  0.66 us (2%)
    ppermute x3, starting transfers between devices, body(): lax.ppermute(pieces[shift], 'bl', [(g, (g + shift) % groups) for g in ran...  7.01 us
    pallas_call x1, Pallas kernels, body(): pl.pallas_call(functools.partial(grid_kernel, (facets, groups, chans, cap...  6.25 us
    ppermute x4, starting transfers between devices, exchange(): lax.ppermute(value, axis, [(n, n ^ shift) for n in range(lax.axis_size(ax...  4.95 us
    ppermute x4, waiting for transfers between devices, exchange(): lax.ppermute(value, axis, [(n, n ^ shift) for n in range(lax.axis_size(ax...  3.6 us
    ppermute x3, waiting for transfers between devices, body(): lax.ppermute(pieces[shift], 'bl', [(g, (g + shift) % groups) for g in ran...  2.35 us
    ppermute x1, waiting for transfers between devices, body(): far_swapped = lax.ppermute(far, 'chan', swap)  1.53 us
    ppermute x1, waiting for transfers between devices, body(): summand = lax.ppermute(other, 'chan', swap)  1.12 us
    pallas_call x1, Pallas kernels, body(): pl.pallas_call(functools.partial(table_kernel, (slots, meta_row), norm),...  1.1 us
  transfers between devices with their start and end apart: 10, of which 7 were waited for; matrix products, arithmetic and copies ran while one was open for 0% of the time, Pallas kernels for 21%

profile of v11, /device:TPU:0, one launch (start us, length us, event | category | flops | bytes accessed | tf_op | source)
XLA Modules:
  0.0 30.0 jit_solution(13440953056053614401)
XLA Ops:
  0.0 1.1 %sort_blocks.1 = (bf16[48,128]{1,0:T(8,128)(2,1)S(1)}, bf16[304,128]{1,0:T(8,128)(2,1)S(1)}, bf16[48,128]{1,0:T(8,128)(2,1)S(1)}, bf16[48,128]{1,0:T(8,128)(2,1)S(1)}, bf16[256,128]{1,0:T(8,128)(2,1)S(1)}) custom-call(s32[1,8]{1,0:T(1,128)} %bitcast.12, s32[1,8]{1,0:T(1,128)} %bitcast.13, bf16[64,128]{1,0:T(8,128)(2,1)} %bitcast.8, bf16[16,128]{1,0:T(8,128)(2,1)} %bitcast.9, ...), custom_call_target="tpu_custom_call" | custom-call | flops 100000 | bytes 100000 | tf_op jit(solution)/shard_map/sort_blocks/pallas_call | solution.py:329
  1.1 3.1 %collective-permute-start = (bf16[304,128]{1,0:T(8,128)(2,1)S(1)}, bf16[304,128]{1,0:T(8,128)(2,1)S(1)}, u32[]{:S(2)}, u32[]{:S(2)}) collective-permute-start(bf16[304,128]{1,0:T(8,128)(2,1)S(1)} %get-tuple-element.18), channel_id=1, source_target_pairs={{0,2},{2,4},{4,6},{6,0},{1,3},{3,5},{5,7},{7,1},{8,10},{10,12},{12... | collective-permute-start | bytes 233480 | tf_op jit(solution)/shard_map/ppermute | solution.py:371
  4.1 2.6 %collective-permute-start.1 = (bf16[48,128]{1,0:T(8,128)(2,1)S(1)}, bf16[48,128]{1,0:T(8,128)(2,1)S(1)}, u32[]{:S(2)}, u32[]{:S(2)}) collective-permute-start(bf16[48,128]{1,0:T(8,128)(2,1)S(1)} %get-tuple-element.19), channel_id=1, source_target_pairs={{0,4},{2,6},{4,0},{6,2},{1,5},{3,7},{5,1},{7,3},{8,12},{10,14},{12... | collective-permute-start | bytes 36872 | tf_op jit(solution)/shard_map/ppermute | solution.py:371
  6.7 1.3 %collective-permute-start.2 = (bf16[48,128]{1,0:T(8,128)(2,1)S(1)}, bf16[48,128]{1,0:T(8,128)(2,1)S(1)}, u32[]{:S(2)}, u32[]{:S(2)}) collective-permute-start(bf16[48,128]{1,0:T(8,128)(2,1)S(1)} %get-tuple-element.20), channel_id=1, source_target_pairs={{0,6},{2,0},{4,2},{6,4},{1,7},{3,1},{5,3},{7,5},{8,14},{10,8},{12,... | collective-permute-start | bytes 36872 | tf_op jit(solution)/shard_map/ppermute | solution.py:371
  8.1 1.0 %collective-permute-done.1.refs_2_ = bf16[48,128]{1,0:T(8,128)(2,1)S(1)} collective-permute-done((bf16[48,128]{1,0:T(8,128)(2,1)S(1)}, bf16[48,128]{1,0:T(8,128)(2,1)S(1)}, u32[]{:S(2)}, u32[]{:S(2)}) %collective-permute-start.1) | collective-permute-done | bytes 12320 | tf_op jit(solution)/shard_map/ppermute | solution.py:371
  9.0 1.4 %collective-permute-done.2.refs_3_ = bf16[48,128]{1,0:T(8,128)(2,1)S(1)} collective-permute-done((bf16[48,128]{1,0:T(8,128)(2,1)S(1)}, bf16[48,128]{1,0:T(8,128)(2,1)S(1)}, u32[]{:S(2)}, u32[]{:S(2)}) %collective-permute-start.2) | collective-permute-done | bytes 12320 | tf_op jit(solution)/shard_map/ppermute | solution.py:371
  10.4 0.0 collective-permute-done.refs_1_
  10.5 1.6 %collective-permute-start.3 = (bf16[704,128]{1,0:T(8,128)(2,1)S(1)}, bf16[704,128]{1,0:T(8,128)(2,1)S(1)}, u32[]{:S(2)}, u32[]{:S(2)}) collective-permute-start(bf16[704,128]{1,0:T(8,128)(2,1)S(1)} %get-tuple-element.22.own), channel_id=1, source_target_pairs={{0,8},{8,0},{16,24},{24,16},{1,9},{9,1},{17,25},{25,17},{2,10},{10... | collective-permute-start | bytes 540680 | tf_op jit(solution)/shard_map/ppermute | solution.py:253
  12.0 1.5 %collective-permute-start.5 = (bf16[192,128]{1,0:T(8,128)(2,1)S(1)}, bf16[192,128]{1,0:T(8,128)(2,1)S(1)}, u32[]{:S(2)}, u32[]{:S(2)}) collective-permute-start(bf16[192,128]{1,0:T(8,128)(2,1)S(1)} %get-tuple-element.21.refs_0_.packed), channel_id=1, source_target_pairs={{0,24},{8,16},{16,8},{24,0},{1,25},{9,17},{17,9},{25,1},{2,26},{10... | collective-permute-start | bytes 147464 | tf_op jit(solution)/shard_map/ppermute | solution.py:253
  13.5 0.5 %collective-permute-start.4 = (bf16[192,128]{1,0:T(8,128)(2,1)S(1)}, bf16[192,128]{1,0:T(8,128)(2,1)S(1)}, u32[]{:S(2)}, u32[]{:S(2)}) collective-permute-start(bf16[192,128]{1,0:T(8,128)(2,1)S(1)} %get-tuple-element.21.refs_0_.packed), channel_id=1, source_target_pairs={{0,16},{8,24},{16,0},{24,8},{1,17},{9,25},{17,1},{25,9},{2,18},{10... | collective-permute-start | bytes 147464 | tf_op jit(solution)/shard_map/ppermute | solution.py:253
  14.0 2.5 %collective-permute-done.3.refs_1_.arrived = bf16[704,128]{1,0:T(8,128)(2,1)S(1)} collective-permute-done((bf16[704,128]{1,0:T(8,128)(2,1)S(1)}, bf16[704,128]{1,0:T(8,128)(2,1)S(1)}, u32[]{:S(2)}, u32[]{:S(2)}) %collective-permute-start.3) | collective-permute-done | bytes 180256 | tf_op jit(solution)/shard_map/ppermute | solution.py:253
  16.6 0.1 collective-permute-start.7
  16.6 1.4 %collective-permute-start.6 = (bf16[1024,128]{1,0:T(8,128)(2,1)S(1)}, bf16[1024,128]{1,0:T(8,128)(2,1)S(1)}, u32[]{:S(2)}, u32[]{:S(2)}) collective-permute-start(bf16[1024,128]{1,0:T(8,128)(2,1)S(1)} %stack.1.refs_0_), channel_id=1, source_target_pairs={{0,16},{8,24},{16,0},{24,8},{1,17},{9,25},{17,1},{25,9},{2,18},{10... | collective-permute-start | bytes 786440 | tf_op jit(solution)/shard_map/ppermute | solution.py:253
  18.0 0.0 collective-permute-done.5.refs_3_
  18.0 0.1 collective-permute-done.4.refs_2_
  18.1 6.3 %grid.1.grids = f32[8,256,128]{2,1,0:T(8,128)S(1)} custom-call(bf16[192,128]{1,0:T(8,128)(2,1)S(1)} %get-tuple-element.21.refs_0_.packed, bf16[704,128]{1,0:T(8,128)(2,1)S(1)} %collective-permute-done.3.refs_1_.arrived, bf16[192,128]{1,0:T(8,128)(2,1)S(1)} %collective-permute-done.4.refs_2_, bf16[192,128]{1,0:T(8,128)(2,1)S(1)} %collective-permute-done.5.refs_3_), custom_call_target="tpu_custom_call" | custom-call | flops 4000000000 | bytes 2000000 | tf_op jit(solution)/shard_map/grid/pallas_call | solution.py:399
  24.4 1.0 %collective-permute-done.6.refs_1_ = bf16[1024,128]{1,0:T(8,128)(2,1)S(1)} collective-permute-done((bf16[1024,128]{1,0:T(8,128)(2,1)S(1)}, bf16[1024,128]{1,0:T(8,128)(2,1)S(1)}, u32[]{:S(2)}, u32[]{:S(2)}) %collective-permute-start.6) | collective-permute-done | bytes 262176 | tf_op jit(solution)/shard_map/ppermute | solution.py:253
  25.4 0.0 collective-permute-start.8
  25.4 0.0 collective-permute-done.7.refs_2_
  25.4 1.5 %collective-permute-done.8.refs_3_ = bf16[1024,128]{1,0:T(8,128)(2,1)S(1)} collective-permute-done((bf16[1024,128]{1,0:T(8,128)(2,1)S(1)}, bf16[1024,128]{1,0:T(8,128)(2,1)S(1)}, u32[]{:S(2)}, u32[]{:S(2)}) %collective-permute-start.8) | collective-permute-done | bytes 262176 | tf_op jit(solution)/shard_map/ppermute | solution.py:418
  26.9 1.1 %apply_tables.1 = (f32[64,256]{1,0:T(8,128)S(1)}, f32[64,256]{1,0:T(8,128)S(1)}) custom-call(f32[8,256,128]{2,1,0:T(8,128)S(1)} %grid.1.grids, bf16[192,128]{1,0:T(8,128)(2,1)S(1)} %get-tuple-element.21.refs_0_.packed, bf16[1024,128]{1,0:T(8,128)(2,1)S(1)} %stack.1.refs_0_, bf16[1024,128]{1,0:T(8,128)(2,1)S(1)} %collective-permute-done.6.refs_1_, ...), custom_call_target="tpu_custom_call" | custom-call | flops 1000000000 | bytes 2000000 | tf_op jit(solution)/shard_map/apply_tables/pallas_call | solution.py:419
  28.0 0.2 collective-permute-start.9
  28.2 1.1 %collective-permute-done.9 = f32[64,256]{1,0:T(8,128)S(1)} collective-permute-done((f32[64,256]{1,0:T(8,128)S(1)}, f32[64,256]{1,0:T(8,128)S(1)}, u32[]{:S(2)}, u32[]{:S(2)}) %collective-permute-start.9) | collective-permute-done | bytes 65568 | tf_op jit(solution)/shard_map/ppermute | solution.py:434
  29.3 0.7 %reshape.19 = f32[1,1,64,2,128]{4,3,2,1,0:T(2,128)} reshape(f32[64,256]{1,0:T(8,128)S(1)} %add.3) | data formatting | bytes 131072 | tf_op jit(solution)/shard_map/reshape | solution.py:435
  (3 shorter events, 0.1 us)
Async XLA Ops:
  1.1 9.4 %collective-permute-start = (bf16[304,128]{1,0:T(8,128)(2,1)S(1)}, bf16[304,128]{1,0:T(8,128)(2,1)S(1)}, u32[]{:S(2)}, u32[]{:S(2)}) collective-permute-start(bf16[304,128]{1,0:T(8,128)(2,1)S(1)} %get-tuple-element.18), channel_id=1, source_target_pairs={{0,2},{2,4},{4,6},{6,0},{1,3},{3,5},{5,7},{7,1},{8,10},{10,12},{12... | collective-permute-start | bytes 233480 | tf_op jit(solution)/shard_map/ppermute | solution.py:371
  4.1 4.9 %collective-permute-start.1 = (bf16[48,128]{1,0:T(8,128)(2,1)S(1)}, bf16[48,128]{1,0:T(8,128)(2,1)S(1)}, u32[]{:S(2)}, u32[]{:S(2)}) collective-permute-start(bf16[48,128]{1,0:T(8,128)(2,1)S(1)} %get-tuple-element.19), channel_id=1, source_target_pairs={{0,4},{2,6},{4,0},{6,2},{1,5},{3,7},{5,1},{7,3},{8,12},{10,14},{12... | collective-permute-start | bytes 36872 | tf_op jit(solution)/shard_map/ppermute | solution.py:371
  6.7 3.7 %collective-permute-start.2 = (bf16[48,128]{1,0:T(8,128)(2,1)S(1)}, bf16[48,128]{1,0:T(8,128)(2,1)S(1)}, u32[]{:S(2)}, u32[]{:S(2)}) collective-permute-start(bf16[48,128]{1,0:T(8,128)(2,1)S(1)} %get-tuple-element.20), channel_id=1, source_target_pairs={{0,6},{2,0},{4,2},{6,4},{1,7},{3,1},{5,3},{7,5},{8,14},{10,8},{12,... | collective-permute-start | bytes 36872 | tf_op jit(solution)/shard_map/ppermute | solution.py:371
  10.5 6.1 %collective-permute-start.3 = (bf16[704,128]{1,0:T(8,128)(2,1)S(1)}, bf16[704,128]{1,0:T(8,128)(2,1)S(1)}, u32[]{:S(2)}, u32[]{:S(2)}) collective-permute-start(bf16[704,128]{1,0:T(8,128)(2,1)S(1)} %get-tuple-element.22.own), channel_id=1, source_target_pairs={{0,8},{8,0},{16,24},{24,16},{1,9},{9,1},{17,25},{25,17},{2,10},{10... | collective-permute-start | bytes 540680 | tf_op jit(solution)/shard_map/ppermute | solution.py:253
  12.0 6.0 %collective-permute-start.5 = (bf16[192,128]{1,0:T(8,128)(2,1)S(1)}, bf16[192,128]{1,0:T(8,128)(2,1)S(1)}, u32[]{:S(2)}, u32[]{:S(2)}) collective-permute-start(bf16[192,128]{1,0:T(8,128)(2,1)S(1)} %get-tuple-element.21.refs_0_.packed), channel_id=1, source_target_pairs={{0,24},{8,16},{16,8},{24,0},{1,25},{9,17},{17,9},{25,1},{2,26},{10... | collective-permute-start | bytes 147464 | tf_op jit(solution)/shard_map/ppermute | solution.py:253
  13.5 4.6 %collective-permute-start.4 = (bf16[192,128]{1,0:T(8,128)(2,1)S(1)}, bf16[192,128]{1,0:T(8,128)(2,1)S(1)}, u32[]{:S(2)}, u32[]{:S(2)}) collective-permute-start(bf16[192,128]{1,0:T(8,128)(2,1)S(1)} %get-tuple-element.21.refs_0_.packed), channel_id=1, source_target_pairs={{0,16},{8,24},{16,0},{24,8},{1,17},{9,25},{17,1},{25,9},{2,18},{10... | collective-permute-start | bytes 147464 | tf_op jit(solution)/shard_map/ppermute | solution.py:253
  16.6 8.8 %collective-permute-start.7 = (bf16[1024,128]{1,0:T(8,128)(2,1)S(1)}, bf16[1024,128]{1,0:T(8,128)(2,1)S(1)}, u32[]{:S(2)}, u32[]{:S(2)}) collective-permute-start(bf16[1024,128]{1,0:T(8,128)(2,1)S(1)} %stack.1.refs_0_), channel_id=1, source_target_pairs={{0,1},{1,0},{2,3},{3,2},{4,5},{5,4},{6,7},{7,6},{8,9},{9,8},{10,11... | collective-permute-start | bytes 786440 | tf_op jit(solution)/shard_map/ppermute | solution.py:397
  16.6 8.7 %collective-permute-start.6 = (bf16[1024,128]{1,0:T(8,128)(2,1)S(1)}, bf16[1024,128]{1,0:T(8,128)(2,1)S(1)}, u32[]{:S(2)}, u32[]{:S(2)}) collective-permute-start(bf16[1024,128]{1,0:T(8,128)(2,1)S(1)} %stack.1.refs_0_), channel_id=1, source_target_pairs={{0,16},{8,24},{16,0},{24,8},{1,17},{9,25},{17,1},{25,9},{2,18},{10... | collective-permute-start | bytes 786440 | tf_op jit(solution)/shard_map/ppermute | solution.py:253
  25.4 1.5 %collective-permute-start.8 = (bf16[1024,128]{1,0:T(8,128)(2,1)S(1)}, bf16[1024,128]{1,0:T(8,128)(2,1)S(1)}, u32[]{:S(2)}, u32[]{:S(2)}) collective-permute-start(bf16[1024,128]{1,0:T(8,128)(2,1)S(1)} %collective-permute-done.6.refs_1_), channel_id=1, source_target_pairs={{0,1},{1,0},{2,3},{3,2},{4,5},{5,4},{6,7},{7,6},{8,9},{9,8},{10,11... | collective-permute-start | bytes 786440 | tf_op jit(solution)/shard_map/ppermute | solution.py:418
  28.0 1.3 %collective-permute-start.9 = (f32[64,256]{1,0:T(8,128)S(1)}, f32[64,256]{1,0:T(8,128)S(1)}, u32[]{:S(2)}, u32[]{:S(2)}) collective-permute-start(f32[64,256]{1,0:T(8,128)S(1)} %get-tuple-element.26), channel_id=1, source_target_pairs={{0,1},{1,0},{2,3},{3,2},{4,5},{5,4},{6,7},{7,6},{8,9},{9,8},{10,11... | collective-permute-start | bytes 196616 | tf_op jit(solution)/shard_map/ppermute | solution.py:434

commit v12 on v11

--- a/solution.py
+++ b/solution.py
@@ -113,20 +113,17 @@
 
 
 def join_kernel(rows, half, *refs):
-    *pieces, here, joined = refs
+    *pieces, joined = refs
     for n, ref in enumerate(pieces):
-        piece = ref[:rows, :]
-        here[n * rows : (n + 1) * rows, :] = piece
-        joined[n * rows : (n + 1) * rows, :] = piece
+        joined[n * rows : (n + 1) * rows, :] = ref[:rows, :]
     at = len(pieces) * rows
     joined[at : at + 2 * SU, :] = half[...]
     joined[at + 2 * SU :, :] = pieces[1][rows:, :]
 
 
-def stack_kernel(skip, own, arrived, out_ref):
-    count = own.shape[0] - skip
-    out_ref[:count, :] = own[skip:, :]
-    out_ref[count:, :] = arrived[skip:, :]
+def collect_kernel(skip, *refs):
+    for n, ref in enumerate(refs[:-1]):
+        refs[-1][n * 4 * SU : (n + 1) * 4 * SU, :] = ref[skip:, :]
 
 
 def grid_kernel(sizes, *refs):
@@ -237,12 +234,12 @@
     steps(whole * UNROLL, REST, lax.div(lax.rem(count, UNROLL) + REST - 1, REST))
 
 
-def local(kernel, operands, shapes, name):
+def local(kernel, operands, shape, name):
     return pl.pallas_call(
         kernel,
-        out_shape=[jax.ShapeDtypeStruct(shape, jnp.bfloat16) for shape in shapes],
+        out_shape=jax.ShapeDtypeStruct(shape, jnp.bfloat16),
         in_specs=[VMEM] * len(operands),
-        out_specs=[VMEM] * len(shapes),
+        out_specs=VMEM,
         compiler_params=PARAMS,
         cost_estimate=pl.CostEstimate(flops=0, bytes_accessed=400_000, transcendentals=0),
         name=name,
@@ -253,10 +250,8 @@
     return lax.ppermute(value, axis, [(n, n ^ shift) for n in range(lax.axis_size(axis))])
 
 
-def table_kernel(sizes, norm, grids, packed, *refs):
+def table_kernel(sizes, norm, grids, packed, ours, theirs, mine_ref, other_ref, table_f, total):
     slots, meta_row = sizes
-    ours, theirs = refs[:2], refs[2:4]
-    mine_ref, other_ref, table_f, total = refs[4:]
     chan = lax.axis_index("chan")
     first = chan == 0
 
@@ -266,9 +261,9 @@
 
     result = jnp.zeros((SU, 2 * SU), jnp.float32)
     for s in range(slots):
-        half, at = divmod(2 * SU * s, ours[0].shape[0])
-        fetched = ours[half][at : at + 2 * SU, :].astype(jnp.float32)
-        swapped = theirs[half][at : at + 2 * SU, :].astype(jnp.float32)
+        at = slice(2 * SU * s, 2 * SU * (s + 1))
+        fetched = ours[at, :].astype(jnp.float32)
+        swapped = theirs[at, :].astype(jnp.float32)
         u_real, u_imag = parts(jnp.where(first, fetched, swapped))
         u_side = jnp.concatenate([u_real.T, u_imag.T], axis=1).astype(jnp.bfloat16)
         grid_real = grids[s, :SU, :]
@@ -372,29 +367,17 @@
         for shift in range(1, groups)
     ]
     vis_rows = groups * rows
-    here, joined = local(
+    joined = local(
         functools.partial(join_kernel, rows),
         [half, pieces[0], *arrived],
-        [(vis_rows, SU), (vis_rows + 4 * SU, SU)],
+        (vis_rows + 4 * SU, SU),
         "join",
     )
-    blocks = [here] + [
-        exchange(joined if shift == 1 else here, "facet", shift) for shift in range(1, facets)
-    ]
-    (near,) = local(
-        functools.partial(stack_kernel, vis_rows), [joined, blocks[1]], [(8 * SU, SU)], "stack"
-    )
-    bit = 2
-    while True:
-        far = exchange(near, "facet", bit)
-        bit *= 2
-        if bit == facets:
-            break
-        (near,) = local(
-            functools.partial(stack_kernel, 0), [near, far], [(2 * near.shape[0], SU)], "stack"
-        )
-    swap = [(c, 1 - c) for c in range(chan_count)]
-    near_swapped = lax.ppermute(near, "chan", swap)
+    blocks = [joined] + [exchange(joined, "facet", shift) for shift in range(1, facets)]
+    fetched = local(
+        functools.partial(collect_kernel, vis_rows), blocks, (facets * 4 * SU, SU), "collect"
+    )
+    swapped = lax.ppermute(fetched, "chan", [(c, 1 - c) for c in range(chan_count)])
 
     grids = pl.pallas_call(
         functools.partial(grid_kernel, (facets, groups, chans, cap, rows)),
@@ -414,12 +397,10 @@
         ),
         name="grid",
     )(*blocks)
-    grids, far = lax.optimization_barrier((grids, far))
-    far_swapped = lax.ppermute(far, "chan", swap)
     mine, other = pl.pallas_call(
         functools.partial(table_kernel, (slots, meta_row), norm),
         out_shape=[jax.ShapeDtypeStruct((half_rows, 2 * SU), jnp.float32)] * 2,
-        in_specs=[VMEM] * 6,
+        in_specs=[VMEM] * 4,
         out_specs=[VMEM, VMEM],
         scratch_shapes=[
             pltpu.VMEM((2 * SU, SU), jnp.float32),
@@ -430,8 +411,8 @@
             flops=1_000_000_000, bytes_accessed=2_000_000, transcendentals=0
         ),
         name="apply_tables",
-    )(grids, here, near, far, near_swapped, far_swapped)
-    summand = lax.ppermute(other, "chan", swap)
+    )(grids, joined, fetched, swapped)
+    summand = lax.ppermute(other, "chan", [(c, 1 - c) for c in range(chan_count)])
     return (mine + summand).reshape(1, 1, half_rows, 2, SU)
 
 

time: 30.2 us -> 29.5 us (0.977)
  waiting for transfers between devices: 8.59 us -> 9.9 us
  Pallas kernels: 8.45 us -> 7.4 us
  starting transfers between devices: 12.2 us -> 11.2 us
    ppermute x4 -> x3, waiting for transfers between devices: 3.6 us -> 6.65 us  [exchange(): lax.ppermute(value, axis, [(n, n ^ shift) for n in range(lax.axis_size(ax...]
    ppermute x3 -> x2, waiting for transfers between devices: 2.65 us -> 0.9 us  [the longest x1 0.9 us: body(): lax.ppermute(other, 'chan', [(c, 1 - c) for c in range(chan_count)])]
    ppermute x4 -> x3, starting transfers between devices: 4.95 us -> 3.55 us  [exchange(): lax.ppermute(value, axis, [(n, n ^ shift) for n in range(lax.axis_size(ax...]
    pallas_call x1, Pallas kernels: 6.25 us -> 5.2 us  [body(): pl.pallas_call(functools.partial(grid_kernel, (facets, groups, chans, cap...]
    ppermute x3 -> x2, starting transfers between devices: 0.28 us -> 0.63 us  [the longest x1 0.56 us: body(): lax.ppermute(other, 'chan', [(c, 1 - c) for c in range(chan_count)])]
  transfers between devices with their start and end apart: 10 -> 8, of which waited for: 7 -> 6; matrix products, arithmetic and copies ran while one was open for 0% -> 0% of each run, Pallas kernels for 21% -> 18%
where the time goes in v12:
time: 29.5 us; the launch traced here: 29.2 us
  starting transfers between devices  11.2 us (38%)
  waiting for transfers between devices  9.9 us (34%)
  Pallas kernels  7.4 us (25%)
  local copies, waits for them, and re-layouts  0.66 us (2%)
    ppermute x3, starting transfers between devices, body(): lax.ppermute(pieces[shift], 'bl', [(g, (g + shift) % groups) for g in ran...  7.01 us
    ppermute x3, waiting for transfers between devices, exchange(): lax.ppermute(value, axis, [(n, n ^ shift) for n in range(lax.axis_size(ax...  6.65 us
    pallas_call x1, Pallas kernels, body(): pl.pallas_call(functools.partial(grid_kernel, (facets, groups, chans, cap...  5.2 us
    ppermute x3, starting transfers between devices, exchange(): lax.ppermute(value, axis, [(n, n ^ shift) for n in range(lax.axis_size(ax...  3.55 us
    ppermute x3, waiting for transfers between devices, body(): lax.ppermute(pieces[shift], 'bl', [(g, (g + shift) % groups) for g in ran...  2.35 us
    pallas_call x1, Pallas kernels, body(): pl.pallas_call(functools.partial(table_kernel, (slots, meta_row), norm),...  1.1 us
    pallas_call x1, Pallas kernels, body(): pl.pallas_call(functools.partial(sort_kernel, (groups, held, chans, cap,...  1.06 us
    ppermute x1, waiting for transfers between devices, body(): lax.ppermute(other, 'chan', [(c, 1 - c) for c in range(chan_count)])  0.9 us
  transfers between devices with their start and end apart: 8, of which 6 were waited for; matrix products, arithmetic and copies ran while one was open for 0% of the time, Pallas kernels for 18%

profile of v12, /device:TPU:0, one launch (start us, length us, event | category | flops | bytes accessed | tf_op | source)
XLA Modules:
  0.0 29.2 jit_solution(5578443051957657055)
XLA Ops:
  0.0 1.1 %sort_blocks.1 = (bf16[48,128]{1,0:T(8,128)(2,1)S(1)}, bf16[304,128]{1,0:T(8,128)(2,1)S(1)}, bf16[48,128]{1,0:T(8,128)(2,1)S(1)}, bf16[48,128]{1,0:T(8,128)(2,1)S(1)}, bf16[256,128]{1,0:T(8,128)(2,1)S(1)}) custom-call(s32[1,8]{1,0:T(1,128)} %bitcast.12, s32[1,8]{1,0:T(1,128)} %bitcast.13, bf16[64,128]{1,0:T(8,128)(2,1)} %bitcast.8, bf16[16,128]{1,0:T(8,128)(2,1)} %bitcast.9, ...), custom_call_target="tpu_custom_call" | custom-call | flops 100000 | bytes 100000 | tf_op jit(solution)/shard_map/sort_blocks/pallas_call | solution.py:324
  1.1 3.1 %collective-permute-start = (bf16[304,128]{1,0:T(8,128)(2,1)S(1)}, bf16[304,128]{1,0:T(8,128)(2,1)S(1)}, u32[]{:S(2)}, u32[]{:S(2)}) collective-permute-start(bf16[304,128]{1,0:T(8,128)(2,1)S(1)} %get-tuple-element.14), channel_id=1, source_target_pairs={{0,2},{2,4},{4,6},{6,0},{1,3},{3,5},{5,7},{7,1},{8,10},{10,12},{12... | collective-permute-start | bytes 233480 | tf_op jit(solution)/shard_map/ppermute | solution.py:366
  4.1 2.6 %collective-permute-start.1 = (bf16[48,128]{1,0:T(8,128)(2,1)S(1)}, bf16[48,128]{1,0:T(8,128)(2,1)S(1)}, u32[]{:S(2)}, u32[]{:S(2)}) collective-permute-start(bf16[48,128]{1,0:T(8,128)(2,1)S(1)} %get-tuple-element.15), channel_id=1, source_target_pairs={{0,4},{2,6},{4,0},{6,2},{1,5},{3,7},{5,1},{7,3},{8,12},{10,14},{12... | collective-permute-start | bytes 36872 | tf_op jit(solution)/shard_map/ppermute | solution.py:366
  6.7 1.3 %collective-permute-start.2 = (bf16[48,128]{1,0:T(8,128)(2,1)S(1)}, bf16[48,128]{1,0:T(8,128)(2,1)S(1)}, u32[]{:S(2)}, u32[]{:S(2)}) collective-permute-start(bf16[48,128]{1,0:T(8,128)(2,1)S(1)} %get-tuple-element.16), channel_id=1, source_target_pairs={{0,6},{2,0},{4,2},{6,4},{1,7},{3,1},{5,3},{7,5},{8,14},{10,8},{12,... | collective-permute-start | bytes 36872 | tf_op jit(solution)/shard_map/ppermute | solution.py:366
  8.1 1.0 %collective-permute-done.1.refs_2_ = bf16[48,128]{1,0:T(8,128)(2,1)S(1)} collective-permute-done((bf16[48,128]{1,0:T(8,128)(2,1)S(1)}, bf16[48,128]{1,0:T(8,128)(2,1)S(1)}, u32[]{:S(2)}, u32[]{:S(2)}) %collective-permute-start.1) | collective-permute-done | bytes 12320 | tf_op jit(solution)/shard_map/ppermute | solution.py:366
  9.0 1.4 %collective-permute-done.2.refs_3_ = bf16[48,128]{1,0:T(8,128)(2,1)S(1)} collective-permute-done((bf16[48,128]{1,0:T(8,128)(2,1)S(1)}, bf16[48,128]{1,0:T(8,128)(2,1)S(1)}, u32[]{:S(2)}, u32[]{:S(2)}) %collective-permute-start.2) | collective-permute-done | bytes 12320 | tf_op jit(solution)/shard_map/ppermute | solution.py:366
  10.4 0.0 collective-permute-done.refs_1_
  10.4 2.5 %collective-permute-start.5 = (bf16[704,128]{1,0:T(8,128)(2,1)S(1)}, bf16[704,128]{1,0:T(8,128)(2,1)S(1)}, u32[]{:S(2)}, u32[]{:S(2)}) collective-permute-start(bf16[704,128]{1,0:T(8,128)(2,1)S(1)} %join.1.refs_0_.packed), channel_id=1, source_target_pairs={{0,24},{8,16},{16,8},{24,0},{1,25},{9,17},{17,9},{25,1},{2,26},{10... | collective-permute-start | bytes 540680 | tf_op jit(solution)/shard_map/ppermute | solution.py:250
  13.0 0.5 %collective-permute-start.4 = (bf16[704,128]{1,0:T(8,128)(2,1)S(1)}, bf16[704,128]{1,0:T(8,128)(2,1)S(1)}, u32[]{:S(2)}, u32[]{:S(2)}) collective-permute-start(bf16[704,128]{1,0:T(8,128)(2,1)S(1)} %join.1.refs_0_.packed), channel_id=1, source_target_pairs={{0,16},{8,24},{16,0},{24,8},{1,17},{9,25},{17,1},{25,9},{2,18},{10... | collective-permute-start | bytes 540680 | tf_op jit(solution)/shard_map/ppermute | solution.py:250
  13.5 0.5 %collective-permute-start.3 = (bf16[704,128]{1,0:T(8,128)(2,1)S(1)}, bf16[704,128]{1,0:T(8,128)(2,1)S(1)}, u32[]{:S(2)}, u32[]{:S(2)}) collective-permute-start(bf16[704,128]{1,0:T(8,128)(2,1)S(1)} %join.1.refs_0_.packed), channel_id=1, source_target_pairs={{0,8},{8,0},{16,24},{24,16},{1,9},{9,1},{17,25},{25,17},{2,10},{10... | collective-permute-start | bytes 540680 | tf_op jit(solution)/shard_map/ppermute | solution.py:250
  14.0 4.5 %collective-permute-done.5.refs_3_ = bf16[704,128]{1,0:T(8,128)(2,1)S(1)} collective-permute-done((bf16[704,128]{1,0:T(8,128)(2,1)S(1)}, bf16[704,128]{1,0:T(8,128)(2,1)S(1)}, u32[]{:S(2)}, u32[]{:S(2)}) %collective-permute-start.5) | collective-permute-done | bytes 180256 | tf_op jit(solution)/shard_map/ppermute | solution.py:250
  18.5 1.9 %collective-permute-done.4.refs_2_ = bf16[704,128]{1,0:T(8,128)(2,1)S(1)} collective-permute-done((bf16[704,128]{1,0:T(8,128)(2,1)S(1)}, bf16[704,128]{1,0:T(8,128)(2,1)S(1)}, u32[]{:S(2)}, u32[]{:S(2)}) %collective-permute-start.4) | collective-permute-done | bytes 180256 | tf_op jit(solution)/shard_map/ppermute | solution.py:250
  20.5 0.2 collective-permute-done.3.refs_1_
  20.7 0.1 collective-permute-start.6
  20.8 5.2 %grid.1.grids = f32[8,256,128]{2,1,0:T(8,128)S(1)} custom-call(bf16[704,128]{1,0:T(8,128)(2,1)S(1)} %join.1.refs_0_.packed, bf16[704,128]{1,0:T(8,128)(2,1)S(1)} %collective-permute-done.3.refs_1_, bf16[704,128]{1,0:T(8,128)(2,1)S(1)} %collective-permute-done.4.refs_2_, bf16[704,128]{1,0:T(8,128)(2,1)S(1)} %collective-permute-done.5.refs_3_), custom_call_target="tpu_custom_call" | custom-call | flops 4000000000 | bytes 2000000 | tf_op jit(solution)/shard_map/grid/pallas_call | solution.py:382
  26.0 0.0 collective-permute-done.6.theirs
  26.0 1.1 %apply_tables.1 = (f32[64,256]{1,0:T(8,128)S(1)}, f32[64,256]{1,0:T(8,128)S(1)}) custom-call(f32[8,256,128]{2,1,0:T(8,128)S(1)} %grid.1.grids, bf16[704,128]{1,0:T(8,128)(2,1)S(1)} %join.1.refs_0_.packed, bf16[2048,128]{1,0:T(8,128)(2,1)S(1)} %collect.1.ours, bf16[2048,128]{1,0:T(8,128)(2,1)S(1)} %collective-permute-done.6.theirs), custom_call_target="tpu_custom_call" | custom-call | flops 1000000000 | bytes 2000000 | tf_op jit(solution)/shard_map/apply_tables/pallas_call | solution.py:400
  27.1 0.6 %collective-permute-start.7 = (f32[64,256]{1,0:T(8,128)S(1)}, f32[64,256]{1,0:T(8,128)S(1)}, u32[]{:S(2)}, u32[]{:S(2)}) collective-permute-start(f32[64,256]{1,0:T(8,128)S(1)} %get-tuple-element.18), channel_id=1, source_target_pairs={{0,1},{1,0},{2,3},{3,2},{4,5},{5,4},{6,7},{7,6},{8,9},{9,8},{10,11... | collective-permute-start | bytes 196616 | tf_op jit(solution)/shard_map/ppermute | solution.py:415
  27.7 0.9 %collective-permute-done.7 = f32[64,256]{1,0:T(8,128)S(1)} collective-permute-done((f32[64,256]{1,0:T(8,128)S(1)}, f32[64,256]{1,0:T(8,128)S(1)}, u32[]{:S(2)}, u32[]{:S(2)}) %collective-permute-start.7) | collective-permute-done | bytes 65568 | tf_op jit(solution)/shard_map/ppermute | solution.py:415
  28.6 0.7 %reshape.19 = f32[1,1,64,2,128]{4,3,2,1,0:T(2,128)} reshape(f32[64,256]{1,0:T(8,128)S(1)} %add.3) | data formatting | bytes 131072 | tf_op jit(solution)/shard_map/reshape | solution.py:416
  (3 shorter events, 0.1 us)
Async XLA Ops:
  1.1 9.4 %collective-permute-start = (bf16[304,128]{1,0:T(8,128)(2,1)S(1)}, bf16[304,128]{1,0:T(8,128)(2,1)S(1)}, u32[]{:S(2)}, u32[]{:S(2)}) collective-permute-start(bf16[304,128]{1,0:T(8,128)(2,1)S(1)} %get-tuple-element.14), channel_id=1, source_target_pairs={{0,2},{2,4},{4,6},{6,0},{1,3},{3,5},{5,7},{7,1},{8,10},{10,12},{12... | collective-permute-start | bytes 233480 | tf_op jit(solution)/shard_map/ppermute | solution.py:366
  4.1 4.9 %collective-permute-start.1 = (bf16[48,128]{1,0:T(8,128)(2,1)S(1)}, bf16[48,128]{1,0:T(8,128)(2,1)S(1)}, u32[]{:S(2)}, u32[]{:S(2)}) collective-permute-start(bf16[48,128]{1,0:T(8,128)(2,1)S(1)} %get-tuple-element.15), channel_id=1, source_target_pairs={{0,4},{2,6},{4,0},{6,2},{1,5},{3,7},{5,1},{7,3},{8,12},{10,14},{12... | collective-permute-start | bytes 36872 | tf_op jit(solution)/shard_map/ppermute | solution.py:366
  6.7 3.7 %collective-permute-start.2 = (bf16[48,128]{1,0:T(8,128)(2,1)S(1)}, bf16[48,128]{1,0:T(8,128)(2,1)S(1)}, u32[]{:S(2)}, u32[]{:S(2)}) collective-permute-start(bf16[48,128]{1,0:T(8,128)(2,1)S(1)} %get-tuple-element.16), channel_id=1, source_target_pairs={{0,6},{2,0},{4,2},{6,4},{1,7},{3,1},{5,3},{7,5},{8,14},{10,8},{12,... | collective-permute-start | bytes 36872 | tf_op jit(solution)/shard_map/ppermute | solution.py:366
  10.4 8.1 %collective-permute-start.5 = (bf16[704,128]{1,0:T(8,128)(2,1)S(1)}, bf16[704,128]{1,0:T(8,128)(2,1)S(1)}, u32[]{:S(2)}, u32[]{:S(2)}) collective-permute-start(bf16[704,128]{1,0:T(8,128)(2,1)S(1)} %join.1.refs_0_.packed), channel_id=1, source_target_pairs={{0,24},{8,16},{16,8},{24,0},{1,25},{9,17},{17,9},{25,1},{2,26},{10... | collective-permute-start | bytes 540680 | tf_op jit(solution)/shard_map/ppermute | solution.py:250
  13.0 7.5 %collective-permute-start.4 = (bf16[704,128]{1,0:T(8,128)(2,1)S(1)}, bf16[704,128]{1,0:T(8,128)(2,1)S(1)}, u32[]{:S(2)}, u32[]{:S(2)}) collective-permute-start(bf16[704,128]{1,0:T(8,128)(2,1)S(1)} %join.1.refs_0_.packed), channel_id=1, source_target_pairs={{0,16},{8,24},{16,0},{24,8},{1,17},{9,25},{17,1},{25,9},{2,18},{10... | collective-permute-start | bytes 540680 | tf_op jit(solution)/shard_map/ppermute | solution.py:250
  13.5 7.2 %collective-permute-start.3 = (bf16[704,128]{1,0:T(8,128)(2,1)S(1)}, bf16[704,128]{1,0:T(8,128)(2,1)S(1)}, u32[]{:S(2)}, u32[]{:S(2)}) collective-permute-start(bf16[704,128]{1,0:T(8,128)(2,1)S(1)} %join.1.refs_0_.packed), channel_id=1, source_target_pairs={{0,8},{8,0},{16,24},{24,16},{1,9},{9,1},{17,25},{25,17},{2,10},{10... | collective-permute-start | bytes 540680 | tf_op jit(solution)/shard_map/ppermute | solution.py:250
  20.7 5.3 %collective-permute-start.6 = (bf16[2048,128]{1,0:T(8,128)(2,1)S(1)}, bf16[2048,128]{1,0:T(8,128)(2,1)S(1)}, u32[]{:S(2)}, u32[]{:S(2)}) collective-permute-start(bf16[2048,128]{1,0:T(8,128)(2,1)S(1)} %collect.1.ours), channel_id=1, source_target_pairs={{0,1},{1,0},{2,3},{3,2},{4,5},{5,4},{6,7},{7,6},{8,9},{9,8},{10,11... | collective-permute-start | bytes 1572872 | tf_op jit(solution)/shard_map/ppermute | solution.py:380
  27.1 1.5 %collective-permute-start.7 = (f32[64,256]{1,0:T(8,128)S(1)}, f32[64,256]{1,0:T(8,128)S(1)}, u32[]{:S(2)}, u32[]{:S(2)}) collective-permute-start(f32[64,256]{1,0:T(8,128)S(1)} %get-tuple-element.18), channel_id=1, source_target_pairs={{0,1},{1,0},{2,3},{3,2},{4,5},{5,4},{6,7},{7,6},{8,9},{9,8},{10,11... | collective-permute-start | bytes 196616 | tf_op jit(solution)/shard_map/ppermute | solution.py:415

commit v13 on v12

--- a/solution.py
+++ b/solution.py
@@ -127,11 +127,13 @@
 
 
 def grid_kernel(sizes, *refs):
-    facets, groups, chans, cap, rows = sizes
-    grids = refs[facets]
-    meta_v, meta_s, order, spots_u, spots_v, turns_real, turns_imag, sem = refs[facets + 1 :]
-    pieces = [ref.at[pl.ds(n * rows, rows)] for ref in refs[:facets] for n in range(groups)]
-    devices = facets * groups
+    facets, groups, chans, cap, rows, count_here = sizes
+    own_ref, grids = refs[0], refs[1 + count_here]
+    meta_v, meta_s, order, spots_u, spots_v, turns_real, turns_imag, sem = refs[2 + count_here :]
+    pieces = [
+        ref.at[pl.ds(n * rows, rows)] for ref in refs[1 : 1 + count_here] for n in range(groups)
+    ]
+    devices = len(pieces)
     slots = 2 * facets
     lines = cap * chans
     meta_row = 2 * (lines + cap)
@@ -141,7 +143,7 @@
     chan = lax.axis_index("chan")
 
     lane = lax.broadcasted_iota(jnp.int32, (1, SU), 1)
-    own = pieces[0][tail : tail + 16, :].astype(jnp.float32)
+    own = own_ref[tail : tail + 16, :].astype(jnp.float32)
     numbers = own[meta_row - tail + 1 : meta_row - tail + 2]
     for d in range(devices):
         meta = pieces[d][tail : tail + 16, :].astype(jnp.float32)
@@ -250,8 +252,9 @@
     return lax.ppermute(value, axis, [(n, n ^ shift) for n in range(lax.axis_size(axis))])
 
 
-def table_kernel(sizes, norm, grids, packed, ours, theirs, mine_ref, other_ref, table_f, total):
+def table_kernel(sizes, norm, packed, ours, theirs, *refs):
     slots, meta_row = sizes
+    grids, (mine_ref, other_ref, table_f, total) = refs[:-4], refs[-4:]
     chan = lax.axis_index("chan")
     first = chan == 0
 
@@ -266,8 +269,9 @@
         swapped = theirs[at, :].astype(jnp.float32)
         u_real, u_imag = parts(jnp.where(first, fetched, swapped))
         u_side = jnp.concatenate([u_real.T, u_imag.T], axis=1).astype(jnp.bfloat16)
-        grid_real = grids[s, :SU, :]
-        grid_imag = grids[s, SU:, :]
+        grid_real, grid_imag = (
+            sum(ref[s, part * SU : (part + 1) * SU, :] for ref in grids) for part in range(2)
+        )
         inner = jnp.concatenate(
             [
                 jnp.concatenate([grid_real, grid_imag], axis=1),
@@ -364,7 +368,7 @@
     )
     arrived = [
         lax.ppermute(pieces[shift], "bl", [(g, (g + shift) % groups) for g in range(groups)])
-        for shift in range(1, groups)
+        for shift in [1, *range(groups - 1, 1, -1)]
     ]
     vis_rows = groups * rows
     joined = local(
@@ -374,33 +378,40 @@
         "join",
     )
     blocks = [joined] + [exchange(joined, "facet", shift) for shift in range(1, facets)]
+    def grid(some):
+        lines = len(some) * groups * cap
+        return pl.pallas_call(
+            functools.partial(grid_kernel, (facets, groups, chans, cap, rows, len(some))),
+            out_shape=jax.ShapeDtypeStruct((slots, 2 * SU, SU), jnp.float32),
+            in_specs=[VMEM] * (1 + len(some)),
+            out_specs=VMEM,
+            scratch_shapes=[
+                pltpu.VMEM((len(some) * groups, SU), jnp.int32),
+                pltpu.SMEM((len(some) * groups, SU), jnp.int32),
+                pltpu.SMEM((lines + REST,), jnp.int32),
+            ]
+            + [pltpu.VMEM((lines * chans + 8, SU), jnp.float32)] * 4
+            + [pltpu.SemaphoreType.DMA],
+            compiler_params=PARAMS,
+            cost_estimate=pl.CostEstimate(
+                flops=len(some) * 1_000_000_000,
+                bytes_accessed=1_000_000,
+                transcendentals=len(some) * 1_000_000,
+            ),
+            name="grid",
+        )(joined, *some)
+
+    grids = [grid(blocks[:1]), grid(blocks[-1:])]
+    blocks, grids = lax.optimization_barrier((blocks, grids))
     fetched = local(
         functools.partial(collect_kernel, vis_rows), blocks, (facets * 4 * SU, SU), "collect"
     )
     swapped = lax.ppermute(fetched, "chan", [(c, 1 - c) for c in range(chan_count)])
-
-    grids = pl.pallas_call(
-        functools.partial(grid_kernel, (facets, groups, chans, cap, rows)),
-        out_shape=jax.ShapeDtypeStruct((slots, 2 * SU, SU), jnp.float32),
-        in_specs=[VMEM] * facets,
-        out_specs=VMEM,
-        scratch_shapes=[
-            pltpu.VMEM((devices, SU), jnp.int32),
-            pltpu.SMEM((devices, SU), jnp.int32),
-            pltpu.SMEM((devices * cap + REST,), jnp.int32),
-        ]
-        + [pltpu.VMEM((devices * cap * chans + 8, SU), jnp.float32)] * 4
-        + [pltpu.SemaphoreType.DMA],
-        compiler_params=PARAMS,
-        cost_estimate=pl.CostEstimate(
-            flops=4_000_000_000, bytes_accessed=2_000_000, transcendentals=4_000_000
-        ),
-        name="grid",
-    )(*blocks)
+    grids.append(grid(blocks[1:-1]))
     mine, other = pl.pallas_call(
         functools.partial(table_kernel, (slots, meta_row), norm),
         out_shape=[jax.ShapeDtypeStruct((half_rows, 2 * SU), jnp.float32)] * 2,
-        in_specs=[VMEM] * 4,
+        in_specs=[VMEM] * (3 + len(grids)),
         out_specs=[VMEM, VMEM],
         scratch_shapes=[
             pltpu.VMEM((2 * SU, SU), jnp.float32),
@@ -411,7 +422,7 @@
             flops=1_000_000_000, bytes_accessed=2_000_000, transcendentals=0
         ),
         name="apply_tables",
-    )(grids, joined, fetched, swapped)
+    )(joined, fetched, swapped, *grids)
     summand = lax.ppermute(other, "chan", [(c, 1 - c) for c in range(chan_count)])
     return (mine + summand).reshape(1, 1, half_rows, 2, SU)
 

time: 29.5 us -> 27.4 us (0.929); the launches traced: 29.2 us -> 27.6 us
  waiting for transfers between devices: 9.9 us -> 7 us
  Pallas kernels: 7.4 us -> 9.56 us
  starting transfers between devices: 11.2 us -> 10.3 us
    ppermute x3, waiting for transfers between devices: 6.65 us -> 2.45 us  [exchange(): lax.ppermute(value, axis, [(n, n ^ shift) for n in range(lax.axis_size(ax...]
    pallas_call x1 -> x3, Pallas kernels: 5.2 us -> 7.32 us  [grid(): pl.pallas_call(functools.partial(grid_kernel, (facets, groups, chans, cap...]
    ppermute x3, waiting for transfers between devices: 2.35 us -> 3.65 us  [body(): lax.ppermute(pieces[shift], 'bl', [(g, (g + shift) % groups) for g in ran...]
    ppermute x3, starting transfers between devices: 7.01 us -> 6.11 us  [body(): lax.ppermute(pieces[shift], 'bl', [(g, (g + shift) % groups) for g in ran...]
  transfers between devices with their start and end apart: 8 -> 8, of which waited for: 6 -> 4; matrix products, arithmetic and copies ran while one was open for 0% -> 0% of each run, Pallas kernels for 18% -> 27%
where the time goes in v13:
time: 27.4 us; the launch traced here: 27.6 us
  starting transfers between devices  10.3 us (38%)
  Pallas kernels  9.56 us (35%)
  waiting for transfers between devices  7 us (26%)
  local copies, waits for them, and re-layouts  0.66 us (2%)
    pallas_call x3, Pallas kernels, grid(): pl.pallas_call(functools.partial(grid_kernel, (facets, groups, chans, cap...  7.32 us
    ppermute x3, starting transfers between devices, body(): lax.ppermute(pieces[shift], 'bl', [(g, (g + shift) % groups) for g in ran...  6.11 us
    ppermute x3, waiting for transfers between devices, body(): lax.ppermute(pieces[shift], 'bl', [(g, (g + shift) % groups) for g in ran...  3.65 us
    ppermute x3, starting transfers between devices, exchange(): lax.ppermute(value, axis, [(n, n ^ shift) for n in range(lax.axis_size(ax...  3.55 us
    ppermute x3, waiting for transfers between devices, exchange(): lax.ppermute(value, axis, [(n, n ^ shift) for n in range(lax.axis_size(ax...  2.45 us
    pallas_call x1, Pallas kernels, body(): pl.pallas_call(functools.partial(table_kernel, (slots, meta_row), norm),...  1.12 us
    pallas_call x1, Pallas kernels, body(): pl.pallas_call(functools.partial(sort_kernel, (groups, held, chans, cap,...  1.06 us
    ppermute x1, waiting for transfers between devices, body(): lax.ppermute(other, 'chan', [(c, 1 - c) for c in range(chan_count)])  0.9 us
  transfers between devices with their start and end apart: 8, of which 4 were waited for; matrix products, arithmetic and copies ran while one was open for 0% of the time, Pallas kernels for 27%

profile of v13, /device:TPU:0, one launch (start us, length us, event | category | flops | bytes accessed | tf_op | source)
XLA Modules:
  0.0 27.6 jit_solution(10481296268952068726)
XLA Ops:
  0.0 1.1 %sort_blocks.1 = (bf16[48,128]{1,0:T(8,128)(2,1)S(1)}, bf16[304,128]{1,0:T(8,128)(2,1)S(1)}, bf16[48,128]{1,0:T(8,128)(2,1)S(1)}, bf16[48,128]{1,0:T(8,128)(2,1)S(1)}, bf16[256,128]{1,0:T(8,128)(2,1)S(1)}) custom-call(s32[1,8]{1,0:T(1,128)} %bitcast.12, s32[1,8]{1,0:T(1,128)} %bitcast.13, bf16[64,128]{1,0:T(8,128)(2,1)} %bitcast.8, bf16[16,128]{1,0:T(8,128)(2,1)} %bitcast.9, ...), custom_call_target="tpu_custom_call" | custom-call | flops 100000 | bytes 100000 | tf_op jit(solution)/shard_map/sort_blocks/pallas_call | solution.py:328
  1.1 3.1 %collective-permute-start = (bf16[304,128]{1,0:T(8,128)(2,1)S(1)}, bf16[304,128]{1,0:T(8,128)(2,1)S(1)}, u32[]{:S(2)}, u32[]{:S(2)}) collective-permute-start(bf16[304,128]{1,0:T(8,128)(2,1)S(1)} %get-tuple-element.20), channel_id=1, source_target_pairs={{0,2},{2,4},{4,6},{6,0},{1,3},{3,5},{5,7},{7,1},{8,10},{10,12},{12... | collective-permute-start | bytes 233480 | tf_op jit(solution)/shard_map/ppermute | solution.py:370
  4.1 2.1 %collective-permute-start.1 = (bf16[48,128]{1,0:T(8,128)(2,1)S(1)}, bf16[48,128]{1,0:T(8,128)(2,1)S(1)}, u32[]{:S(2)}, u32[]{:S(2)}) collective-permute-start(bf16[48,128]{1,0:T(8,128)(2,1)S(1)} %get-tuple-element.21), channel_id=1, source_target_pairs={{0,6},{2,0},{4,2},{6,4},{1,7},{3,1},{5,3},{7,5},{8,14},{10,8},{12,... | collective-permute-start | bytes 36872 | tf_op jit(solution)/shard_map/ppermute | solution.py:370
  6.2 0.9 %collective-permute-start.2 = (bf16[48,128]{1,0:T(8,128)(2,1)S(1)}, bf16[48,128]{1,0:T(8,128)(2,1)S(1)}, u32[]{:S(2)}, u32[]{:S(2)}) collective-permute-start(bf16[48,128]{1,0:T(8,128)(2,1)S(1)} %get-tuple-element.22), channel_id=1, source_target_pairs={{0,4},{2,6},{4,0},{6,2},{1,5},{3,7},{5,1},{7,3},{8,12},{10,14},{12... | collective-permute-start | bytes 36872 | tf_op jit(solution)/shard_map/ppermute | solution.py:370
  7.2 1.4 %collective-permute-done.1.refs_2_ = bf16[48,128]{1,0:T(8,128)(2,1)S(1)} collective-permute-done((bf16[48,128]{1,0:T(8,128)(2,1)S(1)}, bf16[48,128]{1,0:T(8,128)(2,1)S(1)}, u32[]{:S(2)}, u32[]{:S(2)}) %collective-permute-start.1) | collective-permute-done | bytes 12320 | tf_op jit(solution)/shard_map/ppermute | solution.py:370
  8.6 2.3 %collective-permute-done.2.refs_3_ = bf16[48,128]{1,0:T(8,128)(2,1)S(1)} collective-permute-done((bf16[48,128]{1,0:T(8,128)(2,1)S(1)}, bf16[48,128]{1,0:T(8,128)(2,1)S(1)}, u32[]{:S(2)}, u32[]{:S(2)}) %collective-permute-start.2) | collective-permute-done | bytes 12320 | tf_op jit(solution)/shard_map/ppermute | solution.py:370
  10.8 0.0 collective-permute-done.refs_1_
  10.9 2.7 %collective-permute-start.5 = (bf16[704,128]{1,0:T(8,128)(2,1)S(1)}, bf16[704,128]{1,0:T(8,128)(2,1)S(1)}, u32[]{:S(2)}, u32[]{:S(2)}) collective-permute-start(bf16[704,128]{1,0:T(8,128)(2,1)S(1)} %join.1.refs_0_.refs_1_.packed), channel_id=1, source_target_pairs={{0,24},{8,16},{16,8},{24,0},{1,25},{9,17},{17,9},{25,1},{2,26},{10... | collective-permute-start | bytes 540680 | tf_op jit(solution)/shard_map/ppermute | solution.py:252
  13.5 0.5 %collective-permute-start.3 = (bf16[704,128]{1,0:T(8,128)(2,1)S(1)}, bf16[704,128]{1,0:T(8,128)(2,1)S(1)}, u32[]{:S(2)}, u32[]{:S(2)}) collective-permute-start(bf16[704,128]{1,0:T(8,128)(2,1)S(1)} %join.1.refs_0_.refs_1_.packed), channel_id=1, source_target_pairs={{0,8},{8,0},{16,24},{24,16},{1,9},{9,1},{17,25},{25,17},{2,10},{10... | collective-permute-start | bytes 540680 | tf_op jit(solution)/shard_map/ppermute | solution.py:252
  14.1 0.4 %collective-permute-start.4 = (bf16[704,128]{1,0:T(8,128)(2,1)S(1)}, bf16[704,128]{1,0:T(8,128)(2,1)S(1)}, u32[]{:S(2)}, u32[]{:S(2)}) collective-permute-start(bf16[704,128]{1,0:T(8,128)(2,1)S(1)} %join.1.refs_0_.refs_1_.packed), channel_id=1, source_target_pairs={{0,16},{8,24},{16,0},{24,8},{1,17},{9,25},{17,1},{25,9},{2,18},{10... | collective-permute-start | bytes 540680 | tf_op jit(solution)/shard_map/ppermute | solution.py:252
  14.4 1.9 %grid.3.refs_0_ = f32[8,256,128]{2,1,0:T(8,128)S(1)} custom-call(bf16[704,128]{1,0:T(8,128)(2,1)S(1)} %join.1.refs_0_.refs_1_.packed, bf16[704,128]{1,0:T(8,128)(2,1)S(1)} %join.1.refs_0_.refs_1_.packed), custom_call_target="tpu_custom_call" | custom-call | flops 1000000000 | bytes 1000000 | tf_op jit(solution)/shard_map/grid/pallas_call | solution.py:383
  16.3 2.4 %collective-permute-done.5.refs_1_.refs_3_ = bf16[704,128]{1,0:T(8,128)(2,1)S(1)} collective-permute-done((bf16[704,128]{1,0:T(8,128)(2,1)S(1)}, bf16[704,128]{1,0:T(8,128)(2,1)S(1)}, u32[]{:S(2)}, u32[]{:S(2)}) %collective-permute-start.5) | collective-permute-done | bytes 180256 | tf_op jit(solution)/shard_map/ppermute | solution.py:252
  18.7 2.2 %grid.4.refs_1_ = f32[8,256,128]{2,1,0:T(8,128)S(1)} custom-call(bf16[704,128]{1,0:T(8,128)(2,1)S(1)} %join.1.refs_0_.refs_1_.packed, bf16[704,128]{1,0:T(8,128)(2,1)S(1)} %collective-permute-done.5.refs_1_.refs_3_), custom_call_target="tpu_custom_call" | custom-call | flops 1000000000 | bytes 1000000 | tf_op jit(solution)/shard_map/grid/pallas_call | solution.py:383
  20.9 0.0 collective-permute-done.3.refs_1_
  21.0 0.0 collective-permute-done.4.refs_2_
  21.0 0.1 collective-permute-start.6
  21.1 3.2 %grid.5.refs_2_ = f32[8,256,128]{2,1,0:T(8,128)S(1)} custom-call(bf16[704,128]{1,0:T(8,128)(2,1)S(1)} %join.1.refs_0_.refs_1_.packed, bf16[704,128]{1,0:T(8,128)(2,1)S(1)} %collective-permute-done.3.refs_1_, bf16[704,128]{1,0:T(8,128)(2,1)S(1)} %collective-permute-done.4.refs_2_), custom_call_target="tpu_custom_call" | custom-call | flops 2000000000 | bytes 1000000 | tf_op jit(solution)/shard_map/grid/pallas_call | solution.py:383
  24.3 0.0 collective-permute-done.6.theirs
  24.4 1.1 %apply_tables.1 = (f32[64,256]{1,0:T(8,128)S(1)}, f32[64,256]{1,0:T(8,128)S(1)}) custom-call(bf16[704,128]{1,0:T(8,128)(2,1)S(1)} %join.1.refs_0_.refs_1_.packed, bf16[2048,128]{1,0:T(8,128)(2,1)S(1)} %collect.1.ours, bf16[2048,128]{1,0:T(8,128)(2,1)S(1)} %collective-permute-done.6.theirs, f32[8,256,128]{2,1,0:T(8,128)S(1)} %grid.3.refs_0_, ...), custom_call_target="tpu_custom_call" | custom-call | flops 1000000000 | bytes 2000000 | tf_op jit(solution)/shard_map/apply_tables/pallas_call | solution.py:411
  25.5 0.6 %collective-permute-start.7 = (f32[64,256]{1,0:T(8,128)S(1)}, f32[64,256]{1,0:T(8,128)S(1)}, u32[]{:S(2)}, u32[]{:S(2)}) collective-permute-start(f32[64,256]{1,0:T(8,128)S(1)} %get-tuple-element.30), channel_id=1, source_target_pairs={{0,1},{1,0},{2,3},{3,2},{4,5},{5,4},{6,7},{7,6},{8,9},{9,8},{10,11... | collective-permute-start | bytes 196616 | tf_op jit(solution)/shard_map/ppermute | solution.py:426
  26.0 0.9 %collective-permute-done.7 = f32[64,256]{1,0:T(8,128)S(1)} collective-permute-done((f32[64,256]{1,0:T(8,128)S(1)}, f32[64,256]{1,0:T(8,128)S(1)}, u32[]{:S(2)}, u32[]{:S(2)}) %collective-permute-start.7) | collective-permute-done | bytes 65568 | tf_op jit(solution)/shard_map/ppermute | solution.py:426
  27.0 0.7 %reshape.19 = f32[1,1,64,2,128]{4,3,2,1,0:T(2,128)} reshape(f32[64,256]{1,0:T(8,128)S(1)} %add.3) | data formatting | bytes 131072 | tf_op jit(solution)/shard_map/reshape | solution.py:427
  (3 shorter events, 0.1 us)
Async XLA Ops:
  1.1 9.8 %collective-permute-start = (bf16[304,128]{1,0:T(8,128)(2,1)S(1)}, bf16[304,128]{1,0:T(8,128)(2,1)S(1)}, u32[]{:S(2)}, u32[]{:S(2)}) collective-permute-start(bf16[304,128]{1,0:T(8,128)(2,1)S(1)} %get-tuple-element.20), channel_id=1, source_target_pairs={{0,2},{2,4},{4,6},{6,0},{1,3},{3,5},{5,7},{7,1},{8,10},{10,12},{12... | collective-permute-start | bytes 233480 | tf_op jit(solution)/shard_map/ppermute | solution.py:370
  4.1 4.4 %collective-permute-start.1 = (bf16[48,128]{1,0:T(8,128)(2,1)S(1)}, bf16[48,128]{1,0:T(8,128)(2,1)S(1)}, u32[]{:S(2)}, u32[]{:S(2)}) collective-permute-start(bf16[48,128]{1,0:T(8,128)(2,1)S(1)} %get-tuple-element.21), channel_id=1, source_target_pairs={{0,6},{2,0},{4,2},{6,4},{1,7},{3,1},{5,3},{7,5},{8,14},{10,8},{12,... | collective-permute-start | bytes 36872 | tf_op jit(solution)/shard_map/ppermute | solution.py:370
  6.2 4.6 %collective-permute-start.2 = (bf16[48,128]{1,0:T(8,128)(2,1)S(1)}, bf16[48,128]{1,0:T(8,128)(2,1)S(1)}, u32[]{:S(2)}, u32[]{:S(2)}) collective-permute-start(bf16[48,128]{1,0:T(8,128)(2,1)S(1)} %get-tuple-element.22), channel_id=1, source_target_pairs={{0,4},{2,6},{4,0},{6,2},{1,5},{3,7},{5,1},{7,3},{8,12},{10,14},{12... | collective-permute-start | bytes 36872 | tf_op jit(solution)/shard_map/ppermute | solution.py:370
  10.9 7.9 %collective-permute-start.5 = (bf16[704,128]{1,0:T(8,128)(2,1)S(1)}, bf16[704,128]{1,0:T(8,128)(2,1)S(1)}, u32[]{:S(2)}, u32[]{:S(2)}) collective-permute-start(bf16[704,128]{1,0:T(8,128)(2,1)S(1)} %join.1.refs_0_.refs_1_.packed), channel_id=1, source_target_pairs={{0,24},{8,16},{16,8},{24,0},{1,25},{9,17},{17,9},{25,1},{2,26},{10... | collective-permute-start | bytes 540680 | tf_op jit(solution)/shard_map/ppermute | solution.py:252
  13.5 7.4 %collective-permute-start.3 = (bf16[704,128]{1,0:T(8,128)(2,1)S(1)}, bf16[704,128]{1,0:T(8,128)(2,1)S(1)}, u32[]{:S(2)}, u32[]{:S(2)}) collective-permute-start(bf16[704,128]{1,0:T(8,128)(2,1)S(1)} %join.1.refs_0_.refs_1_.packed), channel_id=1, source_target_pairs={{0,8},{8,0},{16,24},{24,16},{1,9},{9,1},{17,25},{25,17},{2,10},{10... | collective-permute-start | bytes 540680 | tf_op jit(solution)/shard_map/ppermute | solution.py:252
  14.1 6.9 %collective-permute-start.4 = (bf16[704,128]{1,0:T(8,128)(2,1)S(1)}, bf16[704,128]{1,0:T(8,128)(2,1)S(1)}, u32[]{:S(2)}, u32[]{:S(2)}) collective-permute-start(bf16[704,128]{1,0:T(8,128)(2,1)S(1)} %join.1.refs_0_.refs_1_.packed), channel_id=1, source_target_pairs={{0,16},{8,24},{16,0},{24,8},{1,17},{9,25},{17,1},{25,9},{2,18},{10... | collective-permute-start | bytes 540680 | tf_op jit(solution)/shard_map/ppermute | solution.py:252
  21.0 3.3 %collective-permute-start.6 = (bf16[2048,128]{1,0:T(8,128)(2,1)S(1)}, bf16[2048,128]{1,0:T(8,128)(2,1)S(1)}, u32[]{:S(2)}, u32[]{:S(2)}) collective-permute-start(bf16[2048,128]{1,0:T(8,128)(2,1)S(1)} %collect.1.ours), channel_id=1, source_target_pairs={{0,1},{1,0},{2,3},{3,2},{4,5},{5,4},{6,7},{7,6},{8,9},{9,8},{10,11... | collective-permute-start | bytes 1572872 | tf_op jit(solution)/shard_map/ppermute | solution.py:409
  25.5 1.5 %collective-permute-start.7 = (f32[64,256]{1,0:T(8,128)S(1)}, f32[64,256]{1,0:T(8,128)S(1)}, u32[]{:S(2)}, u32[]{:S(2)}) collective-permute-start(f32[64,256]{1,0:T(8,128)S(1)} %get-tuple-element.30), channel_id=1, source_target_pairs={{0,1},{1,0},{2,3},{3,2},{4,5},{5,4},{6,7},{7,6},{8,9},{9,8},{10,11... | collective-permute-start | bytes 196616 | tf_op jit(solution)/shard_map/ppermute | solution.py:426

commit v14 on v13

--- a/solution.py
+++ b/solution.py
@@ -12,8 +12,7 @@
 CH = 8
 KERNEL_SPREAD = 1.5
 ALPHA = math.sqrt(math.log2(math.e) / (2.0 * KERNEL_SPREAD * KERNEL_SPREAD))
-UNROLL = 8
-REST = 2
+UNROLL = 4
 NT = (((1,), (1,)), ((), ()))
 VMEM = pl.BlockSpec(memory_space=pltpu.VMEM)
 HBM = pl.BlockSpec(memory_space=pltpu.HBM)
@@ -194,7 +193,7 @@
             code = meta_s[d, k]
             order[count] = code
             count = count + jnp.where(code >= 0, 1, 0)
-    for i in range(REST):
+    for i in range(UNROLL):
         order[count + i] = devices * cap * slots
 
     cells = ALPHA * lax.broadcasted_iota(jnp.int32, (SU, SU), 0).astype(jnp.float32)
@@ -223,17 +222,12 @@
         right = jnp.concatenate(rights, axis=1)
         return slot, lax.dot_general(left, right, NT, preferred_element_type=jnp.float32)
 
-    def steps(first, blocks, number):
-        def step(k, carry):
-            for slot, part in [one_block(first + k * blocks + i) for i in range(blocks)]:
-                grids[slot] += part
-            return carry
-
-        lax.fori_loop(0, number, step, 0)
-
-    whole = lax.div(count, UNROLL)
-    steps(0, UNROLL, whole)
-    steps(whole * UNROLL, REST, lax.div(lax.rem(count, UNROLL) + REST - 1, REST))
+    def step(k, carry):
+        for slot, part in [one_block(k * UNROLL + i) for i in range(UNROLL)]:
+            grids[slot] += part
+        return carry
+
+    lax.fori_loop(0, lax.div(count + UNROLL - 1, UNROLL), step, 0)
 
 
 def local(kernel, operands, shape, name):
@@ -272,14 +266,16 @@
         grid_real, grid_imag = (
             sum(ref[s, part * SU : (part + 1) * SU, :] for ref in grids) for part in range(2)
         )
-        inner = jnp.concatenate(
-            [
-                jnp.concatenate([grid_real, grid_imag], axis=1),
-                jnp.concatenate([-grid_imag, grid_real], axis=1),
-            ],
-            axis=0,
-        )
-        high, low = split_bf16(inner)
+        high, low = (
+            jnp.concatenate(
+                [
+                    jnp.concatenate([real, imag], axis=1),
+                    jnp.concatenate([-imag, real], axis=1),
+                ],
+                axis=0,
+            )
+            for real, imag in zip(split_bf16(grid_real), split_bf16(grid_imag))
+        )
         half = jnp.dot(u_side, high, preferred_element_type=jnp.float32) + jnp.dot(
             u_side, low, preferred_element_type=jnp.float32
         )
@@ -388,7 +384,7 @@
             scratch_shapes=[
                 pltpu.VMEM((len(some) * groups, SU), jnp.int32),
                 pltpu.SMEM((len(some) * groups, SU), jnp.int32),
-                pltpu.SMEM((lines + REST,), jnp.int32),
+                pltpu.SMEM((lines + UNROLL,), jnp.int32),
             ]
             + [pltpu.VMEM((lines * chans + 8, SU), jnp.float32)] * 4
             + [pltpu.SemaphoreType.DMA],

time: 27.4 us -> 28 us (1.022); the launches traced: 27.6 us -> 27.8 us
  Pallas kernels: 9.56 us -> 10.5 us
  waiting for transfers between devices: 7 us -> 6.3 us
    pallas_call x3, Pallas kernels: 7.32 us -> 8.23 us  [grid(): pl.pallas_call(functools.partial(grid_kernel, (facets, groups, chans, cap...]
    ppermute x3, waiting for transfers between devices: 2.45 us -> 1.75 us  [exchange(): lax.ppermute(value, axis, [(n, n ^ shift) for n in range(lax.axis_size(ax...]
  transfers between devices with their start and end apart: 8 -> 8, of which waited for: 4 -> 4; matrix products, arithmetic and copies ran while one was open for 0% -> 0% of each run, Pallas kernels for 27% -> 30%
where the time goes in v14:
time: 28 us; the launch traced here: 27.8 us
  Pallas kernels  10.5 us (38%)
  starting transfers between devices  10.3 us (37%)
  waiting for transfers between devices  6.3 us (22%)
  local copies, waits for them, and re-layouts  0.66 us (2%)
    pallas_call x3, Pallas kernels, grid(): pl.pallas_call(functools.partial(grid_kernel, (facets, groups, chans, cap...  8.23 us
    ppermute x3, starting transfers between devices, body(): lax.ppermute(pieces[shift], 'bl', [(g, (g + shift) % groups) for g in ran...  6.11 us
    ppermute x3, waiting for transfers between devices, body(): lax.ppermute(pieces[shift], 'bl', [(g, (g + shift) % groups) for g in ran...  3.65 us
    ppermute x3, starting transfers between devices, exchange(): lax.ppermute(value, axis, [(n, n ^ shift) for n in range(lax.axis_size(ax...  3.55 us
    ppermute x3, waiting for transfers between devices, exchange(): lax.ppermute(value, axis, [(n, n ^ shift) for n in range(lax.axis_size(ax...  1.75 us
    pallas_call x1, Pallas kernels, body(): pl.pallas_call(functools.partial(table_kernel, (slots, meta_row), norm),...  1.12 us
    pallas_call x1, Pallas kernels, body(): pl.pallas_call(functools.partial(sort_kernel, (groups, held, chans, cap,...  1.06 us
    ppermute x1, waiting for transfers between devices, body(): lax.ppermute(other, 'chan', [(c, 1 - c) for c in range(chan_count)])  0.9 us
  transfers between devices with their start and end apart: 8, of which 4 were waited for; matrix products, arithmetic and copies ran while one was open for 0% of the time, Pallas kernels for 30%

profile of v14, /device:TPU:0, one launch (start us, length us, event | category | flops | bytes accessed | tf_op | source)
XLA Modules:
  0.0 27.8 jit_solution(17107386093953882956)
XLA Ops:
  0.0 1.1 %sort_blocks.1 = (bf16[48,128]{1,0:T(8,128)(2,1)S(1)}, bf16[304,128]{1,0:T(8,128)(2,1)S(1)}, bf16[48,128]{1,0:T(8,128)(2,1)S(1)}, bf16[48,128]{1,0:T(8,128)(2,1)S(1)}, bf16[256,128]{1,0:T(8,128)(2,1)S(1)}) custom-call(s32[1,8]{1,0:T(1,128)} %bitcast.12, s32[1,8]{1,0:T(1,128)} %bitcast.13, bf16[64,128]{1,0:T(8,128)(2,1)} %bitcast.8, bf16[16,128]{1,0:T(8,128)(2,1)} %bitcast.9, ...), custom_call_target="tpu_custom_call" | custom-call | flops 100000 | bytes 100000 | tf_op jit(solution)/shard_map/sort_blocks/pallas_call | solution.py:324
  1.1 3.1 %collective-permute-start = (bf16[304,128]{1,0:T(8,128)(2,1)S(1)}, bf16[304,128]{1,0:T(8,128)(2,1)S(1)}, u32[]{:S(2)}, u32[]{:S(2)}) collective-permute-start(bf16[304,128]{1,0:T(8,128)(2,1)S(1)} %get-tuple-element.20), channel_id=1, source_target_pairs={{0,2},{2,4},{4,6},{6,0},{1,3},{3,5},{5,7},{7,1},{8,10},{10,12},{12... | collective-permute-start | bytes 233480 | tf_op jit(solution)/shard_map/ppermute | solution.py:366
  4.1 2.1 %collective-permute-start.1 = (bf16[48,128]{1,0:T(8,128)(2,1)S(1)}, bf16[48,128]{1,0:T(8,128)(2,1)S(1)}, u32[]{:S(2)}, u32[]{:S(2)}) collective-permute-start(bf16[48,128]{1,0:T(8,128)(2,1)S(1)} %get-tuple-element.21), channel_id=1, source_target_pairs={{0,6},{2,0},{4,2},{6,4},{1,7},{3,1},{5,3},{7,5},{8,14},{10,8},{12,... | collective-permute-start | bytes 36872 | tf_op jit(solution)/shard_map/ppermute | solution.py:366
  6.2 0.9 %collective-permute-start.2 = (bf16[48,128]{1,0:T(8,128)(2,1)S(1)}, bf16[48,128]{1,0:T(8,128)(2,1)S(1)}, u32[]{:S(2)}, u32[]{:S(2)}) collective-permute-start(bf16[48,128]{1,0:T(8,128)(2,1)S(1)} %get-tuple-element.22), channel_id=1, source_target_pairs={{0,4},{2,6},{4,0},{6,2},{1,5},{3,7},{5,1},{7,3},{8,12},{10,14},{12... | collective-permute-start | bytes 36872 | tf_op jit(solution)/shard_map/ppermute | solution.py:366
  7.2 1.4 %collective-permute-done.1.refs_2_ = bf16[48,128]{1,0:T(8,128)(2,1)S(1)} collective-permute-done((bf16[48,128]{1,0:T(8,128)(2,1)S(1)}, bf16[48,128]{1,0:T(8,128)(2,1)S(1)}, u32[]{:S(2)}, u32[]{:S(2)}) %collective-permute-start.1) | collective-permute-done | bytes 12320 | tf_op jit(solution)/shard_map/ppermute | solution.py:366
  8.6 2.3 %collective-permute-done.2.refs_3_ = bf16[48,128]{1,0:T(8,128)(2,1)S(1)} collective-permute-done((bf16[48,128]{1,0:T(8,128)(2,1)S(1)}, bf16[48,128]{1,0:T(8,128)(2,1)S(1)}, u32[]{:S(2)}, u32[]{:S(2)}) %collective-permute-start.2) | collective-permute-done | bytes 12320 | tf_op jit(solution)/shard_map/ppermute | solution.py:366
  10.8 0.0 collective-permute-done.refs_1_
  10.9 2.7 %collective-permute-start.5 = (bf16[704,128]{1,0:T(8,128)(2,1)S(1)}, bf16[704,128]{1,0:T(8,128)(2,1)S(1)}, u32[]{:S(2)}, u32[]{:S(2)}) collective-permute-start(bf16[704,128]{1,0:T(8,128)(2,1)S(1)} %join.1.refs_0_.refs_1_.packed), channel_id=1, source_target_pairs={{0,24},{8,16},{16,8},{24,0},{1,25},{9,17},{17,9},{25,1},{2,26},{10... | collective-permute-start | bytes 540680 | tf_op jit(solution)/shard_map/ppermute | solution.py:246
  13.5 0.5 %collective-permute-start.3 = (bf16[704,128]{1,0:T(8,128)(2,1)S(1)}, bf16[704,128]{1,0:T(8,128)(2,1)S(1)}, u32[]{:S(2)}, u32[]{:S(2)}) collective-permute-start(bf16[704,128]{1,0:T(8,128)(2,1)S(1)} %join.1.refs_0_.refs_1_.packed), channel_id=1, source_target_pairs={{0,8},{8,0},{16,24},{24,16},{1,9},{9,1},{17,25},{25,17},{2,10},{10... | collective-permute-start | bytes 540680 | tf_op jit(solution)/shard_map/ppermute | solution.py:246
  14.1 0.3 %collective-permute-start.4 = (bf16[704,128]{1,0:T(8,128)(2,1)S(1)}, bf16[704,128]{1,0:T(8,128)(2,1)S(1)}, u32[]{:S(2)}, u32[]{:S(2)}) collective-permute-start(bf16[704,128]{1,0:T(8,128)(2,1)S(1)} %join.1.refs_0_.refs_1_.packed), channel_id=1, source_target_pairs={{0,16},{8,24},{16,0},{24,8},{1,17},{9,25},{17,1},{25,9},{2,18},{10... | collective-permute-start | bytes 540680 | tf_op jit(solution)/shard_map/ppermute | solution.py:246
  14.4 2.6 %grid.3.refs_0_ = f32[8,256,128]{2,1,0:T(8,128)S(1)} custom-call(bf16[704,128]{1,0:T(8,128)(2,1)S(1)} %join.1.refs_0_.refs_1_.packed, bf16[704,128]{1,0:T(8,128)(2,1)S(1)} %join.1.refs_0_.refs_1_.packed), custom_call_target="tpu_custom_call" | custom-call | flops 1000000000 | bytes 1000000 | tf_op jit(solution)/shard_map/grid/pallas_call | solution.py:379
  17.0 1.7 %collective-permute-done.5.refs_1_.refs_3_ = bf16[704,128]{1,0:T(8,128)(2,1)S(1)} collective-permute-done((bf16[704,128]{1,0:T(8,128)(2,1)S(1)}, bf16[704,128]{1,0:T(8,128)(2,1)S(1)}, u32[]{:S(2)}, u32[]{:S(2)}) %collective-permute-start.5) | collective-permute-done | bytes 180256 | tf_op jit(solution)/shard_map/ppermute | solution.py:246
  18.7 2.0 %grid.4.refs_1_ = f32[8,256,128]{2,1,0:T(8,128)S(1)} custom-call(bf16[704,128]{1,0:T(8,128)(2,1)S(1)} %join.1.refs_0_.refs_1_.packed, bf16[704,128]{1,0:T(8,128)(2,1)S(1)} %collective-permute-done.5.refs_1_.refs_3_), custom_call_target="tpu_custom_call" | custom-call | flops 1000000000 | bytes 1000000 | tf_op jit(solution)/shard_map/grid/pallas_call | solution.py:379
  20.7 0.0 collective-permute-done.3.refs_1_
  20.7 0.0 collective-permute-done.4.refs_2_
  20.8 0.1 collective-permute-start.6
  20.8 3.7 %grid.5.refs_2_ = f32[8,256,128]{2,1,0:T(8,128)S(1)} custom-call(bf16[704,128]{1,0:T(8,128)(2,1)S(1)} %join.1.refs_0_.refs_1_.packed, bf16[704,128]{1,0:T(8,128)(2,1)S(1)} %collective-permute-done.3.refs_1_, bf16[704,128]{1,0:T(8,128)(2,1)S(1)} %collective-permute-done.4.refs_2_), custom_call_target="tpu_custom_call" | custom-call | flops 2000000000 | bytes 1000000 | tf_op jit(solution)/shard_map/grid/pallas_call | solution.py:379
  24.5 0.0 collective-permute-done.6.theirs
  24.6 1.1 %apply_tables.1 = (f32[64,256]{1,0:T(8,128)S(1)}, f32[64,256]{1,0:T(8,128)S(1)}) custom-call(bf16[704,128]{1,0:T(8,128)(2,1)S(1)} %join.1.refs_0_.refs_1_.packed, bf16[2048,128]{1,0:T(8,128)(2,1)S(1)} %collect.1.ours, bf16[2048,128]{1,0:T(8,128)(2,1)S(1)} %collective-permute-done.6.theirs, f32[8,256,128]{2,1,0:T(8,128)S(1)} %grid.3.refs_0_, ...), custom_call_target="tpu_custom_call" | custom-call | flops 1000000000 | bytes 2000000 | tf_op jit(solution)/shard_map/apply_tables/pallas_call | solution.py:407
  25.7 0.6 %collective-permute-start.7 = (f32[64,256]{1,0:T(8,128)S(1)}, f32[64,256]{1,0:T(8,128)S(1)}, u32[]{:S(2)}, u32[]{:S(2)}) collective-permute-start(f32[64,256]{1,0:T(8,128)S(1)} %get-tuple-element.30), channel_id=1, source_target_pairs={{0,1},{1,0},{2,3},{3,2},{4,5},{5,4},{6,7},{7,6},{8,9},{9,8},{10,11... | collective-permute-start | bytes 196616 | tf_op jit(solution)/shard_map/ppermute | solution.py:422
  26.2 0.9 %collective-permute-done.7 = f32[64,256]{1,0:T(8,128)S(1)} collective-permute-done((f32[64,256]{1,0:T(8,128)S(1)}, f32[64,256]{1,0:T(8,128)S(1)}, u32[]{:S(2)}, u32[]{:S(2)}) %collective-permute-start.7) | collective-permute-done | bytes 65568 | tf_op jit(solution)/shard_map/ppermute | solution.py:422
  27.2 0.7 %reshape.19 = f32[1,1,64,2,128]{4,3,2,1,0:T(2,128)} reshape(f32[64,256]{1,0:T(8,128)S(1)} %add.3) | data formatting | bytes 131072 | tf_op jit(solution)/shard_map/reshape | solution.py:423
  (3 shorter events, 0.1 us)
Async XLA Ops:
  1.1 9.8 %collective-permute-start = (bf16[304,128]{1,0:T(8,128)(2,1)S(1)}, bf16[304,128]{1,0:T(8,128)(2,1)S(1)}, u32[]{:S(2)}, u32[]{:S(2)}) collective-permute-start(bf16[304,128]{1,0:T(8,128)(2,1)S(1)} %get-tuple-element.20), channel_id=1, source_target_pairs={{0,2},{2,4},{4,6},{6,0},{1,3},{3,5},{5,7},{7,1},{8,10},{10,12},{12... | collective-permute-start | bytes 233480 | tf_op jit(solution)/shard_map/ppermute | solution.py:366
  4.1 4.4 %collective-permute-start.1 = (bf16[48,128]{1,0:T(8,128)(2,1)S(1)}, bf16[48,128]{1,0:T(8,128)(2,1)S(1)}, u32[]{:S(2)}, u32[]{:S(2)}) collective-permute-start(bf16[48,128]{1,0:T(8,128)(2,1)S(1)} %get-tuple-element.21), channel_id=1, source_target_pairs={{0,6},{2,0},{4,2},{6,4},{1,7},{3,1},{5,3},{7,5},{8,14},{10,8},{12,... | collective-permute-start | bytes 36872 | tf_op jit(solution)/shard_map/ppermute | solution.py:366
  6.2 4.6 %collective-permute-start.2 = (bf16[48,128]{1,0:T(8,128)(2,1)S(1)}, bf16[48,128]{1,0:T(8,128)(2,1)S(1)}, u32[]{:S(2)}, u32[]{:S(2)}) collective-permute-start(bf16[48,128]{1,0:T(8,128)(2,1)S(1)} %get-tuple-element.22), channel_id=1, source_target_pairs={{0,4},{2,6},{4,0},{6,2},{1,5},{3,7},{5,1},{7,3},{8,12},{10,14},{12... | collective-permute-start | bytes 36872 | tf_op jit(solution)/shard_map/ppermute | solution.py:366
  10.9 7.9 %collective-permute-start.5 = (bf16[704,128]{1,0:T(8,128)(2,1)S(1)}, bf16[704,128]{1,0:T(8,128)(2,1)S(1)}, u32[]{:S(2)}, u32[]{:S(2)}) collective-permute-start(bf16[704,128]{1,0:T(8,128)(2,1)S(1)} %join.1.refs_0_.refs_1_.packed), channel_id=1, source_target_pairs={{0,24},{8,16},{16,8},{24,0},{1,25},{9,17},{17,9},{25,1},{2,26},{10... | collective-permute-start | bytes 540680 | tf_op jit(solution)/shard_map/ppermute | solution.py:246
  13.5 7.2 %collective-permute-start.3 = (bf16[704,128]{1,0:T(8,128)(2,1)S(1)}, bf16[704,128]{1,0:T(8,128)(2,1)S(1)}, u32[]{:S(2)}, u32[]{:S(2)}) collective-permute-start(bf16[704,128]{1,0:T(8,128)(2,1)S(1)} %join.1.refs_0_.refs_1_.packed), channel_id=1, source_target_pairs={{0,8},{8,0},{16,24},{24,16},{1,9},{9,1},{17,25},{25,17},{2,10},{10... | collective-permute-start | bytes 540680 | tf_op jit(solution)/shard_map/ppermute | solution.py:246
  14.1 6.6 %collective-permute-start.4 = (bf16[704,128]{1,0:T(8,128)(2,1)S(1)}, bf16[704,128]{1,0:T(8,128)(2,1)S(1)}, u32[]{:S(2)}, u32[]{:S(2)}) collective-permute-start(bf16[704,128]{1,0:T(8,128)(2,1)S(1)} %join.1.refs_0_.refs_1_.packed), channel_id=1, source_target_pairs={{0,16},{8,24},{16,0},{24,8},{1,17},{9,25},{17,1},{25,9},{2,18},{10... | collective-permute-start | bytes 540680 | tf_op jit(solution)/shard_map/ppermute | solution.py:246
  20.8 3.8 %collective-permute-start.6 = (bf16[2048,128]{1,0:T(8,128)(2,1)S(1)}, bf16[2048,128]{1,0:T(8,128)(2,1)S(1)}, u32[]{:S(2)}, u32[]{:S(2)}) collective-permute-start(bf16[2048,128]{1,0:T(8,128)(2,1)S(1)} %collect.1.ours), channel_id=1, source_target_pairs={{0,1},{1,0},{2,3},{3,2},{4,5},{5,4},{6,7},{7,6},{8,9},{9,8},{10,11... | collective-permute-start | bytes 1572872 | tf_op jit(solution)/shard_map/ppermute | solution.py:405
  25.7 1.5 %collective-permute-start.7 = (f32[64,256]{1,0:T(8,128)S(1)}, f32[64,256]{1,0:T(8,128)S(1)}, u32[]{:S(2)}, u32[]{:S(2)}) collective-permute-start(f32[64,256]{1,0:T(8,128)S(1)} %get-tuple-element.30), channel_id=1, source_target_pairs={{0,1},{1,0},{2,3},{3,2},{4,5},{5,4},{6,7},{7,6},{8,9},{9,8},{10,11... | collective-permute-start | bytes 196616 | tf_op jit(solution)/shard_map/ppermute | solution.py:422

commit v15 on v14

--- a/solution.py
+++ b/solution.py
@@ -128,7 +128,7 @@
 def grid_kernel(sizes, *refs):
     facets, groups, chans, cap, rows, count_here = sizes
     own_ref, grids = refs[0], refs[1 + count_here]
-    meta_v, meta_s, order, spots_u, spots_v, turns_real, turns_imag, sem = refs[2 + count_here :]
+    order, spots_u, spots_v, turns_real, turns_imag = refs[2 + count_here :]
     pieces = [
         ref.at[pl.ds(n * rows, rows)] for ref in refs[1 : 1 + count_here] for n in range(groups)
     ]
@@ -144,14 +144,13 @@
     lane = lax.broadcasted_iota(jnp.int32, (1, SU), 1)
     own = own_ref[tail : tail + 16, :].astype(jnp.float32)
     numbers = own[meta_row - tail + 1 : meta_row - tail + 2]
+    codes = []
     for d in range(devices):
         meta = pieces[d][tail : tail + 16, :].astype(jnp.float32)
         plane = meta[meta_row - tail : meta_row - tail + 1].astype(jnp.int32) - 1
         set_id = jnp.where(lax.rem(plane, groups) == group, 0, 1)
         code = (d * cap + lane) * slots + 2 * (lax.div(plane, groups) ^ facet) + set_id
-        meta_v[d : d + 1, :] = jnp.where(plane >= 0, code, -1)
-    copy = pltpu.make_async_copy(meta_v, meta_s, sem)
-    copy.start()
+        codes.append(jnp.where(plane >= 0, code, -1))
     grids[...] = jnp.zeros_like(grids)
 
     def number(n):
@@ -185,12 +184,11 @@
     last = devices * lines
     for ref in (spots_u, spots_v, turns_real, turns_imag):
         ref[last : last + 8, :] = jnp.zeros((8, SU), jnp.float32)
-    copy.wait()
 
     count = jnp.int32(0)
     for d in range(devices):
         for k in range(cap):
-            code = meta_s[d, k]
+            code = codes[d][0, k]
             order[count] = code
             count = count + jnp.where(code >= 0, 1, 0)
     for i in range(UNROLL):
@@ -200,7 +198,7 @@
 
     def profile(spot):
         apart = spot - cells
-        return jnp.exp2(-(apart * apart)).astype(jnp.bfloat16)
+        return jnp.exp2(-((apart * apart).astype(jnp.bfloat16)))
 
     def tiled(row):
         return jnp.broadcast_to(row, (16, SU)).astype(jnp.bfloat16)[None]
@@ -382,12 +380,9 @@
             in_specs=[VMEM] * (1 + len(some)),
             out_specs=VMEM,
             scratch_shapes=[
-                pltpu.VMEM((len(some) * groups, SU), jnp.int32),
-                pltpu.SMEM((len(some) * groups, SU), jnp.int32),
                 pltpu.SMEM((lines + UNROLL,), jnp.int32),
             ]
-            + [pltpu.VMEM((lines * chans + 8, SU), jnp.float32)] * 4
-            + [pltpu.SemaphoreType.DMA],
+            + [pltpu.VMEM((lines * chans + 8, SU), jnp.float32)] * 4,
             compiler_params=PARAMS,
             cost_estimate=pl.CostEstimate(
                 flops=len(some) * 1_000_000_000,

time: 28 us -> 26.6 us (0.950)
  Pallas kernels: 10.5 us -> 7.73 us
  waiting for transfers between devices: 6.3 us -> 7.65 us
    pallas_call x3, Pallas kernels: 8.23 us -> 5.51 us  [grid(): pl.pallas_call(functools.partial(grid_kernel, (facets, groups, chans, cap...]
    ppermute x3, waiting for transfers between devices: 1.75 us -> 3.1 us  [exchange(): lax.ppermute(value, axis, [(n, n ^ shift) for n in range(lax.axis_size(ax...]
  transfers between devices with their start and end apart: 8 -> 8, of which waited for: 4 -> 5; matrix products, arithmetic and copies ran while one was open for 0% -> 0% of each run, Pallas kernels for 30% -> 21%
where the time goes in v15:
time: 26.6 us; the launch traced here: 26.4 us
  starting transfers between devices  10.3 us (39%)
  Pallas kernels  7.73 us (29%)
  waiting for transfers between devices  7.65 us (29%)
  local copies, waits for them, and re-layouts  0.66 us (2%)
    ppermute x3, starting transfers between devices, body(): lax.ppermute(pieces[shift], 'bl', [(g, (g + shift) % groups) for g in ran...  6.12 us
    pallas_call x3, Pallas kernels, grid(): pl.pallas_call(functools.partial(grid_kernel, (facets, groups, chans, cap...  5.51 us
    ppermute x3, waiting for transfers between devices, body(): lax.ppermute(pieces[shift], 'bl', [(g, (g + shift) % groups) for g in ran...  3.64 us
    ppermute x3, starting transfers between devices, exchange(): lax.ppermute(value, axis, [(n, n ^ shift) for n in range(lax.axis_size(ax...  3.55 us
    ppermute x3, waiting for transfers between devices, exchange(): lax.ppermute(value, axis, [(n, n ^ shift) for n in range(lax.axis_size(ax...  3.1 us
    pallas_call x1, Pallas kernels, body(): pl.pallas_call(functools.partial(table_kernel, (slots, meta_row), norm),...  1.12 us
    pallas_call x1, Pallas kernels, body(): pl.pallas_call(functools.partial(sort_kernel, (groups, held, chans, cap,...  1.06 us
    ppermute x1, waiting for transfers between devices, body(): lax.ppermute(other, 'chan', [(c, 1 - c) for c in range(chan_count)])  0.9 us
  transfers between devices with their start and end apart: 8, of which 5 were waited for; matrix products, arithmetic and copies ran while one was open for 0% of the time, Pallas kernels for 21%

profile of v15, /device:TPU:0, one launch (start us, length us, event | category | flops | bytes accessed | tf_op | source)
XLA Modules:
  0.0 26.4 jit_solution(15258318460684427259)
XLA Ops:
  0.0 1.1 %sort_blocks.1 = (bf16[48,128]{1,0:T(8,128)(2,1)S(1)}, bf16[304,128]{1,0:T(8,128)(2,1)S(1)}, bf16[48,128]{1,0:T(8,128)(2,1)S(1)}, bf16[48,128]{1,0:T(8,128)(2,1)S(1)}, bf16[256,128]{1,0:T(8,128)(2,1)S(1)}) custom-call(s32[1,8]{1,0:T(1,128)} %bitcast.12, s32[1,8]{1,0:T(1,128)} %bitcast.13, bf16[64,128]{1,0:T(8,128)(2,1)} %bitcast.8, bf16[16,128]{1,0:T(8,128)(2,1)} %bitcast.9, ...), custom_call_target="tpu_custom_call" | custom-call | flops 100000 | bytes 100000 | tf_op jit(solution)/shard_map/sort_blocks/pallas_call | solution.py:322
  1.1 3.1 %collective-permute-start = (bf16[304,128]{1,0:T(8,128)(2,1)S(1)}, bf16[304,128]{1,0:T(8,128)(2,1)S(1)}, u32[]{:S(2)}, u32[]{:S(2)}) collective-permute-start(bf16[304,128]{1,0:T(8,128)(2,1)S(1)} %get-tuple-element.20), channel_id=1, source_target_pairs={{0,2},{2,4},{4,6},{6,0},{1,3},{3,5},{5,7},{7,1},{8,10},{10,12},{12... | collective-permute-start | bytes 233480 | tf_op jit(solution)/shard_map/ppermute | solution.py:364
  4.1 2.1 %collective-permute-start.1 = (bf16[48,128]{1,0:T(8,128)(2,1)S(1)}, bf16[48,128]{1,0:T(8,128)(2,1)S(1)}, u32[]{:S(2)}, u32[]{:S(2)}) collective-permute-start(bf16[48,128]{1,0:T(8,128)(2,1)S(1)} %get-tuple-element.21), channel_id=1, source_target_pairs={{0,6},{2,0},{4,2},{6,4},{1,7},{3,1},{5,3},{7,5},{8,14},{10,8},{12,... | collective-permute-start | bytes 36872 | tf_op jit(solution)/shard_map/ppermute | solution.py:364
  6.2 1.0 %collective-permute-start.2 = (bf16[48,128]{1,0:T(8,128)(2,1)S(1)}, bf16[48,128]{1,0:T(8,128)(2,1)S(1)}, u32[]{:S(2)}, u32[]{:S(2)}) collective-permute-start(bf16[48,128]{1,0:T(8,128)(2,1)S(1)} %get-tuple-element.22), channel_id=1, source_target_pairs={{0,4},{2,6},{4,0},{6,2},{1,5},{3,7},{5,1},{7,3},{8,12},{10,14},{12... | collective-permute-start | bytes 36872 | tf_op jit(solution)/shard_map/ppermute | solution.py:364
  7.2 1.4 %collective-permute-done.1.refs_2_ = bf16[48,128]{1,0:T(8,128)(2,1)S(1)} collective-permute-done((bf16[48,128]{1,0:T(8,128)(2,1)S(1)}, bf16[48,128]{1,0:T(8,128)(2,1)S(1)}, u32[]{:S(2)}, u32[]{:S(2)}) %collective-permute-start.1) | collective-permute-done | bytes 12320 | tf_op jit(solution)/shard_map/ppermute | solution.py:364
  8.6 2.3 %collective-permute-done.2.refs_3_ = bf16[48,128]{1,0:T(8,128)(2,1)S(1)} collective-permute-done((bf16[48,128]{1,0:T(8,128)(2,1)S(1)}, bf16[48,128]{1,0:T(8,128)(2,1)S(1)}, u32[]{:S(2)}, u32[]{:S(2)}) %collective-permute-start.2) | collective-permute-done | bytes 12320 | tf_op jit(solution)/shard_map/ppermute | solution.py:364
  10.8 0.0 collective-permute-done.refs_1_
  10.8 2.7 %collective-permute-start.5 = (bf16[704,128]{1,0:T(8,128)(2,1)S(1)}, bf16[704,128]{1,0:T(8,128)(2,1)S(1)}, u32[]{:S(2)}, u32[]{:S(2)}) collective-permute-start(bf16[704,128]{1,0:T(8,128)(2,1)S(1)} %join.1.refs_0_.refs_1_.packed), channel_id=1, source_target_pairs={{0,24},{8,16},{16,8},{24,0},{1,25},{9,17},{17,9},{25,1},{2,26},{10... | collective-permute-start | bytes 540680 | tf_op jit(solution)/shard_map/ppermute | solution.py:244
  13.5 0.5 %collective-permute-start.3 = (bf16[704,128]{1,0:T(8,128)(2,1)S(1)}, bf16[704,128]{1,0:T(8,128)(2,1)S(1)}, u32[]{:S(2)}, u32[]{:S(2)}) collective-permute-start(bf16[704,128]{1,0:T(8,128)(2,1)S(1)} %join.1.refs_0_.refs_1_.packed), channel_id=1, source_target_pairs={{0,8},{8,0},{16,24},{24,16},{1,9},{9,1},{17,25},{25,17},{2,10},{10... | collective-permute-start | bytes 540680 | tf_op jit(solution)/shard_map/ppermute | solution.py:244
  14.1 0.4 %collective-permute-start.4 = (bf16[704,128]{1,0:T(8,128)(2,1)S(1)}, bf16[704,128]{1,0:T(8,128)(2,1)S(1)}, u32[]{:S(2)}, u32[]{:S(2)}) collective-permute-start(bf16[704,128]{1,0:T(8,128)(2,1)S(1)} %join.1.refs_0_.refs_1_.packed), channel_id=1, source_target_pairs={{0,16},{8,24},{16,0},{24,8},{1,17},{9,25},{17,1},{25,9},{2,18},{10... | collective-permute-start | bytes 540680 | tf_op jit(solution)/shard_map/ppermute | solution.py:244
  14.4 1.8 %grid.3.refs_0_ = f32[8,256,128]{2,1,0:T(8,128)S(1)} custom-call(bf16[704,128]{1,0:T(8,128)(2,1)S(1)} %join.1.refs_0_.refs_1_.packed, bf16[704,128]{1,0:T(8,128)(2,1)S(1)} %join.1.refs_0_.refs_1_.packed), custom_call_target="tpu_custom_call" | custom-call | flops 1000000000 | bytes 1000000 | tf_op jit(solution)/shard_map/grid/pallas_call | solution.py:377
  16.2 2.5 %collective-permute-done.5.refs_1_.refs_3_ = bf16[704,128]{1,0:T(8,128)(2,1)S(1)} collective-permute-done((bf16[704,128]{1,0:T(8,128)(2,1)S(1)}, bf16[704,128]{1,0:T(8,128)(2,1)S(1)}, u32[]{:S(2)}, u32[]{:S(2)}) %collective-permute-start.5) | collective-permute-done | bytes 180256 | tf_op jit(solution)/shard_map/ppermute | solution.py:244
  18.7 1.3 %grid.4.refs_1_ = f32[8,256,128]{2,1,0:T(8,128)S(1)} custom-call(bf16[704,128]{1,0:T(8,128)(2,1)S(1)} %join.1.refs_0_.refs_1_.packed, bf16[704,128]{1,0:T(8,128)(2,1)S(1)} %collective-permute-done.5.refs_1_.refs_3_), custom_call_target="tpu_custom_call" | custom-call | flops 1000000000 | bytes 1000000 | tf_op jit(solution)/shard_map/grid/pallas_call | solution.py:377
  20.0 0.6 %collective-permute-done.3.refs_1_ = bf16[704,128]{1,0:T(8,128)(2,1)S(1)} collective-permute-done((bf16[704,128]{1,0:T(8,128)(2,1)S(1)}, bf16[704,128]{1,0:T(8,128)(2,1)S(1)}, u32[]{:S(2)}, u32[]{:S(2)}) %collective-permute-start.3) | collective-permute-done | bytes 180256 | tf_op jit(solution)/shard_map/ppermute | solution.py:244
  20.6 0.0 collective-permute-done.4.refs_2_
  20.6 0.1 collective-permute-start.6
  20.7 2.4 %grid.5.refs_2_ = f32[8,256,128]{2,1,0:T(8,128)S(1)} custom-call(bf16[704,128]{1,0:T(8,128)(2,1)S(1)} %join.1.refs_0_.refs_1_.packed, bf16[704,128]{1,0:T(8,128)(2,1)S(1)} %collective-permute-done.3.refs_1_, bf16[704,128]{1,0:T(8,128)(2,1)S(1)} %collective-permute-done.4.refs_2_), custom_call_target="tpu_custom_call" | custom-call | flops 2000000000 | bytes 1000000 | tf_op jit(solution)/shard_map/grid/pallas_call | solution.py:377
  23.2 0.0 collective-permute-done.6.theirs
  23.2 1.1 %apply_tables.1 = (f32[64,256]{1,0:T(8,128)S(1)}, f32[64,256]{1,0:T(8,128)S(1)}) custom-call(bf16[704,128]{1,0:T(8,128)(2,1)S(1)} %join.1.refs_0_.refs_1_.packed, bf16[2048,128]{1,0:T(8,128)(2,1)S(1)} %collect.1.ours, bf16[2048,128]{1,0:T(8,128)(2,1)S(1)} %collective-permute-done.6.theirs, f32[8,256,128]{2,1,0:T(8,128)S(1)} %grid.3.refs_0_, ...), custom_call_target="tpu_custom_call" | custom-call | flops 1000000000 | bytes 2000000 | tf_op jit(solution)/shard_map/apply_tables/pallas_call | solution.py:402
  24.3 0.6 %collective-permute-start.7 = (f32[64,256]{1,0:T(8,128)S(1)}, f32[64,256]{1,0:T(8,128)S(1)}, u32[]{:S(2)}, u32[]{:S(2)}) collective-permute-start(f32[64,256]{1,0:T(8,128)S(1)} %get-tuple-element.30), channel_id=1, source_target_pairs={{0,1},{1,0},{2,3},{3,2},{4,5},{5,4},{6,7},{7,6},{8,9},{9,8},{10,11... | collective-permute-start | bytes 196616 | tf_op jit(solution)/shard_map/ppermute | solution.py:417
  24.8 0.9 %collective-permute-done.7 = f32[64,256]{1,0:T(8,128)S(1)} collective-permute-done((f32[64,256]{1,0:T(8,128)S(1)}, f32[64,256]{1,0:T(8,128)S(1)}, u32[]{:S(2)}, u32[]{:S(2)}) %collective-permute-start.7) | collective-permute-done | bytes 65568 | tf_op jit(solution)/shard_map/ppermute | solution.py:417
  25.8 0.7 %reshape.19 = f32[1,1,64,2,128]{4,3,2,1,0:T(2,128)} reshape(f32[64,256]{1,0:T(8,128)S(1)} %add.3) | data formatting | bytes 131072 | tf_op jit(solution)/shard_map/reshape | solution.py:418
  (3 shorter events, 0.1 us)
Async XLA Ops:
  1.1 9.8 %collective-permute-start = (bf16[304,128]{1,0:T(8,128)(2,1)S(1)}, bf16[304,128]{1,0:T(8,128)(2,1)S(1)}, u32[]{:S(2)}, u32[]{:S(2)}) collective-permute-start(bf16[304,128]{1,0:T(8,128)(2,1)S(1)} %get-tuple-element.20), channel_id=1, source_target_pairs={{0,2},{2,4},{4,6},{6,0},{1,3},{3,5},{5,7},{7,1},{8,10},{10,12},{12... | collective-permute-start | bytes 233480 | tf_op jit(solution)/shard_map/ppermute | solution.py:364
  4.1 4.4 %collective-permute-start.1 = (bf16[48,128]{1,0:T(8,128)(2,1)S(1)}, bf16[48,128]{1,0:T(8,128)(2,1)S(1)}, u32[]{:S(2)}, u32[]{:S(2)}) collective-permute-start(bf16[48,128]{1,0:T(8,128)(2,1)S(1)} %get-tuple-element.21), channel_id=1, source_target_pairs={{0,6},{2,0},{4,2},{6,4},{1,7},{3,1},{5,3},{7,5},{8,14},{10,8},{12,... | collective-permute-start | bytes 36872 | tf_op jit(solution)/shard_map/ppermute | solution.py:364
  6.2 4.6 %collective-permute-start.2 = (bf16[48,128]{1,0:T(8,128)(2,1)S(1)}, bf16[48,128]{1,0:T(8,128)(2,1)S(1)}, u32[]{:S(2)}, u32[]{:S(2)}) collective-permute-start(bf16[48,128]{1,0:T(8,128)(2,1)S(1)} %get-tuple-element.22), channel_id=1, source_target_pairs={{0,4},{2,6},{4,0},{6,2},{1,5},{3,7},{5,1},{7,3},{8,12},{10,14},{12... | collective-permute-start | bytes 36872 | tf_op jit(solution)/shard_map/ppermute | solution.py:364
  10.8 7.9 %collective-permute-start.5 = (bf16[704,128]{1,0:T(8,128)(2,1)S(1)}, bf16[704,128]{1,0:T(8,128)(2,1)S(1)}, u32[]{:S(2)}, u32[]{:S(2)}) collective-permute-start(bf16[704,128]{1,0:T(8,128)(2,1)S(1)} %join.1.refs_0_.refs_1_.packed), channel_id=1, source_target_pairs={{0,24},{8,16},{16,8},{24,0},{1,25},{9,17},{17,9},{25,1},{2,26},{10... | collective-permute-start | bytes 540680 | tf_op jit(solution)/shard_map/ppermute | solution.py:244
  13.5 7.1 %collective-permute-start.3 = (bf16[704,128]{1,0:T(8,128)(2,1)S(1)}, bf16[704,128]{1,0:T(8,128)(2,1)S(1)}, u32[]{:S(2)}, u32[]{:S(2)}) collective-permute-start(bf16[704,128]{1,0:T(8,128)(2,1)S(1)} %join.1.refs_0_.refs_1_.packed), channel_id=1, source_target_pairs={{0,8},{8,0},{16,24},{24,16},{1,9},{9,1},{17,25},{25,17},{2,10},{10... | collective-permute-start | bytes 540680 | tf_op jit(solution)/shard_map/ppermute | solution.py:244
  14.1 6.6 %collective-permute-start.4 = (bf16[704,128]{1,0:T(8,128)(2,1)S(1)}, bf16[704,128]{1,0:T(8,128)(2,1)S(1)}, u32[]{:S(2)}, u32[]{:S(2)}) collective-permute-start(bf16[704,128]{1,0:T(8,128)(2,1)S(1)} %join.1.refs_0_.refs_1_.packed), channel_id=1, source_target_pairs={{0,16},{8,24},{16,0},{24,8},{1,17},{9,25},{17,1},{25,9},{2,18},{10... | collective-permute-start | bytes 540680 | tf_op jit(solution)/shard_map/ppermute | solution.py:244
  20.6 2.5 %collective-permute-start.6 = (bf16[2048,128]{1,0:T(8,128)(2,1)S(1)}, bf16[2048,128]{1,0:T(8,128)(2,1)S(1)}, u32[]{:S(2)}, u32[]{:S(2)}) collective-permute-start(bf16[2048,128]{1,0:T(8,128)(2,1)S(1)} %collect.1.ours), channel_id=1, source_target_pairs={{0,1},{1,0},{2,3},{3,2},{4,5},{5,4},{6,7},{7,6},{8,9},{9,8},{10,11... | collective-permute-start | bytes 1572872 | tf_op jit(solution)/shard_map/ppermute | solution.py:400
  24.3 1.5 %collective-permute-start.7 = (f32[64,256]{1,0:T(8,128)S(1)}, f32[64,256]{1,0:T(8,128)S(1)}, u32[]{:S(2)}, u32[]{:S(2)}) collective-permute-start(f32[64,256]{1,0:T(8,128)S(1)} %get-tuple-element.30), channel_id=1, source_target_pairs={{0,1},{1,0},{2,3},{3,2},{4,5},{5,4},{6,7},{7,6},{8,9},{9,8},{10,11... | collective-permute-start | bytes 196616 | tf_op jit(solution)/shard_map/ppermute | solution.py:417

commit v16 on v15

--- a/solution.py
+++ b/solution.py
@@ -207,22 +207,25 @@
         code = order[at]
         slot = lax.rem(code, slots)
         base = lax.div(code, slots) * chans
-        lefts_real, lefts_imag, rights = [], [], []
-        for c in range(chans):
-            here = pl.ds(base + c, 1)
-            left = profile(spots_u[here, :]).reshape(SU // 16, 16, SU)
-            lefts_real.append((left * tiled(turns_real[here, :])).reshape(SU, SU))
-            lefts_imag.append((left * tiled(turns_imag[here, :])).reshape(SU, SU))
-            rights.append(profile(spots_v[here, :]))
-        left = jnp.concatenate(
-            [jnp.concatenate(lefts_real, axis=1), jnp.concatenate(lefts_imag, axis=1)], axis=0
-        )
-        right = jnp.concatenate(rights, axis=1)
-        return slot, lax.dot_general(left, right, NT, preferred_element_type=jnp.float32)
+        part = jnp.zeros((2 * SU, SU), jnp.float32)
+        for pair in range(0, chans, 2):
+            lefts_real, lefts_imag, rights = [], [], []
+            for c in range(pair, pair + 2):
+                here = pl.ds(base + c, 1)
+                left = profile(spots_u[here, :]).reshape(SU // 16, 16, SU)
+                lefts_real.append((left * tiled(turns_real[here, :])).reshape(SU, SU))
+                lefts_imag.append((left * tiled(turns_imag[here, :])).reshape(SU, SU))
+                rights.append(profile(spots_v[here, :]))
+            left = jnp.concatenate(
+                [jnp.concatenate(lefts_real, axis=1), jnp.concatenate(lefts_imag, axis=1)], axis=0
+            )
+            right = jnp.concatenate(rights, axis=1)
+            part = part + lax.dot_general(left, right, NT, preferred_element_type=jnp.float32)
+        grids[slot] += part
 
     def step(k, carry):
-        for slot, part in [one_block(k * UNROLL + i) for i in range(UNROLL)]:
-            grids[slot] += part
+        for i in range(UNROLL):
+            one_block(k * UNROLL + i)
         return carry
 
     lax.fori_loop(0, lax.div(count + UNROLL - 1, UNROLL), step, 0)
@@ -392,13 +395,13 @@
             name="grid",
         )(joined, *some)
 
-    grids = [grid(blocks[:1]), grid(blocks[-1:])]
+    grids = [grid([block]) for block in (blocks[0], blocks[-1], *blocks[1:-2])]
     blocks, grids = lax.optimization_barrier((blocks, grids))
     fetched = local(
         functools.partial(collect_kernel, vis_rows), blocks, (facets * 4 * SU, SU), "collect"
     )
     swapped = lax.ppermute(fetched, "chan", [(c, 1 - c) for c in range(chan_count)])
-    grids.append(grid(blocks[1:-1]))
+    grids.append(grid(blocks[-2:-1]))
     mine, other = pl.pallas_call(
         functools.partial(table_kernel, (slots, meta_row), norm),
         out_shape=[jax.ShapeDtypeStruct((half_rows, 2 * SU), jnp.float32)] * 2,

time: 26.6 us -> 27.2 us (1.023)
  waiting for transfers between devices: 7.65 us -> 8.46 us
  starting transfers between devices: 10.3 us -> 9.94 us
    ppermute x1, waiting for transfers between devices: 0.01 us -> 0.61 us  [body(): lax.ppermute(fetched, 'chan', [(c, 1 - c) for c in range(chan_count)])]
    ppermute x1, starting transfers between devices: 0.56 us -> 0.2 us  [body(): lax.ppermute(other, 'chan', [(c, 1 - c) for c in range(chan_count)])]
    pallas_call x3 -> x4, Pallas kernels: 5.51 us -> 5.66 us  [grid(): pl.pallas_call(functools.partial(grid_kernel, (facets, groups, chans, cap...]
  transfers between devices with their start and end apart: 8 -> 8, of which waited for: 5 -> 6; matrix products, arithmetic and copies ran while one was open for 0% -> 0% of each run, Pallas kernels for 21% -> 21%
where the time goes in v16:
time: 27.2 us; the launch traced here: 27.1 us
  starting transfers between devices  9.94 us (37%)
  waiting for transfers between devices  8.46 us (31%)
  Pallas kernels  7.91 us (29%)
  local copies, waits for them, and re-layouts  0.66 us (2%)
    ppermute x3, starting transfers between devices, body(): lax.ppermute(pieces[shift], 'bl', [(g, (g + shift) % groups) for g in ran...  6.11 us
    pallas_call x4, Pallas kernels, grid(): pl.pallas_call(functools.partial(grid_kernel, (facets, groups, chans, cap...  5.66 us
    ppermute x3, waiting for transfers between devices, body(): lax.ppermute(pieces[shift], 'bl', [(g, (g + shift) % groups) for g in ran...  3.65 us
    ppermute x3, starting transfers between devices, exchange(): lax.ppermute(value, axis, [(n, n ^ shift) for n in range(lax.axis_size(ax...  3.55 us
    ppermute x3, waiting for transfers between devices, exchange(): lax.ppermute(value, axis, [(n, n ^ shift) for n in range(lax.axis_size(ax...  3.08 us
    pallas_call x1, Pallas kernels, body(): pl.pallas_call(functools.partial(table_kernel, (slots, meta_row), norm),...  1.14 us
    ppermute x1, waiting for transfers between devices, body(): lax.ppermute(other, 'chan', [(c, 1 - c) for c in range(chan_count)])  1.12 us
    pallas_call x1, Pallas kernels, body(): pl.pallas_call(functools.partial(sort_kernel, (groups, held, chans, cap,...  1.06 us
  transfers between devices with their start and end apart: 8, of which 6 were waited for; matrix products, arithmetic and copies ran while one was open for 0% of the time, Pallas kernels for 21%

profile of v16, /device:TPU:0, one launch (start us, length us, event | category | flops | bytes accessed | tf_op | source)
XLA Modules:
  0.0 27.1 jit_solution(45326446920678375)
XLA Ops:
  0.0 1.1 %sort_blocks.1 = (bf16[48,128]{1,0:T(8,128)(2,1)S(1)}, bf16[304,128]{1,0:T(8,128)(2,1)S(1)}, bf16[48,128]{1,0:T(8,128)(2,1)S(1)}, bf16[48,128]{1,0:T(8,128)(2,1)S(1)}, bf16[256,128]{1,0:T(8,128)(2,1)S(1)}) custom-call(s32[1,8]{1,0:T(1,128)} %bitcast.12, s32[1,8]{1,0:T(1,128)} %bitcast.13, bf16[64,128]{1,0:T(8,128)(2,1)} %bitcast.8, bf16[16,128]{1,0:T(8,128)(2,1)} %bitcast.9, ...), custom_call_target="tpu_custom_call" | custom-call | flops 100000 | bytes 100000 | tf_op jit(solution)/shard_map/sort_blocks/pallas_call | solution.py:325
  1.1 3.1 %collective-permute-start = (bf16[304,128]{1,0:T(8,128)(2,1)S(1)}, bf16[304,128]{1,0:T(8,128)(2,1)S(1)}, u32[]{:S(2)}, u32[]{:S(2)}) collective-permute-start(bf16[304,128]{1,0:T(8,128)(2,1)S(1)} %get-tuple-element.21), channel_id=1, source_target_pairs={{0,2},{2,4},{4,6},{6,0},{1,3},{3,5},{5,7},{7,1},{8,10},{10,12},{12... | collective-permute-start | bytes 233480 | tf_op jit(solution)/shard_map/ppermute | solution.py:367
  4.1 2.1 %collective-permute-start.1 = (bf16[48,128]{1,0:T(8,128)(2,1)S(1)}, bf16[48,128]{1,0:T(8,128)(2,1)S(1)}, u32[]{:S(2)}, u32[]{:S(2)}) collective-permute-start(bf16[48,128]{1,0:T(8,128)(2,1)S(1)} %get-tuple-element.22), channel_id=1, source_target_pairs={{0,6},{2,0},{4,2},{6,4},{1,7},{3,1},{5,3},{7,5},{8,14},{10,8},{12,... | collective-permute-start | bytes 36872 | tf_op jit(solution)/shard_map/ppermute | solution.py:367
  6.2 0.9 %collective-permute-start.2 = (bf16[48,128]{1,0:T(8,128)(2,1)S(1)}, bf16[48,128]{1,0:T(8,128)(2,1)S(1)}, u32[]{:S(2)}, u32[]{:S(2)}) collective-permute-start(bf16[48,128]{1,0:T(8,128)(2,1)S(1)} %get-tuple-element.23), channel_id=1, source_target_pairs={{0,4},{2,6},{4,0},{6,2},{1,5},{3,7},{5,1},{7,3},{8,12},{10,14},{12... | collective-permute-start | bytes 36872 | tf_op jit(solution)/shard_map/ppermute | solution.py:367
  7.2 1.4 %collective-permute-done.1.refs_2_ = bf16[48,128]{1,0:T(8,128)(2,1)S(1)} collective-permute-done((bf16[48,128]{1,0:T(8,128)(2,1)S(1)}, bf16[48,128]{1,0:T(8,128)(2,1)S(1)}, u32[]{:S(2)}, u32[]{:S(2)}) %collective-permute-start.1) | collective-permute-done | bytes 12320 | tf_op jit(solution)/shard_map/ppermute | solution.py:367
  8.6 2.3 %collective-permute-done.2.refs_3_ = bf16[48,128]{1,0:T(8,128)(2,1)S(1)} collective-permute-done((bf16[48,128]{1,0:T(8,128)(2,1)S(1)}, bf16[48,128]{1,0:T(8,128)(2,1)S(1)}, u32[]{:S(2)}, u32[]{:S(2)}) %collective-permute-start.2) | collective-permute-done | bytes 12320 | tf_op jit(solution)/shard_map/ppermute | solution.py:367
  10.8 0.0 collective-permute-done.refs_1_
  10.8 2.7 %collective-permute-start.5 = (bf16[704,128]{1,0:T(8,128)(2,1)S(1)}, bf16[704,128]{1,0:T(8,128)(2,1)S(1)}, u32[]{:S(2)}, u32[]{:S(2)}) collective-permute-start(bf16[704,128]{1,0:T(8,128)(2,1)S(1)} %join.1.refs_0_.refs_1_.packed), channel_id=1, source_target_pairs={{0,24},{8,16},{16,8},{24,0},{1,25},{9,17},{17,9},{25,1},{2,26},{10... | collective-permute-start | bytes 540680 | tf_op jit(solution)/shard_map/ppermute | solution.py:247
  13.5 0.5 %collective-permute-start.3 = (bf16[704,128]{1,0:T(8,128)(2,1)S(1)}, bf16[704,128]{1,0:T(8,128)(2,1)S(1)}, u32[]{:S(2)}, u32[]{:S(2)}) collective-permute-start(bf16[704,128]{1,0:T(8,128)(2,1)S(1)} %join.1.refs_0_.refs_1_.packed), channel_id=1, source_target_pairs={{0,8},{8,0},{16,24},{24,16},{1,9},{9,1},{17,25},{25,17},{2,10},{10... | collective-permute-start | bytes 540680 | tf_op jit(solution)/shard_map/ppermute | solution.py:247
  14.1 0.3 %collective-permute-start.4 = (bf16[704,128]{1,0:T(8,128)(2,1)S(1)}, bf16[704,128]{1,0:T(8,128)(2,1)S(1)}, u32[]{:S(2)}, u32[]{:S(2)}) collective-permute-start(bf16[704,128]{1,0:T(8,128)(2,1)S(1)} %join.1.refs_0_.refs_1_.packed), channel_id=1, source_target_pairs={{0,16},{8,24},{16,0},{24,8},{1,17},{9,25},{17,1},{25,9},{2,18},{10... | collective-permute-start | bytes 540680 | tf_op jit(solution)/shard_map/ppermute | solution.py:247
  14.4 1.3 %grid.4.refs_0_ = f32[8,256,128]{2,1,0:T(8,128)S(1)} custom-call(bf16[704,128]{1,0:T(8,128)(2,1)S(1)} %join.1.refs_0_.refs_1_.packed, bf16[704,128]{1,0:T(8,128)(2,1)S(1)} %join.1.refs_0_.refs_1_.packed), custom_call_target="tpu_custom_call" | custom-call | flops 1000000000 | bytes 1000000 | tf_op jit(solution)/shard_map/grid/pallas_call | solution.py:380
  15.7 3.0 %collective-permute-done.5.refs_1_.refs_3_ = bf16[704,128]{1,0:T(8,128)(2,1)S(1)} collective-permute-done((bf16[704,128]{1,0:T(8,128)(2,1)S(1)}, bf16[704,128]{1,0:T(8,128)(2,1)S(1)}, u32[]{:S(2)}, u32[]{:S(2)}) %collective-permute-start.5) | collective-permute-done | bytes 180256 | tf_op jit(solution)/shard_map/ppermute | solution.py:247
  18.7 1.8 %grid.5.refs_1_ = f32[8,256,128]{2,1,0:T(8,128)S(1)} custom-call(bf16[704,128]{1,0:T(8,128)(2,1)S(1)} %join.1.refs_0_.refs_1_.packed, bf16[704,128]{1,0:T(8,128)(2,1)S(1)} %collective-permute-done.5.refs_1_.refs_3_), custom_call_target="tpu_custom_call" | custom-call | flops 1000000000 | bytes 1000000 | tf_op jit(solution)/shard_map/grid/pallas_call | solution.py:380
  20.5 0.1 collective-permute-done.3.refs_1_
  20.6 1.3 %grid.6.refs_2_ = f32[8,256,128]{2,1,0:T(8,128)S(1)} custom-call(bf16[704,128]{1,0:T(8,128)(2,1)S(1)} %join.1.refs_0_.refs_1_.packed, bf16[704,128]{1,0:T(8,128)(2,1)S(1)} %collective-permute-done.3.refs_1_), custom_call_target="tpu_custom_call" | custom-call | flops 1000000000 | bytes 1000000 | tf_op jit(solution)/shard_map/grid/pallas_call | solution.py:380
  21.9 0.0 collective-permute-done.4.refs_2_.refs_1_
  21.9 0.1 collective-permute-start.6
  22.0 1.3 %grid.7.refs_3_ = f32[8,256,128]{2,1,0:T(8,128)S(1)} custom-call(bf16[704,128]{1,0:T(8,128)(2,1)S(1)} %join.1.refs_0_.refs_1_.packed, bf16[704,128]{1,0:T(8,128)(2,1)S(1)} %collective-permute-done.4.refs_2_.refs_1_), custom_call_target="tpu_custom_call" | custom-call | flops 1000000000 | bytes 1000000 | tf_op jit(solution)/shard_map/grid/pallas_call | solution.py:380
  23.3 0.6 %collective-permute-done.6.theirs = bf16[2048,128]{1,0:T(8,128)(2,1)S(1)} collective-permute-done((bf16[2048,128]{1,0:T(8,128)(2,1)S(1)}, bf16[2048,128]{1,0:T(8,128)(2,1)S(1)}, u32[]{:S(2)}, u32[]{:S(2)}) %collective-permute-start.6) | collective-permute-done | bytes 524320 | tf_op jit(solution)/shard_map/ppermute | solution.py:403
  23.9 1.1 %apply_tables.1 = (f32[64,256]{1,0:T(8,128)S(1)}, f32[64,256]{1,0:T(8,128)S(1)}) custom-call(bf16[704,128]{1,0:T(8,128)(2,1)S(1)} %join.1.refs_0_.refs_1_.packed, bf16[2048,128]{1,0:T(8,128)(2,1)S(1)} %collect.1.ours, bf16[2048,128]{1,0:T(8,128)(2,1)S(1)} %collective-permute-done.6.theirs, f32[8,256,128]{2,1,0:T(8,128)S(1)} %grid.4.refs_0_, ...), custom_call_target="tpu_custom_call" | custom-call | flops 1000000000 | bytes 2000000 | tf_op jit(solution)/shard_map/apply_tables/pallas_call | solution.py:405
  25.1 0.2 collective-permute-start.7
  25.3 1.1 %collective-permute-done.7 = f32[64,256]{1,0:T(8,128)S(1)} collective-permute-done((f32[64,256]{1,0:T(8,128)S(1)}, f32[64,256]{1,0:T(8,128)S(1)}, u32[]{:S(2)}, u32[]{:S(2)}) %collective-permute-start.7) | collective-permute-done | bytes 65568 | tf_op jit(solution)/shard_map/ppermute | solution.py:420
  26.4 0.7 %reshape.19 = f32[1,1,64,2,128]{4,3,2,1,0:T(2,128)} reshape(f32[64,256]{1,0:T(8,128)S(1)} %add.3) | data formatting | bytes 131072 | tf_op jit(solution)/shard_map/reshape | solution.py:421
  (3 shorter events, 0.1 us)
Async XLA Ops:
  1.1 9.8 %collective-permute-start = (bf16[304,128]{1,0:T(8,128)(2,1)S(1)}, bf16[304,128]{1,0:T(8,128)(2,1)S(1)}, u32[]{:S(2)}, u32[]{:S(2)}) collective-permute-start(bf16[304,128]{1,0:T(8,128)(2,1)S(1)} %get-tuple-element.21), channel_id=1, source_target_pairs={{0,2},{2,4},{4,6},{6,0},{1,3},{3,5},{5,7},{7,1},{8,10},{10,12},{12... | collective-permute-start | bytes 233480 | tf_op jit(solution)/shard_map/ppermute | solution.py:367
  4.1 4.4 %collective-permute-start.1 = (bf16[48,128]{1,0:T(8,128)(2,1)S(1)}, bf16[48,128]{1,0:T(8,128)(2,1)S(1)}, u32[]{:S(2)}, u32[]{:S(2)}) collective-permute-start(bf16[48,128]{1,0:T(8,128)(2,1)S(1)} %get-tuple-element.22), channel_id=1, source_target_pairs={{0,6},{2,0},{4,2},{6,4},{1,7},{3,1},{5,3},{7,5},{8,14},{10,8},{12,... | collective-permute-start | bytes 36872 | tf_op jit(solution)/shard_map/ppermute | solution.py:367
  6.2 4.6 %collective-permute-start.2 = (bf16[48,128]{1,0:T(8,128)(2,1)S(1)}, bf16[48,128]{1,0:T(8,128)(2,1)S(1)}, u32[]{:S(2)}, u32[]{:S(2)}) collective-permute-start(bf16[48,128]{1,0:T(8,128)(2,1)S(1)} %get-tuple-element.23), channel_id=1, source_target_pairs={{0,4},{2,6},{4,0},{6,2},{1,5},{3,7},{5,1},{7,3},{8,12},{10,14},{12... | collective-permute-start | bytes 36872 | tf_op jit(solution)/shard_map/ppermute | solution.py:367
  10.8 7.9 %collective-permute-start.5 = (bf16[704,128]{1,0:T(8,128)(2,1)S(1)}, bf16[704,128]{1,0:T(8,128)(2,1)S(1)}, u32[]{:S(2)}, u32[]{:S(2)}) collective-permute-start(bf16[704,128]{1,0:T(8,128)(2,1)S(1)} %join.1.refs_0_.refs_1_.packed), channel_id=1, source_target_pairs={{0,24},{8,16},{16,8},{24,0},{1,25},{9,17},{17,9},{25,1},{2,26},{10... | collective-permute-start | bytes 540680 | tf_op jit(solution)/shard_map/ppermute | solution.py:247
  13.5 7.1 %collective-permute-start.3 = (bf16[704,128]{1,0:T(8,128)(2,1)S(1)}, bf16[704,128]{1,0:T(8,128)(2,1)S(1)}, u32[]{:S(2)}, u32[]{:S(2)}) collective-permute-start(bf16[704,128]{1,0:T(8,128)(2,1)S(1)} %join.1.refs_0_.refs_1_.packed), channel_id=1, source_target_pairs={{0,8},{8,0},{16,24},{24,16},{1,9},{9,1},{17,25},{25,17},{2,10},{10... | collective-permute-start | bytes 540680 | tf_op jit(solution)/shard_map/ppermute | solution.py:247
  14.1 7.8 %collective-permute-start.4 = (bf16[704,128]{1,0:T(8,128)(2,1)S(1)}, bf16[704,128]{1,0:T(8,128)(2,1)S(1)}, u32[]{:S(2)}, u32[]{:S(2)}) collective-permute-start(bf16[704,128]{1,0:T(8,128)(2,1)S(1)} %join.1.refs_0_.refs_1_.packed), channel_id=1, source_target_pairs={{0,16},{8,24},{16,0},{24,8},{1,17},{9,25},{17,1},{25,9},{2,18},{10... | collective-permute-start | bytes 540680 | tf_op jit(solution)/shard_map/ppermute | solution.py:247
  21.9 2.0 %collective-permute-start.6 = (bf16[2048,128]{1,0:T(8,128)(2,1)S(1)}, bf16[2048,128]{1,0:T(8,128)(2,1)S(1)}, u32[]{:S(2)}, u32[]{:S(2)}) collective-permute-start(bf16[2048,128]{1,0:T(8,128)(2,1)S(1)} %collect.1.ours), channel_id=1, source_target_pairs={{0,1},{1,0},{2,3},{3,2},{4,5},{5,4},{6,7},{7,6},{8,9},{9,8},{10,11... | collective-permute-start | bytes 1572872 | tf_op jit(solution)/shard_map/ppermute | solution.py:403
  25.1 1.3 %collective-permute-start.7 = (f32[64,256]{1,0:T(8,128)S(1)}, f32[64,256]{1,0:T(8,128)S(1)}, u32[]{:S(2)}, u32[]{:S(2)}) collective-permute-start(f32[64,256]{1,0:T(8,128)S(1)} %get-tuple-element.32), channel_id=1, source_target_pairs={{0,1},{1,0},{2,3},{3,2},{4,5},{5,4},{6,7},{7,6},{8,9},{9,8},{10,11... | collective-permute-start | bytes 196616 | tf_op jit(solution)/shard_map/ppermute | solution.py:420

commit v17 on v15

--- a/solution.py
+++ b/solution.py
@@ -218,7 +218,7 @@
             [jnp.concatenate(lefts_real, axis=1), jnp.concatenate(lefts_imag, axis=1)], axis=0
         )
         right = jnp.concatenate(rights, axis=1)
-        return slot, lax.dot_general(left, right, NT, preferred_element_type=jnp.float32)
+        return slot, lax.dot_general(right, left, NT, preferred_element_type=jnp.float32)
 
     def step(k, carry):
         for slot, part in [one_block(k * UNROLL + i) for i in range(UNROLL)]:
@@ -259,38 +259,37 @@
         at = slice(2 * SU * s, 2 * SU * (s + 1))
         fetched = ours[at, :].astype(jnp.float32)
         swapped = theirs[at, :].astype(jnp.float32)
-        u_real, u_imag = parts(jnp.where(first, fetched, swapped))
-        u_side = jnp.concatenate([u_real.T, u_imag.T], axis=1).astype(jnp.bfloat16)
-        grid_real, grid_imag = (
-            sum(ref[s, part * SU : (part + 1) * SU, :] for ref in grids) for part in range(2)
-        )
+        v_real, v_imag = parts(jnp.where(first, swapped, fetched))
+        v_side = jnp.concatenate([v_real.T, v_imag.T], axis=1).astype(jnp.bfloat16)
+        grid = sum(ref[s] for ref in grids)
         high, low = (
             jnp.concatenate(
                 [
-                    jnp.concatenate([real, imag], axis=1),
-                    jnp.concatenate([-imag, real], axis=1),
+                    part,
+                    jnp.concatenate([-part[:, SU:], part[:, :SU]], axis=1),
                 ],
                 axis=0,
             )
-            for real, imag in zip(split_bf16(grid_real), split_bf16(grid_imag))
-        )
-        half = jnp.dot(u_side, high, preferred_element_type=jnp.float32) + jnp.dot(
-            u_side, low, preferred_element_type=jnp.float32
-        )
-        v_real, v_imag = parts(jnp.where(first, swapped, fetched))
-        v_side = jnp.concatenate(
+            for part in split_bf16(grid)
+        )
+        half = jnp.dot(v_side, high, preferred_element_type=jnp.float32) + jnp.dot(
+            v_side, low, preferred_element_type=jnp.float32
+        )
+        u_real, u_imag = parts(jnp.where(first, fetched, swapped))
+        u_side = jnp.concatenate(
             [
-                jnp.concatenate([v_real, v_imag], axis=1),
-                jnp.concatenate([-v_imag, v_real], axis=1),
+                jnp.concatenate([u_real, u_imag], axis=1),
+                jnp.concatenate([-u_imag, u_real], axis=1),
             ],
             axis=0,
         ).astype(jnp.bfloat16)
         high, low = split_bf16(half)
         result = (
             result
-            + jnp.dot(high, v_side, preferred_element_type=jnp.float32)
-            + jnp.dot(low, v_side, preferred_element_type=jnp.float32)
-        )
+            + jnp.dot(high, u_side, preferred_element_type=jnp.float32)
+            + jnp.dot(low, u_side, preferred_element_type=jnp.float32)
+        )
+    result = jnp.concatenate([result[:, :SU].T, result[:, SU:].T], axis=1)
     tail = meta_row // 16 * 16
     wide = packed[tail : tail + 16, :].astype(jnp.float32)
     at = meta_row - tail + 2
@@ -376,7 +375,7 @@
         lines = len(some) * groups * cap
         return pl.pallas_call(
             functools.partial(grid_kernel, (facets, groups, chans, cap, rows, len(some))),
-            out_shape=jax.ShapeDtypeStruct((slots, 2 * SU, SU), jnp.float32),
+            out_shape=jax.ShapeDtypeStruct((slots, SU, 2 * SU), jnp.float32),
             in_specs=[VMEM] * (1 + len(some)),
             out_specs=VMEM,
             scratch_shapes=[

time: 26.6 us -> 27.1 us (1.019); the launches traced: 26.4 us -> 26.6 us
  Pallas kernels: 7.73 us -> 8.08 us
  transfers between devices with their start and end apart: 8 -> 8, of which waited for: 5 -> 5; matrix products, arithmetic and copies ran while one was open for 0% -> 0% of each run, Pallas kernels for 21% -> 22%
where the time goes in v17:
time: 27.1 us; the launch traced here: 26.6 us
  starting transfers between devices  10.3 us (38%)
  Pallas kernels  8.08 us (30%)
  waiting for transfers between devices  7.48 us (28%)
  local copies, waits for them, and re-layouts  0.66 us (2%)
    ppermute x3, starting transfers between devices, body(): lax.ppermute(pieces[shift], 'bl', [(g, (g + shift) % groups) for g in ran...  6.12 us
    pallas_call x3, Pallas kernels, grid(): pl.pallas_call(functools.partial(grid_kernel, (facets, groups, chans, cap...  5.76 us
    ppermute x3, waiting for transfers between devices, body(): lax.ppermute(pieces[shift], 'bl', [(g, (g + shift) % groups) for g in ran...  3.64 us
    ppermute x3, starting transfers between devices, exchange(): lax.ppermute(value, axis, [(n, n ^ shift) for n in range(lax.axis_size(ax...  3.55 us
    ppermute x3, waiting for transfers between devices, exchange(): lax.ppermute(value, axis, [(n, n ^ shift) for n in range(lax.axis_size(ax...  2.94 us
    pallas_call x1, Pallas kernels, body(): pl.pallas_call(functools.partial(table_kernel, (slots, meta_row), norm),...  1.21 us
    pallas_call x1, Pallas kernels, body(): pl.pallas_call(functools.partial(sort_kernel, (groups, held, chans, cap,...  1.06 us
    ppermute x1, waiting for transfers between devices, body(): lax.ppermute(other, 'chan', [(c, 1 - c) for c in range(chan_count)])  0.9 us
  transfers between devices with their start and end apart: 8, of which 5 were waited for; matrix products, arithmetic and copies ran while one was open for 0% of the time, Pallas kernels for 22%

profile of v17, /device:TPU:0, one launch (start us, length us, event | category | flops | bytes accessed | tf_op | source)
XLA Modules:
  0.0 26.6 jit_solution(7619539101535896781)
XLA Ops:
  0.0 1.1 %sort_blocks.1 = (bf16[48,128]{1,0:T(8,128)(2,1)S(1)}, bf16[304,128]{1,0:T(8,128)(2,1)S(1)}, bf16[48,128]{1,0:T(8,128)(2,1)S(1)}, bf16[48,128]{1,0:T(8,128)(2,1)S(1)}, bf16[256,128]{1,0:T(8,128)(2,1)S(1)}) custom-call(s32[1,8]{1,0:T(1,128)} %bitcast.12, s32[1,8]{1,0:T(1,128)} %bitcast.13, bf16[64,128]{1,0:T(8,128)(2,1)} %bitcast.8, bf16[16,128]{1,0:T(8,128)(2,1)} %bitcast.9, ...), custom_call_target="tpu_custom_call" | custom-call | flops 100000 | bytes 100000 | tf_op jit(solution)/shard_map/sort_blocks/pallas_call | solution.py:321
  1.1 3.1 %collective-permute-start = (bf16[304,128]{1,0:T(8,128)(2,1)S(1)}, bf16[304,128]{1,0:T(8,128)(2,1)S(1)}, u32[]{:S(2)}, u32[]{:S(2)}) collective-permute-start(bf16[304,128]{1,0:T(8,128)(2,1)S(1)} %get-tuple-element.20), channel_id=1, source_target_pairs={{0,2},{2,4},{4,6},{6,0},{1,3},{3,5},{5,7},{7,1},{8,10},{10,12},{12... | collective-permute-start | bytes 233480 | tf_op jit(solution)/shard_map/ppermute | solution.py:363
  4.1 2.1 %collective-permute-start.1 = (bf16[48,128]{1,0:T(8,128)(2,1)S(1)}, bf16[48,128]{1,0:T(8,128)(2,1)S(1)}, u32[]{:S(2)}, u32[]{:S(2)}) collective-permute-start(bf16[48,128]{1,0:T(8,128)(2,1)S(1)} %get-tuple-element.21), channel_id=1, source_target_pairs={{0,6},{2,0},{4,2},{6,4},{1,7},{3,1},{5,3},{7,5},{8,14},{10,8},{12,... | collective-permute-start | bytes 36872 | tf_op jit(solution)/shard_map/ppermute | solution.py:363
  6.2 1.0 %collective-permute-start.2 = (bf16[48,128]{1,0:T(8,128)(2,1)S(1)}, bf16[48,128]{1,0:T(8,128)(2,1)S(1)}, u32[]{:S(2)}, u32[]{:S(2)}) collective-permute-start(bf16[48,128]{1,0:T(8,128)(2,1)S(1)} %get-tuple-element.22), channel_id=1, source_target_pairs={{0,4},{2,6},{4,0},{6,2},{1,5},{3,7},{5,1},{7,3},{8,12},{10,14},{12... | collective-permute-start | bytes 36872 | tf_op jit(solution)/shard_map/ppermute | solution.py:363
  7.2 1.4 %collective-permute-done.1.refs_2_ = bf16[48,128]{1,0:T(8,128)(2,1)S(1)} collective-permute-done((bf16[48,128]{1,0:T(8,128)(2,1)S(1)}, bf16[48,128]{1,0:T(8,128)(2,1)S(1)}, u32[]{:S(2)}, u32[]{:S(2)}) %collective-permute-start.1) | collective-permute-done | bytes 12320 | tf_op jit(solution)/shard_map/ppermute | solution.py:363
  8.6 2.3 %collective-permute-done.2.refs_3_ = bf16[48,128]{1,0:T(8,128)(2,1)S(1)} collective-permute-done((bf16[48,128]{1,0:T(8,128)(2,1)S(1)}, bf16[48,128]{1,0:T(8,128)(2,1)S(1)}, u32[]{:S(2)}, u32[]{:S(2)}) %collective-permute-start.2) | collective-permute-done | bytes 12320 | tf_op jit(solution)/shard_map/ppermute | solution.py:363
  10.8 0.0 collective-permute-done.refs_1_
  10.8 2.7 %collective-permute-start.5 = (bf16[704,128]{1,0:T(8,128)(2,1)S(1)}, bf16[704,128]{1,0:T(8,128)(2,1)S(1)}, u32[]{:S(2)}, u32[]{:S(2)}) collective-permute-start(bf16[704,128]{1,0:T(8,128)(2,1)S(1)} %join.1.refs_0_.refs_1_.packed), channel_id=1, source_target_pairs={{0,24},{8,16},{16,8},{24,0},{1,25},{9,17},{17,9},{25,1},{2,26},{10... | collective-permute-start | bytes 540680 | tf_op jit(solution)/shard_map/ppermute | solution.py:244
  13.5 0.5 %collective-permute-start.3 = (bf16[704,128]{1,0:T(8,128)(2,1)S(1)}, bf16[704,128]{1,0:T(8,128)(2,1)S(1)}, u32[]{:S(2)}, u32[]{:S(2)}) collective-permute-start(bf16[704,128]{1,0:T(8,128)(2,1)S(1)} %join.1.refs_0_.refs_1_.packed), channel_id=1, source_target_pairs={{0,8},{8,0},{16,24},{24,16},{1,9},{9,1},{17,25},{25,17},{2,10},{10... | collective-permute-start | bytes 540680 | tf_op jit(solution)/shard_map/ppermute | solution.py:244
  14.1 0.3 %collective-permute-start.4 = (bf16[704,128]{1,0:T(8,128)(2,1)S(1)}, bf16[704,128]{1,0:T(8,128)(2,1)S(1)}, u32[]{:S(2)}, u32[]{:S(2)}) collective-permute-start(bf16[704,128]{1,0:T(8,128)(2,1)S(1)} %join.1.refs_0_.refs_1_.packed), channel_id=1, source_target_pairs={{0,16},{8,24},{16,0},{24,8},{1,17},{9,25},{17,1},{25,9},{2,18},{10... | collective-permute-start | bytes 540680 | tf_op jit(solution)/shard_map/ppermute | solution.py:244
  14.4 1.9 %grid.3.refs_0_ = f32[8,128,256]{2,1,0:T(8,128)S(1)} custom-call(bf16[704,128]{1,0:T(8,128)(2,1)S(1)} %join.1.refs_0_.refs_1_.packed, bf16[704,128]{1,0:T(8,128)(2,1)S(1)} %join.1.refs_0_.refs_1_.packed), custom_call_target="tpu_custom_call" | custom-call | flops 1000000000 | bytes 1000000 | tf_op jit(solution)/shard_map/grid/pallas_call | solution.py:376
  16.3 2.4 %collective-permute-done.5.refs_1_.refs_3_ = bf16[704,128]{1,0:T(8,128)(2,1)S(1)} collective-permute-done((bf16[704,128]{1,0:T(8,128)(2,1)S(1)}, bf16[704,128]{1,0:T(8,128)(2,1)S(1)}, u32[]{:S(2)}, u32[]{:S(2)}) %collective-permute-start.5) | collective-permute-done | bytes 180256 | tf_op jit(solution)/shard_map/ppermute | solution.py:244
  18.7 1.3 %grid.4.refs_1_ = f32[8,128,256]{2,1,0:T(8,128)S(1)} custom-call(bf16[704,128]{1,0:T(8,128)(2,1)S(1)} %join.1.refs_0_.refs_1_.packed, bf16[704,128]{1,0:T(8,128)(2,1)S(1)} %collective-permute-done.5.refs_1_.refs_3_), custom_call_target="tpu_custom_call" | custom-call | flops 1000000000 | bytes 1000000 | tf_op jit(solution)/shard_map/grid/pallas_call | solution.py:376
  20.1 0.5 %collective-permute-done.3.refs_1_ = bf16[704,128]{1,0:T(8,128)(2,1)S(1)} collective-permute-done((bf16[704,128]{1,0:T(8,128)(2,1)S(1)}, bf16[704,128]{1,0:T(8,128)(2,1)S(1)}, u32[]{:S(2)}, u32[]{:S(2)}) %collective-permute-start.3) | collective-permute-done | bytes 180256 | tf_op jit(solution)/shard_map/ppermute | solution.py:244
  20.6 0.0 collective-permute-done.4.refs_2_
  20.6 0.1 collective-permute-start.6
  20.7 2.5 %grid.5.refs_2_ = f32[8,128,256]{2,1,0:T(8,128)S(1)} custom-call(bf16[704,128]{1,0:T(8,128)(2,1)S(1)} %join.1.refs_0_.refs_1_.packed, bf16[704,128]{1,0:T(8,128)(2,1)S(1)} %collective-permute-done.3.refs_1_, bf16[704,128]{1,0:T(8,128)(2,1)S(1)} %collective-permute-done.4.refs_2_), custom_call_target="tpu_custom_call" | custom-call | flops 2000000000 | bytes 1000000 | tf_op jit(solution)/shard_map/grid/pallas_call | solution.py:376
  23.2 0.0 collective-permute-done.6.theirs
  23.3 1.2 %apply_tables.1 = (f32[64,256]{1,0:T(8,128)S(1)}, f32[64,256]{1,0:T(8,128)S(1)}) custom-call(bf16[704,128]{1,0:T(8,128)(2,1)S(1)} %join.1.refs_0_.refs_1_.packed, bf16[2048,128]{1,0:T(8,128)(2,1)S(1)} %collect.1.ours, bf16[2048,128]{1,0:T(8,128)(2,1)S(1)} %collective-permute-done.6.theirs, f32[8,128,256]{2,1,0:T(8,128)S(1)} %grid.3.refs_0_, ...), custom_call_target="tpu_custom_call" | custom-call | flops 1000000000 | bytes 2000000 | tf_op jit(solution)/shard_map/apply_tables/pallas_call | solution.py:401
  24.5 0.6 %collective-permute-start.7 = (f32[64,256]{1,0:T(8,128)S(1)}, f32[64,256]{1,0:T(8,128)S(1)}, u32[]{:S(2)}, u32[]{:S(2)}) collective-permute-start(f32[64,256]{1,0:T(8,128)S(1)} %get-tuple-element.30), channel_id=1, source_target_pairs={{0,1},{1,0},{2,3},{3,2},{4,5},{5,4},{6,7},{7,6},{8,9},{9,8},{10,11... | collective-permute-start | bytes 196616 | tf_op jit(solution)/shard_map/ppermute | solution.py:416
  25.0 0.9 %collective-permute-done.7 = f32[64,256]{1,0:T(8,128)S(1)} collective-permute-done((f32[64,256]{1,0:T(8,128)S(1)}, f32[64,256]{1,0:T(8,128)S(1)}, u32[]{:S(2)}, u32[]{:S(2)}) %collective-permute-start.7) | collective-permute-done | bytes 65568 | tf_op jit(solution)/shard_map/ppermute | solution.py:416
  25.9 0.7 %reshape.19 = f32[1,1,64,2,128]{4,3,2,1,0:T(2,128)} reshape(f32[64,256]{1,0:T(8,128)S(1)} %add.3) | data formatting | bytes 131072 | tf_op jit(solution)/shard_map/reshape | solution.py:417
  (3 shorter events, 0.1 us)
Async XLA Ops:
  1.1 9.8 %collective-permute-start = (bf16[304,128]{1,0:T(8,128)(2,1)S(1)}, bf16[304,128]{1,0:T(8,128)(2,1)S(1)}, u32[]{:S(2)}, u32[]{:S(2)}) collective-permute-start(bf16[304,128]{1,0:T(8,128)(2,1)S(1)} %get-tuple-element.20), channel_id=1, source_target_pairs={{0,2},{2,4},{4,6},{6,0},{1,3},{3,5},{5,7},{7,1},{8,10},{10,12},{12... | collective-permute-start | bytes 233480 | tf_op jit(solution)/shard_map/ppermute | solution.py:363
  4.1 4.4 %collective-permute-start.1 = (bf16[48,128]{1,0:T(8,128)(2,1)S(1)}, bf16[48,128]{1,0:T(8,128)(2,1)S(1)}, u32[]{:S(2)}, u32[]{:S(2)}) collective-permute-start(bf16[48,128]{1,0:T(8,128)(2,1)S(1)} %get-tuple-element.21), channel_id=1, source_target_pairs={{0,6},{2,0},{4,2},{6,4},{1,7},{3,1},{5,3},{7,5},{8,14},{10,8},{12,... | collective-permute-start | bytes 36872 | tf_op jit(solution)/shard_map/ppermute | solution.py:363
  6.2 4.6 %collective-permute-start.2 = (bf16[48,128]{1,0:T(8,128)(2,1)S(1)}, bf16[48,128]{1,0:T(8,128)(2,1)S(1)}, u32[]{:S(2)}, u32[]{:S(2)}) collective-permute-start(bf16[48,128]{1,0:T(8,128)(2,1)S(1)} %get-tuple-element.22), channel_id=1, source_target_pairs={{0,4},{2,6},{4,0},{6,2},{1,5},{3,7},{5,1},{7,3},{8,12},{10,14},{12... | collective-permute-start | bytes 36872 | tf_op jit(solution)/shard_map/ppermute | solution.py:363
  10.8 7.9 %collective-permute-start.5 = (bf16[704,128]{1,0:T(8,128)(2,1)S(1)}, bf16[704,128]{1,0:T(8,128)(2,1)S(1)}, u32[]{:S(2)}, u32[]{:S(2)}) collective-permute-start(bf16[704,128]{1,0:T(8,128)(2,1)S(1)} %join.1.refs_0_.refs_1_.packed), channel_id=1, source_target_pairs={{0,24},{8,16},{16,8},{24,0},{1,25},{9,17},{17,9},{25,1},{2,26},{10... | collective-permute-start | bytes 540680 | tf_op jit(solution)/shard_map/ppermute | solution.py:244
  13.5 7.1 %collective-permute-start.3 = (bf16[704,128]{1,0:T(8,128)(2,1)S(1)}, bf16[704,128]{1,0:T(8,128)(2,1)S(1)}, u32[]{:S(2)}, u32[]{:S(2)}) collective-permute-start(bf16[704,128]{1,0:T(8,128)(2,1)S(1)} %join.1.refs_0_.refs_1_.packed), channel_id=1, source_target_pairs={{0,8},{8,0},{16,24},{24,16},{1,9},{9,1},{17,25},{25,17},{2,10},{10... | collective-permute-start | bytes 540680 | tf_op jit(solution)/shard_map/ppermute | solution.py:244
  14.1 6.5 %collective-permute-start.4 = (bf16[704,128]{1,0:T(8,128)(2,1)S(1)}, bf16[704,128]{1,0:T(8,128)(2,1)S(1)}, u32[]{:S(2)}, u32[]{:S(2)}) collective-permute-start(bf16[704,128]{1,0:T(8,128)(2,1)S(1)} %join.1.refs_0_.refs_1_.packed), channel_id=1, source_target_pairs={{0,16},{8,24},{16,0},{24,8},{1,17},{9,25},{17,1},{25,9},{2,18},{10... | collective-permute-start | bytes 540680 | tf_op jit(solution)/shard_map/ppermute | solution.py:244
  20.6 2.6 %collective-permute-start.6 = (bf16[2048,128]{1,0:T(8,128)(2,1)S(1)}, bf16[2048,128]{1,0:T(8,128)(2,1)S(1)}, u32[]{:S(2)}, u32[]{:S(2)}) collective-permute-start(bf16[2048,128]{1,0:T(8,128)(2,1)S(1)} %collect.1.ours), channel_id=1, source_target_pairs={{0,1},{1,0},{2,3},{3,2},{4,5},{5,4},{6,7},{7,6},{8,9},{9,8},{10,11... | collective-permute-start | bytes 1572872 | tf_op jit(solution)/shard_map/ppermute | solution.py:399
  24.5 1.5 %collective-permute-start.7 = (f32[64,256]{1,0:T(8,128)S(1)}, f32[64,256]{1,0:T(8,128)S(1)}, u32[]{:S(2)}, u32[]{:S(2)}) collective-permute-start(f32[64,256]{1,0:T(8,128)S(1)} %get-tuple-element.30), channel_id=1, source_target_pairs={{0,1},{1,0},{2,3},{3,2},{4,5},{5,4},{6,7},{7,6},{8,9},{9,8},{10,11... | collective-permute-start | bytes 196616 | tf_op jit(solution)/shard_map/ppermute | solution.py:416

commit v18 on v17

--- a/solution.py
+++ b/solution.py
@@ -112,17 +112,23 @@
 
 
 def join_kernel(rows, half, *refs):
-    *pieces, joined = refs
+    *pieces, here, tables, joined = refs
+    at = len(pieces) * rows
     for n, ref in enumerate(pieces):
-        joined[n * rows : (n + 1) * rows, :] = ref[:rows, :]
-    at = len(pieces) * rows
-    joined[at : at + 2 * SU, :] = half[...]
-    joined[at + 2 * SU :, :] = pieces[1][rows:, :]
-
-
-def collect_kernel(skip, *refs):
-    for n, ref in enumerate(refs[:-1]):
-        refs[-1][n * 4 * SU : (n + 1) * 4 * SU, :] = ref[skip:, :]
+        piece = ref[:rows, :]
+        here[n * rows : (n + 1) * rows, :] = piece
+        joined[n * rows : (n + 1) * rows, :] = piece
+    for n, ref in enumerate((half, pieces[1].at[pl.ds(rows, 2 * SU)])):
+        table = ref[...]
+        tables[n * 2 * SU : (n + 1) * 2 * SU, :] = table
+        joined[at + n * 2 * SU : at + (n + 1) * 2 * SU, :] = table
+
+
+def collect_kernel(tables, *refs):
+    *joined, diagonal, out_ref = refs
+    for n, ref in enumerate((tables, *joined, diagonal)):
+        start = ref.shape[0] - 4 * SU
+        out_ref[n * 4 * SU : (n + 1) * 4 * SU, :] = ref[start:, :]
 
 
 def grid_kernel(sizes, *refs):
@@ -228,12 +234,12 @@
     lax.fori_loop(0, lax.div(count + UNROLL - 1, UNROLL), step, 0)
 
 
-def local(kernel, operands, shape, name):
+def local(kernel, operands, shapes, name):
     return pl.pallas_call(
         kernel,
-        out_shape=jax.ShapeDtypeStruct(shape, jnp.bfloat16),
+        out_shape=[jax.ShapeDtypeStruct(shape, jnp.bfloat16) for shape in shapes],
         in_specs=[VMEM] * len(operands),
-        out_specs=VMEM,
+        out_specs=[VMEM] * len(shapes),
         compiler_params=PARAMS,
         cost_estimate=pl.CostEstimate(flops=0, bytes_accessed=400_000, transcendentals=0),
         name=name,
@@ -364,13 +370,19 @@
         for shift in [1, *range(groups - 1, 1, -1)]
     ]
     vis_rows = groups * rows
-    joined = local(
+    here, both, joined = local(
         functools.partial(join_kernel, rows),
         [half, pieces[0], *arrived],
-        (vis_rows + 4 * SU, SU),
+        [(vis_rows, SU), (4 * SU, SU), (vis_rows + 4 * SU, SU)],
         "join",
     )
-    blocks = [joined] + [exchange(joined, "facet", shift) for shift in range(1, facets)]
+    blocks = (
+        [here]
+        + [exchange(joined, "facet", shift) for shift in range(1, facets - 1)]
+        + [exchange(here, "facet", facets - 1)]
+    )
+    last_tables = exchange(both, "facet", facets - 1)
+
     def grid(some):
         lines = len(some) * groups * cap
         return pl.pallas_call(
@@ -389,15 +401,18 @@
                 transcendentals=len(some) * 1_000_000,
             ),
             name="grid",
-        )(joined, *some)
-
-    grids = [grid(blocks[:1]), grid(blocks[-1:])]
-    blocks, grids = lax.optimization_barrier((blocks, grids))
-    fetched = local(
-        functools.partial(collect_kernel, vis_rows), blocks, (facets * 4 * SU, SU), "collect"
+        )(here, *some)
+
+    grids = [grid(blocks[:1]), grid([blocks[-1], *blocks[1:-2]])]
+    blocks, last_tables, grids = lax.optimization_barrier((blocks, last_tables, grids))
+    (fetched,) = local(
+        collect_kernel,
+        [both, *blocks[1:-1], last_tables],
+        [(facets * 4 * SU, SU)],
+        "collect",
     )
     swapped = lax.ppermute(fetched, "chan", [(c, 1 - c) for c in range(chan_count)])
-    grids.append(grid(blocks[1:-1]))
+    grids.append(grid(blocks[-2:-1]))
     mine, other = pl.pallas_call(
         functools.partial(table_kernel, (slots, meta_row), norm),
         out_shape=[jax.ShapeDtypeStruct((half_rows, 2 * SU), jnp.float32)] * 2,
@@ -412,7 +427,7 @@
             flops=1_000_000_000, bytes_accessed=2_000_000, transcendentals=0
         ),
         name="apply_tables",
-    )(joined, fetched, swapped, *grids)
+    )(here, fetched, swapped, *grids)
     summand = lax.ppermute(other, "chan", [(c, 1 - c) for c in range(chan_count)])
     return (mine + summand).reshape(1, 1, half_rows, 2, SU)
 

time: 27.1 us -> 28 us (1.033); the launches traced: 26.6 us -> 28.1 us
  starting transfers between devices: 10.3 us -> 12.5 us
  waiting for transfers between devices: 7.48 us -> 6.72 us
    ppermute x3 -> x4, starting transfers between devices: 3.55 us -> 6.16 us  [exchange(): lax.ppermute(value, axis, [(n, n ^ shift) for n in range(lax.axis_size(ax...]
    ppermute x3 -> x4, waiting for transfers between devices: 2.94 us -> 1.4 us  [exchange(): lax.ppermute(value, axis, [(n, n ^ shift) for n in range(lax.axis_size(ax...]
    ppermute x1, waiting for transfers between devices: 0.01 us -> 0.55 us  [body(): lax.ppermute(fetched, 'chan', [(c, 1 - c) for c in range(chan_count)])]
    ppermute x1, starting transfers between devices: 0.56 us -> 0.2 us  [body(): lax.ppermute(other, 'chan', [(c, 1 - c) for c in range(chan_count)])]
  transfers between devices with their start and end apart: 8 -> 9, of which waited for: 5 -> 5; matrix products, arithmetic and copies ran while one was open for 0% -> 0% of each run, Pallas kernels for 22% -> 21%
where the time goes in v18:
time: 28 us; the launch traced here: 28.1 us
  starting transfers between devices  12.5 us (45%)
  Pallas kernels  8.12 us (29%)
  waiting for transfers between devices  6.72 us (24%)
  local copies, waits for them, and re-layouts  0.66 us (2%)
    ppermute x4, starting transfers between devices, exchange(): lax.ppermute(value, axis, [(n, n ^ shift) for n in range(lax.axis_size(ax...  6.16 us
    ppermute x3, starting transfers between devices, body(): lax.ppermute(pieces[shift], 'bl', [(g, (g + shift) % groups) for g in ran...  6.11 us
    pallas_call x3, Pallas kernels, grid(): pl.pallas_call(functools.partial(grid_kernel, (facets, groups, chans, cap...  5.76 us
    ppermute x3, waiting for transfers between devices, body(): lax.ppermute(pieces[shift], 'bl', [(g, (g + shift) % groups) for g in ran...  3.65 us
    ppermute x4, waiting for transfers between devices, exchange(): lax.ppermute(value, axis, [(n, n ^ shift) for n in range(lax.axis_size(ax...  1.4 us
    pallas_call x1, Pallas kernels, body(): pl.pallas_call(functools.partial(table_kernel, (slots, meta_row), norm),...  1.21 us
    ppermute x1, waiting for transfers between devices, body(): lax.ppermute(other, 'chan', [(c, 1 - c) for c in range(chan_count)])  1.12 us
    pallas_call x1, Pallas kernels, body(): pl.pallas_call(functools.partial(sort_kernel, (groups, held, chans, cap,...  1.06 us
  transfers between devices with their start and end apart: 9, of which 5 were waited for; matrix products, arithmetic and copies ran while one was open for 0% of the time, Pallas kernels for 21%

profile of v18, /device:TPU:0, one launch (start us, length us, event | category | flops | bytes accessed | tf_op | source)
XLA Modules:
  0.0 28.1 jit_solution(9938303843958423831)
XLA Ops:
  0.0 1.1 %sort_blocks.1 = (bf16[48,128]{1,0:T(8,128)(2,1)S(1)}, bf16[304,128]{1,0:T(8,128)(2,1)S(1)}, bf16[48,128]{1,0:T(8,128)(2,1)S(1)}, bf16[48,128]{1,0:T(8,128)(2,1)S(1)}, bf16[256,128]{1,0:T(8,128)(2,1)S(1)}) custom-call(s32[1,8]{1,0:T(1,128)} %bitcast.12, s32[1,8]{1,0:T(1,128)} %bitcast.13, bf16[64,128]{1,0:T(8,128)(2,1)} %bitcast.8, bf16[16,128]{1,0:T(8,128)(2,1)} %bitcast.9, ...), custom_call_target="tpu_custom_call" | custom-call | flops 100000 | bytes 100000 | tf_op jit(solution)/shard_map/sort_blocks/pallas_call | solution.py:327
  1.1 3.1 %collective-permute-start = (bf16[304,128]{1,0:T(8,128)(2,1)S(1)}, bf16[304,128]{1,0:T(8,128)(2,1)S(1)}, u32[]{:S(2)}, u32[]{:S(2)}) collective-permute-start(bf16[304,128]{1,0:T(8,128)(2,1)S(1)} %get-tuple-element.22), channel_id=1, source_target_pairs={{0,2},{2,4},{4,6},{6,0},{1,3},{3,5},{5,7},{7,1},{8,10},{10,12},{12... | collective-permute-start | bytes 233480 | tf_op jit(solution)/shard_map/ppermute | solution.py:369
  4.1 2.1 %collective-permute-start.1 = (bf16[48,128]{1,0:T(8,128)(2,1)S(1)}, bf16[48,128]{1,0:T(8,128)(2,1)S(1)}, u32[]{:S(2)}, u32[]{:S(2)}) collective-permute-start(bf16[48,128]{1,0:T(8,128)(2,1)S(1)} %get-tuple-element.23), channel_id=1, source_target_pairs={{0,6},{2,0},{4,2},{6,4},{1,7},{3,1},{5,3},{7,5},{8,14},{10,8},{12,... | collective-permute-start | bytes 36872 | tf_op jit(solution)/shard_map/ppermute | solution.py:369
  6.2 0.9 %collective-permute-start.2 = (bf16[48,128]{1,0:T(8,128)(2,1)S(1)}, bf16[48,128]{1,0:T(8,128)(2,1)S(1)}, u32[]{:S(2)}, u32[]{:S(2)}) collective-permute-start(bf16[48,128]{1,0:T(8,128)(2,1)S(1)} %get-tuple-element.24), channel_id=1, source_target_pairs={{0,4},{2,6},{4,0},{6,2},{1,5},{3,7},{5,1},{7,3},{8,12},{10,14},{12... | collective-permute-start | bytes 36872 | tf_op jit(solution)/shard_map/ppermute | solution.py:369
  7.2 1.4 %collective-permute-done.1.refs_2_ = bf16[48,128]{1,0:T(8,128)(2,1)S(1)} collective-permute-done((bf16[48,128]{1,0:T(8,128)(2,1)S(1)}, bf16[48,128]{1,0:T(8,128)(2,1)S(1)}, u32[]{:S(2)}, u32[]{:S(2)}) %collective-permute-start.1) | collective-permute-done | bytes 12320 | tf_op jit(solution)/shard_map/ppermute | solution.py:369
  8.6 2.3 %collective-permute-done.2.refs_3_ = bf16[48,128]{1,0:T(8,128)(2,1)S(1)} collective-permute-done((bf16[48,128]{1,0:T(8,128)(2,1)S(1)}, bf16[48,128]{1,0:T(8,128)(2,1)S(1)}, u32[]{:S(2)}, u32[]{:S(2)}) %collective-permute-start.2) | collective-permute-done | bytes 12320 | tf_op jit(solution)/shard_map/ppermute | solution.py:369
  10.8 0.0 collective-permute-done.refs_1_
  10.9 1.7 %collective-permute-start.3 = (bf16[704,128]{1,0:T(8,128)(2,1)S(1)}, bf16[704,128]{1,0:T(8,128)(2,1)S(1)}, u32[]{:S(2)}, u32[]{:S(2)}) collective-permute-start(bf16[704,128]{1,0:T(8,128)(2,1)S(1)} %get-tuple-element.27), channel_id=1, source_target_pairs={{0,8},{8,0},{16,24},{24,16},{1,9},{9,1},{17,25},{25,17},{2,10},{10... | collective-permute-start | bytes 540680 | tf_op jit(solution)/shard_map/ppermute | solution.py:250
  12.6 1.5 %collective-permute-start.4 = (bf16[704,128]{1,0:T(8,128)(2,1)S(1)}, bf16[704,128]{1,0:T(8,128)(2,1)S(1)}, u32[]{:S(2)}, u32[]{:S(2)}) collective-permute-start(bf16[704,128]{1,0:T(8,128)(2,1)S(1)} %get-tuple-element.27), channel_id=1, source_target_pairs={{0,16},{8,24},{16,0},{24,8},{1,17},{9,25},{17,1},{25,9},{2,18},{10... | collective-permute-start | bytes 540680 | tf_op jit(solution)/shard_map/ppermute | solution.py:250
  14.1 0.3 %collective-permute-start.5 = (bf16[192,128]{1,0:T(8,128)(2,1)S(1)}, bf16[192,128]{1,0:T(8,128)(2,1)S(1)}, u32[]{:S(2)}, u32[]{:S(2)}) collective-permute-start(bf16[192,128]{1,0:T(8,128)(2,1)S(1)} %get-tuple-element.25.refs_0_.refs_1_.packed), channel_id=1, source_target_pairs={{0,24},{8,16},{16,8},{24,0},{1,25},{9,17},{17,9},{25,1},{2,26},{10... | collective-permute-start | bytes 147464 | tf_op jit(solution)/shard_map/ppermute | solution.py:250
  14.4 2.6 %collective-permute-start.6 = (bf16[512,128]{1,0:T(8,128)(2,1)S(1)}, bf16[512,128]{1,0:T(8,128)(2,1)S(1)}, u32[]{:S(2)}, u32[]{:S(2)}) collective-permute-start(bf16[512,128]{1,0:T(8,128)(2,1)S(1)} %get-tuple-element.26.tables), channel_id=1, source_target_pairs={{0,24},{8,16},{16,8},{24,0},{1,25},{9,17},{17,9},{25,1},{2,26},{10... | collective-permute-start | bytes 393224 | tf_op jit(solution)/shard_map/ppermute | solution.py:250
  17.0 1.3 %grid.3.refs_0_ = f32[8,128,256]{2,1,0:T(8,128)S(1)} custom-call(bf16[192,128]{1,0:T(8,128)(2,1)S(1)} %get-tuple-element.25.refs_0_.refs_1_.packed, bf16[192,128]{1,0:T(8,128)(2,1)S(1)} %get-tuple-element.25.refs_0_.refs_1_.packed), custom_call_target="tpu_custom_call" | custom-call | flops 1000000000 | bytes 1000000 | tf_op jit(solution)/shard_map/grid/pallas_call | solution.py:388
  18.4 1.4 %collective-permute-done.5.refs_1_ = bf16[192,128]{1,0:T(8,128)(2,1)S(1)} collective-permute-done((bf16[192,128]{1,0:T(8,128)(2,1)S(1)}, bf16[192,128]{1,0:T(8,128)(2,1)S(1)}, u32[]{:S(2)}, u32[]{:S(2)}) %collective-permute-start.5) | collective-permute-done | bytes 49184 | tf_op jit(solution)/shard_map/ppermute | solution.py:250
  19.8 0.0 collective-permute-done.3.refs_2_.refs_0_
  19.8 3.1 %grid.4.refs_1_ = f32[8,128,256]{2,1,0:T(8,128)S(1)} custom-call(bf16[192,128]{1,0:T(8,128)(2,1)S(1)} %get-tuple-element.25.refs_0_.refs_1_.packed, bf16[192,128]{1,0:T(8,128)(2,1)S(1)} %collective-permute-done.5.refs_1_, bf16[704,128]{1,0:T(8,128)(2,1)S(1)} %collective-permute-done.3.refs_2_.refs_0_), custom_call_target="tpu_custom_call" | custom-call | flops 2000000000 | bytes 1000000 | tf_op jit(solution)/shard_map/grid/pallas_call | solution.py:388
  22.9 0.0 collective-permute-done.6.refs_2_
  22.9 0.0 collective-permute-done.4.refs_1_
  22.9 0.1 collective-permute-start.7
  23.0 1.3 %grid.5.refs_2_ = f32[8,128,256]{2,1,0:T(8,128)S(1)} custom-call(bf16[192,128]{1,0:T(8,128)(2,1)S(1)} %get-tuple-element.25.refs_0_.refs_1_.packed, bf16[704,128]{1,0:T(8,128)(2,1)S(1)} %collective-permute-done.4.refs_1_), custom_call_target="tpu_custom_call" | custom-call | flops 1000000000 | bytes 1000000 | tf_op jit(solution)/shard_map/grid/pallas_call | solution.py:388
  24.4 0.5 %collective-permute-done.7.theirs = bf16[2048,128]{1,0:T(8,128)(2,1)S(1)} collective-permute-done((bf16[2048,128]{1,0:T(8,128)(2,1)S(1)}, bf16[2048,128]{1,0:T(8,128)(2,1)S(1)}, u32[]{:S(2)}, u32[]{:S(2)}) %collective-permute-start.7) | collective-permute-done | bytes 524320 | tf_op jit(solution)/shard_map/ppermute | solution.py:414
  24.9 1.2 %apply_tables.1 = (f32[64,256]{1,0:T(8,128)S(1)}, f32[64,256]{1,0:T(8,128)S(1)}) custom-call(bf16[192,128]{1,0:T(8,128)(2,1)S(1)} %get-tuple-element.25.refs_0_.refs_1_.packed, bf16[2048,128]{1,0:T(8,128)(2,1)S(1)} %collect.1.ours, bf16[2048,128]{1,0:T(8,128)(2,1)S(1)} %collective-permute-done.7.theirs, f32[8,128,256]{2,1,0:T(8,128)S(1)} %grid.3.refs_0_, ...), custom_call_target="tpu_custom_call" | custom-call | flops 1000000000 | bytes 2000000 | tf_op jit(solution)/shard_map/apply_tables/pallas_call | solution.py:416
  26.1 0.2 collective-permute-start.8
  26.3 1.1 %collective-permute-done.8 = f32[64,256]{1,0:T(8,128)S(1)} collective-permute-done((f32[64,256]{1,0:T(8,128)S(1)}, f32[64,256]{1,0:T(8,128)S(1)}, u32[]{:S(2)}, u32[]{:S(2)}) %collective-permute-start.8) | collective-permute-done | bytes 65568 | tf_op jit(solution)/shard_map/ppermute | solution.py:431
  27.5 0.7 %reshape.19 = f32[1,1,64,2,128]{4,3,2,1,0:T(2,128)} reshape(f32[64,256]{1,0:T(8,128)S(1)} %add.3) | data formatting | bytes 131072 | tf_op jit(solution)/shard_map/reshape | solution.py:432
  (3 shorter events, 0.1 us)
Async XLA Ops:
  1.1 9.8 %collective-permute-start = (bf16[304,128]{1,0:T(8,128)(2,1)S(1)}, bf16[304,128]{1,0:T(8,128)(2,1)S(1)}, u32[]{:S(2)}, u32[]{:S(2)}) collective-permute-start(bf16[304,128]{1,0:T(8,128)(2,1)S(1)} %get-tuple-element.22), channel_id=1, source_target_pairs={{0,2},{2,4},{4,6},{6,0},{1,3},{3,5},{5,7},{7,1},{8,10},{10,12},{12... | collective-permute-start | bytes 233480 | tf_op jit(solution)/shard_map/ppermute | solution.py:369
  4.1 4.4 %collective-permute-start.1 = (bf16[48,128]{1,0:T(8,128)(2,1)S(1)}, bf16[48,128]{1,0:T(8,128)(2,1)S(1)}, u32[]{:S(2)}, u32[]{:S(2)}) collective-permute-start(bf16[48,128]{1,0:T(8,128)(2,1)S(1)} %get-tuple-element.23), channel_id=1, source_target_pairs={{0,6},{2,0},{4,2},{6,4},{1,7},{3,1},{5,3},{7,5},{8,14},{10,8},{12,... | collective-permute-start | bytes 36872 | tf_op jit(solution)/shard_map/ppermute | solution.py:369
  6.2 4.6 %collective-permute-start.2 = (bf16[48,128]{1,0:T(8,128)(2,1)S(1)}, bf16[48,128]{1,0:T(8,128)(2,1)S(1)}, u32[]{:S(2)}, u32[]{:S(2)}) collective-permute-start(bf16[48,128]{1,0:T(8,128)(2,1)S(1)} %get-tuple-element.24), channel_id=1, source_target_pairs={{0,4},{2,6},{4,0},{6,2},{1,5},{3,7},{5,1},{7,3},{8,12},{10,14},{12... | collective-permute-start | bytes 36872 | tf_op jit(solution)/shard_map/ppermute | solution.py:369
  10.9 8.9 %collective-permute-start.3 = (bf16[704,128]{1,0:T(8,128)(2,1)S(1)}, bf16[704,128]{1,0:T(8,128)(2,1)S(1)}, u32[]{:S(2)}, u32[]{:S(2)}) collective-permute-start(bf16[704,128]{1,0:T(8,128)(2,1)S(1)} %get-tuple-element.27), channel_id=1, source_target_pairs={{0,8},{8,0},{16,24},{24,16},{1,9},{9,1},{17,25},{25,17},{2,10},{10... | collective-permute-start | bytes 540680 | tf_op jit(solution)/shard_map/ppermute | solution.py:250
  12.6 10.3 %collective-permute-start.4 = (bf16[704,128]{1,0:T(8,128)(2,1)S(1)}, bf16[704,128]{1,0:T(8,128)(2,1)S(1)}, u32[]{:S(2)}, u32[]{:S(2)}) collective-permute-start(bf16[704,128]{1,0:T(8,128)(2,1)S(1)} %get-tuple-element.27), channel_id=1, source_target_pairs={{0,16},{8,24},{16,0},{24,8},{1,17},{9,25},{17,1},{25,9},{2,18},{10... | collective-permute-start | bytes 540680 | tf_op jit(solution)/shard_map/ppermute | solution.py:250
  14.1 5.7 %collective-permute-start.5 = (bf16[192,128]{1,0:T(8,128)(2,1)S(1)}, bf16[192,128]{1,0:T(8,128)(2,1)S(1)}, u32[]{:S(2)}, u32[]{:S(2)}) collective-permute-start(bf16[192,128]{1,0:T(8,128)(2,1)S(1)} %get-tuple-element.25.refs_0_.refs_1_.packed), channel_id=1, source_target_pairs={{0,24},{8,16},{16,8},{24,0},{1,25},{9,17},{17,9},{25,1},{2,26},{10... | collective-permute-start | bytes 147464 | tf_op jit(solution)/shard_map/ppermute | solution.py:250
  14.4 8.4 %collective-permute-start.6 = (bf16[512,128]{1,0:T(8,128)(2,1)S(1)}, bf16[512,128]{1,0:T(8,128)(2,1)S(1)}, u32[]{:S(2)}, u32[]{:S(2)}) collective-permute-start(bf16[512,128]{1,0:T(8,128)(2,1)S(1)} %get-tuple-element.26.tables), channel_id=1, source_target_pairs={{0,24},{8,16},{16,8},{24,0},{1,25},{9,17},{17,9},{25,1},{2,26},{10... | collective-permute-start | bytes 393224 | tf_op jit(solution)/shard_map/ppermute | solution.py:250
  22.9 2.0 %collective-permute-start.7 = (bf16[2048,128]{1,0:T(8,128)(2,1)S(1)}, bf16[2048,128]{1,0:T(8,128)(2,1)S(1)}, u32[]{:S(2)}, u32[]{:S(2)}) collective-permute-start(bf16[2048,128]{1,0:T(8,128)(2,1)S(1)} %collect.1.ours), channel_id=1, source_target_pairs={{0,1},{1,0},{2,3},{3,2},{4,5},{5,4},{6,7},{7,6},{8,9},{9,8},{10,11... | collective-permute-start | bytes 1572872 | tf_op jit(solution)/shard_map/ppermute | solution.py:414
  26.1 1.3 %collective-permute-start.8 = (f32[64,256]{1,0:T(8,128)S(1)}, f32[64,256]{1,0:T(8,128)S(1)}, u32[]{:S(2)}, u32[]{:S(2)}) collective-permute-start(f32[64,256]{1,0:T(8,128)S(1)} %get-tuple-element.34), channel_id=1, source_target_pairs={{0,1},{1,0},{2,3},{3,2},{4,5},{5,4},{6,7},{7,6},{8,9},{9,8},{10,11... | collective-permute-start | bytes 196616 | tf_op jit(solution)/shard_map/ppermute | solution.py:431

commit v19 on v17

--- a/solution.py
+++ b/solution.py
@@ -13,6 +13,7 @@
 KERNEL_SPREAD = 1.5
 ALPHA = math.sqrt(math.log2(math.e) / (2.0 * KERNEL_SPREAD * KERNEL_SPREAD))
 UNROLL = 4
+REST = 2
 NT = (((1,), (1,)), ((), ()))
 VMEM = pl.BlockSpec(memory_space=pltpu.VMEM)
 HBM = pl.BlockSpec(memory_space=pltpu.HBM)
@@ -128,7 +129,7 @@
 def grid_kernel(sizes, *refs):
     facets, groups, chans, cap, rows, count_here = sizes
     own_ref, grids = refs[0], refs[1 + count_here]
-    order, spots_u, spots_v, turns_real, turns_imag = refs[2 + count_here :]
+    order, spots_u, spots_v, turns_real, turns_imag, cells = refs[2 + count_here :]
     pieces = [
         ref.at[pl.ds(n * rows, rows)] for ref in refs[1 : 1 + count_here] for n in range(groups)
     ]
@@ -194,10 +195,10 @@
     for i in range(UNROLL):
         order[count + i] = devices * cap * slots
 
-    cells = ALPHA * lax.broadcasted_iota(jnp.int32, (SU, SU), 0).astype(jnp.float32)
+    cells[...] = ALPHA * lax.broadcasted_iota(jnp.int32, (SU, SU), 0).astype(jnp.float32)
 
     def profile(spot):
-        apart = spot - cells
+        apart = spot - cells[...]
         return jnp.exp2(-((apart * apart).astype(jnp.bfloat16)))
 
     def tiled(row):
@@ -220,12 +221,17 @@
         right = jnp.concatenate(rights, axis=1)
         return slot, lax.dot_general(right, left, NT, preferred_element_type=jnp.float32)
 
-    def step(k, carry):
-        for slot, part in [one_block(k * UNROLL + i) for i in range(UNROLL)]:
-            grids[slot] += part
-        return carry
-
-    lax.fori_loop(0, lax.div(count + UNROLL - 1, UNROLL), step, 0)
+    def steps(first, blocks, number):
+        def step(k, carry):
+            for slot, part in [one_block(first + k * blocks + i) for i in range(blocks)]:
+                grids[slot] += part
+            return carry
+
+        lax.fori_loop(0, number, step, 0)
+
+    whole = lax.div(count, UNROLL)
+    steps(0, UNROLL, whole)
+    steps(whole * UNROLL, REST, lax.div(lax.rem(count, UNROLL) + REST - 1, REST))
 
 
 def local(kernel, operands, shape, name):
@@ -381,7 +387,8 @@
             scratch_shapes=[
                 pltpu.SMEM((lines + UNROLL,), jnp.int32),
             ]
-            + [pltpu.VMEM((lines * chans + 8, SU), jnp.float32)] * 4,
+            + [pltpu.VMEM((lines * chans + 8, SU), jnp.float32)] * 4
+            + [pltpu.VMEM((SU, SU), jnp.float32)],
             compiler_params=PARAMS,
             cost_estimate=pl.CostEstimate(
                 flops=len(some) * 1_000_000_000,

time: 27.1 us -> 27 us (level); the launches traced: 26.6 us -> 26.8 us
  waiting for transfers between devices: 7.48 us -> 7.82 us
    ppermute x3, waiting for transfers between devices: 2.94 us -> 3.26 us  [exchange(): lax.ppermute(value, axis, [(n, n ^ shift) for n in range(lax.axis_size(ax...]
  transfers between devices with their start and end apart: 8 -> 8, of which waited for: 5 -> 5; matrix products, arithmetic and copies ran while one was open for 0% -> 0% of each run, Pallas kernels for 22% -> 21%
where the time goes in v19:
time: 27 us; the launch traced here: 26.8 us
  starting transfers between devices  10.3 us (38%)
  Pallas kernels  7.95 us (29%)
  waiting for transfers between devices  7.82 us (29%)
  local copies, waits for them, and re-layouts  0.66 us (2%)
    ppermute x3, starting transfers between devices, body(): lax.ppermute(pieces[shift], 'bl', [(g, (g + shift) % groups) for g in ran...  6.12 us
    pallas_call x3, Pallas kernels, grid(): pl.pallas_call(functools.partial(grid_kernel, (facets, groups, chans, cap...  5.64 us
    ppermute x3, waiting for transfers between devices, body(): lax.ppermute(pieces[shift], 'bl', [(g, (g + shift) % groups) for g in ran...  3.65 us
    ppermute x3, starting transfers between devices, exchange(): lax.ppermute(value, axis, [(n, n ^ shift) for n in range(lax.axis_size(ax...  3.55 us
    ppermute x3, waiting for transfers between devices, exchange(): lax.ppermute(value, axis, [(n, n ^ shift) for n in range(lax.axis_size(ax...  3.26 us
    pallas_call x1, Pallas kernels, body(): pl.pallas_call(functools.partial(table_kernel, (slots, meta_row), norm),...  1.21 us
    pallas_call x1, Pallas kernels, body(): pl.pallas_call(functools.partial(sort_kernel, (groups, held, chans, cap,...  1.06 us
    ppermute x1, waiting for transfers between devices, body(): lax.ppermute(other, 'chan', [(c, 1 - c) for c in range(chan_count)])  0.9 us
  transfers between devices with their start and end apart: 8, of which 5 were waited for; matrix products, arithmetic and copies ran while one was open for 0% of the time, Pallas kernels for 21%

profile of v19, /device:TPU:0, one launch (start us, length us, event | category | flops | bytes accessed | tf_op | source)
XLA Modules:
  0.0 26.8 jit_solution(17842409291606964287)
XLA Ops:
  0.0 1.1 %sort_blocks.1 = (bf16[48,128]{1,0:T(8,128)(2,1)S(1)}, bf16[304,128]{1,0:T(8,128)(2,1)S(1)}, bf16[48,128]{1,0:T(8,128)(2,1)S(1)}, bf16[48,128]{1,0:T(8,128)(2,1)S(1)}, bf16[256,128]{1,0:T(8,128)(2,1)S(1)}) custom-call(s32[1,8]{1,0:T(1,128)} %bitcast.12, s32[1,8]{1,0:T(1,128)} %bitcast.13, bf16[64,128]{1,0:T(8,128)(2,1)} %bitcast.8, bf16[16,128]{1,0:T(8,128)(2,1)} %bitcast.9, ...), custom_call_target="tpu_custom_call" | custom-call | flops 100000 | bytes 100000 | tf_op jit(solution)/shard_map/sort_blocks/pallas_call | solution.py:327
  1.1 3.1 %collective-permute-start = (bf16[304,128]{1,0:T(8,128)(2,1)S(1)}, bf16[304,128]{1,0:T(8,128)(2,1)S(1)}, u32[]{:S(2)}, u32[]{:S(2)}) collective-permute-start(bf16[304,128]{1,0:T(8,128)(2,1)S(1)} %get-tuple-element.20), channel_id=1, source_target_pairs={{0,2},{2,4},{4,6},{6,0},{1,3},{3,5},{5,7},{7,1},{8,10},{10,12},{12... | collective-permute-start | bytes 233480 | tf_op jit(solution)/shard_map/ppermute | solution.py:369
  4.1 2.1 %collective-permute-start.1 = (bf16[48,128]{1,0:T(8,128)(2,1)S(1)}, bf16[48,128]{1,0:T(8,128)(2,1)S(1)}, u32[]{:S(2)}, u32[]{:S(2)}) collective-permute-start(bf16[48,128]{1,0:T(8,128)(2,1)S(1)} %get-tuple-element.21), channel_id=1, source_target_pairs={{0,6},{2,0},{4,2},{6,4},{1,7},{3,1},{5,3},{7,5},{8,14},{10,8},{12,... | collective-permute-start | bytes 36872 | tf_op jit(solution)/shard_map/ppermute | solution.py:369
  6.2 0.9 %collective-permute-start.2 = (bf16[48,128]{1,0:T(8,128)(2,1)S(1)}, bf16[48,128]{1,0:T(8,128)(2,1)S(1)}, u32[]{:S(2)}, u32[]{:S(2)}) collective-permute-start(bf16[48,128]{1,0:T(8,128)(2,1)S(1)} %get-tuple-element.22), channel_id=1, source_target_pairs={{0,4},{2,6},{4,0},{6,2},{1,5},{3,7},{5,1},{7,3},{8,12},{10,14},{12... | collective-permute-start | bytes 36872 | tf_op jit(solution)/shard_map/ppermute | solution.py:369
  7.2 1.4 %collective-permute-done.1.refs_2_ = bf16[48,128]{1,0:T(8,128)(2,1)S(1)} collective-permute-done((bf16[48,128]{1,0:T(8,128)(2,1)S(1)}, bf16[48,128]{1,0:T(8,128)(2,1)S(1)}, u32[]{:S(2)}, u32[]{:S(2)}) %collective-permute-start.1) | collective-permute-done | bytes 12320 | tf_op jit(solution)/shard_map/ppermute | solution.py:369
  8.6 2.3 %collective-permute-done.2.refs_3_ = bf16[48,128]{1,0:T(8,128)(2,1)S(1)} collective-permute-done((bf16[48,128]{1,0:T(8,128)(2,1)S(1)}, bf16[48,128]{1,0:T(8,128)(2,1)S(1)}, u32[]{:S(2)}, u32[]{:S(2)}) %collective-permute-start.2) | collective-permute-done | bytes 12320 | tf_op jit(solution)/shard_map/ppermute | solution.py:369
  10.8 0.0 collective-permute-done.refs_1_
  10.9 2.7 %collective-permute-start.5 = (bf16[704,128]{1,0:T(8,128)(2,1)S(1)}, bf16[704,128]{1,0:T(8,128)(2,1)S(1)}, u32[]{:S(2)}, u32[]{:S(2)}) collective-permute-start(bf16[704,128]{1,0:T(8,128)(2,1)S(1)} %join.1.refs_0_.refs_1_.packed), channel_id=1, source_target_pairs={{0,24},{8,16},{16,8},{24,0},{1,25},{9,17},{17,9},{25,1},{2,26},{10... | collective-permute-start | bytes 540680 | tf_op jit(solution)/shard_map/ppermute | solution.py:250
  13.5 0.5 %collective-permute-start.3 = (bf16[704,128]{1,0:T(8,128)(2,1)S(1)}, bf16[704,128]{1,0:T(8,128)(2,1)S(1)}, u32[]{:S(2)}, u32[]{:S(2)}) collective-permute-start(bf16[704,128]{1,0:T(8,128)(2,1)S(1)} %join.1.refs_0_.refs_1_.packed), channel_id=1, source_target_pairs={{0,8},{8,0},{16,24},{24,16},{1,9},{9,1},{17,25},{25,17},{2,10},{10... | collective-permute-start | bytes 540680 | tf_op jit(solution)/shard_map/ppermute | solution.py:250
  14.1 0.4 %collective-permute-start.4 = (bf16[704,128]{1,0:T(8,128)(2,1)S(1)}, bf16[704,128]{1,0:T(8,128)(2,1)S(1)}, u32[]{:S(2)}, u32[]{:S(2)}) collective-permute-start(bf16[704,128]{1,0:T(8,128)(2,1)S(1)} %join.1.refs_0_.refs_1_.packed), channel_id=1, source_target_pairs={{0,16},{8,24},{16,0},{24,8},{1,17},{9,25},{17,1},{25,9},{2,18},{10... | collective-permute-start | bytes 540680 | tf_op jit(solution)/shard_map/ppermute | solution.py:250
  14.4 1.3 %grid.3.refs_0_ = f32[8,128,256]{2,1,0:T(8,128)S(1)} custom-call(bf16[704,128]{1,0:T(8,128)(2,1)S(1)} %join.1.refs_0_.refs_1_.packed, bf16[704,128]{1,0:T(8,128)(2,1)S(1)} %join.1.refs_0_.refs_1_.packed), custom_call_target="tpu_custom_call" | custom-call | flops 1000000000 | bytes 1000000 | tf_op jit(solution)/shard_map/grid/pallas_call | solution.py:382
  15.7 3.0 %collective-permute-done.5.refs_1_.refs_3_ = bf16[704,128]{1,0:T(8,128)(2,1)S(1)} collective-permute-done((bf16[704,128]{1,0:T(8,128)(2,1)S(1)}, bf16[704,128]{1,0:T(8,128)(2,1)S(1)}, u32[]{:S(2)}, u32[]{:S(2)}) %collective-permute-start.5) | collective-permute-done | bytes 180256 | tf_op jit(solution)/shard_map/ppermute | solution.py:250
  18.7 1.6 %grid.4.refs_1_ = f32[8,128,256]{2,1,0:T(8,128)S(1)} custom-call(bf16[704,128]{1,0:T(8,128)(2,1)S(1)} %join.1.refs_0_.refs_1_.packed, bf16[704,128]{1,0:T(8,128)(2,1)S(1)} %collective-permute-done.5.refs_1_.refs_3_), custom_call_target="tpu_custom_call" | custom-call | flops 1000000000 | bytes 1000000 | tf_op jit(solution)/shard_map/grid/pallas_call | solution.py:382
  20.4 0.2 collective-permute-done.3.refs_1_
  20.6 0.0 collective-permute-done.4.refs_2_
  20.6 0.1 collective-permute-start.6
  20.7 2.7 %grid.5.refs_2_ = f32[8,128,256]{2,1,0:T(8,128)S(1)} custom-call(bf16[704,128]{1,0:T(8,128)(2,1)S(1)} %join.1.refs_0_.refs_1_.packed, bf16[704,128]{1,0:T(8,128)(2,1)S(1)} %collective-permute-done.3.refs_1_, bf16[704,128]{1,0:T(8,128)(2,1)S(1)} %collective-permute-done.4.refs_2_), custom_call_target="tpu_custom_call" | custom-call | flops 2000000000 | bytes 1000000 | tf_op jit(solution)/shard_map/grid/pallas_call | solution.py:382
  23.5 0.0 collective-permute-done.6.theirs
  23.5 1.2 %apply_tables.1 = (f32[64,256]{1,0:T(8,128)S(1)}, f32[64,256]{1,0:T(8,128)S(1)}) custom-call(bf16[704,128]{1,0:T(8,128)(2,1)S(1)} %join.1.refs_0_.refs_1_.packed, bf16[2048,128]{1,0:T(8,128)(2,1)S(1)} %collect.1.ours, bf16[2048,128]{1,0:T(8,128)(2,1)S(1)} %collective-permute-done.6.theirs, f32[8,128,256]{2,1,0:T(8,128)S(1)} %grid.3.refs_0_, ...), custom_call_target="tpu_custom_call" | custom-call | flops 1000000000 | bytes 2000000 | tf_op jit(solution)/shard_map/apply_tables/pallas_call | solution.py:408
  24.7 0.6 %collective-permute-start.7 = (f32[64,256]{1,0:T(8,128)S(1)}, f32[64,256]{1,0:T(8,128)S(1)}, u32[]{:S(2)}, u32[]{:S(2)}) collective-permute-start(f32[64,256]{1,0:T(8,128)S(1)} %get-tuple-element.30), channel_id=1, source_target_pairs={{0,1},{1,0},{2,3},{3,2},{4,5},{5,4},{6,7},{7,6},{8,9},{9,8},{10,11... | collective-permute-start | bytes 196616 | tf_op jit(solution)/shard_map/ppermute | solution.py:423
  25.2 0.9 %collective-permute-done.7 = f32[64,256]{1,0:T(8,128)S(1)} collective-permute-done((f32[64,256]{1,0:T(8,128)S(1)}, f32[64,256]{1,0:T(8,128)S(1)}, u32[]{:S(2)}, u32[]{:S(2)}) %collective-permute-start.7) | collective-permute-done | bytes 65568 | tf_op jit(solution)/shard_map/ppermute | solution.py:423
  26.2 0.7 %reshape.19 = f32[1,1,64,2,128]{4,3,2,1,0:T(2,128)} reshape(f32[64,256]{1,0:T(8,128)S(1)} %add.3) | data formatting | bytes 131072 | tf_op jit(solution)/shard_map/reshape | solution.py:424
  (3 shorter events, 0.1 us)
Async XLA Ops:
  1.1 9.8 %collective-permute-start = (bf16[304,128]{1,0:T(8,128)(2,1)S(1)}, bf16[304,128]{1,0:T(8,128)(2,1)S(1)}, u32[]{:S(2)}, u32[]{:S(2)}) collective-permute-start(bf16[304,128]{1,0:T(8,128)(2,1)S(1)} %get-tuple-element.20), channel_id=1, source_target_pairs={{0,2},{2,4},{4,6},{6,0},{1,3},{3,5},{5,7},{7,1},{8,10},{10,12},{12... | collective-permute-start | bytes 233480 | tf_op jit(solution)/shard_map/ppermute | solution.py:369
  4.1 4.4 %collective-permute-start.1 = (bf16[48,128]{1,0:T(8,128)(2,1)S(1)}, bf16[48,128]{1,0:T(8,128)(2,1)S(1)}, u32[]{:S(2)}, u32[]{:S(2)}) collective-permute-start(bf16[48,128]{1,0:T(8,128)(2,1)S(1)} %get-tuple-element.21), channel_id=1, source_target_pairs={{0,6},{2,0},{4,2},{6,4},{1,7},{3,1},{5,3},{7,5},{8,14},{10,8},{12,... | collective-permute-start | bytes 36872 | tf_op jit(solution)/shard_map/ppermute | solution.py:369
  6.2 4.6 %collective-permute-start.2 = (bf16[48,128]{1,0:T(8,128)(2,1)S(1)}, bf16[48,128]{1,0:T(8,128)(2,1)S(1)}, u32[]{:S(2)}, u32[]{:S(2)}) collective-permute-start(bf16[48,128]{1,0:T(8,128)(2,1)S(1)} %get-tuple-element.22), channel_id=1, source_target_pairs={{0,4},{2,6},{4,0},{6,2},{1,5},{3,7},{5,1},{7,3},{8,12},{10,14},{12... | collective-permute-start | bytes 36872 | tf_op jit(solution)/shard_map/ppermute | solution.py:369
  10.9 7.9 %collective-permute-start.5 = (bf16[704,128]{1,0:T(8,128)(2,1)S(1)}, bf16[704,128]{1,0:T(8,128)(2,1)S(1)}, u32[]{:S(2)}, u32[]{:S(2)}) collective-permute-start(bf16[704,128]{1,0:T(8,128)(2,1)S(1)} %join.1.refs_0_.refs_1_.packed), channel_id=1, source_target_pairs={{0,24},{8,16},{16,8},{24,0},{1,25},{9,17},{17,9},{25,1},{2,26},{10... | collective-permute-start | bytes 540680 | tf_op jit(solution)/shard_map/ppermute | solution.py:250
  13.5 7.1 %collective-permute-start.3 = (bf16[704,128]{1,0:T(8,128)(2,1)S(1)}, bf16[704,128]{1,0:T(8,128)(2,1)S(1)}, u32[]{:S(2)}, u32[]{:S(2)}) collective-permute-start(bf16[704,128]{1,0:T(8,128)(2,1)S(1)} %join.1.refs_0_.refs_1_.packed), channel_id=1, source_target_pairs={{0,8},{8,0},{16,24},{24,16},{1,9},{9,1},{17,25},{25,17},{2,10},{10... | collective-permute-start | bytes 540680 | tf_op jit(solution)/shard_map/ppermute | solution.py:250
  14.1 6.5 %collective-permute-start.4 = (bf16[704,128]{1,0:T(8,128)(2,1)S(1)}, bf16[704,128]{1,0:T(8,128)(2,1)S(1)}, u32[]{:S(2)}, u32[]{:S(2)}) collective-permute-start(bf16[704,128]{1,0:T(8,128)(2,1)S(1)} %join.1.refs_0_.refs_1_.packed), channel_id=1, source_target_pairs={{0,16},{8,24},{16,0},{24,8},{1,17},{9,25},{17,1},{25,9},{2,18},{10... | collective-permute-start | bytes 540680 | tf_op jit(solution)/shard_map/ppermute | solution.py:250
  20.6 2.8 %collective-permute-start.6 = (bf16[2048,128]{1,0:T(8,128)(2,1)S(1)}, bf16[2048,128]{1,0:T(8,128)(2,1)S(1)}, u32[]{:S(2)}, u32[]{:S(2)}) collective-permute-start(bf16[2048,128]{1,0:T(8,128)(2,1)S(1)} %collect.1.ours), channel_id=1, source_target_pairs={{0,1},{1,0},{2,3},{3,2},{4,5},{5,4},{6,7},{7,6},{8,9},{9,8},{10,11... | collective-permute-start | bytes 1572872 | tf_op jit(solution)/shard_map/ppermute | solution.py:406
  24.7 1.5 %collective-permute-start.7 = (f32[64,256]{1,0:T(8,128)S(1)}, f32[64,256]{1,0:T(8,128)S(1)}, u32[]{:S(2)}, u32[]{:S(2)}) collective-permute-start(f32[64,256]{1,0:T(8,128)S(1)} %get-tuple-element.30), channel_id=1, source_target_pairs={{0,1},{1,0},{2,3},{3,2},{4,5},{5,4},{6,7},{7,6},{8,9},{9,8},{10,11... | collective-permute-start | bytes 196616 | tf_op jit(solution)/shard_map/ppermute | solution.py:423

commit v20 on v19

--- a/solution.py
+++ b/solution.py
@@ -398,13 +398,13 @@
             name="grid",
         )(joined, *some)
 
-    grids = [grid(blocks[:1]), grid(blocks[-1:])]
+    grids = [grid(blocks[:1]), grid(blocks[1:-1])]
     blocks, grids = lax.optimization_barrier((blocks, grids))
     fetched = local(
         functools.partial(collect_kernel, vis_rows), blocks, (facets * 4 * SU, SU), "collect"
     )
     swapped = lax.ppermute(fetched, "chan", [(c, 1 - c) for c in range(chan_count)])
-    grids.append(grid(blocks[1:-1]))
+    grids.append(grid(blocks[-1:]))
     mine, other = pl.pallas_call(
         functools.partial(table_kernel, (slots, meta_row), norm),
         out_shape=[jax.ShapeDtypeStruct((half_rows, 2 * SU), jnp.float32)] * 2,

time: 27 us -> 29.1 us (1.078)
  waiting for transfers between devices: 7.82 us -> 10.8 us
  Pallas kernels: 7.95 us -> 7.25 us
  starting transfers between devices: 10.3 us -> 9.94 us
    ppermute x3, waiting for transfers between devices: 3.26 us -> 5.47 us  [exchange(): lax.ppermute(value, axis, [(n, n ^ shift) for n in range(lax.axis_size(ax...]
    pallas_call x3, Pallas kernels: 5.64 us -> 4.94 us  [grid(): pl.pallas_call(functools.partial(grid_kernel, (facets, groups, chans, cap...]
    ppermute x1, waiting for transfers between devices: 0.01 us -> 0.6 us  [body(): lax.ppermute(fetched, 'chan', [(c, 1 - c) for c in range(chan_count)])]
    ppermute x1, starting transfers between devices: 0.56 us -> 0.2 us  [body(): lax.ppermute(other, 'chan', [(c, 1 - c) for c in range(chan_count)])]
  transfers between devices with their start and end apart: 8 -> 8, of which waited for: 5 -> 6; matrix products, arithmetic and copies ran while one was open for 0% -> 0% of each run, Pallas kernels for 21% -> 17%
where the time goes in v20:
time: 29.1 us; the launch traced here: 28.8 us
  waiting for transfers between devices  10.8 us (37%)
  starting transfers between devices  9.94 us (34%)
  Pallas kernels  7.25 us (25%)
  local copies, waits for them, and re-layouts  0.66 us (2%)
    ppermute x3, starting transfers between devices, body(): lax.ppermute(pieces[shift], 'bl', [(g, (g + shift) % groups) for g in ran...  6.12 us
    ppermute x3, waiting for transfers between devices, exchange(): lax.ppermute(value, axis, [(n, n ^ shift) for n in range(lax.axis_size(ax...  5.47 us
    pallas_call x3, Pallas kernels, grid(): pl.pallas_call(functools.partial(grid_kernel, (facets, groups, chans, cap...  4.94 us
    ppermute x3, waiting for transfers between devices, body(): lax.ppermute(pieces[shift], 'bl', [(g, (g + shift) % groups) for g in ran...  3.64 us
    ppermute x3, starting transfers between devices, exchange(): lax.ppermute(value, axis, [(n, n ^ shift) for n in range(lax.axis_size(ax...  3.55 us
    pallas_call x1, Pallas kernels, body(): pl.pallas_call(functools.partial(table_kernel, (slots, meta_row), norm),...  1.21 us
    ppermute x1, waiting for transfers between devices, body(): lax.ppermute(other, 'chan', [(c, 1 - c) for c in range(chan_count)])  1.12 us
    pallas_call x1, Pallas kernels, body(): pl.pallas_call(functools.partial(sort_kernel, (groups, held, chans, cap,...  1.06 us
  transfers between devices with their start and end apart: 8, of which 6 were waited for; matrix products, arithmetic and copies ran while one was open for 0% of the time, Pallas kernels for 17%

profile of v20, /device:TPU:0, one launch (start us, length us, event | category | flops | bytes accessed | tf_op | source)
XLA Modules:
  0.0 28.8 jit_solution(6607810040176900689)
XLA Ops:
  0.0 1.1 %sort_blocks.1 = (bf16[48,128]{1,0:T(8,128)(2,1)S(1)}, bf16[304,128]{1,0:T(8,128)(2,1)S(1)}, bf16[48,128]{1,0:T(8,128)(2,1)S(1)}, bf16[48,128]{1,0:T(8,128)(2,1)S(1)}, bf16[256,128]{1,0:T(8,128)(2,1)S(1)}) custom-call(s32[1,8]{1,0:T(1,128)} %bitcast.12, s32[1,8]{1,0:T(1,128)} %bitcast.13, bf16[64,128]{1,0:T(8,128)(2,1)} %bitcast.8, bf16[16,128]{1,0:T(8,128)(2,1)} %bitcast.9, ...), custom_call_target="tpu_custom_call" | custom-call | flops 100000 | bytes 100000 | tf_op jit(solution)/shard_map/sort_blocks/pallas_call | solution.py:327
  1.1 3.1 %collective-permute-start = (bf16[304,128]{1,0:T(8,128)(2,1)S(1)}, bf16[304,128]{1,0:T(8,128)(2,1)S(1)}, u32[]{:S(2)}, u32[]{:S(2)}) collective-permute-start(bf16[304,128]{1,0:T(8,128)(2,1)S(1)} %get-tuple-element.20), channel_id=1, source_target_pairs={{0,2},{2,4},{4,6},{6,0},{1,3},{3,5},{5,7},{7,1},{8,10},{10,12},{12... | collective-permute-start | bytes 233480 | tf_op jit(solution)/shard_map/ppermute | solution.py:369
  4.1 2.1 %collective-permute-start.1 = (bf16[48,128]{1,0:T(8,128)(2,1)S(1)}, bf16[48,128]{1,0:T(8,128)(2,1)S(1)}, u32[]{:S(2)}, u32[]{:S(2)}) collective-permute-start(bf16[48,128]{1,0:T(8,128)(2,1)S(1)} %get-tuple-element.21), channel_id=1, source_target_pairs={{0,6},{2,0},{4,2},{6,4},{1,7},{3,1},{5,3},{7,5},{8,14},{10,8},{12,... | collective-permute-start | bytes 36872 | tf_op jit(solution)/shard_map/ppermute | solution.py:369
  6.2 1.0 %collective-permute-start.2 = (bf16[48,128]{1,0:T(8,128)(2,1)S(1)}, bf16[48,128]{1,0:T(8,128)(2,1)S(1)}, u32[]{:S(2)}, u32[]{:S(2)}) collective-permute-start(bf16[48,128]{1,0:T(8,128)(2,1)S(1)} %get-tuple-element.22), channel_id=1, source_target_pairs={{0,4},{2,6},{4,0},{6,2},{1,5},{3,7},{5,1},{7,3},{8,12},{10,14},{12... | collective-permute-start | bytes 36872 | tf_op jit(solution)/shard_map/ppermute | solution.py:369
  7.2 1.4 %collective-permute-done.1.refs_2_ = bf16[48,128]{1,0:T(8,128)(2,1)S(1)} collective-permute-done((bf16[48,128]{1,0:T(8,128)(2,1)S(1)}, bf16[48,128]{1,0:T(8,128)(2,1)S(1)}, u32[]{:S(2)}, u32[]{:S(2)}) %collective-permute-start.1) | collective-permute-done | bytes 12320 | tf_op jit(solution)/shard_map/ppermute | solution.py:369
  8.6 2.3 %collective-permute-done.2.refs_3_ = bf16[48,128]{1,0:T(8,128)(2,1)S(1)} collective-permute-done((bf16[48,128]{1,0:T(8,128)(2,1)S(1)}, bf16[48,128]{1,0:T(8,128)(2,1)S(1)}, u32[]{:S(2)}, u32[]{:S(2)}) %collective-permute-start.2) | collective-permute-done | bytes 12320 | tf_op jit(solution)/shard_map/ppermute | solution.py:369
  10.8 0.0 collective-permute-done.refs_1_
  10.8 1.7 %collective-permute-start.3 = (bf16[704,128]{1,0:T(8,128)(2,1)S(1)}, bf16[704,128]{1,0:T(8,128)(2,1)S(1)}, u32[]{:S(2)}, u32[]{:S(2)}) collective-permute-start(bf16[704,128]{1,0:T(8,128)(2,1)S(1)} %join.1.refs_0_.refs_1_.packed), channel_id=1, source_target_pairs={{0,8},{8,0},{16,24},{24,16},{1,9},{9,1},{17,25},{25,17},{2,10},{10... | collective-permute-start | bytes 540680 | tf_op jit(solution)/shard_map/ppermute | solution.py:250
  12.6 1.5 %collective-permute-start.4 = (bf16[704,128]{1,0:T(8,128)(2,1)S(1)}, bf16[704,128]{1,0:T(8,128)(2,1)S(1)}, u32[]{:S(2)}, u32[]{:S(2)}) collective-permute-start(bf16[704,128]{1,0:T(8,128)(2,1)S(1)} %join.1.refs_0_.refs_1_.packed), channel_id=1, source_target_pairs={{0,16},{8,24},{16,0},{24,8},{1,17},{9,25},{17,1},{25,9},{2,18},{10... | collective-permute-start | bytes 540680 | tf_op jit(solution)/shard_map/ppermute | solution.py:250
  14.1 0.3 %collective-permute-start.5 = (bf16[704,128]{1,0:T(8,128)(2,1)S(1)}, bf16[704,128]{1,0:T(8,128)(2,1)S(1)}, u32[]{:S(2)}, u32[]{:S(2)}) collective-permute-start(bf16[704,128]{1,0:T(8,128)(2,1)S(1)} %join.1.refs_0_.refs_1_.packed), channel_id=1, source_target_pairs={{0,24},{8,16},{16,8},{24,0},{1,25},{9,17},{17,9},{25,1},{2,26},{10... | collective-permute-start | bytes 540680 | tf_op jit(solution)/shard_map/ppermute | solution.py:250
  14.4 1.4 %grid.3.refs_0_ = f32[8,128,256]{2,1,0:T(8,128)S(1)} custom-call(bf16[704,128]{1,0:T(8,128)(2,1)S(1)} %join.1.refs_0_.refs_1_.packed, bf16[704,128]{1,0:T(8,128)(2,1)S(1)} %join.1.refs_0_.refs_1_.packed), custom_call_target="tpu_custom_call" | custom-call | flops 1000000000 | bytes 1000000 | tf_op jit(solution)/shard_map/grid/pallas_call | solution.py:382
  15.9 2.3 %collective-permute-done.3.refs_1_ = bf16[704,128]{1,0:T(8,128)(2,1)S(1)} collective-permute-done((bf16[704,128]{1,0:T(8,128)(2,1)S(1)}, bf16[704,128]{1,0:T(8,128)(2,1)S(1)}, u32[]{:S(2)}, u32[]{:S(2)}) %collective-permute-start.3) | collective-permute-done | bytes 180256 | tf_op jit(solution)/shard_map/ppermute | solution.py:250
  18.2 3.2 %collective-permute-done.4.refs_2_ = bf16[704,128]{1,0:T(8,128)(2,1)S(1)} collective-permute-done((bf16[704,128]{1,0:T(8,128)(2,1)S(1)}, bf16[704,128]{1,0:T(8,128)(2,1)S(1)}, u32[]{:S(2)}, u32[]{:S(2)}) %collective-permute-start.4) | collective-permute-done | bytes 180256 | tf_op jit(solution)/shard_map/ppermute | solution.py:250
  21.3 2.2 %grid.4.refs_1_ = f32[8,128,256]{2,1,0:T(8,128)S(1)} custom-call(bf16[704,128]{1,0:T(8,128)(2,1)S(1)} %join.1.refs_0_.refs_1_.packed, bf16[704,128]{1,0:T(8,128)(2,1)S(1)} %collective-permute-done.3.refs_1_, bf16[704,128]{1,0:T(8,128)(2,1)S(1)} %collective-permute-done.4.refs_2_), custom_call_target="tpu_custom_call" | custom-call | flops 2000000000 | bytes 1000000 | tf_op jit(solution)/shard_map/grid/pallas_call | solution.py:382
  23.5 0.0 collective-permute-done.5.refs_3_.refs_1_
  23.6 0.1 collective-permute-start.6
  23.7 1.3 %grid.5.refs_2_ = f32[8,128,256]{2,1,0:T(8,128)S(1)} custom-call(bf16[704,128]{1,0:T(8,128)(2,1)S(1)} %join.1.refs_0_.refs_1_.packed, bf16[704,128]{1,0:T(8,128)(2,1)S(1)} %collective-permute-done.5.refs_3_.refs_1_), custom_call_target="tpu_custom_call" | custom-call | flops 1000000000 | bytes 1000000 | tf_op jit(solution)/shard_map/grid/pallas_call | solution.py:382
  25.0 0.6 %collective-permute-done.6.theirs = bf16[2048,128]{1,0:T(8,128)(2,1)S(1)} collective-permute-done((bf16[2048,128]{1,0:T(8,128)(2,1)S(1)}, bf16[2048,128]{1,0:T(8,128)(2,1)S(1)}, u32[]{:S(2)}, u32[]{:S(2)}) %collective-permute-start.6) | collective-permute-done | bytes 524320 | tf_op jit(solution)/shard_map/ppermute | solution.py:406
  25.6 1.2 %apply_tables.1 = (f32[64,256]{1,0:T(8,128)S(1)}, f32[64,256]{1,0:T(8,128)S(1)}) custom-call(bf16[704,128]{1,0:T(8,128)(2,1)S(1)} %join.1.refs_0_.refs_1_.packed, bf16[2048,128]{1,0:T(8,128)(2,1)S(1)} %collect.1.ours, bf16[2048,128]{1,0:T(8,128)(2,1)S(1)} %collective-permute-done.6.theirs, f32[8,128,256]{2,1,0:T(8,128)S(1)} %grid.3.refs_0_, ...), custom_call_target="tpu_custom_call" | custom-call | flops 1000000000 | bytes 2000000 | tf_op jit(solution)/shard_map/apply_tables/pallas_call | solution.py:408
  26.8 0.2 collective-permute-start.7
  27.0 1.1 %collective-permute-done.7 = f32[64,256]{1,0:T(8,128)S(1)} collective-permute-done((f32[64,256]{1,0:T(8,128)S(1)}, f32[64,256]{1,0:T(8,128)S(1)}, u32[]{:S(2)}, u32[]{:S(2)}) %collective-permute-start.7) | collective-permute-done | bytes 65568 | tf_op jit(solution)/shard_map/ppermute | solution.py:423
  28.1 0.7 %reshape.19 = f32[1,1,64,2,128]{4,3,2,1,0:T(2,128)} reshape(f32[64,256]{1,0:T(8,128)S(1)} %add.3) | data formatting | bytes 131072 | tf_op jit(solution)/shard_map/reshape | solution.py:424
  (3 shorter events, 0.1 us)
Async XLA Ops:
  1.1 9.8 %collective-permute-start = (bf16[304,128]{1,0:T(8,128)(2,1)S(1)}, bf16[304,128]{1,0:T(8,128)(2,1)S(1)}, u32[]{:S(2)}, u32[]{:S(2)}) collective-permute-start(bf16[304,128]{1,0:T(8,128)(2,1)S(1)} %get-tuple-element.20), channel_id=1, source_target_pairs={{0,2},{2,4},{4,6},{6,0},{1,3},{3,5},{5,7},{7,1},{8,10},{10,12},{12... | collective-permute-start | bytes 233480 | tf_op jit(solution)/shard_map/ppermute | solution.py:369
  4.1 4.4 %collective-permute-start.1 = (bf16[48,128]{1,0:T(8,128)(2,1)S(1)}, bf16[48,128]{1,0:T(8,128)(2,1)S(1)}, u32[]{:S(2)}, u32[]{:S(2)}) collective-permute-start(bf16[48,128]{1,0:T(8,128)(2,1)S(1)} %get-tuple-element.21), channel_id=1, source_target_pairs={{0,6},{2,0},{4,2},{6,4},{1,7},{3,1},{5,3},{7,5},{8,14},{10,8},{12,... | collective-permute-start | bytes 36872 | tf_op jit(solution)/shard_map/ppermute | solution.py:369
  6.2 4.6 %collective-permute-start.2 = (bf16[48,128]{1,0:T(8,128)(2,1)S(1)}, bf16[48,128]{1,0:T(8,128)(2,1)S(1)}, u32[]{:S(2)}, u32[]{:S(2)}) collective-permute-start(bf16[48,128]{1,0:T(8,128)(2,1)S(1)} %get-tuple-element.22), channel_id=1, source_target_pairs={{0,4},{2,6},{4,0},{6,2},{1,5},{3,7},{5,1},{7,3},{8,12},{10,14},{12... | collective-permute-start | bytes 36872 | tf_op jit(solution)/shard_map/ppermute | solution.py:369
  10.8 7.3 %collective-permute-start.3 = (bf16[704,128]{1,0:T(8,128)(2,1)S(1)}, bf16[704,128]{1,0:T(8,128)(2,1)S(1)}, u32[]{:S(2)}, u32[]{:S(2)}) collective-permute-start(bf16[704,128]{1,0:T(8,128)(2,1)S(1)} %join.1.refs_0_.refs_1_.packed), channel_id=1, source_target_pairs={{0,8},{8,0},{16,24},{24,16},{1,9},{9,1},{17,25},{25,17},{2,10},{10... | collective-permute-start | bytes 540680 | tf_op jit(solution)/shard_map/ppermute | solution.py:250
  12.6 8.8 %collective-permute-start.4 = (bf16[704,128]{1,0:T(8,128)(2,1)S(1)}, bf16[704,128]{1,0:T(8,128)(2,1)S(1)}, u32[]{:S(2)}, u32[]{:S(2)}) collective-permute-start(bf16[704,128]{1,0:T(8,128)(2,1)S(1)} %join.1.refs_0_.refs_1_.packed), channel_id=1, source_target_pairs={{0,16},{8,24},{16,0},{24,8},{1,17},{9,25},{17,1},{25,9},{2,18},{10... | collective-permute-start | bytes 540680 | tf_op jit(solution)/shard_map/ppermute | solution.py:250
  14.1 9.5 %collective-permute-start.5 = (bf16[704,128]{1,0:T(8,128)(2,1)S(1)}, bf16[704,128]{1,0:T(8,128)(2,1)S(1)}, u32[]{:S(2)}, u32[]{:S(2)}) collective-permute-start(bf16[704,128]{1,0:T(8,128)(2,1)S(1)} %join.1.refs_0_.refs_1_.packed), channel_id=1, source_target_pairs={{0,24},{8,16},{16,8},{24,0},{1,25},{9,17},{17,9},{25,1},{2,26},{10... | collective-permute-start | bytes 540680 | tf_op jit(solution)/shard_map/ppermute | solution.py:250
  23.6 2.0 %collective-permute-start.6 = (bf16[2048,128]{1,0:T(8,128)(2,1)S(1)}, bf16[2048,128]{1,0:T(8,128)(2,1)S(1)}, u32[]{:S(2)}, u32[]{:S(2)}) collective-permute-start(bf16[2048,128]{1,0:T(8,128)(2,1)S(1)} %collect.1.ours), channel_id=1, source_target_pairs={{0,1},{1,0},{2,3},{3,2},{4,5},{5,4},{6,7},{7,6},{8,9},{9,8},{10,11... | collective-permute-start | bytes 1572872 | tf_op jit(solution)/shard_map/ppermute | solution.py:406
  26.8 1.3 %collective-permute-start.7 = (f32[64,256]{1,0:T(8,128)S(1)}, f32[64,256]{1,0:T(8,128)S(1)}, u32[]{:S(2)}, u32[]{:S(2)}) collective-permute-start(f32[64,256]{1,0:T(8,128)S(1)} %get-tuple-element.30), channel_id=1, source_target_pairs={{0,1},{1,0},{2,3},{3,2},{4,5},{5,4},{6,7},{7,6},{8,9},{9,8},{10,11... | collective-permute-start | bytes 196616 | tf_op jit(solution)/shard_map/ppermute | solution.py:423

commit v21 on v18

--- a/solution.py
+++ b/solution.py
@@ -13,6 +13,7 @@
 KERNEL_SPREAD = 1.5
 ALPHA = math.sqrt(math.log2(math.e) / (2.0 * KERNEL_SPREAD * KERNEL_SPREAD))
 UNROLL = 4
+REST = 2
 NT = (((1,), (1,)), ((), ()))
 VMEM = pl.BlockSpec(memory_space=pltpu.VMEM)
 HBM = pl.BlockSpec(memory_space=pltpu.HBM)
@@ -134,7 +135,7 @@
 def grid_kernel(sizes, *refs):
     facets, groups, chans, cap, rows, count_here = sizes
     own_ref, grids = refs[0], refs[1 + count_here]
-    order, spots_u, spots_v, turns_real, turns_imag = refs[2 + count_here :]
+    order, spots_u, spots_v, turns_real, turns_imag, cells = refs[2 + count_here :]
     pieces = [
         ref.at[pl.ds(n * rows, rows)] for ref in refs[1 : 1 + count_here] for n in range(groups)
     ]
@@ -200,10 +201,10 @@
     for i in range(UNROLL):
         order[count + i] = devices * cap * slots
 
-    cells = ALPHA * lax.broadcasted_iota(jnp.int32, (SU, SU), 0).astype(jnp.float32)
+    cells[...] = ALPHA * lax.broadcasted_iota(jnp.int32, (SU, SU), 0).astype(jnp.float32)
 
     def profile(spot):
-        apart = spot - cells
+        apart = spot - cells[...]
         return jnp.exp2(-((apart * apart).astype(jnp.bfloat16)))
 
     def tiled(row):
@@ -226,12 +227,17 @@
         right = jnp.concatenate(rights, axis=1)
         return slot, lax.dot_general(right, left, NT, preferred_element_type=jnp.float32)
 
-    def step(k, carry):
-        for slot, part in [one_block(k * UNROLL + i) for i in range(UNROLL)]:
-            grids[slot] += part
-        return carry
-
-    lax.fori_loop(0, lax.div(count + UNROLL - 1, UNROLL), step, 0)
+    def steps(first, blocks, number):
+        def step(k, carry):
+            for slot, part in [one_block(first + k * blocks + i) for i in range(blocks)]:
+                grids[slot] += part
+            return carry
+
+        lax.fori_loop(0, number, step, 0)
+
+    whole = lax.div(count, UNROLL)
+    steps(0, UNROLL, whole)
+    steps(whole * UNROLL, REST, lax.div(lax.rem(count, UNROLL) + REST - 1, REST))
 
 
 def local(kernel, operands, shapes, name):
@@ -393,7 +399,8 @@
             scratch_shapes=[
                 pltpu.SMEM((lines + UNROLL,), jnp.int32),
             ]
-            + [pltpu.VMEM((lines * chans + 8, SU), jnp.float32)] * 4,
+            + [pltpu.VMEM((lines * chans + 8, SU), jnp.float32)] * 4
+            + [pltpu.VMEM((SU, SU), jnp.float32)],
             compiler_params=PARAMS,
             cost_estimate=pl.CostEstimate(
                 flops=len(some) * 1_000_000_000,

time: 28 us -> 27.8 us (level); the launches traced: 28.1 us -> 27.4 us
  Pallas kernels: 8.12 us -> 7.66 us
    pallas_call x3, Pallas kernels: 5.76 us -> 5.3 us  [grid(): pl.pallas_call(functools.partial(grid_kernel, (facets, groups, chans, cap...]
    ppermute x4, waiting for transfers between devices: 1.4 us -> 1.11 us  [exchange(): lax.ppermute(value, axis, [(n, n ^ shift) for n in range(lax.axis_size(ax...]
  transfers between devices with their start and end apart: 9 -> 9, of which waited for: 5 -> 5; matrix products, arithmetic and copies ran while one was open for 0% -> 0% of each run, Pallas kernels for 21% -> 19%
where the time goes in v21:
time: 27.8 us; the launch traced here: 27.4 us
  starting transfers between devices  12.5 us (45%)
  Pallas kernels  7.66 us (28%)
  waiting for transfers between devices  6.48 us (23%)
  local copies, waits for them, and re-layouts  0.66 us (2%)
    ppermute x4, starting transfers between devices, exchange(): lax.ppermute(value, axis, [(n, n ^ shift) for n in range(lax.axis_size(ax...  6.16 us
    ppermute x3, starting transfers between devices, body(): lax.ppermute(pieces[shift], 'bl', [(g, (g + shift) % groups) for g in ran...  6.12 us
    pallas_call x3, Pallas kernels, grid(): pl.pallas_call(functools.partial(grid_kernel, (facets, groups, chans, cap...  5.3 us
    ppermute x3, waiting for transfers between devices, body(): lax.ppermute(pieces[shift], 'bl', [(g, (g + shift) % groups) for g in ran...  3.65 us
    pallas_call x1, Pallas kernels, body(): pl.pallas_call(functools.partial(table_kernel, (slots, meta_row), norm),...  1.21 us
    ppermute x1, waiting for transfers between devices, body(): lax.ppermute(other, 'chan', [(c, 1 - c) for c in range(chan_count)])  1.12 us
    ppermute x4, waiting for transfers between devices, exchange(): lax.ppermute(value, axis, [(n, n ^ shift) for n in range(lax.axis_size(ax...  1.11 us
    pallas_call x1, Pallas kernels, body(): pl.pallas_call(functools.partial(sort_kernel, (groups, held, chans, cap,...  1.06 us
  transfers between devices with their start and end apart: 9, of which 5 were waited for; matrix products, arithmetic and copies ran while one was open for 0% of the time, Pallas kernels for 19%

profile of v21, /device:TPU:0, one launch (start us, length us, event | category | flops | bytes accessed | tf_op | source)
XLA Modules:
  0.0 27.4 jit_solution(12665428491978268221)
XLA Ops:
  0.0 1.1 %sort_blocks.1 = (bf16[48,128]{1,0:T(8,128)(2,1)S(1)}, bf16[304,128]{1,0:T(8,128)(2,1)S(1)}, bf16[48,128]{1,0:T(8,128)(2,1)S(1)}, bf16[48,128]{1,0:T(8,128)(2,1)S(1)}, bf16[256,128]{1,0:T(8,128)(2,1)S(1)}) custom-call(s32[1,8]{1,0:T(1,128)} %bitcast.12, s32[1,8]{1,0:T(1,128)} %bitcast.13, bf16[64,128]{1,0:T(8,128)(2,1)} %bitcast.8, bf16[16,128]{1,0:T(8,128)(2,1)} %bitcast.9, ...), custom_call_target="tpu_custom_call" | custom-call | flops 100000 | bytes 100000 | tf_op jit(solution)/shard_map/sort_blocks/pallas_call | solution.py:333
  1.1 3.1 %collective-permute-start = (bf16[304,128]{1,0:T(8,128)(2,1)S(1)}, bf16[304,128]{1,0:T(8,128)(2,1)S(1)}, u32[]{:S(2)}, u32[]{:S(2)}) collective-permute-start(bf16[304,128]{1,0:T(8,128)(2,1)S(1)} %get-tuple-element.22), channel_id=1, source_target_pairs={{0,2},{2,4},{4,6},{6,0},{1,3},{3,5},{5,7},{7,1},{8,10},{10,12},{12... | collective-permute-start | bytes 233480 | tf_op jit(solution)/shard_map/ppermute | solution.py:375
  4.1 2.1 %collective-permute-start.1 = (bf16[48,128]{1,0:T(8,128)(2,1)S(1)}, bf16[48,128]{1,0:T(8,128)(2,1)S(1)}, u32[]{:S(2)}, u32[]{:S(2)}) collective-permute-start(bf16[48,128]{1,0:T(8,128)(2,1)S(1)} %get-tuple-element.23), channel_id=1, source_target_pairs={{0,6},{2,0},{4,2},{6,4},{1,7},{3,1},{5,3},{7,5},{8,14},{10,8},{12,... | collective-permute-start | bytes 36872 | tf_op jit(solution)/shard_map/ppermute | solution.py:375
  6.2 0.9 %collective-permute-start.2 = (bf16[48,128]{1,0:T(8,128)(2,1)S(1)}, bf16[48,128]{1,0:T(8,128)(2,1)S(1)}, u32[]{:S(2)}, u32[]{:S(2)}) collective-permute-start(bf16[48,128]{1,0:T(8,128)(2,1)S(1)} %get-tuple-element.24), channel_id=1, source_target_pairs={{0,4},{2,6},{4,0},{6,2},{1,5},{3,7},{5,1},{7,3},{8,12},{10,14},{12... | collective-permute-start | bytes 36872 | tf_op jit(solution)/shard_map/ppermute | solution.py:375
  7.2 1.4 %collective-permute-done.1.refs_2_ = bf16[48,128]{1,0:T(8,128)(2,1)S(1)} collective-permute-done((bf16[48,128]{1,0:T(8,128)(2,1)S(1)}, bf16[48,128]{1,0:T(8,128)(2,1)S(1)}, u32[]{:S(2)}, u32[]{:S(2)}) %collective-permute-start.1) | collective-permute-done | bytes 12320 | tf_op jit(solution)/shard_map/ppermute | solution.py:375
  8.6 2.3 %collective-permute-done.2.refs_3_ = bf16[48,128]{1,0:T(8,128)(2,1)S(1)} collective-permute-done((bf16[48,128]{1,0:T(8,128)(2,1)S(1)}, bf16[48,128]{1,0:T(8,128)(2,1)S(1)}, u32[]{:S(2)}, u32[]{:S(2)}) %collective-permute-start.2) | collective-permute-done | bytes 12320 | tf_op jit(solution)/shard_map/ppermute | solution.py:375
  10.8 0.0 collective-permute-done.refs_1_
  10.9 1.7 %collective-permute-start.3 = (bf16[704,128]{1,0:T(8,128)(2,1)S(1)}, bf16[704,128]{1,0:T(8,128)(2,1)S(1)}, u32[]{:S(2)}, u32[]{:S(2)}) collective-permute-start(bf16[704,128]{1,0:T(8,128)(2,1)S(1)} %get-tuple-element.27), channel_id=1, source_target_pairs={{0,8},{8,0},{16,24},{24,16},{1,9},{9,1},{17,25},{25,17},{2,10},{10... | collective-permute-start | bytes 540680 | tf_op jit(solution)/shard_map/ppermute | solution.py:256
  12.6 1.5 %collective-permute-start.4 = (bf16[704,128]{1,0:T(8,128)(2,1)S(1)}, bf16[704,128]{1,0:T(8,128)(2,1)S(1)}, u32[]{:S(2)}, u32[]{:S(2)}) collective-permute-start(bf16[704,128]{1,0:T(8,128)(2,1)S(1)} %get-tuple-element.27), channel_id=1, source_target_pairs={{0,16},{8,24},{16,0},{24,8},{1,17},{9,25},{17,1},{25,9},{2,18},{10... | collective-permute-start | bytes 540680 | tf_op jit(solution)/shard_map/ppermute | solution.py:256
  14.1 0.3 %collective-permute-start.5 = (bf16[192,128]{1,0:T(8,128)(2,1)S(1)}, bf16[192,128]{1,0:T(8,128)(2,1)S(1)}, u32[]{:S(2)}, u32[]{:S(2)}) collective-permute-start(bf16[192,128]{1,0:T(8,128)(2,1)S(1)} %get-tuple-element.25.refs_0_.refs_1_.packed), channel_id=1, source_target_pairs={{0,24},{8,16},{16,8},{24,0},{1,25},{9,17},{17,9},{25,1},{2,26},{10... | collective-permute-start | bytes 147464 | tf_op jit(solution)/shard_map/ppermute | solution.py:256
  14.4 2.6 %collective-permute-start.6 = (bf16[512,128]{1,0:T(8,128)(2,1)S(1)}, bf16[512,128]{1,0:T(8,128)(2,1)S(1)}, u32[]{:S(2)}, u32[]{:S(2)}) collective-permute-start(bf16[512,128]{1,0:T(8,128)(2,1)S(1)} %get-tuple-element.26.tables), channel_id=1, source_target_pairs={{0,24},{8,16},{16,8},{24,0},{1,25},{9,17},{17,9},{25,1},{2,26},{10... | collective-permute-start | bytes 393224 | tf_op jit(solution)/shard_map/ppermute | solution.py:256
  17.0 1.6 %grid.3.refs_0_ = f32[8,128,256]{2,1,0:T(8,128)S(1)} custom-call(bf16[192,128]{1,0:T(8,128)(2,1)S(1)} %get-tuple-element.25.refs_0_.refs_1_.packed, bf16[192,128]{1,0:T(8,128)(2,1)S(1)} %get-tuple-element.25.refs_0_.refs_1_.packed), custom_call_target="tpu_custom_call" | custom-call | flops 1000000000 | bytes 1000000 | tf_op jit(solution)/shard_map/grid/pallas_call | solution.py:394
  18.7 1.1 %collective-permute-done.5.refs_1_ = bf16[192,128]{1,0:T(8,128)(2,1)S(1)} collective-permute-done((bf16[192,128]{1,0:T(8,128)(2,1)S(1)}, bf16[192,128]{1,0:T(8,128)(2,1)S(1)}, u32[]{:S(2)}, u32[]{:S(2)}) %collective-permute-start.5) | collective-permute-done | bytes 49184 | tf_op jit(solution)/shard_map/ppermute | solution.py:256
  19.8 0.0 collective-permute-done.3.refs_2_.refs_0_
  19.8 2.4 %grid.4.refs_1_ = f32[8,128,256]{2,1,0:T(8,128)S(1)} custom-call(bf16[192,128]{1,0:T(8,128)(2,1)S(1)} %get-tuple-element.25.refs_0_.refs_1_.packed, bf16[192,128]{1,0:T(8,128)(2,1)S(1)} %collective-permute-done.5.refs_1_, bf16[704,128]{1,0:T(8,128)(2,1)S(1)} %collective-permute-done.3.refs_2_.refs_0_), custom_call_target="tpu_custom_call" | custom-call | flops 2000000000 | bytes 1000000 | tf_op jit(solution)/shard_map/grid/pallas_call | solution.py:394
  22.2 0.0 collective-permute-done.6.refs_2_
  22.2 0.0 collective-permute-done.4.refs_1_
  22.3 0.1 collective-permute-start.7
  22.3 1.3 %grid.5.refs_2_ = f32[8,128,256]{2,1,0:T(8,128)S(1)} custom-call(bf16[192,128]{1,0:T(8,128)(2,1)S(1)} %get-tuple-element.25.refs_0_.refs_1_.packed, bf16[704,128]{1,0:T(8,128)(2,1)S(1)} %collective-permute-done.4.refs_1_), custom_call_target="tpu_custom_call" | custom-call | flops 1000000000 | bytes 1000000 | tf_op jit(solution)/shard_map/grid/pallas_call | solution.py:394
  23.6 0.6 %collective-permute-done.7.theirs = bf16[2048,128]{1,0:T(8,128)(2,1)S(1)} collective-permute-done((bf16[2048,128]{1,0:T(8,128)(2,1)S(1)}, bf16[2048,128]{1,0:T(8,128)(2,1)S(1)}, u32[]{:S(2)}, u32[]{:S(2)}) %collective-permute-start.7) | collective-permute-done | bytes 524320 | tf_op jit(solution)/shard_map/ppermute | solution.py:421
  24.2 1.2 %apply_tables.1 = (f32[64,256]{1,0:T(8,128)S(1)}, f32[64,256]{1,0:T(8,128)S(1)}) custom-call(bf16[192,128]{1,0:T(8,128)(2,1)S(1)} %get-tuple-element.25.refs_0_.refs_1_.packed, bf16[2048,128]{1,0:T(8,128)(2,1)S(1)} %collect.1.ours, bf16[2048,128]{1,0:T(8,128)(2,1)S(1)} %collective-permute-done.7.theirs, f32[8,128,256]{2,1,0:T(8,128)S(1)} %grid.3.refs_0_, ...), custom_call_target="tpu_custom_call" | custom-call | flops 1000000000 | bytes 2000000 | tf_op jit(solution)/shard_map/apply_tables/pallas_call | solution.py:423
  25.4 0.2 collective-permute-start.8
  25.6 1.1 %collective-permute-done.8 = f32[64,256]{1,0:T(8,128)S(1)} collective-permute-done((f32[64,256]{1,0:T(8,128)S(1)}, f32[64,256]{1,0:T(8,128)S(1)}, u32[]{:S(2)}, u32[]{:S(2)}) %collective-permute-start.8) | collective-permute-done | bytes 65568 | tf_op jit(solution)/shard_map/ppermute | solution.py:438
  26.8 0.7 %reshape.19 = f32[1,1,64,2,128]{4,3,2,1,0:T(2,128)} reshape(f32[64,256]{1,0:T(8,128)S(1)} %add.3) | data formatting | bytes 131072 | tf_op jit(solution)/shard_map/reshape | solution.py:439
  (3 shorter events, 0.1 us)
Async XLA Ops:
  1.1 9.8 %collective-permute-start = (bf16[304,128]{1,0:T(8,128)(2,1)S(1)}, bf16[304,128]{1,0:T(8,128)(2,1)S(1)}, u32[]{:S(2)}, u32[]{:S(2)}) collective-permute-start(bf16[304,128]{1,0:T(8,128)(2,1)S(1)} %get-tuple-element.22), channel_id=1, source_target_pairs={{0,2},{2,4},{4,6},{6,0},{1,3},{3,5},{5,7},{7,1},{8,10},{10,12},{12... | collective-permute-start | bytes 233480 | tf_op jit(solution)/shard_map/ppermute | solution.py:375
  4.1 4.4 %collective-permute-start.1 = (bf16[48,128]{1,0:T(8,128)(2,1)S(1)}, bf16[48,128]{1,0:T(8,128)(2,1)S(1)}, u32[]{:S(2)}, u32[]{:S(2)}) collective-permute-start(bf16[48,128]{1,0:T(8,128)(2,1)S(1)} %get-tuple-element.23), channel_id=1, source_target_pairs={{0,6},{2,0},{4,2},{6,4},{1,7},{3,1},{5,3},{7,5},{8,14},{10,8},{12,... | collective-permute-start | bytes 36872 | tf_op jit(solution)/shard_map/ppermute | solution.py:375
  6.2 4.6 %collective-permute-start.2 = (bf16[48,128]{1,0:T(8,128)(2,1)S(1)}, bf16[48,128]{1,0:T(8,128)(2,1)S(1)}, u32[]{:S(2)}, u32[]{:S(2)}) collective-permute-start(bf16[48,128]{1,0:T(8,128)(2,1)S(1)} %get-tuple-element.24), channel_id=1, source_target_pairs={{0,4},{2,6},{4,0},{6,2},{1,5},{3,7},{5,1},{7,3},{8,12},{10,14},{12... | collective-permute-start | bytes 36872 | tf_op jit(solution)/shard_map/ppermute | solution.py:375
  10.9 8.9 %collective-permute-start.3 = (bf16[704,128]{1,0:T(8,128)(2,1)S(1)}, bf16[704,128]{1,0:T(8,128)(2,1)S(1)}, u32[]{:S(2)}, u32[]{:S(2)}) collective-permute-start(bf16[704,128]{1,0:T(8,128)(2,1)S(1)} %get-tuple-element.27), channel_id=1, source_target_pairs={{0,8},{8,0},{16,24},{24,16},{1,9},{9,1},{17,25},{25,17},{2,10},{10... | collective-permute-start | bytes 540680 | tf_op jit(solution)/shard_map/ppermute | solution.py:256
  12.6 9.6 %collective-permute-start.4 = (bf16[704,128]{1,0:T(8,128)(2,1)S(1)}, bf16[704,128]{1,0:T(8,128)(2,1)S(1)}, u32[]{:S(2)}, u32[]{:S(2)}) collective-permute-start(bf16[704,128]{1,0:T(8,128)(2,1)S(1)} %get-tuple-element.27), channel_id=1, source_target_pairs={{0,16},{8,24},{16,0},{24,8},{1,17},{9,25},{17,1},{25,9},{2,18},{10... | collective-permute-start | bytes 540680 | tf_op jit(solution)/shard_map/ppermute | solution.py:256
  14.1 5.7 %collective-permute-start.5 = (bf16[192,128]{1,0:T(8,128)(2,1)S(1)}, bf16[192,128]{1,0:T(8,128)(2,1)S(1)}, u32[]{:S(2)}, u32[]{:S(2)}) collective-permute-start(bf16[192,128]{1,0:T(8,128)(2,1)S(1)} %get-tuple-element.25.refs_0_.refs_1_.packed), channel_id=1, source_target_pairs={{0,24},{8,16},{16,8},{24,0},{1,25},{9,17},{17,9},{25,1},{2,26},{10... | collective-permute-start | bytes 147464 | tf_op jit(solution)/shard_map/ppermute | solution.py:256
  14.4 7.7 %collective-permute-start.6 = (bf16[512,128]{1,0:T(8,128)(2,1)S(1)}, bf16[512,128]{1,0:T(8,128)(2,1)S(1)}, u32[]{:S(2)}, u32[]{:S(2)}) collective-permute-start(bf16[512,128]{1,0:T(8,128)(2,1)S(1)} %get-tuple-element.26.tables), channel_id=1, source_target_pairs={{0,24},{8,16},{16,8},{24,0},{1,25},{9,17},{17,9},{25,1},{2,26},{10... | collective-permute-start | bytes 393224 | tf_op jit(solution)/shard_map/ppermute | solution.py:256
  22.3 2.0 %collective-permute-start.7 = (bf16[2048,128]{1,0:T(8,128)(2,1)S(1)}, bf16[2048,128]{1,0:T(8,128)(2,1)S(1)}, u32[]{:S(2)}, u32[]{:S(2)}) collective-permute-start(bf16[2048,128]{1,0:T(8,128)(2,1)S(1)} %collect.1.ours), channel_id=1, source_target_pairs={{0,1},{1,0},{2,3},{3,2},{4,5},{5,4},{6,7},{7,6},{8,9},{9,8},{10,11... | collective-permute-start | bytes 1572872 | tf_op jit(solution)/shard_map/ppermute | solution.py:421
  25.4 1.3 %collective-permute-start.8 = (f32[64,256]{1,0:T(8,128)S(1)}, f32[64,256]{1,0:T(8,128)S(1)}, u32[]{:S(2)}, u32[]{:S(2)}) collective-permute-start(f32[64,256]{1,0:T(8,128)S(1)} %get-tuple-element.34), channel_id=1, source_target_pairs={{0,1},{1,0},{2,3},{3,2},{4,5},{5,4},{6,7},{7,6},{8,9},{9,8},{10,11... | collective-permute-start | bytes 196616 | tf_op jit(solution)/shard_map/ppermute | solution.py:438

commit v22 on v19

--- a/solution.py
+++ b/solution.py
@@ -113,17 +113,24 @@
 
 
 def join_kernel(rows, half, *refs):
-    *pieces, joined = refs
+    *pieces, joined, short = refs
+    at = len(pieces) * rows
     for n, ref in enumerate(pieces):
-        joined[n * rows : (n + 1) * rows, :] = ref[:rows, :]
-    at = len(pieces) * rows
-    joined[at : at + 2 * SU, :] = half[...]
-    joined[at + 2 * SU :, :] = pieces[1][rows:, :]
+        piece = ref[:rows, :]
+        joined[n * rows : (n + 1) * rows, :] = piece
+        short[n * rows : (n + 1) * rows, :] = piece
+    table = pieces[1][rows:, :]
+    joined[at : at + 2 * SU, :] = table
+    short[at:, :] = table
+    joined[at + 2 * SU :, :] = half[...]
 
 
 def collect_kernel(skip, *refs):
-    for n, ref in enumerate(refs[:-1]):
-        refs[-1][n * 4 * SU : (n + 1) * 4 * SU, :] = ref[skip:, :]
+    *joined, last_own, out_ref = refs
+    for n, ref in enumerate(joined):
+        count = ref.shape[0] - skip
+        out_ref[n * 4 * SU : n * 4 * SU + count, :] = ref[skip:, :]
+    out_ref[out_ref.shape[0] - 2 * SU :, :] = last_own[lax.axis_index("chan")]
 
 
 def grid_kernel(sizes, *refs):
@@ -149,7 +156,7 @@
     for d in range(devices):
         meta = pieces[d][tail : tail + 16, :].astype(jnp.float32)
         plane = meta[meta_row - tail : meta_row - tail + 1].astype(jnp.int32) - 1
-        set_id = jnp.where(lax.rem(plane, groups) == group, 0, 1)
+        set_id = jnp.where(lax.rem(plane, groups) == group, 1, 0)
         code = (d * cap + lane) * slots + 2 * (lax.div(plane, groups) ^ facet) + set_id
         codes.append(jnp.where(plane >= 0, code, -1))
     grids[...] = jnp.zeros_like(grids)
@@ -234,12 +241,12 @@
     steps(whole * UNROLL, REST, lax.div(lax.rem(count, UNROLL) + REST - 1, REST))
 
 
-def local(kernel, operands, shape, name):
+def local(kernel, operands, shapes, name):
     return pl.pallas_call(
         kernel,
-        out_shape=jax.ShapeDtypeStruct(shape, jnp.bfloat16),
+        out_shape=[jax.ShapeDtypeStruct(shape, jnp.bfloat16) for shape in shapes],
         in_specs=[VMEM] * len(operands),
-        out_specs=VMEM,
+        out_specs=[VMEM] * len(shapes),
         compiler_params=PARAMS,
         cost_estimate=pl.CostEstimate(flops=0, bytes_accessed=400_000, transcendentals=0),
         name=name,
@@ -370,13 +377,20 @@
         for shift in [1, *range(groups - 1, 1, -1)]
     ]
     vis_rows = groups * rows
-    joined = local(
+    last_own = exchange(own_table, "facet", facets - 1)
+    arrived, last_own = lax.optimization_barrier((arrived, last_own))
+    joined, short = local(
         functools.partial(join_kernel, rows),
         [half, pieces[0], *arrived],
-        (vis_rows + 4 * SU, SU),
+        [(vis_rows + 4 * SU, SU), (vis_rows + 2 * SU, SU)],
         "join",
     )
-    blocks = [joined] + [exchange(joined, "facet", shift) for shift in range(1, facets)]
+    blocks = (
+        [joined]
+        + [exchange(joined, "facet", shift) for shift in range(1, facets - 1)]
+        + [exchange(short, "facet", facets - 1)]
+    )
+
     def grid(some):
         lines = len(some) * groups * cap
         return pl.pallas_call(
@@ -400,8 +414,11 @@
 
     grids = [grid(blocks[:1]), grid(blocks[-1:])]
     blocks, grids = lax.optimization_barrier((blocks, grids))
-    fetched = local(
-        functools.partial(collect_kernel, vis_rows), blocks, (facets * 4 * SU, SU), "collect"
+    (fetched,) = local(
+        functools.partial(collect_kernel, vis_rows),
+        [*blocks, last_own],
+        [(facets * 4 * SU, SU)],
+        "collect",
     )
     swapped = lax.ppermute(fetched, "chan", [(c, 1 - c) for c in range(chan_count)])
     grids.append(grid(blocks[1:-1]))

time: 27 us -> 27.2 us (level)
  starting transfers between devices: 10.3 us -> 12.7 us
  waiting for transfers between devices: 7.82 us -> 6.46 us
  Pallas kernels: 7.95 us -> 6.93 us
    ppermute x3 -> x4, starting transfers between devices: 3.55 us -> 7.45 us  [exchange(): lax.ppermute(value, axis, [(n, n ^ shift) for n in range(lax.axis_size(ax...]
    ppermute x3 -> x4, waiting for transfers between devices: 3.26 us -> 1.73 us  [exchange(): lax.ppermute(value, axis, [(n, n ^ shift) for n in range(lax.axis_size(ax...]
    ppermute x3, starting transfers between devices: 6.12 us -> 4.67 us  [body(): lax.ppermute(pieces[shift], 'bl', [(g, (g + shift) % groups) for g in ran...]
    pallas_call x3, Pallas kernels: 5.64 us -> 4.59 us  [grid(): pl.pallas_call(functools.partial(grid_kernel, (facets, groups, chans, cap...]
  transfers between devices with their start and end apart: 8 -> 9, of which waited for: 5 -> 5; matrix products, arithmetic and copies ran while one was open for 0% -> 0% of each run, Pallas kernels for 21% -> 21%
where the time goes in v22:
time: 27.2 us; the launch traced here: 26.9 us
  starting transfers between devices  12.7 us (47%)
  Pallas kernels  6.93 us (25%)
  waiting for transfers between devices  6.46 us (24%)
  local copies, waits for them, and re-layouts  0.66 us (2%)
    ppermute x4, starting transfers between devices, exchange(): lax.ppermute(value, axis, [(n, n ^ shift) for n in range(lax.axis_size(ax...  7.45 us
    ppermute x3, starting transfers between devices, body(): lax.ppermute(pieces[shift], 'bl', [(g, (g + shift) % groups) for g in ran...  4.67 us
    pallas_call x3, Pallas kernels, grid(): pl.pallas_call(functools.partial(grid_kernel, (facets, groups, chans, cap...  4.59 us
    ppermute x3, waiting for transfers between devices, body(): lax.ppermute(pieces[shift], 'bl', [(g, (g + shift) % groups) for g in ran...  3.8 us
    ppermute x4, waiting for transfers between devices, exchange(): lax.ppermute(value, axis, [(n, n ^ shift) for n in range(lax.axis_size(ax...  1.73 us
    pallas_call x1, Pallas kernels, body(): pl.pallas_call(functools.partial(table_kernel, (slots, meta_row), norm),...  1.21 us
    pallas_call x1, Pallas kernels, body(): pl.pallas_call(functools.partial(sort_kernel, (groups, held, chans, cap,...  1.06 us
    ppermute x1, waiting for transfers between devices, body(): lax.ppermute(other, 'chan', [(c, 1 - c) for c in range(chan_count)])  0.9 us
  transfers between devices with their start and end apart: 9, of which 5 were waited for; matrix products, arithmetic and copies ran while one was open for 0% of the time, Pallas kernels for 21%

profile of v22, /device:TPU:0, one launch (start us, length us, event | category | flops | bytes accessed | tf_op | source)
XLA Modules:
  0.0 26.9 jit_solution(16480837069185090168)
XLA Ops:
  0.0 3.9 %collective-permute-start.3 = (bf16[2,256,128]{2,1,0:T(8,128)(2,1)}, bf16[2,256,128]{2,1,0:T(8,128)(2,1)S(1)}, u32[]{:S(2)}, u32[]{:S(2)}) collective-permute-start(bf16[2,256,128]{2,1,0:T(8,128)(2,1)} %bitcast.7), channel_id=1, source_target_pairs={{0,24},{8,16},{16,8},{24,0},{1,25},{9,17},{17,9},{25,1},{2,26},{10... | collective-permute-start | bytes 393224 | tf_op jit(solution)/shard_map/ppermute | solution.py:257
  3.9 1.1 %sort_blocks.1 = (bf16[48,128]{1,0:T(8,128)(2,1)S(1)}, bf16[304,128]{1,0:T(8,128)(2,1)S(1)}, bf16[48,128]{1,0:T(8,128)(2,1)S(1)}, bf16[48,128]{1,0:T(8,128)(2,1)S(1)}, bf16[256,128]{1,0:T(8,128)(2,1)S(1)}) custom-call(s32[1,8]{1,0:T(1,128)} %bitcast.13, s32[1,8]{1,0:T(1,128)} %bitcast.14, bf16[64,128]{1,0:T(8,128)(2,1)} %bitcast.9, ...), custom_call_target="tpu_custom_call" | custom-call | flops 100000 | bytes 100000 | tf_op jit(solution)/shard_map/sort_blocks/pallas_call | solution.py:334
  5.0 1.6 %collective-permute-start = (bf16[304,128]{1,0:T(8,128)(2,1)S(1)}, bf16[304,128]{1,0:T(8,128)(2,1)S(1)}, u32[]{:S(2)}, u32[]{:S(2)}) collective-permute-start(bf16[304,128]{1,0:T(8,128)(2,1)S(1)} %get-tuple-element.26), channel_id=1, source_target_pairs={{0,2},{2,4},{4,6},{6,0},{1,3},{3,5},{5,7},{7,1},{8,10},{10,12},{12... | collective-permute-start | bytes 233480 | tf_op jit(solution)/shard_map/ppermute | solution.py:376
  6.6 2.2 %collective-permute-start.1 = (bf16[48,128]{1,0:T(8,128)(2,1)S(1)}, bf16[48,128]{1,0:T(8,128)(2,1)S(1)}, u32[]{:S(2)}, u32[]{:S(2)}) collective-permute-start(bf16[48,128]{1,0:T(8,128)(2,1)S(1)} %get-tuple-element.27), channel_id=1, source_target_pairs={{0,6},{2,0},{4,2},{6,4},{1,7},{3,1},{5,3},{7,5},{8,14},{10,8},{12,... | collective-permute-start | bytes 36872 | tf_op jit(solution)/shard_map/ppermute | solution.py:376
  8.8 0.8 %collective-permute-start.2 = (bf16[48,128]{1,0:T(8,128)(2,1)S(1)}, bf16[48,128]{1,0:T(8,128)(2,1)S(1)}, u32[]{:S(2)}, u32[]{:S(2)}) collective-permute-start(bf16[48,128]{1,0:T(8,128)(2,1)S(1)} %get-tuple-element.28), channel_id=1, source_target_pairs={{0,4},{2,6},{4,0},{6,2},{1,5},{3,7},{5,1},{7,3},{8,12},{10,14},{12... | collective-permute-start | bytes 36872 | tf_op jit(solution)/shard_map/ppermute | solution.py:376
  9.6 0.7 %collective-permute-done.1.refs_2_ = bf16[48,128]{1,0:T(8,128)(2,1)S(1)} collective-permute-done((bf16[48,128]{1,0:T(8,128)(2,1)S(1)}, bf16[48,128]{1,0:T(8,128)(2,1)S(1)}, u32[]{:S(2)}, u32[]{:S(2)}) %collective-permute-start.1) | collective-permute-done | bytes 12320 | tf_op jit(solution)/shard_map/ppermute | solution.py:376
  10.3 3.1 %collective-permute-done.2.refs_3_ = bf16[48,128]{1,0:T(8,128)(2,1)S(1)} collective-permute-done((bf16[48,128]{1,0:T(8,128)(2,1)S(1)}, bf16[48,128]{1,0:T(8,128)(2,1)S(1)}, u32[]{:S(2)}, u32[]{:S(2)}) %collective-permute-start.2) | collective-permute-done | bytes 12320 | tf_op jit(solution)/shard_map/ppermute | solution.py:376
  13.4 0.0 collective-permute-done.refs_1_
  13.4 0.0 collective-permute-done.3.refs_4_
  13.5 0.4 %collective-permute-start.6 = (bf16[448,128]{1,0:T(8,128)(2,1)S(1)}, bf16[448,128]{1,0:T(8,128)(2,1)S(1)}, u32[]{:S(2)}, u32[]{:S(2)}) collective-permute-start(bf16[448,128]{1,0:T(8,128)(2,1)S(1)} %get-tuple-element.33), channel_id=1, source_target_pairs={{0,24},{8,16},{16,8},{24,0},{1,25},{9,17},{17,9},{25,1},{2,26},{10... | collective-permute-start | bytes 344072 | tf_op jit(solution)/shard_map/ppermute | solution.py:257
  13.9 1.7 %collective-permute-start.4 = (bf16[704,128]{1,0:T(8,128)(2,1)S(1)}, bf16[704,128]{1,0:T(8,128)(2,1)S(1)}, u32[]{:S(2)}, u32[]{:S(2)}) collective-permute-start(bf16[704,128]{1,0:T(8,128)(2,1)S(1)} %get-tuple-element.34.refs_0_.refs_1_.packed), channel_id=1, source_target_pairs={{0,8},{8,0},{16,24},{24,16},{1,9},{9,1},{17,25},{25,17},{2,10},{10... | collective-permute-start | bytes 540680 | tf_op jit(solution)/shard_map/ppermute | solution.py:257
  15.5 1.5 %collective-permute-start.5 = (bf16[704,128]{1,0:T(8,128)(2,1)S(1)}, bf16[704,128]{1,0:T(8,128)(2,1)S(1)}, u32[]{:S(2)}, u32[]{:S(2)}) collective-permute-start(bf16[704,128]{1,0:T(8,128)(2,1)S(1)} %get-tuple-element.34.refs_0_.refs_1_.packed), channel_id=1, source_target_pairs={{0,16},{8,24},{16,0},{24,8},{1,17},{9,25},{17,1},{25,9},{2,18},{10... | collective-permute-start | bytes 540680 | tf_op jit(solution)/shard_map/ppermute | solution.py:257
  17.0 1.4 %grid.3.refs_0_ = f32[8,128,256]{2,1,0:T(8,128)S(1)} custom-call(bf16[704,128]{1,0:T(8,128)(2,1)S(1)} %get-tuple-element.34.refs_0_.refs_1_.packed, bf16[704,128]{1,0:T(8,128)(2,1)S(1)} %get-tuple-element.34.refs_0_.refs_1_.packed), custom_call_target="tpu_custom_call" | custom-call | flops 1000000000 | bytes 1000000 | tf_op jit(solution)/shard_map/grid/pallas_call | solution.py:396
  18.5 1.1 %collective-permute-done.6.refs_1_.refs_3_ = bf16[448,128]{1,0:T(8,128)(2,1)S(1)} collective-permute-done((bf16[448,128]{1,0:T(8,128)(2,1)S(1)}, bf16[448,128]{1,0:T(8,128)(2,1)S(1)}, u32[]{:S(2)}, u32[]{:S(2)}) %collective-permute-start.6) | collective-permute-done | bytes 114720 | tf_op jit(solution)/shard_map/ppermute | solution.py:257
  19.6 1.3 %grid.4.refs_1_ = f32[8,128,256]{2,1,0:T(8,128)S(1)} custom-call(bf16[704,128]{1,0:T(8,128)(2,1)S(1)} %get-tuple-element.34.refs_0_.refs_1_.packed, bf16[448,128]{1,0:T(8,128)(2,1)S(1)} %collective-permute-done.6.refs_1_.refs_3_), custom_call_target="tpu_custom_call" | custom-call | flops 1000000000 | bytes 1000000 | tf_op jit(solution)/shard_map/grid/pallas_call | solution.py:396
  20.9 0.0 collective-permute-done.4.refs_1_
  20.9 0.6 %collective-permute-done.5.refs_2_ = bf16[704,128]{1,0:T(8,128)(2,1)S(1)} collective-permute-done((bf16[704,128]{1,0:T(8,128)(2,1)S(1)}, bf16[704,128]{1,0:T(8,128)(2,1)S(1)}, u32[]{:S(2)}, u32[]{:S(2)}) %collective-permute-start.5) | collective-permute-done | bytes 180256 | tf_op jit(solution)/shard_map/ppermute | solution.py:257
  21.6 0.1 collective-permute-start.7
  21.6 1.9 %grid.5.refs_2_ = f32[8,128,256]{2,1,0:T(8,128)S(1)} custom-call(bf16[704,128]{1,0:T(8,128)(2,1)S(1)} %get-tuple-element.34.refs_0_.refs_1_.packed, bf16[704,128]{1,0:T(8,128)(2,1)S(1)} %collective-permute-done.4.refs_1_, bf16[704,128]{1,0:T(8,128)(2,1)S(1)} %collective-permute-done.5.refs_2_), custom_call_target="tpu_custom_call" | custom-call | flops 2000000000 | bytes 1000000 | tf_op jit(solution)/shard_map/grid/pallas_call | solution.py:396
  23.5 0.0 collective-permute-done.7.theirs
  23.5 1.2 %apply_tables.1 = (f32[64,256]{1,0:T(8,128)S(1)}, f32[64,256]{1,0:T(8,128)S(1)}) custom-call(bf16[704,128]{1,0:T(8,128)(2,1)S(1)} %get-tuple-element.34.refs_0_.refs_1_.packed, bf16[2048,128]{1,0:T(8,128)(2,1)S(1)} %collect.1.ours, bf16[2048,128]{1,0:T(8,128)(2,1)S(1)} %collective-permute-done.7.theirs, f32[8,128,256]{2,1,0:T(8,128)S(1)} %grid.3.refs_0_, ...), custom_call_target="tpu_custom_call" | custom-call | flops 1000000000 | bytes 2000000 | tf_op jit(solution)/shard_map/apply_tables/pallas_call | solution.py:425
  24.7 0.5 %collective-permute-start.8 = (f32[64,256]{1,0:T(8,128)S(1)}, f32[64,256]{1,0:T(8,128)S(1)}, u32[]{:S(2)}, u32[]{:S(2)}) collective-permute-start(f32[64,256]{1,0:T(8,128)S(1)} %get-tuple-element.42), channel_id=1, source_target_pairs={{0,1},{1,0},{2,3},{3,2},{4,5},{5,4},{6,7},{7,6},{8,9},{9,8},{10,11... | collective-permute-start | bytes 196616 | tf_op jit(solution)/shard_map/ppermute | solution.py:440
  25.3 0.9 %collective-permute-done.8 = f32[64,256]{1,0:T(8,128)S(1)} collective-permute-done((f32[64,256]{1,0:T(8,128)S(1)}, f32[64,256]{1,0:T(8,128)S(1)}, u32[]{:S(2)}, u32[]{:S(2)}) %collective-permute-start.8) | collective-permute-done | bytes 65568 | tf_op jit(solution)/shard_map/ppermute | solution.py:440
  26.2 0.7 %reshape.19 = f32[1,1,64,2,128]{4,3,2,1,0:T(2,128)} reshape(f32[64,256]{1,0:T(8,128)S(1)} %add.3) | data formatting | bytes 131072 | tf_op jit(solution)/shard_map/reshape | solution.py:441
  (3 shorter events, 0.1 us)
Async XLA Ops:
  0.0 13.4 %collective-permute-start.3 = (bf16[2,256,128]{2,1,0:T(8,128)(2,1)}, bf16[2,256,128]{2,1,0:T(8,128)(2,1)S(1)}, u32[]{:S(2)}, u32[]{:S(2)}) collective-permute-start(bf16[2,256,128]{2,1,0:T(8,128)(2,1)} %bitcast.7), channel_id=1, source_target_pairs={{0,24},{8,16},{16,8},{24,0},{1,25},{9,17},{17,9},{25,1},{2,26},{10... | collective-permute-start | bytes 393224 | tf_op jit(solution)/shard_map/ppermute | solution.py:257
  5.0 8.5 %collective-permute-start = (bf16[304,128]{1,0:T(8,128)(2,1)S(1)}, bf16[304,128]{1,0:T(8,128)(2,1)S(1)}, u32[]{:S(2)}, u32[]{:S(2)}) collective-permute-start(bf16[304,128]{1,0:T(8,128)(2,1)S(1)} %get-tuple-element.26), channel_id=1, source_target_pairs={{0,2},{2,4},{4,6},{6,0},{1,3},{3,5},{5,7},{7,1},{8,10},{10,12},{12... | collective-permute-start | bytes 233480 | tf_op jit(solution)/shard_map/ppermute | solution.py:376
  6.6 3.7 %collective-permute-start.1 = (bf16[48,128]{1,0:T(8,128)(2,1)S(1)}, bf16[48,128]{1,0:T(8,128)(2,1)S(1)}, u32[]{:S(2)}, u32[]{:S(2)}) collective-permute-start(bf16[48,128]{1,0:T(8,128)(2,1)S(1)} %get-tuple-element.27), channel_id=1, source_target_pairs={{0,6},{2,0},{4,2},{6,4},{1,7},{3,1},{5,3},{7,5},{8,14},{10,8},{12,... | collective-permute-start | bytes 36872 | tf_op jit(solution)/shard_map/ppermute | solution.py:376
  8.8 4.6 %collective-permute-start.2 = (bf16[48,128]{1,0:T(8,128)(2,1)S(1)}, bf16[48,128]{1,0:T(8,128)(2,1)S(1)}, u32[]{:S(2)}, u32[]{:S(2)}) collective-permute-start(bf16[48,128]{1,0:T(8,128)(2,1)S(1)} %get-tuple-element.28), channel_id=1, source_target_pairs={{0,4},{2,6},{4,0},{6,2},{1,5},{3,7},{5,1},{7,3},{8,12},{10,14},{12... | collective-permute-start | bytes 36872 | tf_op jit(solution)/shard_map/ppermute | solution.py:376
  13.5 6.2 %collective-permute-start.6 = (bf16[448,128]{1,0:T(8,128)(2,1)S(1)}, bf16[448,128]{1,0:T(8,128)(2,1)S(1)}, u32[]{:S(2)}, u32[]{:S(2)}) collective-permute-start(bf16[448,128]{1,0:T(8,128)(2,1)S(1)} %get-tuple-element.33), channel_id=1, source_target_pairs={{0,24},{8,16},{16,8},{24,0},{1,25},{9,17},{17,9},{25,1},{2,26},{10... | collective-permute-start | bytes 344072 | tf_op jit(solution)/shard_map/ppermute | solution.py:257
  13.9 7.1 %collective-permute-start.4 = (bf16[704,128]{1,0:T(8,128)(2,1)S(1)}, bf16[704,128]{1,0:T(8,128)(2,1)S(1)}, u32[]{:S(2)}, u32[]{:S(2)}) collective-permute-start(bf16[704,128]{1,0:T(8,128)(2,1)S(1)} %get-tuple-element.34.refs_0_.refs_1_.packed), channel_id=1, source_target_pairs={{0,8},{8,0},{16,24},{24,16},{1,9},{9,1},{17,25},{25,17},{2,10},{10... | collective-permute-start | bytes 540680 | tf_op jit(solution)/shard_map/ppermute | solution.py:257
  15.5 6.0 %collective-permute-start.5 = (bf16[704,128]{1,0:T(8,128)(2,1)S(1)}, bf16[704,128]{1,0:T(8,128)(2,1)S(1)}, u32[]{:S(2)}, u32[]{:S(2)}) collective-permute-start(bf16[704,128]{1,0:T(8,128)(2,1)S(1)} %get-tuple-element.34.refs_0_.refs_1_.packed), channel_id=1, source_target_pairs={{0,16},{8,24},{16,0},{24,8},{1,17},{9,25},{17,1},{25,9},{2,18},{10... | collective-permute-start | bytes 540680 | tf_op jit(solution)/shard_map/ppermute | solution.py:257
  21.6 2.0 %collective-permute-start.7 = (bf16[2048,128]{1,0:T(8,128)(2,1)S(1)}, bf16[2048,128]{1,0:T(8,128)(2,1)S(1)}, u32[]{:S(2)}, u32[]{:S(2)}) collective-permute-start(bf16[2048,128]{1,0:T(8,128)(2,1)S(1)} %collect.1.ours), channel_id=1, source_target_pairs={{0,1},{1,0},{2,3},{3,2},{4,5},{5,4},{6,7},{7,6},{8,9},{9,8},{10,11... | collective-permute-start | bytes 1572872 | tf_op jit(solution)/shard_map/ppermute | solution.py:423
  24.7 1.4 %collective-permute-start.8 = (f32[64,256]{1,0:T(8,128)S(1)}, f32[64,256]{1,0:T(8,128)S(1)}, u32[]{:S(2)}, u32[]{:S(2)}) collective-permute-start(f32[64,256]{1,0:T(8,128)S(1)} %get-tuple-element.42), channel_id=1, source_target_pairs={{0,1},{1,0},{2,3},{3,2},{4,5},{5,4},{6,7},{7,6},{8,9},{9,8},{10,11... | collective-permute-start | bytes 196616 | tf_op jit(solution)/shard_map/ppermute | solution.py:440

commit v23 on v19

--- a/solution.py
+++ b/solution.py
@@ -59,13 +59,13 @@
     table_hbm, outs, half = refs[7], refs[8 : 8 + groups], refs[8 + groups]
     targets = refs[9 + groups : 16 + groups]
     plane_ref, group_ref, samples_b, place_b, offsets_ref, centre_ref, gain_ref = targets
-    samples, place, sorted_, filled, sems = refs[16 + groups :]
+    samples, place, sorted_, filled, table_b, table_f, sems = refs[16 + groups :]
     facet = lax.axis_index("facet")
     copies = [
         pltpu.make_async_copy(source, target, sems.at[n])
         for n, (source, target) in enumerate(zip(refs[:7], targets))
     ]
-    table = pltpu.make_async_copy(table_hbm.at[lax.axis_index("chan")], half, sems.at[7])
+    table = pltpu.make_async_copy(table_hbm.at[lax.axis_index("chan")], table_b, sems.at[7])
     for copy in copies + [table]:
         copy.start()
     sorted_[...] = jnp.zeros_like(sorted_)
@@ -109,7 +109,12 @@
         g = lax.rem(lax.axis_index("bl") + shift, groups)
         out_ref[:rows, :] = sorted_[g].astype(jnp.bfloat16)
     table.wait()
-    outs[1][rows:, :] = half[...]
+    table_f[...] = table_b[...].astype(jnp.float32)
+    for part in range(2):
+        matrix = table_f[pl.ds(part, SU, stride=2), :]
+        matrix = jnp.where(lax.axis_index("chan") == 0, matrix, matrix.T).astype(jnp.bfloat16)
+        half[part * SU : (part + 1) * SU, :] = matrix
+        outs[1][rows + part * SU : rows + (part + 1) * SU, :] = matrix
 
 
 def join_kernel(rows, half, *refs):
@@ -252,21 +257,17 @@
 
 def table_kernel(sizes, norm, packed, ours, theirs, *refs):
     slots, meta_row = sizes
-    grids, (mine_ref, other_ref, table_f, total) = refs[:-4], refs[-4:]
+    grids, (mine_ref, other_ref, total) = refs[:-3], refs[-3:]
     chan = lax.axis_index("chan")
     first = chan == 0
-
-    def parts(table):
-        table_f[...] = table
-        return table_f[pl.ds(0, SU, stride=2), :], table_f[pl.ds(1, SU, stride=2), :]
 
     result = jnp.zeros((SU, 2 * SU), jnp.float32)
     for s in range(slots):
         at = slice(2 * SU * s, 2 * SU * (s + 1))
-        fetched = ours[at, :].astype(jnp.float32)
-        swapped = theirs[at, :].astype(jnp.float32)
-        v_real, v_imag = parts(jnp.where(first, swapped, fetched))
-        v_side = jnp.concatenate([v_real.T, v_imag.T], axis=1).astype(jnp.bfloat16)
+        fetched = ours[at, :]
+        swapped = theirs[at, :]
+        v_table = jnp.where(first, swapped, fetched)
+        v_side = jnp.concatenate([v_table[:SU], v_table[SU:]], axis=1)
         grid = sum(ref[s] for ref in grids)
         high, low = (
             jnp.concatenate(
@@ -281,14 +282,14 @@
         half = jnp.dot(v_side, high, preferred_element_type=jnp.float32) + jnp.dot(
             v_side, low, preferred_element_type=jnp.float32
         )
-        u_real, u_imag = parts(jnp.where(first, fetched, swapped))
+        u_table = jnp.where(first, fetched, swapped)
         u_side = jnp.concatenate(
             [
-                jnp.concatenate([u_real, u_imag], axis=1),
-                jnp.concatenate([-u_imag, u_real], axis=1),
+                jnp.concatenate([u_table[:SU], u_table[SU:]], axis=1),
+                jnp.concatenate([-u_table[SU:], u_table[:SU]], axis=1),
             ],
             axis=0,
-        ).astype(jnp.bfloat16)
+        )
         high, low = split_bf16(half)
         result = (
             result
@@ -345,6 +346,8 @@
             pltpu.VMEM((held * 2, SU), jnp.float32),
             pltpu.VMEM((groups, rows, SU), jnp.float32),
             pltpu.SMEM((groups,), jnp.int32),
+            pltpu.VMEM((2 * SU, SU), jnp.bfloat16),
+            pltpu.VMEM((2 * SU, SU), jnp.float32),
             pltpu.SemaphoreType.DMA((8,)),
         ],
         compiler_params=PARAMS,
@@ -411,7 +414,6 @@
         in_specs=[VMEM] * (3 + len(grids)),
         out_specs=[VMEM, VMEM],
         scratch_shapes=[
-            pltpu.VMEM((2 * SU, SU), jnp.float32),
             pltpu.VMEM((SU, 2 * SU), jnp.float32),
         ],
         compiler_params=PARAMS,

time: 27 us -> 27 us (level)
    pallas_call x3, Pallas kernels: 5.64 us -> 5.99 us  [grid(): pl.pallas_call(functools.partial(grid_kernel, (facets, groups, chans, cap...]
  transfers between devices with their start and end apart: 8 -> 8, of which waited for: 5 -> 5; matrix products, arithmetic and copies ran while one was open for 0% -> 0% of each run, Pallas kernels for 21% -> 22%
where the time goes in v23:
time: 27 us; the launch traced here: 27.1 us
  starting transfers between devices  10.3 us (38%)
  Pallas kernels  8.2 us (30%)
  waiting for transfers between devices  7.82 us (29%)
  local copies, waits for them, and re-layouts  0.66 us (2%)
    ppermute x3, starting transfers between devices, body(): lax.ppermute(pieces[shift], 'bl', [(g, (g + shift) % groups) for g in ran...  6.11 us
    pallas_call x3, Pallas kernels, grid(): pl.pallas_call(functools.partial(grid_kernel, (facets, groups, chans, cap...  5.99 us
    ppermute x3, waiting for transfers between devices, body(): lax.ppermute(pieces[shift], 'bl', [(g, (g + shift) % groups) for g in ran...  3.65 us
    ppermute x3, starting transfers between devices, exchange(): lax.ppermute(value, axis, [(n, n ^ shift) for n in range(lax.axis_size(ax...  3.55 us
    ppermute x3, waiting for transfers between devices, exchange(): lax.ppermute(value, axis, [(n, n ^ shift) for n in range(lax.axis_size(ax...  3.27 us
    pallas_call x1, Pallas kernels, body(): pl.pallas_call(functools.partial(sort_kernel, (groups, held, chans, cap,...  1.17 us
    pallas_call x1, Pallas kernels, body(): pl.pallas_call(functools.partial(table_kernel, (slots, meta_row), norm),...  1 us
    ppermute x1, waiting for transfers between devices, body(): lax.ppermute(other, 'chan', [(c, 1 - c) for c in range(chan_count)])  0.9 us
  transfers between devices with their start and end apart: 8, of which 5 were waited for; matrix products, arithmetic and copies ran while one was open for 0% of the time, Pallas kernels for 22%

profile of v23, /device:TPU:0, one launch (start us, length us, event | category | flops | bytes accessed | tf_op | source)
XLA Modules:
  0.0 27.1 jit_solution(17211614768041942049)
XLA Ops:
  0.0 1.2 %sort_blocks.1 = (bf16[48,128]{1,0:T(8,128)(2,1)S(1)}, bf16[304,128]{1,0:T(8,128)(2,1)S(1)}, bf16[48,128]{1,0:T(8,128)(2,1)S(1)}, bf16[48,128]{1,0:T(8,128)(2,1)S(1)}, bf16[256,128]{1,0:T(8,128)(2,1)S(1)}) custom-call(s32[1,8]{1,0:T(1,128)} %bitcast.12, s32[1,8]{1,0:T(1,128)} %bitcast.13, bf16[64,128]{1,0:T(8,128)(2,1)} %bitcast.8, bf16[16,128]{1,0:T(8,128)(2,1)} %bitcast.9, ...), custom_call_target="tpu_custom_call" | custom-call | flops 100000 | bytes 100000 | tf_op jit(solution)/shard_map/sort_blocks/pallas_call | solution.py:328
  1.2 3.1 %collective-permute-start = (bf16[304,128]{1,0:T(8,128)(2,1)S(1)}, bf16[304,128]{1,0:T(8,128)(2,1)S(1)}, u32[]{:S(2)}, u32[]{:S(2)}) collective-permute-start(bf16[304,128]{1,0:T(8,128)(2,1)S(1)} %get-tuple-element.20), channel_id=1, source_target_pairs={{0,2},{2,4},{4,6},{6,0},{1,3},{3,5},{5,7},{7,1},{8,10},{10,12},{12... | collective-permute-start | bytes 233480 | tf_op jit(solution)/shard_map/ppermute | solution.py:372
  4.3 2.1 %collective-permute-start.1 = (bf16[48,128]{1,0:T(8,128)(2,1)S(1)}, bf16[48,128]{1,0:T(8,128)(2,1)S(1)}, u32[]{:S(2)}, u32[]{:S(2)}) collective-permute-start(bf16[48,128]{1,0:T(8,128)(2,1)S(1)} %get-tuple-element.21), channel_id=1, source_target_pairs={{0,6},{2,0},{4,2},{6,4},{1,7},{3,1},{5,3},{7,5},{8,14},{10,8},{12,... | collective-permute-start | bytes 36872 | tf_op jit(solution)/shard_map/ppermute | solution.py:372
  6.3 0.9 %collective-permute-start.2 = (bf16[48,128]{1,0:T(8,128)(2,1)S(1)}, bf16[48,128]{1,0:T(8,128)(2,1)S(1)}, u32[]{:S(2)}, u32[]{:S(2)}) collective-permute-start(bf16[48,128]{1,0:T(8,128)(2,1)S(1)} %get-tuple-element.22), channel_id=1, source_target_pairs={{0,4},{2,6},{4,0},{6,2},{1,5},{3,7},{5,1},{7,3},{8,12},{10,14},{12... | collective-permute-start | bytes 36872 | tf_op jit(solution)/shard_map/ppermute | solution.py:372
  7.3 1.4 %collective-permute-done.1.refs_2_ = bf16[48,128]{1,0:T(8,128)(2,1)S(1)} collective-permute-done((bf16[48,128]{1,0:T(8,128)(2,1)S(1)}, bf16[48,128]{1,0:T(8,128)(2,1)S(1)}, u32[]{:S(2)}, u32[]{:S(2)}) %collective-permute-start.1) | collective-permute-done | bytes 12320 | tf_op jit(solution)/shard_map/ppermute | solution.py:372
  8.7 2.3 %collective-permute-done.2.refs_3_ = bf16[48,128]{1,0:T(8,128)(2,1)S(1)} collective-permute-done((bf16[48,128]{1,0:T(8,128)(2,1)S(1)}, bf16[48,128]{1,0:T(8,128)(2,1)S(1)}, u32[]{:S(2)}, u32[]{:S(2)}) %collective-permute-start.2) | collective-permute-done | bytes 12320 | tf_op jit(solution)/shard_map/ppermute | solution.py:372
  10.9 0.0 collective-permute-done.refs_1_
  11.0 2.7 %collective-permute-start.5 = (bf16[704,128]{1,0:T(8,128)(2,1)S(1)}, bf16[704,128]{1,0:T(8,128)(2,1)S(1)}, u32[]{:S(2)}, u32[]{:S(2)}) collective-permute-start(bf16[704,128]{1,0:T(8,128)(2,1)S(1)} %join.1.refs_0_.refs_1_.packed), channel_id=1, source_target_pairs={{0,24},{8,16},{16,8},{24,0},{1,25},{9,17},{17,9},{25,1},{2,26},{10... | collective-permute-start | bytes 540680 | tf_op jit(solution)/shard_map/ppermute | solution.py:255
  13.6 0.5 %collective-permute-start.3 = (bf16[704,128]{1,0:T(8,128)(2,1)S(1)}, bf16[704,128]{1,0:T(8,128)(2,1)S(1)}, u32[]{:S(2)}, u32[]{:S(2)}) collective-permute-start(bf16[704,128]{1,0:T(8,128)(2,1)S(1)} %join.1.refs_0_.refs_1_.packed), channel_id=1, source_target_pairs={{0,8},{8,0},{16,24},{24,16},{1,9},{9,1},{17,25},{25,17},{2,10},{10... | collective-permute-start | bytes 540680 | tf_op jit(solution)/shard_map/ppermute | solution.py:255
  14.2 0.3 %collective-permute-start.4 = (bf16[704,128]{1,0:T(8,128)(2,1)S(1)}, bf16[704,128]{1,0:T(8,128)(2,1)S(1)}, u32[]{:S(2)}, u32[]{:S(2)}) collective-permute-start(bf16[704,128]{1,0:T(8,128)(2,1)S(1)} %join.1.refs_0_.refs_1_.packed), channel_id=1, source_target_pairs={{0,16},{8,24},{16,0},{24,8},{1,17},{9,25},{17,1},{25,9},{2,18},{10... | collective-permute-start | bytes 540680 | tf_op jit(solution)/shard_map/ppermute | solution.py:255
  14.5 1.6 %grid.3.refs_0_ = f32[8,128,256]{2,1,0:T(8,128)S(1)} custom-call(bf16[704,128]{1,0:T(8,128)(2,1)S(1)} %join.1.refs_0_.refs_1_.packed, bf16[704,128]{1,0:T(8,128)(2,1)S(1)} %join.1.refs_0_.refs_1_.packed), custom_call_target="tpu_custom_call" | custom-call | flops 1000000000 | bytes 1000000 | tf_op jit(solution)/shard_map/grid/pallas_call | solution.py:385
  16.2 2.7 %collective-permute-done.5.refs_1_.refs_3_ = bf16[704,128]{1,0:T(8,128)(2,1)S(1)} collective-permute-done((bf16[704,128]{1,0:T(8,128)(2,1)S(1)}, bf16[704,128]{1,0:T(8,128)(2,1)S(1)}, u32[]{:S(2)}, u32[]{:S(2)}) %collective-permute-start.5) | collective-permute-done | bytes 180256 | tf_op jit(solution)/shard_map/ppermute | solution.py:255
  18.8 1.3 %grid.4.refs_1_ = f32[8,128,256]{2,1,0:T(8,128)S(1)} custom-call(bf16[704,128]{1,0:T(8,128)(2,1)S(1)} %join.1.refs_0_.refs_1_.packed, bf16[704,128]{1,0:T(8,128)(2,1)S(1)} %collective-permute-done.5.refs_1_.refs_3_), custom_call_target="tpu_custom_call" | custom-call | flops 1000000000 | bytes 1000000 | tf_op jit(solution)/shard_map/grid/pallas_call | solution.py:385
  20.1 0.6 %collective-permute-done.3.refs_1_ = bf16[704,128]{1,0:T(8,128)(2,1)S(1)} collective-permute-done((bf16[704,128]{1,0:T(8,128)(2,1)S(1)}, bf16[704,128]{1,0:T(8,128)(2,1)S(1)}, u32[]{:S(2)}, u32[]{:S(2)}) %collective-permute-start.3) | collective-permute-done | bytes 180256 | tf_op jit(solution)/shard_map/ppermute | solution.py:255
  20.7 0.0 collective-permute-done.4.refs_2_
  20.7 0.1 collective-permute-start.6
  20.8 3.1 %grid.5.refs_2_ = f32[8,128,256]{2,1,0:T(8,128)S(1)} custom-call(bf16[704,128]{1,0:T(8,128)(2,1)S(1)} %join.1.refs_0_.refs_1_.packed, bf16[704,128]{1,0:T(8,128)(2,1)S(1)} %collective-permute-done.3.refs_1_, bf16[704,128]{1,0:T(8,128)(2,1)S(1)} %collective-permute-done.4.refs_2_), custom_call_target="tpu_custom_call" | custom-call | flops 2000000000 | bytes 1000000 | tf_op jit(solution)/shard_map/grid/pallas_call | solution.py:385
  23.9 0.0 collective-permute-done.6.theirs
  23.9 1.0 %apply_tables.1 = (f32[64,256]{1,0:T(8,128)S(1)}, f32[64,256]{1,0:T(8,128)S(1)}) custom-call(bf16[704,128]{1,0:T(8,128)(2,1)S(1)} %join.1.refs_0_.refs_1_.packed, bf16[2048,128]{1,0:T(8,128)(2,1)S(1)} %collect.1.ours, bf16[2048,128]{1,0:T(8,128)(2,1)S(1)} %collective-permute-done.6.theirs, f32[8,128,256]{2,1,0:T(8,128)S(1)} %grid.3.refs_0_, ...), custom_call_target="tpu_custom_call" | custom-call | flops 1000000000 | bytes 2000000 | tf_op jit(solution)/shard_map/apply_tables/pallas_call | solution.py:411
  24.9 0.6 %collective-permute-start.7 = (f32[64,256]{1,0:T(8,128)S(1)}, f32[64,256]{1,0:T(8,128)S(1)}, u32[]{:S(2)}, u32[]{:S(2)}) collective-permute-start(f32[64,256]{1,0:T(8,128)S(1)} %get-tuple-element.30), channel_id=1, source_target_pairs={{0,1},{1,0},{2,3},{3,2},{4,5},{5,4},{6,7},{7,6},{8,9},{9,8},{10,11... | collective-permute-start | bytes 196616 | tf_op jit(solution)/shard_map/ppermute | solution.py:425
  25.5 0.9 %collective-permute-done.7 = f32[64,256]{1,0:T(8,128)S(1)} collective-permute-done((f32[64,256]{1,0:T(8,128)S(1)}, f32[64,256]{1,0:T(8,128)S(1)}, u32[]{:S(2)}, u32[]{:S(2)}) %collective-permute-start.7) | collective-permute-done | bytes 65568 | tf_op jit(solution)/shard_map/ppermute | solution.py:425
  26.4 0.7 %reshape.19 = f32[1,1,64,2,128]{4,3,2,1,0:T(2,128)} reshape(f32[64,256]{1,0:T(8,128)S(1)} %add.3) | data formatting | bytes 131072 | tf_op jit(solution)/shard_map/reshape | solution.py:426
  (3 shorter events, 0.1 us)
Async XLA Ops:
  1.2 9.8 %collective-permute-start = (bf16[304,128]{1,0:T(8,128)(2,1)S(1)}, bf16[304,128]{1,0:T(8,128)(2,1)S(1)}, u32[]{:S(2)}, u32[]{:S(2)}) collective-permute-start(bf16[304,128]{1,0:T(8,128)(2,1)S(1)} %get-tuple-element.20), channel_id=1, source_target_pairs={{0,2},{2,4},{4,6},{6,0},{1,3},{3,5},{5,7},{7,1},{8,10},{10,12},{12... | collective-permute-start | bytes 233480 | tf_op jit(solution)/shard_map/ppermute | solution.py:372
  4.3 4.4 %collective-permute-start.1 = (bf16[48,128]{1,0:T(8,128)(2,1)S(1)}, bf16[48,128]{1,0:T(8,128)(2,1)S(1)}, u32[]{:S(2)}, u32[]{:S(2)}) collective-permute-start(bf16[48,128]{1,0:T(8,128)(2,1)S(1)} %get-tuple-element.21), channel_id=1, source_target_pairs={{0,6},{2,0},{4,2},{6,4},{1,7},{3,1},{5,3},{7,5},{8,14},{10,8},{12,... | collective-permute-start | bytes 36872 | tf_op jit(solution)/shard_map/ppermute | solution.py:372
  6.3 4.6 %collective-permute-start.2 = (bf16[48,128]{1,0:T(8,128)(2,1)S(1)}, bf16[48,128]{1,0:T(8,128)(2,1)S(1)}, u32[]{:S(2)}, u32[]{:S(2)}) collective-permute-start(bf16[48,128]{1,0:T(8,128)(2,1)S(1)} %get-tuple-element.22), channel_id=1, source_target_pairs={{0,4},{2,6},{4,0},{6,2},{1,5},{3,7},{5,1},{7,3},{8,12},{10,14},{12... | collective-permute-start | bytes 36872 | tf_op jit(solution)/shard_map/ppermute | solution.py:372
  11.0 7.9 %collective-permute-start.5 = (bf16[704,128]{1,0:T(8,128)(2,1)S(1)}, bf16[704,128]{1,0:T(8,128)(2,1)S(1)}, u32[]{:S(2)}, u32[]{:S(2)}) collective-permute-start(bf16[704,128]{1,0:T(8,128)(2,1)S(1)} %join.1.refs_0_.refs_1_.packed), channel_id=1, source_target_pairs={{0,24},{8,16},{16,8},{24,0},{1,25},{9,17},{17,9},{25,1},{2,26},{10... | collective-permute-start | bytes 540680 | tf_op jit(solution)/shard_map/ppermute | solution.py:255
  13.6 7.1 %collective-permute-start.3 = (bf16[704,128]{1,0:T(8,128)(2,1)S(1)}, bf16[704,128]{1,0:T(8,128)(2,1)S(1)}, u32[]{:S(2)}, u32[]{:S(2)}) collective-permute-start(bf16[704,128]{1,0:T(8,128)(2,1)S(1)} %join.1.refs_0_.refs_1_.packed), channel_id=1, source_target_pairs={{0,8},{8,0},{16,24},{24,16},{1,9},{9,1},{17,25},{25,17},{2,10},{10... | collective-permute-start | bytes 540680 | tf_op jit(solution)/shard_map/ppermute | solution.py:255
  14.2 6.5 %collective-permute-start.4 = (bf16[704,128]{1,0:T(8,128)(2,1)S(1)}, bf16[704,128]{1,0:T(8,128)(2,1)S(1)}, u32[]{:S(2)}, u32[]{:S(2)}) collective-permute-start(bf16[704,128]{1,0:T(8,128)(2,1)S(1)} %join.1.refs_0_.refs_1_.packed), channel_id=1, source_target_pairs={{0,16},{8,24},{16,0},{24,8},{1,17},{9,25},{17,1},{25,9},{2,18},{10... | collective-permute-start | bytes 540680 | tf_op jit(solution)/shard_map/ppermute | solution.py:255
  20.7 3.2 %collective-permute-start.6 = (bf16[2048,128]{1,0:T(8,128)(2,1)S(1)}, bf16[2048,128]{1,0:T(8,128)(2,1)S(1)}, u32[]{:S(2)}, u32[]{:S(2)}) collective-permute-start(bf16[2048,128]{1,0:T(8,128)(2,1)S(1)} %collect.1.ours), channel_id=1, source_target_pairs={{0,1},{1,0},{2,3},{3,2},{4,5},{5,4},{6,7},{7,6},{8,9},{9,8},{10,11... | collective-permute-start | bytes 1572872 | tf_op jit(solution)/shard_map/ppermute | solution.py:409
  24.9 1.5 %collective-permute-start.7 = (f32[64,256]{1,0:T(8,128)S(1)}, f32[64,256]{1,0:T(8,128)S(1)}, u32[]{:S(2)}, u32[]{:S(2)}) collective-permute-start(f32[64,256]{1,0:T(8,128)S(1)} %get-tuple-element.30), channel_id=1, source_target_pairs={{0,1},{1,0},{2,3},{3,2},{4,5},{5,4},{6,7},{7,6},{8,9},{9,8},{10,11... | collective-permute-start | bytes 196616 | tf_op jit(solution)/shard_map/ppermute | solution.py:425

commit v24 on v23

--- a/solution.py
+++ b/solution.py
@@ -133,8 +133,10 @@
 
 def grid_kernel(sizes, *refs):
     facets, groups, chans, cap, rows, count_here = sizes
-    own_ref, grids = refs[0], refs[1 + count_here]
-    order, spots_u, spots_v, turns_real, turns_imag, cells = refs[2 + count_here :]
+    own_ref = refs[0]
+    before = refs[1 + count_here : -7]
+    grids = refs[-7]
+    order, spots_u, spots_v, turns_real, turns_imag, cells = refs[-6:]
     pieces = [
         ref.at[pl.ds(n * rows, rows)] for ref in refs[1 : 1 + count_here] for n in range(groups)
     ]
@@ -157,7 +159,7 @@
         set_id = jnp.where(lax.rem(plane, groups) == group, 0, 1)
         code = (d * cap + lane) * slots + 2 * (lax.div(plane, groups) ^ facet) + set_id
         codes.append(jnp.where(plane >= 0, code, -1))
-    grids[...] = jnp.zeros_like(grids)
+    grids[...] = before[0][...] if before else jnp.zeros_like(grids)
 
     def number(n):
         return jnp.broadcast_to(numbers[:, n : n + 1], (lines, SU))
@@ -255,9 +257,8 @@
     return lax.ppermute(value, axis, [(n, n ^ shift) for n in range(lax.axis_size(axis))])
 
 
-def table_kernel(sizes, norm, packed, ours, theirs, *refs):
+def table_kernel(sizes, norm, packed, ours, theirs, grids, mine_ref, other_ref, total):
     slots, meta_row = sizes
-    grids, (mine_ref, other_ref, total) = refs[:-3], refs[-3:]
     chan = lax.axis_index("chan")
     first = chan == 0
 
@@ -268,7 +269,6 @@
         swapped = theirs[at, :]
         v_table = jnp.where(first, swapped, fetched)
         v_side = jnp.concatenate([v_table[:SU], v_table[SU:]], axis=1)
-        grid = sum(ref[s] for ref in grids)
         high, low = (
             jnp.concatenate(
                 [
@@ -277,7 +277,7 @@
                 ],
                 axis=0,
             )
-            for part in split_bf16(grid)
+            for part in split_bf16(grids[s])
         )
         half = jnp.dot(v_side, high, preferred_element_type=jnp.float32) + jnp.dot(
             v_side, low, preferred_element_type=jnp.float32
@@ -290,12 +290,10 @@
             ],
             axis=0,
         )
-        high, low = split_bf16(half)
-        result = (
-            result
-            + jnp.dot(high, u_side, preferred_element_type=jnp.float32)
-            + jnp.dot(low, u_side, preferred_element_type=jnp.float32)
-        )
+        both = jnp.dot(
+            jnp.concatenate(split_bf16(half), axis=0), u_side, preferred_element_type=jnp.float32
+        )
+        result = result + both[:SU] + both[SU:]
     result = jnp.concatenate([result[:, :SU].T, result[:, SU:].T], axis=1)
     tail = meta_row // 16 * 16
     wide = packed[tail : tail + 16, :].astype(jnp.float32)
@@ -380,12 +378,12 @@
         "join",
     )
     blocks = [joined] + [exchange(joined, "facet", shift) for shift in range(1, facets)]
-    def grid(some):
+    def grid(some, before=()):
         lines = len(some) * groups * cap
         return pl.pallas_call(
             functools.partial(grid_kernel, (facets, groups, chans, cap, rows, len(some))),
             out_shape=jax.ShapeDtypeStruct((slots, SU, 2 * SU), jnp.float32),
-            in_specs=[VMEM] * (1 + len(some)),
+            in_specs=[VMEM] * (1 + len(some) + len(before)),
             out_specs=VMEM,
             scratch_shapes=[
                 pltpu.SMEM((lines + UNROLL,), jnp.int32),
@@ -399,19 +397,19 @@
                 transcendentals=len(some) * 1_000_000,
             ),
             name="grid",
-        )(joined, *some)
-
-    grids = [grid(blocks[:1]), grid(blocks[-1:])]
+        )(joined, *some, *before)
+
+    grids = grid(blocks[-1:], [grid(blocks[:1])])
     blocks, grids = lax.optimization_barrier((blocks, grids))
     fetched = local(
         functools.partial(collect_kernel, vis_rows), blocks, (facets * 4 * SU, SU), "collect"
     )
     swapped = lax.ppermute(fetched, "chan", [(c, 1 - c) for c in range(chan_count)])
-    grids.append(grid(blocks[1:-1]))
+    grids = grid(blocks[1:-1], [grids])
     mine, other = pl.pallas_call(
         functools.partial(table_kernel, (slots, meta_row), norm),
         out_shape=[jax.ShapeDtypeStruct((half_rows, 2 * SU), jnp.float32)] * 2,
-        in_specs=[VMEM] * (3 + len(grids)),
+        in_specs=[VMEM] * 4,
         out_specs=[VMEM, VMEM],
         scratch_shapes=[
             pltpu.VMEM((SU, 2 * SU), jnp.float32),
@@ -421,7 +419,7 @@
             flops=1_000_000_000, bytes_accessed=2_000_000, transcendentals=0
         ),
         name="apply_tables",
-    )(joined, fetched, swapped, *grids)
+    )(joined, fetched, swapped, grids)
     summand = lax.ppermute(other, "chan", [(c, 1 - c) for c in range(chan_count)])
     return (mine + summand).reshape(1, 1, half_rows, 2, SU)
 

time: 27 us -> 26.5 us (0.981)
  Pallas kernels: 8.2 us -> 7.62 us
    pallas_call x3, Pallas kernels: 5.99 us -> 5.43 us  [grid(): pl.pallas_call(functools.partial(grid_kernel, (facets, groups, chans, cap...]
  transfers between devices with their start and end apart: 8 -> 8, of which waited for: 5 -> 5; matrix products, arithmetic and copies ran while one was open for 0% -> 0% of each run, Pallas kernels for 22% -> 21%
where the time goes in v24:
time: 26.5 us; the launch traced here: 26.3 us
  starting transfers between devices  10.3 us (39%)
  waiting for transfers between devices  7.68 us (29%)
  Pallas kernels  7.62 us (29%)
  local copies, waits for them, and re-layouts  0.66 us (2%)
    ppermute x3, starting transfers between devices, body(): lax.ppermute(pieces[shift], 'bl', [(g, (g + shift) % groups) for g in ran...  6.11 us
    pallas_call x3, Pallas kernels, grid(): pl.pallas_call(functools.partial(grid_kernel, (facets, groups, chans, cap...  5.43 us
    ppermute x3, waiting for transfers between devices, body(): lax.ppermute(pieces[shift], 'bl', [(g, (g + shift) % groups) for g in ran...  3.65 us
    ppermute x3, starting transfers between devices, exchange(): lax.ppermute(value, axis, [(n, n ^ shift) for n in range(lax.axis_size(ax...  3.55 us
    ppermute x3, waiting for transfers between devices, exchange(): lax.ppermute(value, axis, [(n, n ^ shift) for n in range(lax.axis_size(ax...  3.13 us
    pallas_call x1, Pallas kernels, body(): pl.pallas_call(functools.partial(sort_kernel, (groups, held, chans, cap,...  1.17 us
    pallas_call x1, Pallas kernels, body(): pl.pallas_call(functools.partial(table_kernel, (slots, meta_row), norm),...  0.98 us
    ppermute x1, waiting for transfers between devices, body(): lax.ppermute(other, 'chan', [(c, 1 - c) for c in range(chan_count)])  0.9 us
  transfers between devices with their start and end apart: 8, of which 5 were waited for; matrix products, arithmetic and copies ran while one was open for 0% of the time, Pallas kernels for 21%

profile of v24, /device:TPU:0, one launch (start us, length us, event | category | flops | bytes accessed | tf_op | source)
XLA Modules:
  0.0 26.3 jit_solution(17786072104146638935)
XLA Ops:
  0.0 1.2 %sort_blocks.1 = (bf16[48,128]{1,0:T(8,128)(2,1)S(1)}, bf16[304,128]{1,0:T(8,128)(2,1)S(1)}, bf16[48,128]{1,0:T(8,128)(2,1)S(1)}, bf16[48,128]{1,0:T(8,128)(2,1)S(1)}, bf16[256,128]{1,0:T(8,128)(2,1)S(1)}) custom-call(s32[1,8]{1,0:T(1,128)} %bitcast.12, s32[1,8]{1,0:T(1,128)} %bitcast.13, bf16[64,128]{1,0:T(8,128)(2,1)} %bitcast.8, bf16[16,128]{1,0:T(8,128)(2,1)} %bitcast.9, ...), custom_call_target="tpu_custom_call" | custom-call | flops 100000 | bytes 100000 | tf_op jit(solution)/shard_map/sort_blocks/pallas_call | solution.py:326
  1.2 3.1 %collective-permute-start = (bf16[304,128]{1,0:T(8,128)(2,1)S(1)}, bf16[304,128]{1,0:T(8,128)(2,1)S(1)}, u32[]{:S(2)}, u32[]{:S(2)}) collective-permute-start(bf16[304,128]{1,0:T(8,128)(2,1)S(1)} %get-tuple-element.19), channel_id=1, source_target_pairs={{0,2},{2,4},{4,6},{6,0},{1,3},{3,5},{5,7},{7,1},{8,10},{10,12},{12... | collective-permute-start | bytes 233480 | tf_op jit(solution)/shard_map/ppermute | solution.py:370
  4.3 2.1 %collective-permute-start.1 = (bf16[48,128]{1,0:T(8,128)(2,1)S(1)}, bf16[48,128]{1,0:T(8,128)(2,1)S(1)}, u32[]{:S(2)}, u32[]{:S(2)}) collective-permute-start(bf16[48,128]{1,0:T(8,128)(2,1)S(1)} %get-tuple-element.20), channel_id=1, source_target_pairs={{0,6},{2,0},{4,2},{6,4},{1,7},{3,1},{5,3},{7,5},{8,14},{10,8},{12,... | collective-permute-start | bytes 36872 | tf_op jit(solution)/shard_map/ppermute | solution.py:370
  6.3 0.9 %collective-permute-start.2 = (bf16[48,128]{1,0:T(8,128)(2,1)S(1)}, bf16[48,128]{1,0:T(8,128)(2,1)S(1)}, u32[]{:S(2)}, u32[]{:S(2)}) collective-permute-start(bf16[48,128]{1,0:T(8,128)(2,1)S(1)} %get-tuple-element.21), channel_id=1, source_target_pairs={{0,4},{2,6},{4,0},{6,2},{1,5},{3,7},{5,1},{7,3},{8,12},{10,14},{12... | collective-permute-start | bytes 36872 | tf_op jit(solution)/shard_map/ppermute | solution.py:370
  7.3 1.4 %collective-permute-done.1.refs_2_ = bf16[48,128]{1,0:T(8,128)(2,1)S(1)} collective-permute-done((bf16[48,128]{1,0:T(8,128)(2,1)S(1)}, bf16[48,128]{1,0:T(8,128)(2,1)S(1)}, u32[]{:S(2)}, u32[]{:S(2)}) %collective-permute-start.1) | collective-permute-done | bytes 12320 | tf_op jit(solution)/shard_map/ppermute | solution.py:370
  8.7 2.3 %collective-permute-done.2.refs_3_ = bf16[48,128]{1,0:T(8,128)(2,1)S(1)} collective-permute-done((bf16[48,128]{1,0:T(8,128)(2,1)S(1)}, bf16[48,128]{1,0:T(8,128)(2,1)S(1)}, u32[]{:S(2)}, u32[]{:S(2)}) %collective-permute-start.2) | collective-permute-done | bytes 12320 | tf_op jit(solution)/shard_map/ppermute | solution.py:370
  10.9 0.0 collective-permute-done.refs_1_
  11.0 2.7 %collective-permute-start.5 = (bf16[704,128]{1,0:T(8,128)(2,1)S(1)}, bf16[704,128]{1,0:T(8,128)(2,1)S(1)}, u32[]{:S(2)}, u32[]{:S(2)}) collective-permute-start(bf16[704,128]{1,0:T(8,128)(2,1)S(1)} %join.1.refs_0_.refs_1_.packed), channel_id=1, source_target_pairs={{0,24},{8,16},{16,8},{24,0},{1,25},{9,17},{17,9},{25,1},{2,26},{10... | collective-permute-start | bytes 540680 | tf_op jit(solution)/shard_map/ppermute | solution.py:257
  13.6 0.5 %collective-permute-start.3 = (bf16[704,128]{1,0:T(8,128)(2,1)S(1)}, bf16[704,128]{1,0:T(8,128)(2,1)S(1)}, u32[]{:S(2)}, u32[]{:S(2)}) collective-permute-start(bf16[704,128]{1,0:T(8,128)(2,1)S(1)} %join.1.refs_0_.refs_1_.packed), channel_id=1, source_target_pairs={{0,8},{8,0},{16,24},{24,16},{1,9},{9,1},{17,25},{25,17},{2,10},{10... | collective-permute-start | bytes 540680 | tf_op jit(solution)/shard_map/ppermute | solution.py:257
  14.2 0.4 %collective-permute-start.4 = (bf16[704,128]{1,0:T(8,128)(2,1)S(1)}, bf16[704,128]{1,0:T(8,128)(2,1)S(1)}, u32[]{:S(2)}, u32[]{:S(2)}) collective-permute-start(bf16[704,128]{1,0:T(8,128)(2,1)S(1)} %join.1.refs_0_.refs_1_.packed), channel_id=1, source_target_pairs={{0,16},{8,24},{16,0},{24,8},{1,17},{9,25},{17,1},{25,9},{2,18},{10... | collective-permute-start | bytes 540680 | tf_op jit(solution)/shard_map/ppermute | solution.py:257
  14.5 1.6 %grid.3.refs_2_ = f32[8,128,256]{2,1,0:T(8,128)S(1)} custom-call(bf16[704,128]{1,0:T(8,128)(2,1)S(1)} %join.1.refs_0_.refs_1_.packed, bf16[704,128]{1,0:T(8,128)(2,1)S(1)} %join.1.refs_0_.refs_1_.packed), custom_call_target="tpu_custom_call" | custom-call | flops 1000000000 | bytes 1000000 | tf_op jit(solution)/shard_map/grid/pallas_call | solution.py:383
  16.1 2.7 %collective-permute-done.5.refs_1_.refs_3_ = bf16[704,128]{1,0:T(8,128)(2,1)S(1)} collective-permute-done((bf16[704,128]{1,0:T(8,128)(2,1)S(1)}, bf16[704,128]{1,0:T(8,128)(2,1)S(1)}, u32[]{:S(2)}, u32[]{:S(2)}) %collective-permute-start.5) | collective-permute-done | bytes 180256 | tf_op jit(solution)/shard_map/ppermute | solution.py:257
  18.8 1.4 %grid.4.refs_3_ = f32[8,128,256]{2,1,0:T(8,128)S(1)} custom-call(bf16[704,128]{1,0:T(8,128)(2,1)S(1)} %join.1.refs_0_.refs_1_.packed, bf16[704,128]{1,0:T(8,128)(2,1)S(1)} %collective-permute-done.5.refs_1_.refs_3_, f32[8,128,256]{2,1,0:T(8,128)S(1)} %grid.3.refs_2_), custom_call_target="tpu_custom_call" | custom-call | flops 1000000000 | bytes 1000000 | tf_op jit(solution)/shard_map/grid/pallas_call | solution.py:383
  20.3 0.5 %collective-permute-done.3.refs_1_ = bf16[704,128]{1,0:T(8,128)(2,1)S(1)} collective-permute-done((bf16[704,128]{1,0:T(8,128)(2,1)S(1)}, bf16[704,128]{1,0:T(8,128)(2,1)S(1)}, u32[]{:S(2)}, u32[]{:S(2)}) %collective-permute-start.3) | collective-permute-done | bytes 180256 | tf_op jit(solution)/shard_map/ppermute | solution.py:257
  20.7 0.0 collective-permute-done.4.refs_2_
  20.7 0.1 collective-permute-start.6
  20.8 2.4 %grid.5.grids = f32[8,128,256]{2,1,0:T(8,128)S(1)} custom-call(bf16[704,128]{1,0:T(8,128)(2,1)S(1)} %join.1.refs_0_.refs_1_.packed, bf16[704,128]{1,0:T(8,128)(2,1)S(1)} %collective-permute-done.3.refs_1_, bf16[704,128]{1,0:T(8,128)(2,1)S(1)} %collective-permute-done.4.refs_2_, f32[8,128,256]{2,1,0:T(8,128)S(1)} %grid.4.refs_3_), custom_call_target="tpu_custom_call" | custom-call | flops 2000000000 | bytes 1000000 | tf_op jit(solution)/shard_map/grid/pallas_call | solution.py:383
  23.2 0.0 collective-permute-done.6.theirs
  23.2 1.0 %apply_tables.1 = (f32[64,256]{1,0:T(8,128)S(1)}, f32[64,256]{1,0:T(8,128)S(1)}) custom-call(bf16[704,128]{1,0:T(8,128)(2,1)S(1)} %join.1.refs_0_.refs_1_.packed, bf16[2048,128]{1,0:T(8,128)(2,1)S(1)} %collect.1.ours, bf16[2048,128]{1,0:T(8,128)(2,1)S(1)} %collective-permute-done.6.theirs, f32[8,128,256]{2,1,0:T(8,128)S(1)} %grid.5.grids), custom_call_target="tpu_custom_call" | custom-call | flops 1000000000 | bytes 2000000 | tf_op jit(solution)/shard_map/apply_tables/pallas_call | solution.py:409
  24.2 0.6 %collective-permute-start.7 = (f32[64,256]{1,0:T(8,128)S(1)}, f32[64,256]{1,0:T(8,128)S(1)}, u32[]{:S(2)}, u32[]{:S(2)}) collective-permute-start(f32[64,256]{1,0:T(8,128)S(1)} %get-tuple-element.28), channel_id=1, source_target_pairs={{0,1},{1,0},{2,3},{3,2},{4,5},{5,4},{6,7},{7,6},{8,9},{9,8},{10,11... | collective-permute-start | bytes 196616 | tf_op jit(solution)/shard_map/ppermute | solution.py:423
  24.8 0.9 %collective-permute-done.7 = f32[64,256]{1,0:T(8,128)S(1)} collective-permute-done((f32[64,256]{1,0:T(8,128)S(1)}, f32[64,256]{1,0:T(8,128)S(1)}, u32[]{:S(2)}, u32[]{:S(2)}) %collective-permute-start.7) | collective-permute-done | bytes 65568 | tf_op jit(solution)/shard_map/ppermute | solution.py:423
  25.7 0.7 %reshape.19 = f32[1,1,64,2,128]{4,3,2,1,0:T(2,128)} reshape(f32[64,256]{1,0:T(8,128)S(1)} %add.3) | data formatting | bytes 131072 | tf_op jit(solution)/shard_map/reshape | solution.py:424
  (3 shorter events, 0.1 us)
Async XLA Ops:
  1.2 9.8 %collective-permute-start = (bf16[304,128]{1,0:T(8,128)(2,1)S(1)}, bf16[304,128]{1,0:T(8,128)(2,1)S(1)}, u32[]{:S(2)}, u32[]{:S(2)}) collective-permute-start(bf16[304,128]{1,0:T(8,128)(2,1)S(1)} %get-tuple-element.19), channel_id=1, source_target_pairs={{0,2},{2,4},{4,6},{6,0},{1,3},{3,5},{5,7},{7,1},{8,10},{10,12},{12... | collective-permute-start | bytes 233480 | tf_op jit(solution)/shard_map/ppermute | solution.py:370
  4.3 4.4 %collective-permute-start.1 = (bf16[48,128]{1,0:T(8,128)(2,1)S(1)}, bf16[48,128]{1,0:T(8,128)(2,1)S(1)}, u32[]{:S(2)}, u32[]{:S(2)}) collective-permute-start(bf16[48,128]{1,0:T(8,128)(2,1)S(1)} %get-tuple-element.20), channel_id=1, source_target_pairs={{0,6},{2,0},{4,2},{6,4},{1,7},{3,1},{5,3},{7,5},{8,14},{10,8},{12,... | collective-permute-start | bytes 36872 | tf_op jit(solution)/shard_map/ppermute | solution.py:370
  6.3 4.6 %collective-permute-start.2 = (bf16[48,128]{1,0:T(8,128)(2,1)S(1)}, bf16[48,128]{1,0:T(8,128)(2,1)S(1)}, u32[]{:S(2)}, u32[]{:S(2)}) collective-permute-start(bf16[48,128]{1,0:T(8,128)(2,1)S(1)} %get-tuple-element.21), channel_id=1, source_target_pairs={{0,4},{2,6},{4,0},{6,2},{1,5},{3,7},{5,1},{7,3},{8,12},{10,14},{12... | collective-permute-start | bytes 36872 | tf_op jit(solution)/shard_map/ppermute | solution.py:370
  11.0 7.9 %collective-permute-start.5 = (bf16[704,128]{1,0:T(8,128)(2,1)S(1)}, bf16[704,128]{1,0:T(8,128)(2,1)S(1)}, u32[]{:S(2)}, u32[]{:S(2)}) collective-permute-start(bf16[704,128]{1,0:T(8,128)(2,1)S(1)} %join.1.refs_0_.refs_1_.packed), channel_id=1, source_target_pairs={{0,24},{8,16},{16,8},{24,0},{1,25},{9,17},{17,9},{25,1},{2,26},{10... | collective-permute-start | bytes 540680 | tf_op jit(solution)/shard_map/ppermute | solution.py:257
  13.6 7.1 %collective-permute-start.3 = (bf16[704,128]{1,0:T(8,128)(2,1)S(1)}, bf16[704,128]{1,0:T(8,128)(2,1)S(1)}, u32[]{:S(2)}, u32[]{:S(2)}) collective-permute-start(bf16[704,128]{1,0:T(8,128)(2,1)S(1)} %join.1.refs_0_.refs_1_.packed), channel_id=1, source_target_pairs={{0,8},{8,0},{16,24},{24,16},{1,9},{9,1},{17,25},{25,17},{2,10},{10... | collective-permute-start | bytes 540680 | tf_op jit(solution)/shard_map/ppermute | solution.py:257
  14.2 6.5 %collective-permute-start.4 = (bf16[704,128]{1,0:T(8,128)(2,1)S(1)}, bf16[704,128]{1,0:T(8,128)(2,1)S(1)}, u32[]{:S(2)}, u32[]{:S(2)}) collective-permute-start(bf16[704,128]{1,0:T(8,128)(2,1)S(1)} %join.1.refs_0_.refs_1_.packed), channel_id=1, source_target_pairs={{0,16},{8,24},{16,0},{24,8},{1,17},{9,25},{17,1},{25,9},{2,18},{10... | collective-permute-start | bytes 540680 | tf_op jit(solution)/shard_map/ppermute | solution.py:257
  20.7 2.5 %collective-permute-start.6 = (bf16[2048,128]{1,0:T(8,128)(2,1)S(1)}, bf16[2048,128]{1,0:T(8,128)(2,1)S(1)}, u32[]{:S(2)}, u32[]{:S(2)}) collective-permute-start(bf16[2048,128]{1,0:T(8,128)(2,1)S(1)} %collect.1.ours), channel_id=1, source_target_pairs={{0,1},{1,0},{2,3},{3,2},{4,5},{5,4},{6,7},{7,6},{8,9},{9,8},{10,11... | collective-permute-start | bytes 1572872 | tf_op jit(solution)/shard_map/ppermute | solution.py:407
  24.2 1.5 %collective-permute-start.7 = (f32[64,256]{1,0:T(8,128)S(1)}, f32[64,256]{1,0:T(8,128)S(1)}, u32[]{:S(2)}, u32[]{:S(2)}) collective-permute-start(f32[64,256]{1,0:T(8,128)S(1)} %get-tuple-element.28), channel_id=1, source_target_pairs={{0,1},{1,0},{2,3},{3,2},{4,5},{5,4},{6,7},{7,6},{8,9},{9,8},{10,11... | collective-permute-start | bytes 196616 | tf_op jit(solution)/shard_map/ppermute | solution.py:423

commit v25 on v23

--- a/solution.py
+++ b/solution.py
@@ -106,24 +106,22 @@
             lane == k, (plane_ref[0, i] + 1).astype(jnp.float32), 0.0
         )
     for shift, out_ref in enumerate(outs):
-        g = lax.rem(lax.axis_index("bl") + shift, groups)
-        out_ref[:rows, :] = sorted_[g].astype(jnp.bfloat16)
+        out_ref[...] = sorted_[lax.axis_index("bl") ^ shift].astype(jnp.bfloat16)
     table.wait()
     table_f[...] = table_b[...].astype(jnp.float32)
     for part in range(2):
         matrix = table_f[pl.ds(part, SU, stride=2), :]
         matrix = jnp.where(lax.axis_index("chan") == 0, matrix, matrix.T).astype(jnp.bfloat16)
         half[part * SU : (part + 1) * SU, :] = matrix
-        outs[1][rows + part * SU : rows + (part + 1) * SU, :] = matrix
-
-
-def join_kernel(rows, half, *refs):
+
+
+def join_kernel(rows, half, shifted, *refs):
     *pieces, joined = refs
     for n, ref in enumerate(pieces):
-        joined[n * rows : (n + 1) * rows, :] = ref[:rows, :]
+        joined[n * rows : (n + 1) * rows, :] = ref[...]
     at = len(pieces) * rows
     joined[at : at + 2 * SU, :] = half[...]
-    joined[at + 2 * SU :, :] = pieces[1][rows:, :]
+    joined[at + 2 * SU :, :] = shifted[...]
 
 
 def collect_kernel(skip, *refs):
@@ -327,10 +325,7 @@
     own_table = tables.reshape(2, 2 * SU, SU)
     *pieces, half = pl.pallas_call(
         functools.partial(sort_kernel, (groups, held, chans, cap, rows)),
-        out_shape=[
-            jax.ShapeDtypeStruct((rows + (2 * SU if shift == 1 else 0), SU), jnp.bfloat16)
-            for shift in range(groups)
-        ]
+        out_shape=[jax.ShapeDtypeStruct((rows, SU), jnp.bfloat16)] * groups
         + [jax.ShapeDtypeStruct((2 * SU, SU), jnp.bfloat16)],
         in_specs=[HBM] * 8,
         out_specs=[VMEM] * (groups + 1),
@@ -368,14 +363,12 @@
             )
         )
     )
-    arrived = [
-        lax.ppermute(pieces[shift], "bl", [(g, (g + shift) % groups) for g in range(groups)])
-        for shift in [1, *range(groups - 1, 1, -1)]
-    ]
+    shifted = lax.ppermute(half, "bl", [(g, (g + 1) % groups) for g in range(groups)])
+    arrived = [exchange(pieces[shift], "bl", shift) for shift in range(groups - 1, 0, -1)]
     vis_rows = groups * rows
     joined = local(
         functools.partial(join_kernel, rows),
-        [half, pieces[0], *arrived],
+        [half, shifted, pieces[0], *arrived],
         (vis_rows + 4 * SU, SU),
         "join",
     )

time: 27 us -> 26.9 us (level); the launches traced: 27.1 us -> 26.7 us
  starting transfers between devices: 10.3 us -> 11.6 us
  waiting for transfers between devices: 7.82 us -> 6.62 us
  Pallas kernels: 8.2 us -> 7.68 us
    ppermute x3 -> x6, starting transfers between devices: 3.55 us -> 7.94 us  [exchange(): lax.ppermute(value, axis, [(n, n ^ shift) for n in range(lax.axis_size(ax...]
    ppermute x3 -> x1, waiting for transfers between devices: 3.65 us -> 0.01 us  [body(): lax.ppermute(half, 'bl', [(g, (g + 1) % groups) for g in range(groups)])]
    ppermute x3 -> x1, starting transfers between devices: 6.11 us -> 3.07 us  [body(): lax.ppermute(half, 'bl', [(g, (g + 1) % groups) for g in range(groups)])]
    ppermute x3 -> x6, waiting for transfers between devices: 3.27 us -> 5.71 us  [exchange(): lax.ppermute(value, axis, [(n, n ^ shift) for n in range(lax.axis_size(ax...]
    pallas_call x3, Pallas kernels: 5.99 us -> 5.47 us  [grid(): pl.pallas_call(functools.partial(grid_kernel, (facets, groups, chans, cap...]
  transfers between devices with their start and end apart: 8 -> 9, of which waited for: 5 -> 6; matrix products, arithmetic and copies ran while one was open for 0% -> 0% of each run, Pallas kernels for 22% -> 20%
where the time goes in v25:
time: 26.9 us; the launch traced here: 26.7 us
  starting transfers between devices  11.6 us (43%)
  Pallas kernels  7.68 us (29%)
  waiting for transfers between devices  6.62 us (25%)
  local copies, waits for them, and re-layouts  0.66 us (2%)
    ppermute x6, starting transfers between devices, exchange(): lax.ppermute(value, axis, [(n, n ^ shift) for n in range(lax.axis_size(ax...  7.94 us
    ppermute x6, waiting for transfers between devices, exchange(): lax.ppermute(value, axis, [(n, n ^ shift) for n in range(lax.axis_size(ax...  5.71 us
    pallas_call x3, Pallas kernels, grid(): pl.pallas_call(functools.partial(grid_kernel, (facets, groups, chans, cap...  5.47 us
    ppermute x1, starting transfers between devices, body(): lax.ppermute(half, 'bl', [(g, (g + 1) % groups) for g in range(groups)])  3.07 us
    pallas_call x1, Pallas kernels, body(): pl.pallas_call(functools.partial(sort_kernel, (groups, held, chans, cap,...  1.17 us
    pallas_call x1, Pallas kernels, body(): pl.pallas_call(functools.partial(table_kernel, (slots, meta_row), norm),...  1 us
    ppermute x1, waiting for transfers between devices, body(): lax.ppermute(other, 'chan', [(c, 1 - c) for c in range(chan_count)])  0.9 us
    reshape x1, local copies, waits for them, and re-layouts, body(): return (mine + summand).reshape(1, 1, half_rows, 2, SU)  0.66 us
  transfers between devices with their start and end apart: 9, of which 6 were waited for; matrix products, arithmetic and copies ran while one was open for 0% of the time, Pallas kernels for 20%

profile of v25, /device:TPU:0, one launch (start us, length us, event | category | flops | bytes accessed | tf_op | source)
XLA Modules:
  0.0 26.7 jit_solution(4434778940875692271)
XLA Ops:
  0.0 1.2 %sort_blocks.1 = (bf16[48,128]{1,0:T(8,128)(2,1)S(1)}, bf16[48,128]{1,0:T(8,128)(2,1)S(1)}, bf16[48,128]{1,0:T(8,128)(2,1)S(1)}, bf16[48,128]{1,0:T(8,128)(2,1)S(1)}, bf16[256,128]{1,0:T(8,128)(2,1)S(1)}) custom-call(s32[1,8]{1,0:T(1,128)} %bitcast.12, s32[1,8]{1,0:T(1,128)} %bitcast.13, bf16[64,128]{1,0:T(8,128)(2,1)} %bitcast.8, bf16[16,128]{1,0:T(8,128)(2,1)} %bitcast.9, ...), custom_call_target="tpu_custom_call" | custom-call | flops 100000 | bytes 100000 | tf_op jit(solution)/shard_map/sort_blocks/pallas_call | solution.py:326
  1.2 3.1 %collective-permute-start = (bf16[256,128]{1,0:T(8,128)(2,1)S(1)}, bf16[256,128]{1,0:T(8,128)(2,1)S(1)}, u32[]{:S(2)}, u32[]{:S(2)}) collective-permute-start(bf16[256,128]{1,0:T(8,128)(2,1)S(1)} %get-tuple-element.18.half), channel_id=1, source_target_pairs={{0,2},{2,4},{4,6},{6,0},{1,3},{3,5},{5,7},{7,1},{8,10},{10,12},{12... | collective-permute-start | bytes 196616 | tf_op jit(solution)/shard_map/ppermute | solution.py:366
  4.2 2.1 %collective-permute-start.1 = (bf16[48,128]{1,0:T(8,128)(2,1)S(1)}, bf16[48,128]{1,0:T(8,128)(2,1)S(1)}, u32[]{:S(2)}, u32[]{:S(2)}) collective-permute-start(bf16[48,128]{1,0:T(8,128)(2,1)S(1)} %get-tuple-element.20), channel_id=1, source_target_pairs={{0,6},{2,4},{4,2},{6,0},{1,7},{3,5},{5,3},{7,1},{8,14},{10,12},{12... | collective-permute-start | bytes 36872 | tf_op jit(solution)/shard_map/ppermute | solution.py:253
  6.4 0.9 %collective-permute-start.2 = (bf16[48,128]{1,0:T(8,128)(2,1)S(1)}, bf16[48,128]{1,0:T(8,128)(2,1)S(1)}, u32[]{:S(2)}, u32[]{:S(2)}) collective-permute-start(bf16[48,128]{1,0:T(8,128)(2,1)S(1)} %get-tuple-element.21), channel_id=1, source_target_pairs={{0,4},{2,6},{4,0},{6,2},{1,5},{3,7},{5,1},{7,3},{8,12},{10,14},{12... | collective-permute-start | bytes 36872 | tf_op jit(solution)/shard_map/ppermute | solution.py:253
  7.3 1.3 %collective-permute-start.3 = (bf16[48,128]{1,0:T(8,128)(2,1)S(1)}, bf16[48,128]{1,0:T(8,128)(2,1)S(1)}, u32[]{:S(2)}, u32[]{:S(2)}) collective-permute-start(bf16[48,128]{1,0:T(8,128)(2,1)S(1)} %get-tuple-element.22), channel_id=1, source_target_pairs={{0,2},{2,0},{4,6},{6,4},{1,3},{3,1},{5,7},{7,5},{8,10},{10,8},{12,... | collective-permute-start | bytes 36872 | tf_op jit(solution)/shard_map/ppermute | solution.py:253
  8.6 1.2 %collective-permute-done.1.refs_1_ = bf16[48,128]{1,0:T(8,128)(2,1)S(1)} collective-permute-done((bf16[48,128]{1,0:T(8,128)(2,1)S(1)}, bf16[48,128]{1,0:T(8,128)(2,1)S(1)}, u32[]{:S(2)}, u32[]{:S(2)}) %collective-permute-start.1) | collective-permute-done | bytes 12320 | tf_op jit(solution)/shard_map/ppermute | solution.py:253
  9.9 1.1 %collective-permute-done.2.refs_2_ = bf16[48,128]{1,0:T(8,128)(2,1)S(1)} collective-permute-done((bf16[48,128]{1,0:T(8,128)(2,1)S(1)}, bf16[48,128]{1,0:T(8,128)(2,1)S(1)}, u32[]{:S(2)}, u32[]{:S(2)}) %collective-permute-start.2) | collective-permute-done | bytes 12320 | tf_op jit(solution)/shard_map/ppermute | solution.py:253
  11.0 0.1 collective-permute-done.3.refs_3_
  11.1 0.0 collective-permute-done.shifted
  11.1 2.6 %collective-permute-start.6 = (bf16[704,128]{1,0:T(8,128)(2,1)S(1)}, bf16[704,128]{1,0:T(8,128)(2,1)S(1)}, u32[]{:S(2)}, u32[]{:S(2)}) collective-permute-start(bf16[704,128]{1,0:T(8,128)(2,1)S(1)} %join.1.refs_0_.refs_1_.packed), channel_id=1, source_target_pairs={{0,24},{8,16},{16,8},{24,0},{1,25},{9,17},{17,9},{25,1},{2,26},{10... | collective-permute-start | bytes 540680 | tf_op jit(solution)/shard_map/ppermute | solution.py:253
  13.7 0.5 %collective-permute-start.4 = (bf16[704,128]{1,0:T(8,128)(2,1)S(1)}, bf16[704,128]{1,0:T(8,128)(2,1)S(1)}, u32[]{:S(2)}, u32[]{:S(2)}) collective-permute-start(bf16[704,128]{1,0:T(8,128)(2,1)S(1)} %join.1.refs_0_.refs_1_.packed), channel_id=1, source_target_pairs={{0,8},{8,0},{16,24},{24,16},{1,9},{9,1},{17,25},{25,17},{2,10},{10... | collective-permute-start | bytes 540680 | tf_op jit(solution)/shard_map/ppermute | solution.py:253
  14.2 0.5 %collective-permute-start.5 = (bf16[704,128]{1,0:T(8,128)(2,1)S(1)}, bf16[704,128]{1,0:T(8,128)(2,1)S(1)}, u32[]{:S(2)}, u32[]{:S(2)}) collective-permute-start(bf16[704,128]{1,0:T(8,128)(2,1)S(1)} %join.1.refs_0_.refs_1_.packed), channel_id=1, source_target_pairs={{0,16},{8,24},{16,0},{24,8},{1,17},{9,25},{17,1},{25,9},{2,18},{10... | collective-permute-start | bytes 540680 | tf_op jit(solution)/shard_map/ppermute | solution.py:253
  14.7 1.4 %grid.3.refs_0_ = f32[8,128,256]{2,1,0:T(8,128)S(1)} custom-call(bf16[704,128]{1,0:T(8,128)(2,1)S(1)} %join.1.refs_0_.refs_1_.packed, bf16[704,128]{1,0:T(8,128)(2,1)S(1)} %join.1.refs_0_.refs_1_.packed), custom_call_target="tpu_custom_call" | custom-call | flops 1000000000 | bytes 1000000 | tf_op jit(solution)/shard_map/grid/pallas_call | solution.py:378
  16.1 3.0 %collective-permute-done.6.refs_1_.refs_3_ = bf16[704,128]{1,0:T(8,128)(2,1)S(1)} collective-permute-done((bf16[704,128]{1,0:T(8,128)(2,1)S(1)}, bf16[704,128]{1,0:T(8,128)(2,1)S(1)}, u32[]{:S(2)}, u32[]{:S(2)}) %collective-permute-start.6) | collective-permute-done | bytes 180256 | tf_op jit(solution)/shard_map/ppermute | solution.py:253
  19.1 1.6 %grid.4.refs_1_ = f32[8,128,256]{2,1,0:T(8,128)S(1)} custom-call(bf16[704,128]{1,0:T(8,128)(2,1)S(1)} %join.1.refs_0_.refs_1_.packed, bf16[704,128]{1,0:T(8,128)(2,1)S(1)} %collective-permute-done.6.refs_1_.refs_3_), custom_call_target="tpu_custom_call" | custom-call | flops 1000000000 | bytes 1000000 | tf_op jit(solution)/shard_map/grid/pallas_call | solution.py:378
  20.8 0.2 collective-permute-done.4.refs_1_
  21.0 0.0 collective-permute-done.5.refs_2_
  21.1 0.1 collective-permute-start.7
  21.1 2.4 %grid.5.refs_2_ = f32[8,128,256]{2,1,0:T(8,128)S(1)} custom-call(bf16[704,128]{1,0:T(8,128)(2,1)S(1)} %join.1.refs_0_.refs_1_.packed, bf16[704,128]{1,0:T(8,128)(2,1)S(1)} %collective-permute-done.4.refs_1_, bf16[704,128]{1,0:T(8,128)(2,1)S(1)} %collective-permute-done.5.refs_2_), custom_call_target="tpu_custom_call" | custom-call | flops 2000000000 | bytes 1000000 | tf_op jit(solution)/shard_map/grid/pallas_call | solution.py:378
  23.5 0.0 collective-permute-done.7.theirs
  23.5 1.0 %apply_tables.1 = (f32[64,256]{1,0:T(8,128)S(1)}, f32[64,256]{1,0:T(8,128)S(1)}) custom-call(bf16[704,128]{1,0:T(8,128)(2,1)S(1)} %join.1.refs_0_.refs_1_.packed, bf16[2048,128]{1,0:T(8,128)(2,1)S(1)} %collect.1.ours, bf16[2048,128]{1,0:T(8,128)(2,1)S(1)} %collective-permute-done.7.theirs, f32[8,128,256]{2,1,0:T(8,128)S(1)} %grid.3.refs_0_, ...), custom_call_target="tpu_custom_call" | custom-call | flops 1000000000 | bytes 2000000 | tf_op jit(solution)/shard_map/apply_tables/pallas_call | solution.py:404
  24.5 0.6 %collective-permute-start.8 = (f32[64,256]{1,0:T(8,128)S(1)}, f32[64,256]{1,0:T(8,128)S(1)}, u32[]{:S(2)}, u32[]{:S(2)}) collective-permute-start(f32[64,256]{1,0:T(8,128)S(1)} %get-tuple-element.30), channel_id=1, source_target_pairs={{0,1},{1,0},{2,3},{3,2},{4,5},{5,4},{6,7},{7,6},{8,9},{9,8},{10,11... | collective-permute-start | bytes 196616 | tf_op jit(solution)/shard_map/ppermute | solution.py:418
  25.1 0.9 %collective-permute-done.8 = f32[64,256]{1,0:T(8,128)S(1)} collective-permute-done((f32[64,256]{1,0:T(8,128)S(1)}, f32[64,256]{1,0:T(8,128)S(1)}, u32[]{:S(2)}, u32[]{:S(2)}) %collective-permute-start.8) | collective-permute-done | bytes 65568 | tf_op jit(solution)/shard_map/ppermute | solution.py:418
  26.0 0.7 %reshape.19 = f32[1,1,64,2,128]{4,3,2,1,0:T(2,128)} reshape(f32[64,256]{1,0:T(8,128)S(1)} %add.3) | data formatting | bytes 131072 | tf_op jit(solution)/shard_map/reshape | solution.py:419
  (3 shorter events, 0.1 us)
Async XLA Ops:
  1.2 9.9 %collective-permute-start = (bf16[256,128]{1,0:T(8,128)(2,1)S(1)}, bf16[256,128]{1,0:T(8,128)(2,1)S(1)}, u32[]{:S(2)}, u32[]{:S(2)}) collective-permute-start(bf16[256,128]{1,0:T(8,128)(2,1)S(1)} %get-tuple-element.18.half), channel_id=1, source_target_pairs={{0,2},{2,4},{4,6},{6,0},{1,3},{3,5},{5,7},{7,1},{8,10},{10,12},{12... | collective-permute-start | bytes 196616 | tf_op jit(solution)/shard_map/ppermute | solution.py:366
  4.2 5.6 %collective-permute-start.1 = (bf16[48,128]{1,0:T(8,128)(2,1)S(1)}, bf16[48,128]{1,0:T(8,128)(2,1)S(1)}, u32[]{:S(2)}, u32[]{:S(2)}) collective-permute-start(bf16[48,128]{1,0:T(8,128)(2,1)S(1)} %get-tuple-element.20), channel_id=1, source_target_pairs={{0,6},{2,4},{4,2},{6,0},{1,7},{3,5},{5,3},{7,1},{8,14},{10,12},{12... | collective-permute-start | bytes 36872 | tf_op jit(solution)/shard_map/ppermute | solution.py:253
  6.4 4.6 %collective-permute-start.2 = (bf16[48,128]{1,0:T(8,128)(2,1)S(1)}, bf16[48,128]{1,0:T(8,128)(2,1)S(1)}, u32[]{:S(2)}, u32[]{:S(2)}) collective-permute-start(bf16[48,128]{1,0:T(8,128)(2,1)S(1)} %get-tuple-element.21), channel_id=1, source_target_pairs={{0,4},{2,6},{4,0},{6,2},{1,5},{3,7},{5,1},{7,3},{8,12},{10,14},{12... | collective-permute-start | bytes 36872 | tf_op jit(solution)/shard_map/ppermute | solution.py:253
  7.3 3.8 %collective-permute-start.3 = (bf16[48,128]{1,0:T(8,128)(2,1)S(1)}, bf16[48,128]{1,0:T(8,128)(2,1)S(1)}, u32[]{:S(2)}, u32[]{:S(2)}) collective-permute-start(bf16[48,128]{1,0:T(8,128)(2,1)S(1)} %get-tuple-element.22), channel_id=1, source_target_pairs={{0,2},{2,0},{4,6},{6,4},{1,3},{3,1},{5,7},{7,5},{8,10},{10,8},{12,... | collective-permute-start | bytes 36872 | tf_op jit(solution)/shard_map/ppermute | solution.py:253
  11.1 8.0 %collective-permute-start.6 = (bf16[704,128]{1,0:T(8,128)(2,1)S(1)}, bf16[704,128]{1,0:T(8,128)(2,1)S(1)}, u32[]{:S(2)}, u32[]{:S(2)}) collective-permute-start(bf16[704,128]{1,0:T(8,128)(2,1)S(1)} %join.1.refs_0_.refs_1_.packed), channel_id=1, source_target_pairs={{0,24},{8,16},{16,8},{24,0},{1,25},{9,17},{17,9},{25,1},{2,26},{10... | collective-permute-start | bytes 540680 | tf_op jit(solution)/shard_map/ppermute | solution.py:253
  13.7 7.4 %collective-permute-start.4 = (bf16[704,128]{1,0:T(8,128)(2,1)S(1)}, bf16[704,128]{1,0:T(8,128)(2,1)S(1)}, u32[]{:S(2)}, u32[]{:S(2)}) collective-permute-start(bf16[704,128]{1,0:T(8,128)(2,1)S(1)} %join.1.refs_0_.refs_1_.packed), channel_id=1, source_target_pairs={{0,8},{8,0},{16,24},{24,16},{1,9},{9,1},{17,25},{25,17},{2,10},{10... | collective-permute-start | bytes 540680 | tf_op jit(solution)/shard_map/ppermute | solution.py:253
  14.2 6.8 %collective-permute-start.5 = (bf16[704,128]{1,0:T(8,128)(2,1)S(1)}, bf16[704,128]{1,0:T(8,128)(2,1)S(1)}, u32[]{:S(2)}, u32[]{:S(2)}) collective-permute-start(bf16[704,128]{1,0:T(8,128)(2,1)S(1)} %join.1.refs_0_.refs_1_.packed), channel_id=1, source_target_pairs={{0,16},{8,24},{16,0},{24,8},{1,17},{9,25},{17,1},{25,9},{2,18},{10... | collective-permute-start | bytes 540680 | tf_op jit(solution)/shard_map/ppermute | solution.py:253
  21.1 2.5 %collective-permute-start.7 = (bf16[2048,128]{1,0:T(8,128)(2,1)S(1)}, bf16[2048,128]{1,0:T(8,128)(2,1)S(1)}, u32[]{:S(2)}, u32[]{:S(2)}) collective-permute-start(bf16[2048,128]{1,0:T(8,128)(2,1)S(1)} %collect.1.ours), channel_id=1, source_target_pairs={{0,1},{1,0},{2,3},{3,2},{4,5},{5,4},{6,7},{7,6},{8,9},{9,8},{10,11... | collective-permute-start | bytes 1572872 | tf_op jit(solution)/shard_map/ppermute | solution.py:402
  24.5 1.5 %collective-permute-start.8 = (f32[64,256]{1,0:T(8,128)S(1)}, f32[64,256]{1,0:T(8,128)S(1)}, u32[]{:S(2)}, u32[]{:S(2)}) collective-permute-start(f32[64,256]{1,0:T(8,128)S(1)} %get-tuple-element.30), channel_id=1, source_target_pairs={{0,1},{1,0},{2,3},{3,2},{4,5},{5,4},{6,7},{7,6},{8,9},{9,8},{10,11... | collective-permute-start | bytes 196616 | tf_op jit(solution)/shard_map/ppermute | solution.py:418

commit v26 on v23

--- a/solution.py
+++ b/solution.py
@@ -110,11 +110,21 @@
         out_ref[:rows, :] = sorted_[g].astype(jnp.bfloat16)
     table.wait()
     table_f[...] = table_b[...].astype(jnp.float32)
-    for part in range(2):
-        matrix = table_f[pl.ds(part, SU, stride=2), :]
-        matrix = jnp.where(lax.axis_index("chan") == 0, matrix, matrix.T).astype(jnp.bfloat16)
-        half[part * SU : (part + 1) * SU, :] = matrix
-        outs[1][rows + part * SU : rows + (part + 1) * SU, :] = matrix
+
+    def put(turned):
+        for part in range(2):
+            matrix = table_f[pl.ds(part, SU, stride=2), :]
+            matrix = (matrix.T if turned else matrix).astype(jnp.bfloat16)
+            half[part * SU : (part + 1) * SU, :] = matrix
+            outs[1][rows + part * SU : rows + (part + 1) * SU, :] = matrix
+
+    @pl.when(lax.axis_index("chan") == 0)
+    def _():
+        put(False)
+
+    @pl.when(lax.axis_index("chan") != 0)
+    def _():
+        put(True)
 
 
 def join_kernel(rows, half, *refs):
@@ -234,9 +244,9 @@
 
         lax.fori_loop(0, number, step, 0)
 
-    whole = lax.div(count, UNROLL)
+    whole = lax.div(count + UNROLL - REST - 1, UNROLL)
     steps(0, UNROLL, whole)
-    steps(whole * UNROLL, REST, lax.div(lax.rem(count, UNROLL) + REST - 1, REST))
+    steps(whole * UNROLL, REST, jnp.where(count > whole * UNROLL, 1, 0))
 
 
 def local(kernel, operands, shape, name):
@@ -290,12 +300,10 @@
             ],
             axis=0,
         )
-        high, low = split_bf16(half)
-        result = (
-            result
-            + jnp.dot(high, u_side, preferred_element_type=jnp.float32)
-            + jnp.dot(low, u_side, preferred_element_type=jnp.float32)
-        )
+        both = jnp.dot(
+            jnp.concatenate(split_bf16(half), axis=0), u_side, preferred_element_type=jnp.float32
+        )
+        result = result + both[:SU] + both[SU:]
     result = jnp.concatenate([result[:, :SU].T, result[:, SU:].T], axis=1)
     tail = meta_row // 16 * 16
     wide = packed[tail : tail + 16, :].astype(jnp.float32)

time: 27 us -> 26.8 us (level); the launches traced: 27.1 us -> 26.4 us
  Pallas kernels: 8.2 us -> 7.37 us
    pallas_call x3, Pallas kernels: 5.99 us -> 5.24 us  [grid(): pl.pallas_call(functools.partial(grid_kernel, (facets, groups, chans, cap...]
  transfers between devices with their start and end apart: 8 -> 8, of which waited for: 5 -> 5; matrix products, arithmetic and copies ran while one was open for 0% -> 0% of each run, Pallas kernels for 22% -> 20%
where the time goes in v26:
time: 26.8 us; the launch traced here: 26.4 us
  starting transfers between devices  10.3 us (38%)
  waiting for transfers between devices  7.97 us (30%)
  Pallas kernels  7.37 us (28%)
  local copies, waits for them, and re-layouts  0.66 us (2%)
    ppermute x3, starting transfers between devices, body(): lax.ppermute(pieces[shift], 'bl', [(g, (g + shift) % groups) for g in ran...  6.11 us
    pallas_call x3, Pallas kernels, grid(): pl.pallas_call(functools.partial(grid_kernel, (facets, groups, chans, cap...  5.24 us
    ppermute x3, waiting for transfers between devices, body(): lax.ppermute(pieces[shift], 'bl', [(g, (g + shift) % groups) for g in ran...  3.65 us
    ppermute x3, starting transfers between devices, exchange(): lax.ppermute(value, axis, [(n, n ^ shift) for n in range(lax.axis_size(ax...  3.55 us
    ppermute x3, waiting for transfers between devices, exchange(): lax.ppermute(value, axis, [(n, n ^ shift) for n in range(lax.axis_size(ax...  3.42 us
    pallas_call x1, Pallas kernels, body(): pl.pallas_call(functools.partial(sort_kernel, (groups, held, chans, cap,...  1.08 us
    pallas_call x1, Pallas kernels, body(): pl.pallas_call(functools.partial(table_kernel, (slots, meta_row), norm),...  1 us
    ppermute x1, waiting for transfers between devices, body(): lax.ppermute(other, 'chan', [(c, 1 - c) for c in range(chan_count)])  0.9 us
  transfers between devices with their start and end apart: 8, of which 5 were waited for; matrix products, arithmetic and copies ran while one was open for 0% of the time, Pallas kernels for 20%

profile of v26, /device:TPU:0, one launch (start us, length us, event | category | flops | bytes accessed | tf_op | source)
XLA Modules:
  0.0 26.4 jit_solution(6431865421922958008)
XLA Ops:
  0.0 1.1 %sort_blocks.1 = (bf16[48,128]{1,0:T(8,128)(2,1)S(1)}, bf16[304,128]{1,0:T(8,128)(2,1)S(1)}, bf16[48,128]{1,0:T(8,128)(2,1)S(1)}, bf16[48,128]{1,0:T(8,128)(2,1)S(1)}, bf16[256,128]{1,0:T(8,128)(2,1)S(1)}) custom-call(s32[1,8]{1,0:T(1,128)} %bitcast.12, s32[1,8]{1,0:T(1,128)} %bitcast.13, bf16[64,128]{1,0:T(8,128)(2,1)} %bitcast.8, bf16[16,128]{1,0:T(8,128)(2,1)} %bitcast.9, ...), custom_call_target="tpu_custom_call" | custom-call | flops 100000 | bytes 100000 | tf_op jit(solution)/shard_map/sort_blocks/pallas_call | solution.py:336
  1.1 3.1 %collective-permute-start = (bf16[304,128]{1,0:T(8,128)(2,1)S(1)}, bf16[304,128]{1,0:T(8,128)(2,1)S(1)}, u32[]{:S(2)}, u32[]{:S(2)}) collective-permute-start(bf16[304,128]{1,0:T(8,128)(2,1)S(1)} %get-tuple-element.20), channel_id=1, source_target_pairs={{0,2},{2,4},{4,6},{6,0},{1,3},{3,5},{5,7},{7,1},{8,10},{10,12},{12... | collective-permute-start | bytes 233480 | tf_op jit(solution)/shard_map/ppermute | solution.py:380
  4.2 2.1 %collective-permute-start.1 = (bf16[48,128]{1,0:T(8,128)(2,1)S(1)}, bf16[48,128]{1,0:T(8,128)(2,1)S(1)}, u32[]{:S(2)}, u32[]{:S(2)}) collective-permute-start(bf16[48,128]{1,0:T(8,128)(2,1)S(1)} %get-tuple-element.21), channel_id=1, source_target_pairs={{0,6},{2,0},{4,2},{6,4},{1,7},{3,1},{5,3},{7,5},{8,14},{10,8},{12,... | collective-permute-start | bytes 36872 | tf_op jit(solution)/shard_map/ppermute | solution.py:380
  6.3 0.9 %collective-permute-start.2 = (bf16[48,128]{1,0:T(8,128)(2,1)S(1)}, bf16[48,128]{1,0:T(8,128)(2,1)S(1)}, u32[]{:S(2)}, u32[]{:S(2)}) collective-permute-start(bf16[48,128]{1,0:T(8,128)(2,1)S(1)} %get-tuple-element.22), channel_id=1, source_target_pairs={{0,4},{2,6},{4,0},{6,2},{1,5},{3,7},{5,1},{7,3},{8,12},{10,14},{12... | collective-permute-start | bytes 36872 | tf_op jit(solution)/shard_map/ppermute | solution.py:380
  7.2 1.5 %collective-permute-done.1.refs_2_ = bf16[48,128]{1,0:T(8,128)(2,1)S(1)} collective-permute-done((bf16[48,128]{1,0:T(8,128)(2,1)S(1)}, bf16[48,128]{1,0:T(8,128)(2,1)S(1)}, u32[]{:S(2)}, u32[]{:S(2)}) %collective-permute-start.1) | collective-permute-done | bytes 12320 | tf_op jit(solution)/shard_map/ppermute | solution.py:380
  8.7 2.1 %collective-permute-done.2.refs_3_ = bf16[48,128]{1,0:T(8,128)(2,1)S(1)} collective-permute-done((bf16[48,128]{1,0:T(8,128)(2,1)S(1)}, bf16[48,128]{1,0:T(8,128)(2,1)S(1)}, u32[]{:S(2)}, u32[]{:S(2)}) %collective-permute-start.2) | collective-permute-done | bytes 12320 | tf_op jit(solution)/shard_map/ppermute | solution.py:380
  10.8 0.0 collective-permute-done.refs_1_
  10.9 2.7 %collective-permute-start.5 = (bf16[704,128]{1,0:T(8,128)(2,1)S(1)}, bf16[704,128]{1,0:T(8,128)(2,1)S(1)}, u32[]{:S(2)}, u32[]{:S(2)}) collective-permute-start(bf16[704,128]{1,0:T(8,128)(2,1)S(1)} %join.1.refs_0_.refs_1_.packed), channel_id=1, source_target_pairs={{0,24},{8,16},{16,8},{24,0},{1,25},{9,17},{17,9},{25,1},{2,26},{10... | collective-permute-start | bytes 540680 | tf_op jit(solution)/shard_map/ppermute | solution.py:265
  13.5 0.5 %collective-permute-start.3 = (bf16[704,128]{1,0:T(8,128)(2,1)S(1)}, bf16[704,128]{1,0:T(8,128)(2,1)S(1)}, u32[]{:S(2)}, u32[]{:S(2)}) collective-permute-start(bf16[704,128]{1,0:T(8,128)(2,1)S(1)} %join.1.refs_0_.refs_1_.packed), channel_id=1, source_target_pairs={{0,8},{8,0},{16,24},{24,16},{1,9},{9,1},{17,25},{25,17},{2,10},{10... | collective-permute-start | bytes 540680 | tf_op jit(solution)/shard_map/ppermute | solution.py:265
  14.1 0.3 %collective-permute-start.4 = (bf16[704,128]{1,0:T(8,128)(2,1)S(1)}, bf16[704,128]{1,0:T(8,128)(2,1)S(1)}, u32[]{:S(2)}, u32[]{:S(2)}) collective-permute-start(bf16[704,128]{1,0:T(8,128)(2,1)S(1)} %join.1.refs_0_.refs_1_.packed), channel_id=1, source_target_pairs={{0,16},{8,24},{16,0},{24,8},{1,17},{9,25},{17,1},{25,9},{2,18},{10... | collective-permute-start | bytes 540680 | tf_op jit(solution)/shard_map/ppermute | solution.py:265
  14.4 1.3 %grid.3.refs_0_ = f32[8,128,256]{2,1,0:T(8,128)S(1)} custom-call(bf16[704,128]{1,0:T(8,128)(2,1)S(1)} %join.1.refs_0_.refs_1_.packed, bf16[704,128]{1,0:T(8,128)(2,1)S(1)} %join.1.refs_0_.refs_1_.packed), custom_call_target="tpu_custom_call" | custom-call | flops 1000000000 | bytes 1000000 | tf_op jit(solution)/shard_map/grid/pallas_call | solution.py:393
  15.7 3.1 %collective-permute-done.5.refs_1_.refs_3_ = bf16[704,128]{1,0:T(8,128)(2,1)S(1)} collective-permute-done((bf16[704,128]{1,0:T(8,128)(2,1)S(1)}, bf16[704,128]{1,0:T(8,128)(2,1)S(1)}, u32[]{:S(2)}, u32[]{:S(2)}) %collective-permute-start.5) | collective-permute-done | bytes 180256 | tf_op jit(solution)/shard_map/ppermute | solution.py:265
  18.8 1.6 %grid.4.refs_1_ = f32[8,128,256]{2,1,0:T(8,128)S(1)} custom-call(bf16[704,128]{1,0:T(8,128)(2,1)S(1)} %join.1.refs_0_.refs_1_.packed, bf16[704,128]{1,0:T(8,128)(2,1)S(1)} %collective-permute-done.5.refs_1_.refs_3_), custom_call_target="tpu_custom_call" | custom-call | flops 1000000000 | bytes 1000000 | tf_op jit(solution)/shard_map/grid/pallas_call | solution.py:393
  20.4 0.3 %collective-permute-done.3.refs_1_ = bf16[704,128]{1,0:T(8,128)(2,1)S(1)} collective-permute-done((bf16[704,128]{1,0:T(8,128)(2,1)S(1)}, bf16[704,128]{1,0:T(8,128)(2,1)S(1)}, u32[]{:S(2)}, u32[]{:S(2)}) %collective-permute-start.3) | collective-permute-done | bytes 180256 | tf_op jit(solution)/shard_map/ppermute | solution.py:265
  20.7 0.0 collective-permute-done.4.refs_2_
  20.8 0.1 collective-permute-start.6
  20.8 2.4 %grid.5.refs_2_ = f32[8,128,256]{2,1,0:T(8,128)S(1)} custom-call(bf16[704,128]{1,0:T(8,128)(2,1)S(1)} %join.1.refs_0_.refs_1_.packed, bf16[704,128]{1,0:T(8,128)(2,1)S(1)} %collective-permute-done.3.refs_1_, bf16[704,128]{1,0:T(8,128)(2,1)S(1)} %collective-permute-done.4.refs_2_), custom_call_target="tpu_custom_call" | custom-call | flops 2000000000 | bytes 1000000 | tf_op jit(solution)/shard_map/grid/pallas_call | solution.py:393
  23.2 0.0 collective-permute-done.6.theirs
  23.2 1.0 %apply_tables.1 = (f32[64,256]{1,0:T(8,128)S(1)}, f32[64,256]{1,0:T(8,128)S(1)}) custom-call(bf16[704,128]{1,0:T(8,128)(2,1)S(1)} %join.1.refs_0_.refs_1_.packed, bf16[2048,128]{1,0:T(8,128)(2,1)S(1)} %collect.1.ours, bf16[2048,128]{1,0:T(8,128)(2,1)S(1)} %collective-permute-done.6.theirs, f32[8,128,256]{2,1,0:T(8,128)S(1)} %grid.3.refs_0_, ...), custom_call_target="tpu_custom_call" | custom-call | flops 1000000000 | bytes 2000000 | tf_op jit(solution)/shard_map/apply_tables/pallas_call | solution.py:419
  24.2 0.6 %collective-permute-start.7 = (f32[64,256]{1,0:T(8,128)S(1)}, f32[64,256]{1,0:T(8,128)S(1)}, u32[]{:S(2)}, u32[]{:S(2)}) collective-permute-start(f32[64,256]{1,0:T(8,128)S(1)} %get-tuple-element.30), channel_id=1, source_target_pairs={{0,1},{1,0},{2,3},{3,2},{4,5},{5,4},{6,7},{7,6},{8,9},{9,8},{10,11... | collective-permute-start | bytes 196616 | tf_op jit(solution)/shard_map/ppermute | solution.py:433
  24.8 0.9 %collective-permute-done.7 = f32[64,256]{1,0:T(8,128)S(1)} collective-permute-done((f32[64,256]{1,0:T(8,128)S(1)}, f32[64,256]{1,0:T(8,128)S(1)}, u32[]{:S(2)}, u32[]{:S(2)}) %collective-permute-start.7) | collective-permute-done | bytes 65568 | tf_op jit(solution)/shard_map/ppermute | solution.py:433
  25.7 0.7 %reshape.19 = f32[1,1,64,2,128]{4,3,2,1,0:T(2,128)} reshape(f32[64,256]{1,0:T(8,128)S(1)} %add.3) | data formatting | bytes 131072 | tf_op jit(solution)/shard_map/reshape | solution.py:434
  (3 shorter events, 0.1 us)
Async XLA Ops:
  1.1 9.8 %collective-permute-start = (bf16[304,128]{1,0:T(8,128)(2,1)S(1)}, bf16[304,128]{1,0:T(8,128)(2,1)S(1)}, u32[]{:S(2)}, u32[]{:S(2)}) collective-permute-start(bf16[304,128]{1,0:T(8,128)(2,1)S(1)} %get-tuple-element.20), channel_id=1, source_target_pairs={{0,2},{2,4},{4,6},{6,0},{1,3},{3,5},{5,7},{7,1},{8,10},{10,12},{12... | collective-permute-start | bytes 233480 | tf_op jit(solution)/shard_map/ppermute | solution.py:380
  4.2 4.5 %collective-permute-start.1 = (bf16[48,128]{1,0:T(8,128)(2,1)S(1)}, bf16[48,128]{1,0:T(8,128)(2,1)S(1)}, u32[]{:S(2)}, u32[]{:S(2)}) collective-permute-start(bf16[48,128]{1,0:T(8,128)(2,1)S(1)} %get-tuple-element.21), channel_id=1, source_target_pairs={{0,6},{2,0},{4,2},{6,4},{1,7},{3,1},{5,3},{7,5},{8,14},{10,8},{12,... | collective-permute-start | bytes 36872 | tf_op jit(solution)/shard_map/ppermute | solution.py:380
  6.3 4.6 %collective-permute-start.2 = (bf16[48,128]{1,0:T(8,128)(2,1)S(1)}, bf16[48,128]{1,0:T(8,128)(2,1)S(1)}, u32[]{:S(2)}, u32[]{:S(2)}) collective-permute-start(bf16[48,128]{1,0:T(8,128)(2,1)S(1)} %get-tuple-element.22), channel_id=1, source_target_pairs={{0,4},{2,6},{4,0},{6,2},{1,5},{3,7},{5,1},{7,3},{8,12},{10,14},{12... | collective-permute-start | bytes 36872 | tf_op jit(solution)/shard_map/ppermute | solution.py:380
  10.9 8.0 %collective-permute-start.5 = (bf16[704,128]{1,0:T(8,128)(2,1)S(1)}, bf16[704,128]{1,0:T(8,128)(2,1)S(1)}, u32[]{:S(2)}, u32[]{:S(2)}) collective-permute-start(bf16[704,128]{1,0:T(8,128)(2,1)S(1)} %join.1.refs_0_.refs_1_.packed), channel_id=1, source_target_pairs={{0,24},{8,16},{16,8},{24,0},{1,25},{9,17},{17,9},{25,1},{2,26},{10... | collective-permute-start | bytes 540680 | tf_op jit(solution)/shard_map/ppermute | solution.py:265
  13.5 7.2 %collective-permute-start.3 = (bf16[704,128]{1,0:T(8,128)(2,1)S(1)}, bf16[704,128]{1,0:T(8,128)(2,1)S(1)}, u32[]{:S(2)}, u32[]{:S(2)}) collective-permute-start(bf16[704,128]{1,0:T(8,128)(2,1)S(1)} %join.1.refs_0_.refs_1_.packed), channel_id=1, source_target_pairs={{0,8},{8,0},{16,24},{24,16},{1,9},{9,1},{17,25},{25,17},{2,10},{10... | collective-permute-start | bytes 540680 | tf_op jit(solution)/shard_map/ppermute | solution.py:265
  14.1 6.6 %collective-permute-start.4 = (bf16[704,128]{1,0:T(8,128)(2,1)S(1)}, bf16[704,128]{1,0:T(8,128)(2,1)S(1)}, u32[]{:S(2)}, u32[]{:S(2)}) collective-permute-start(bf16[704,128]{1,0:T(8,128)(2,1)S(1)} %join.1.refs_0_.refs_1_.packed), channel_id=1, source_target_pairs={{0,16},{8,24},{16,0},{24,8},{1,17},{9,25},{17,1},{25,9},{2,18},{10... | collective-permute-start | bytes 540680 | tf_op jit(solution)/shard_map/ppermute | solution.py:265
  20.8 2.5 %collective-permute-start.6 = (bf16[2048,128]{1,0:T(8,128)(2,1)S(1)}, bf16[2048,128]{1,0:T(8,128)(2,1)S(1)}, u32[]{:S(2)}, u32[]{:S(2)}) collective-permute-start(bf16[2048,128]{1,0:T(8,128)(2,1)S(1)} %collect.1.ours), channel_id=1, source_target_pairs={{0,1},{1,0},{2,3},{3,2},{4,5},{5,4},{6,7},{7,6},{8,9},{9,8},{10,11... | collective-permute-start | bytes 1572872 | tf_op jit(solution)/shard_map/ppermute | solution.py:417
  24.2 1.5 %collective-permute-start.7 = (f32[64,256]{1,0:T(8,128)S(1)}, f32[64,256]{1,0:T(8,128)S(1)}, u32[]{:S(2)}, u32[]{:S(2)}) collective-permute-start(f32[64,256]{1,0:T(8,128)S(1)} %get-tuple-element.30), channel_id=1, source_target_pairs={{0,1},{1,0},{2,3},{3,2},{4,5},{5,4},{6,7},{7,6},{8,9},{9,8},{10,11... | collective-permute-start | bytes 196616 | tf_op jit(solution)/shard_map/ppermute | solution.py:433

commit v27 on v23

--- a/solution.py
+++ b/solution.py
@@ -256,12 +256,15 @@
 
 
 def table_kernel(sizes, norm, packed, ours, theirs, *refs):
-    slots, meta_row = sizes
-    grids, (mine_ref, other_ref, total) = refs[:-3], refs[-3:]
-    chan = lax.axis_index("chan")
-    first = chan == 0
-
-    result = jnp.zeros((SU, 2 * SU), jnp.float32)
+    slots, meta_row, own = sizes
+    grids, out_ref = refs[:-1], refs[-1]
+    first = lax.axis_index("chan") == 0
+    half_rows = SU // 2
+
+    def side(low, high):
+        return jnp.where(first, low, high) if own else jnp.where(first, high, low)
+
+    result = jnp.zeros((SU, SU), jnp.float32)
     for s in range(slots):
         at = slice(2 * SU * s, 2 * SU * (s + 1))
         fetched = ours[at, :]
@@ -283,6 +286,7 @@
             v_side, low, preferred_element_type=jnp.float32
         )
         u_table = jnp.where(first, fetched, swapped)
+        u_table = side(u_table[:, :half_rows], u_table[:, half_rows:])
         u_side = jnp.concatenate(
             [
                 jnp.concatenate([u_table[:SU], u_table[SU:]], axis=1),
@@ -296,17 +300,15 @@
             + jnp.dot(high, u_side, preferred_element_type=jnp.float32)
             + jnp.dot(low, u_side, preferred_element_type=jnp.float32)
         )
-    result = jnp.concatenate([result[:, :SU].T, result[:, SU:].T], axis=1)
+    result = result.T
+    result = jnp.concatenate([result[:half_rows], result[half_rows:]], axis=1)
     tail = meta_row // 16 * 16
     wide = packed[tail : tail + 16, :].astype(jnp.float32)
     at = meta_row - tail + 2
     gain = (wide[at : at + 2] + wide[at + 2 : at + 4]) + wide[at + 4 : at + 6]
     gain_u = jnp.broadcast_to(gain[0:1], (SU, SU)).T
-    gains = gain_u * gain[1:2] * norm
-    total[...] = result * jnp.concatenate([gains, gains], axis=1)
-    half_rows = mine_ref.shape[0]
-    mine_ref[...] = total[pl.ds(pl.multiple_of(chan * half_rows, half_rows), half_rows), :]
-    other_ref[...] = total[pl.ds(pl.multiple_of((1 - chan) * half_rows, half_rows), half_rows), :]
+    gains = side(gain_u[:half_rows], gain_u[half_rows:]) * gain[1:2] * norm
+    out_ref[...] = result * jnp.concatenate([gains, gains], axis=1)
 
 
 def body(
@@ -408,21 +410,22 @@
     )
     swapped = lax.ppermute(fetched, "chan", [(c, 1 - c) for c in range(chan_count)])
     grids.append(grid(blocks[1:-1]))
-    mine, other = pl.pallas_call(
-        functools.partial(table_kernel, (slots, meta_row), norm),
-        out_shape=[jax.ShapeDtypeStruct((half_rows, 2 * SU), jnp.float32)] * 2,
-        in_specs=[VMEM] * (3 + len(grids)),
-        out_specs=[VMEM, VMEM],
-        scratch_shapes=[
-            pltpu.VMEM((SU, 2 * SU), jnp.float32),
-        ],
-        compiler_params=PARAMS,
-        cost_estimate=pl.CostEstimate(
-            flops=1_000_000_000, bytes_accessed=2_000_000, transcendentals=0
-        ),
-        name="apply_tables",
-    )(joined, fetched, swapped, *grids)
+    def apply(own):
+        return pl.pallas_call(
+            functools.partial(table_kernel, (slots, meta_row, own), norm),
+            out_shape=jax.ShapeDtypeStruct((half_rows, 2 * SU), jnp.float32),
+            in_specs=[VMEM] * (3 + len(grids)),
+            out_specs=VMEM,
+            compiler_params=PARAMS,
+            cost_estimate=pl.CostEstimate(
+                flops=1_000_000_000, bytes_accessed=2_000_000, transcendentals=0
+            ),
+            name="apply_tables",
+        )(joined, fetched, swapped, *grids)
+
+    other = apply(False)
     summand = lax.ppermute(other, "chan", [(c, 1 - c) for c in range(chan_count)])
+    mine = apply(True)
     return (mine + summand).reshape(1, 1, half_rows, 2, SU)
 
 

time: 27 us -> 27.2 us (level); the launches traced: 27.1 us -> 26.8 us
  waiting for transfers between devices: 7.82 us -> 6.92 us
  Pallas kernels: 8.2 us -> 8.77 us
    pallas_call x1 -> x2, Pallas kernels: 1 us -> 2.43 us  [apply(): pl.pallas_call(functools.partial(table_kernel, (slots, meta_row, own), no...]
    ppermute x1, waiting for transfers between devices: 0.9 us -> 0.01 us  [body(): lax.ppermute(other, 'chan', [(c, 1 - c) for c in range(chan_count)])]
    pallas_call x3, Pallas kernels: 5.99 us -> 5.12 us  [grid(): pl.pallas_call(functools.partial(grid_kernel, (facets, groups, chans, cap...]
  transfers between devices with their start and end apart: 8 -> 8, of which waited for: 5 -> 4; matrix products, arithmetic and copies ran while one was open for 0% -> 0% of each run, Pallas kernels for 22% -> 24%
where the time goes in v27:
time: 27.2 us; the launch traced here: 26.8 us
  starting transfers between devices  10.3 us (38%)
  Pallas kernels  8.77 us (32%)
  waiting for transfers between devices  6.92 us (25%)
  local copies, waits for them, and re-layouts  0.66 us (2%)
    ppermute x3, starting transfers between devices, body(): lax.ppermute(pieces[shift], 'bl', [(g, (g + shift) % groups) for g in ran...  6.11 us
    pallas_call x3, Pallas kernels, grid(): pl.pallas_call(functools.partial(grid_kernel, (facets, groups, chans, cap...  5.12 us
    ppermute x3, waiting for transfers between devices, body(): lax.ppermute(pieces[shift], 'bl', [(g, (g + shift) % groups) for g in ran...  3.65 us
    ppermute x3, starting transfers between devices, exchange(): lax.ppermute(value, axis, [(n, n ^ shift) for n in range(lax.axis_size(ax...  3.55 us
    ppermute x3, waiting for transfers between devices, exchange(): lax.ppermute(value, axis, [(n, n ^ shift) for n in range(lax.axis_size(ax...  3.27 us
    pallas_call x2, Pallas kernels, apply(): pl.pallas_call(functools.partial(table_kernel, (slots, meta_row, own), no...  2.43 us
    pallas_call x1, Pallas kernels, body(): pl.pallas_call(functools.partial(sort_kernel, (groups, held, chans, cap,...  1.17 us
    reshape x1, local copies, waits for them, and re-layouts, body(): return (mine + summand).reshape(1, 1, half_rows, 2, SU)  0.66 us
  transfers between devices with their start and end apart: 8, of which 4 were waited for; matrix products, arithmetic and copies ran while one was open for 0% of the time, Pallas kernels for 24%

profile of v27, /device:TPU:0, one launch (start us, length us, event | category | flops | bytes accessed | tf_op | source)
XLA Modules:
  0.0 26.8 jit_solution(6624064915501792508)
XLA Ops:
  0.0 1.2 %sort_blocks.1 = (bf16[48,128]{1,0:T(8,128)(2,1)S(1)}, bf16[304,128]{1,0:T(8,128)(2,1)S(1)}, bf16[48,128]{1,0:T(8,128)(2,1)S(1)}, bf16[48,128]{1,0:T(8,128)(2,1)S(1)}, bf16[256,128]{1,0:T(8,128)(2,1)S(1)}) custom-call(s32[1,8]{1,0:T(1,128)} %bitcast.12, s32[1,8]{1,0:T(1,128)} %bitcast.13, bf16[64,128]{1,0:T(8,128)(2,1)} %bitcast.8, bf16[16,128]{1,0:T(8,128)(2,1)} %bitcast.9, ...), custom_call_target="tpu_custom_call" | custom-call | flops 100000 | bytes 100000 | tf_op jit(solution)/shard_map/sort_blocks/pallas_call | solution.py:330
  1.2 3.1 %collective-permute-start = (bf16[304,128]{1,0:T(8,128)(2,1)S(1)}, bf16[304,128]{1,0:T(8,128)(2,1)S(1)}, u32[]{:S(2)}, u32[]{:S(2)}) collective-permute-start(bf16[304,128]{1,0:T(8,128)(2,1)S(1)} %get-tuple-element.18), channel_id=1, source_target_pairs={{0,2},{2,4},{4,6},{6,0},{1,3},{3,5},{5,7},{7,1},{8,10},{10,12},{12... | collective-permute-start | bytes 233480 | tf_op jit(solution)/shard_map/ppermute | solution.py:374
  4.2 2.1 %collective-permute-start.1 = (bf16[48,128]{1,0:T(8,128)(2,1)S(1)}, bf16[48,128]{1,0:T(8,128)(2,1)S(1)}, u32[]{:S(2)}, u32[]{:S(2)}) collective-permute-start(bf16[48,128]{1,0:T(8,128)(2,1)S(1)} %get-tuple-element.19), channel_id=1, source_target_pairs={{0,6},{2,0},{4,2},{6,4},{1,7},{3,1},{5,3},{7,5},{8,14},{10,8},{12,... | collective-permute-start | bytes 36872 | tf_op jit(solution)/shard_map/ppermute | solution.py:374
  6.3 1.0 %collective-permute-start.2 = (bf16[48,128]{1,0:T(8,128)(2,1)S(1)}, bf16[48,128]{1,0:T(8,128)(2,1)S(1)}, u32[]{:S(2)}, u32[]{:S(2)}) collective-permute-start(bf16[48,128]{1,0:T(8,128)(2,1)S(1)} %get-tuple-element.20), channel_id=1, source_target_pairs={{0,4},{2,6},{4,0},{6,2},{1,5},{3,7},{5,1},{7,3},{8,12},{10,14},{12... | collective-permute-start | bytes 36872 | tf_op jit(solution)/shard_map/ppermute | solution.py:374
  7.3 1.4 %collective-permute-done.1.refs_2_ = bf16[48,128]{1,0:T(8,128)(2,1)S(1)} collective-permute-done((bf16[48,128]{1,0:T(8,128)(2,1)S(1)}, bf16[48,128]{1,0:T(8,128)(2,1)S(1)}, u32[]{:S(2)}, u32[]{:S(2)}) %collective-permute-start.1) | collective-permute-done | bytes 12320 | tf_op jit(solution)/shard_map/ppermute | solution.py:374
  8.7 2.3 %collective-permute-done.2.refs_3_ = bf16[48,128]{1,0:T(8,128)(2,1)S(1)} collective-permute-done((bf16[48,128]{1,0:T(8,128)(2,1)S(1)}, bf16[48,128]{1,0:T(8,128)(2,1)S(1)}, u32[]{:S(2)}, u32[]{:S(2)}) %collective-permute-start.2) | collective-permute-done | bytes 12320 | tf_op jit(solution)/shard_map/ppermute | solution.py:374
  10.9 0.0 collective-permute-done.refs_1_
  11.0 2.7 %collective-permute-start.5 = (bf16[704,128]{1,0:T(8,128)(2,1)S(1)}, bf16[704,128]{1,0:T(8,128)(2,1)S(1)}, u32[]{:S(2)}, u32[]{:S(2)}) collective-permute-start(bf16[704,128]{1,0:T(8,128)(2,1)S(1)} %join.1.refs_0_.refs_1_.packed), channel_id=1, source_target_pairs={{0,24},{8,16},{16,8},{24,0},{1,25},{9,17},{17,9},{25,1},{2,26},{10... | collective-permute-start | bytes 540680 | tf_op jit(solution)/shard_map/ppermute | solution.py:255
  13.6 0.5 %collective-permute-start.3 = (bf16[704,128]{1,0:T(8,128)(2,1)S(1)}, bf16[704,128]{1,0:T(8,128)(2,1)S(1)}, u32[]{:S(2)}, u32[]{:S(2)}) collective-permute-start(bf16[704,128]{1,0:T(8,128)(2,1)S(1)} %join.1.refs_0_.refs_1_.packed), channel_id=1, source_target_pairs={{0,8},{8,0},{16,24},{24,16},{1,9},{9,1},{17,25},{25,17},{2,10},{10... | collective-permute-start | bytes 540680 | tf_op jit(solution)/shard_map/ppermute | solution.py:255
  14.2 0.3 %collective-permute-start.4 = (bf16[704,128]{1,0:T(8,128)(2,1)S(1)}, bf16[704,128]{1,0:T(8,128)(2,1)S(1)}, u32[]{:S(2)}, u32[]{:S(2)}) collective-permute-start(bf16[704,128]{1,0:T(8,128)(2,1)S(1)} %join.1.refs_0_.refs_1_.packed), channel_id=1, source_target_pairs={{0,16},{8,24},{16,0},{24,8},{1,17},{9,25},{17,1},{25,9},{2,18},{10... | collective-permute-start | bytes 540680 | tf_op jit(solution)/shard_map/ppermute | solution.py:255
  14.5 1.6 %grid.3.refs_0_ = f32[8,128,256]{2,1,0:T(8,128)S(1)} custom-call(bf16[704,128]{1,0:T(8,128)(2,1)S(1)} %join.1.refs_0_.refs_1_.packed, bf16[704,128]{1,0:T(8,128)(2,1)S(1)} %join.1.refs_0_.refs_1_.packed), custom_call_target="tpu_custom_call" | custom-call | flops 1000000000 | bytes 1000000 | tf_op jit(solution)/shard_map/grid/pallas_call | solution.py:387
  16.1 2.7 %collective-permute-done.5.refs_1_.refs_3_ = bf16[704,128]{1,0:T(8,128)(2,1)S(1)} collective-permute-done((bf16[704,128]{1,0:T(8,128)(2,1)S(1)}, bf16[704,128]{1,0:T(8,128)(2,1)S(1)}, u32[]{:S(2)}, u32[]{:S(2)}) %collective-permute-start.5) | collective-permute-done | bytes 180256 | tf_op jit(solution)/shard_map/ppermute | solution.py:255
  18.8 1.3 %grid.4.refs_1_ = f32[8,128,256]{2,1,0:T(8,128)S(1)} custom-call(bf16[704,128]{1,0:T(8,128)(2,1)S(1)} %join.1.refs_0_.refs_1_.packed, bf16[704,128]{1,0:T(8,128)(2,1)S(1)} %collective-permute-done.5.refs_1_.refs_3_), custom_call_target="tpu_custom_call" | custom-call | flops 1000000000 | bytes 1000000 | tf_op jit(solution)/shard_map/grid/pallas_call | solution.py:387
  20.1 0.6 %collective-permute-done.3.refs_1_ = bf16[704,128]{1,0:T(8,128)(2,1)S(1)} collective-permute-done((bf16[704,128]{1,0:T(8,128)(2,1)S(1)}, bf16[704,128]{1,0:T(8,128)(2,1)S(1)}, u32[]{:S(2)}, u32[]{:S(2)}) %collective-permute-start.3) | collective-permute-done | bytes 180256 | tf_op jit(solution)/shard_map/ppermute | solution.py:255
  20.7 0.0 collective-permute-done.4.refs_2_
  20.8 0.1 collective-permute-start.6
  20.8 2.2 %grid.5.refs_2_ = f32[8,128,256]{2,1,0:T(8,128)S(1)} custom-call(bf16[704,128]{1,0:T(8,128)(2,1)S(1)} %join.1.refs_0_.refs_1_.packed, bf16[704,128]{1,0:T(8,128)(2,1)S(1)} %collective-permute-done.3.refs_1_, bf16[704,128]{1,0:T(8,128)(2,1)S(1)} %collective-permute-done.4.refs_2_), custom_call_target="tpu_custom_call" | custom-call | flops 2000000000 | bytes 1000000 | tf_op jit(solution)/shard_map/grid/pallas_call | solution.py:387
  23.0 0.0 collective-permute-done.6.theirs
  23.1 1.2 %apply_tables.3 = f32[64,256]{1,0:T(8,128)S(1)} custom-call(bf16[704,128]{1,0:T(8,128)(2,1)S(1)} %join.1.refs_0_.refs_1_.packed, bf16[2048,128]{1,0:T(8,128)(2,1)S(1)} %collect.1.ours, bf16[2048,128]{1,0:T(8,128)(2,1)S(1)} %collective-permute-done.6.theirs, f32[8,128,256]{2,1,0:T(8,128)S(1)} %grid.3.refs_0_, f32[8,128,256]{2,1,0:T(8,128)S(1)} %grid.4.refs_1_, ...), custom_call_target="tpu_custom_call" | custom-call | flops 1000000000 | bytes 2000000 | tf_op jit(solution)/shard_map/apply_tables/pallas_call | solution.py:414
  24.3 0.6 %collective-permute-start.7 = (f32[64,256]{1,0:T(8,128)S(1)}, f32[64,256]{1,0:T(8,128)S(1)}, u32[]{:S(2)}, u32[]{:S(2)}) collective-permute-start(f32[64,256]{1,0:T(8,128)S(1)} %apply_tables.3), channel_id=1, source_target_pairs={{0,1},{1,0},{2,3},{3,2},{4,5},{5,4},{6,7},{7,6},{8,9},{9,8},{10,11... | collective-permute-start | bytes 196616 | tf_op jit(solution)/shard_map/ppermute | solution.py:427
  24.8 1.2 %apply_tables.2 = f32[64,256]{1,0:T(8,128)S(1)} custom-call(bf16[704,128]{1,0:T(8,128)(2,1)S(1)} %join.1.refs_0_.refs_1_.packed, bf16[2048,128]{1,0:T(8,128)(2,1)S(1)} %collect.1.ours, bf16[2048,128]{1,0:T(8,128)(2,1)S(1)} %collective-permute-done.6.theirs, f32[8,128,256]{2,1,0:T(8,128)S(1)} %grid.3.refs_0_, f32[8,128,256]{2,1,0:T(8,128)S(1)} %grid.4.refs_1_, ...), custom_call_target="tpu_custom_call" | custom-call | flops 1000000000 | bytes 2000000 | tf_op jit(solution)/shard_map/apply_tables/pallas_call | solution.py:414
  26.1 0.0 collective-permute-done.7
  26.1 0.7 %reshape.19 = f32[1,1,64,2,128]{4,3,2,1,0:T(2,128)} reshape(f32[64,256]{1,0:T(8,128)S(1)} %add.3) | data formatting | bytes 131072 | tf_op jit(solution)/shard_map/reshape | solution.py:429
  (3 shorter events, 0.1 us)
Async XLA Ops:
  1.2 9.8 %collective-permute-start = (bf16[304,128]{1,0:T(8,128)(2,1)S(1)}, bf16[304,128]{1,0:T(8,128)(2,1)S(1)}, u32[]{:S(2)}, u32[]{:S(2)}) collective-permute-start(bf16[304,128]{1,0:T(8,128)(2,1)S(1)} %get-tuple-element.18), channel_id=1, source_target_pairs={{0,2},{2,4},{4,6},{6,0},{1,3},{3,5},{5,7},{7,1},{8,10},{10,12},{12... | collective-permute-start | bytes 233480 | tf_op jit(solution)/shard_map/ppermute | solution.py:374
  4.2 4.4 %collective-permute-start.1 = (bf16[48,128]{1,0:T(8,128)(2,1)S(1)}, bf16[48,128]{1,0:T(8,128)(2,1)S(1)}, u32[]{:S(2)}, u32[]{:S(2)}) collective-permute-start(bf16[48,128]{1,0:T(8,128)(2,1)S(1)} %get-tuple-element.19), channel_id=1, source_target_pairs={{0,6},{2,0},{4,2},{6,4},{1,7},{3,1},{5,3},{7,5},{8,14},{10,8},{12,... | collective-permute-start | bytes 36872 | tf_op jit(solution)/shard_map/ppermute | solution.py:374
  6.3 4.6 %collective-permute-start.2 = (bf16[48,128]{1,0:T(8,128)(2,1)S(1)}, bf16[48,128]{1,0:T(8,128)(2,1)S(1)}, u32[]{:S(2)}, u32[]{:S(2)}) collective-permute-start(bf16[48,128]{1,0:T(8,128)(2,1)S(1)} %get-tuple-element.20), channel_id=1, source_target_pairs={{0,4},{2,6},{4,0},{6,2},{1,5},{3,7},{5,1},{7,3},{8,12},{10,14},{12... | collective-permute-start | bytes 36872 | tf_op jit(solution)/shard_map/ppermute | solution.py:374
  11.0 7.9 %collective-permute-start.5 = (bf16[704,128]{1,0:T(8,128)(2,1)S(1)}, bf16[704,128]{1,0:T(8,128)(2,1)S(1)}, u32[]{:S(2)}, u32[]{:S(2)}) collective-permute-start(bf16[704,128]{1,0:T(8,128)(2,1)S(1)} %join.1.refs_0_.refs_1_.packed), channel_id=1, source_target_pairs={{0,24},{8,16},{16,8},{24,0},{1,25},{9,17},{17,9},{25,1},{2,26},{10... | collective-permute-start | bytes 540680 | tf_op jit(solution)/shard_map/ppermute | solution.py:255
  13.6 7.1 %collective-permute-start.3 = (bf16[704,128]{1,0:T(8,128)(2,1)S(1)}, bf16[704,128]{1,0:T(8,128)(2,1)S(1)}, u32[]{:S(2)}, u32[]{:S(2)}) collective-permute-start(bf16[704,128]{1,0:T(8,128)(2,1)S(1)} %join.1.refs_0_.refs_1_.packed), channel_id=1, source_target_pairs={{0,8},{8,0},{16,24},{24,16},{1,9},{9,1},{17,25},{25,17},{2,10},{10... | collective-permute-start | bytes 540680 | tf_op jit(solution)/shard_map/ppermute | solution.py:255
  14.2 6.5 %collective-permute-start.4 = (bf16[704,128]{1,0:T(8,128)(2,1)S(1)}, bf16[704,128]{1,0:T(8,128)(2,1)S(1)}, u32[]{:S(2)}, u32[]{:S(2)}) collective-permute-start(bf16[704,128]{1,0:T(8,128)(2,1)S(1)} %join.1.refs_0_.refs_1_.packed), channel_id=1, source_target_pairs={{0,16},{8,24},{16,0},{24,8},{1,17},{9,25},{17,1},{25,9},{2,18},{10... | collective-permute-start | bytes 540680 | tf_op jit(solution)/shard_map/ppermute | solution.py:255
  20.8 2.3 %collective-permute-start.6 = (bf16[2048,128]{1,0:T(8,128)(2,1)S(1)}, bf16[2048,128]{1,0:T(8,128)(2,1)S(1)}, u32[]{:S(2)}, u32[]{:S(2)}) collective-permute-start(bf16[2048,128]{1,0:T(8,128)(2,1)S(1)} %collect.1.ours), channel_id=1, source_target_pairs={{0,1},{1,0},{2,3},{3,2},{4,5},{5,4},{6,7},{7,6},{8,9},{9,8},{10,11... | collective-permute-start | bytes 1572872 | tf_op jit(solution)/shard_map/ppermute | solution.py:411
  24.3 1.8 %collective-permute-start.7 = (f32[64,256]{1,0:T(8,128)S(1)}, f32[64,256]{1,0:T(8,128)S(1)}, u32[]{:S(2)}, u32[]{:S(2)}) collective-permute-start(f32[64,256]{1,0:T(8,128)S(1)} %apply_tables.3), channel_id=1, source_target_pairs={{0,1},{1,0},{2,3},{3,2},{4,5},{5,4},{6,7},{7,6},{8,9},{9,8},{10,11... | collective-permute-start | bytes 196616 | tf_op jit(solution)/shard_map/ppermute | solution.py:427

commit v28 on v26

--- a/solution.py
+++ b/solution.py
@@ -244,9 +244,9 @@
 
         lax.fori_loop(0, number, step, 0)
 
-    whole = lax.div(count + UNROLL - REST - 1, UNROLL)
+    whole = lax.div(count, UNROLL)
     steps(0, UNROLL, whole)
-    steps(whole * UNROLL, REST, jnp.where(count > whole * UNROLL, 1, 0))
+    steps(whole * UNROLL, REST, lax.div(lax.rem(count, UNROLL) + REST - 1, REST))
 
 
 def local(kernel, operands, shape, name):
@@ -300,10 +300,12 @@
             ],
             axis=0,
         )
-        both = jnp.dot(
-            jnp.concatenate(split_bf16(half), axis=0), u_side, preferred_element_type=jnp.float32
-        )
-        result = result + both[:SU] + both[SU:]
+        high, low = split_bf16(half)
+        result = (
+            result
+            + jnp.dot(high, u_side, preferred_element_type=jnp.float32)
+            + jnp.dot(low, u_side, preferred_element_type=jnp.float32)
+        )
     result = jnp.concatenate([result[:, :SU].T, result[:, SU:].T], axis=1)
     tail = meta_row // 16 * 16
     wide = packed[tail : tail + 16, :].astype(jnp.float32)

time: 26.8 us -> 27.1 us (1.011)
  waiting for transfers between devices: 7.97 us -> 8.25 us
    ppermute x3, waiting for transfers between devices: 3.42 us -> 3.69 us  [exchange(): lax.ppermute(value, axis, [(n, n ^ shift) for n in range(lax.axis_size(ax...]
where the time goes in v28:
time: 27.1 us; the launch traced here: 26.7 us
  starting transfers between devices  10.3 us (38%)
  waiting for transfers between devices  8.25 us (30%)
  Pallas kernels  7.43 us (27%)
  local copies, waits for them, and re-layouts  0.66 us (2%)
    ppermute x3, starting transfers between devices, body(): lax.ppermute(pieces[shift], 'bl', [(g, (g + shift) % groups) for g in ran...  6.12 us
    pallas_call x3, Pallas kernels, grid(): pl.pallas_call(functools.partial(grid_kernel, (facets, groups, chans, cap...  5.3 us
    ppermute x3, waiting for transfers between devices, exchange(): lax.ppermute(value, axis, [(n, n ^ shift) for n in range(lax.axis_size(ax...  3.69 us
    ppermute x3, waiting for transfers between devices, body(): lax.ppermute(pieces[shift], 'bl', [(g, (g + shift) % groups) for g in ran...  3.65 us
    ppermute x3, starting transfers between devices, exchange(): lax.ppermute(value, axis, [(n, n ^ shift) for n in range(lax.axis_size(ax...  3.55 us
    pallas_call x1, Pallas kernels, body(): pl.pallas_call(functools.partial(sort_kernel, (groups, held, chans, cap,...  1.08 us
    pallas_call x1, Pallas kernels, body(): pl.pallas_call(functools.partial(table_kernel, (slots, meta_row), norm),...  1 us
    ppermute x1, waiting for transfers between devices, body(): lax.ppermute(other, 'chan', [(c, 1 - c) for c in range(chan_count)])  0.9 us
  transfers between devices with their start and end apart: 8, of which 5 were waited for; matrix products, arithmetic and copies ran while one was open for 0% of the time, Pallas kernels for 20%

profile of v28, /device:TPU:0, one launch (start us, length us, event | category | flops | bytes accessed | tf_op | source)
XLA Modules:
  0.0 26.7 jit_solution(15465271682854178966)
XLA Ops:
  0.0 1.1 %sort_blocks.1 = (bf16[48,128]{1,0:T(8,128)(2,1)S(1)}, bf16[304,128]{1,0:T(8,128)(2,1)S(1)}, bf16[48,128]{1,0:T(8,128)(2,1)S(1)}, bf16[48,128]{1,0:T(8,128)(2,1)S(1)}, bf16[256,128]{1,0:T(8,128)(2,1)S(1)}) custom-call(s32[1,8]{1,0:T(1,128)} %bitcast.12, s32[1,8]{1,0:T(1,128)} %bitcast.13, bf16[64,128]{1,0:T(8,128)(2,1)} %bitcast.8, bf16[16,128]{1,0:T(8,128)(2,1)} %bitcast.9, ...), custom_call_target="tpu_custom_call" | custom-call | flops 100000 | bytes 100000 | tf_op jit(solution)/shard_map/sort_blocks/pallas_call | solution.py:338
  1.1 3.1 %collective-permute-start = (bf16[304,128]{1,0:T(8,128)(2,1)S(1)}, bf16[304,128]{1,0:T(8,128)(2,1)S(1)}, u32[]{:S(2)}, u32[]{:S(2)}) collective-permute-start(bf16[304,128]{1,0:T(8,128)(2,1)S(1)} %get-tuple-element.20), channel_id=1, source_target_pairs={{0,2},{2,4},{4,6},{6,0},{1,3},{3,5},{5,7},{7,1},{8,10},{10,12},{12... | collective-permute-start | bytes 233480 | tf_op jit(solution)/shard_map/ppermute | solution.py:382
  4.2 2.1 %collective-permute-start.1 = (bf16[48,128]{1,0:T(8,128)(2,1)S(1)}, bf16[48,128]{1,0:T(8,128)(2,1)S(1)}, u32[]{:S(2)}, u32[]{:S(2)}) collective-permute-start(bf16[48,128]{1,0:T(8,128)(2,1)S(1)} %get-tuple-element.21), channel_id=1, source_target_pairs={{0,6},{2,0},{4,2},{6,4},{1,7},{3,1},{5,3},{7,5},{8,14},{10,8},{12,... | collective-permute-start | bytes 36872 | tf_op jit(solution)/shard_map/ppermute | solution.py:382
  6.3 0.9 %collective-permute-start.2 = (bf16[48,128]{1,0:T(8,128)(2,1)S(1)}, bf16[48,128]{1,0:T(8,128)(2,1)S(1)}, u32[]{:S(2)}, u32[]{:S(2)}) collective-permute-start(bf16[48,128]{1,0:T(8,128)(2,1)S(1)} %get-tuple-element.22), channel_id=1, source_target_pairs={{0,4},{2,6},{4,0},{6,2},{1,5},{3,7},{5,1},{7,3},{8,12},{10,14},{12... | collective-permute-start | bytes 36872 | tf_op jit(solution)/shard_map/ppermute | solution.py:382
  7.2 1.5 %collective-permute-done.1.refs_2_ = bf16[48,128]{1,0:T(8,128)(2,1)S(1)} collective-permute-done((bf16[48,128]{1,0:T(8,128)(2,1)S(1)}, bf16[48,128]{1,0:T(8,128)(2,1)S(1)}, u32[]{:S(2)}, u32[]{:S(2)}) %collective-permute-start.1) | collective-permute-done | bytes 12320 | tf_op jit(solution)/shard_map/ppermute | solution.py:382
  8.7 2.1 %collective-permute-done.2.refs_3_ = bf16[48,128]{1,0:T(8,128)(2,1)S(1)} collective-permute-done((bf16[48,128]{1,0:T(8,128)(2,1)S(1)}, bf16[48,128]{1,0:T(8,128)(2,1)S(1)}, u32[]{:S(2)}, u32[]{:S(2)}) %collective-permute-start.2) | collective-permute-done | bytes 12320 | tf_op jit(solution)/shard_map/ppermute | solution.py:382
  10.9 0.0 collective-permute-done.refs_1_
  10.9 2.7 %collective-permute-start.5 = (bf16[704,128]{1,0:T(8,128)(2,1)S(1)}, bf16[704,128]{1,0:T(8,128)(2,1)S(1)}, u32[]{:S(2)}, u32[]{:S(2)}) collective-permute-start(bf16[704,128]{1,0:T(8,128)(2,1)S(1)} %join.1.refs_0_.refs_1_.packed), channel_id=1, source_target_pairs={{0,24},{8,16},{16,8},{24,0},{1,25},{9,17},{17,9},{25,1},{2,26},{10... | collective-permute-start | bytes 540680 | tf_op jit(solution)/shard_map/ppermute | solution.py:265
  13.5 0.5 %collective-permute-start.3 = (bf16[704,128]{1,0:T(8,128)(2,1)S(1)}, bf16[704,128]{1,0:T(8,128)(2,1)S(1)}, u32[]{:S(2)}, u32[]{:S(2)}) collective-permute-start(bf16[704,128]{1,0:T(8,128)(2,1)S(1)} %join.1.refs_0_.refs_1_.packed), channel_id=1, source_target_pairs={{0,8},{8,0},{16,24},{24,16},{1,9},{9,1},{17,25},{25,17},{2,10},{10... | collective-permute-start | bytes 540680 | tf_op jit(solution)/shard_map/ppermute | solution.py:265
  14.1 0.4 %collective-permute-start.4 = (bf16[704,128]{1,0:T(8,128)(2,1)S(1)}, bf16[704,128]{1,0:T(8,128)(2,1)S(1)}, u32[]{:S(2)}, u32[]{:S(2)}) collective-permute-start(bf16[704,128]{1,0:T(8,128)(2,1)S(1)} %join.1.refs_0_.refs_1_.packed), channel_id=1, source_target_pairs={{0,16},{8,24},{16,0},{24,8},{1,17},{9,25},{17,1},{25,9},{2,18},{10... | collective-permute-start | bytes 540680 | tf_op jit(solution)/shard_map/ppermute | solution.py:265
  14.4 1.3 %grid.3.refs_0_ = f32[8,128,256]{2,1,0:T(8,128)S(1)} custom-call(bf16[704,128]{1,0:T(8,128)(2,1)S(1)} %join.1.refs_0_.refs_1_.packed, bf16[704,128]{1,0:T(8,128)(2,1)S(1)} %join.1.refs_0_.refs_1_.packed), custom_call_target="tpu_custom_call" | custom-call | flops 1000000000 | bytes 1000000 | tf_op jit(solution)/shard_map/grid/pallas_call | solution.py:395
  15.7 3.1 %collective-permute-done.5.refs_1_.refs_3_ = bf16[704,128]{1,0:T(8,128)(2,1)S(1)} collective-permute-done((bf16[704,128]{1,0:T(8,128)(2,1)S(1)}, bf16[704,128]{1,0:T(8,128)(2,1)S(1)}, u32[]{:S(2)}, u32[]{:S(2)}) %collective-permute-start.5) | collective-permute-done | bytes 180256 | tf_op jit(solution)/shard_map/ppermute | solution.py:265
  18.8 1.3 %grid.4.refs_1_ = f32[8,128,256]{2,1,0:T(8,128)S(1)} custom-call(bf16[704,128]{1,0:T(8,128)(2,1)S(1)} %join.1.refs_0_.refs_1_.packed, bf16[704,128]{1,0:T(8,128)(2,1)S(1)} %collective-permute-done.5.refs_1_.refs_3_), custom_call_target="tpu_custom_call" | custom-call | flops 1000000000 | bytes 1000000 | tf_op jit(solution)/shard_map/grid/pallas_call | solution.py:395
  20.1 0.6 %collective-permute-done.3.refs_1_ = bf16[704,128]{1,0:T(8,128)(2,1)S(1)} collective-permute-done((bf16[704,128]{1,0:T(8,128)(2,1)S(1)}, bf16[704,128]{1,0:T(8,128)(2,1)S(1)}, u32[]{:S(2)}, u32[]{:S(2)}) %collective-permute-start.3) | collective-permute-done | bytes 180256 | tf_op jit(solution)/shard_map/ppermute | solution.py:265
  20.7 0.0 collective-permute-done.4.refs_2_
  20.7 0.1 collective-permute-start.6
  20.8 2.7 %grid.5.refs_2_ = f32[8,128,256]{2,1,0:T(8,128)S(1)} custom-call(bf16[704,128]{1,0:T(8,128)(2,1)S(1)} %join.1.refs_0_.refs_1_.packed, bf16[704,128]{1,0:T(8,128)(2,1)S(1)} %collective-permute-done.3.refs_1_, bf16[704,128]{1,0:T(8,128)(2,1)S(1)} %collective-permute-done.4.refs_2_), custom_call_target="tpu_custom_call" | custom-call | flops 2000000000 | bytes 1000000 | tf_op jit(solution)/shard_map/grid/pallas_call | solution.py:395
  23.6 0.0 collective-permute-done.6.theirs
  23.6 1.0 %apply_tables.1 = (f32[64,256]{1,0:T(8,128)S(1)}, f32[64,256]{1,0:T(8,128)S(1)}) custom-call(bf16[704,128]{1,0:T(8,128)(2,1)S(1)} %join.1.refs_0_.refs_1_.packed, bf16[2048,128]{1,0:T(8,128)(2,1)S(1)} %collect.1.ours, bf16[2048,128]{1,0:T(8,128)(2,1)S(1)} %collective-permute-done.6.theirs, f32[8,128,256]{2,1,0:T(8,128)S(1)} %grid.3.refs_0_, ...), custom_call_target="tpu_custom_call" | custom-call | flops 1000000000 | bytes 2000000 | tf_op jit(solution)/shard_map/apply_tables/pallas_call | solution.py:421
  24.6 0.6 %collective-permute-start.7 = (f32[64,256]{1,0:T(8,128)S(1)}, f32[64,256]{1,0:T(8,128)S(1)}, u32[]{:S(2)}, u32[]{:S(2)}) collective-permute-start(f32[64,256]{1,0:T(8,128)S(1)} %get-tuple-element.30), channel_id=1, source_target_pairs={{0,1},{1,0},{2,3},{3,2},{4,5},{5,4},{6,7},{7,6},{8,9},{9,8},{10,11... | collective-permute-start | bytes 196616 | tf_op jit(solution)/shard_map/ppermute | solution.py:435
  25.1 0.9 %collective-permute-done.7 = f32[64,256]{1,0:T(8,128)S(1)} collective-permute-done((f32[64,256]{1,0:T(8,128)S(1)}, f32[64,256]{1,0:T(8,128)S(1)}, u32[]{:S(2)}, u32[]{:S(2)}) %collective-permute-start.7) | collective-permute-done | bytes 65568 | tf_op jit(solution)/shard_map/ppermute | solution.py:435
  26.1 0.7 %reshape.19 = f32[1,1,64,2,128]{4,3,2,1,0:T(2,128)} reshape(f32[64,256]{1,0:T(8,128)S(1)} %add.3) | data formatting | bytes 131072 | tf_op jit(solution)/shard_map/reshape | solution.py:436
  (3 shorter events, 0.1 us)
Async XLA Ops:
  1.1 9.8 %collective-permute-start = (bf16[304,128]{1,0:T(8,128)(2,1)S(1)}, bf16[304,128]{1,0:T(8,128)(2,1)S(1)}, u32[]{:S(2)}, u32[]{:S(2)}) collective-permute-start(bf16[304,128]{1,0:T(8,128)(2,1)S(1)} %get-tuple-element.20), channel_id=1, source_target_pairs={{0,2},{2,4},{4,6},{6,0},{1,3},{3,5},{5,7},{7,1},{8,10},{10,12},{12... | collective-permute-start | bytes 233480 | tf_op jit(solution)/shard_map/ppermute | solution.py:382
  4.2 4.5 %collective-permute-start.1 = (bf16[48,128]{1,0:T(8,128)(2,1)S(1)}, bf16[48,128]{1,0:T(8,128)(2,1)S(1)}, u32[]{:S(2)}, u32[]{:S(2)}) collective-permute-start(bf16[48,128]{1,0:T(8,128)(2,1)S(1)} %get-tuple-element.21), channel_id=1, source_target_pairs={{0,6},{2,0},{4,2},{6,4},{1,7},{3,1},{5,3},{7,5},{8,14},{10,8},{12,... | collective-permute-start | bytes 36872 | tf_op jit(solution)/shard_map/ppermute | solution.py:382
  6.3 4.6 %collective-permute-start.2 = (bf16[48,128]{1,0:T(8,128)(2,1)S(1)}, bf16[48,128]{1,0:T(8,128)(2,1)S(1)}, u32[]{:S(2)}, u32[]{:S(2)}) collective-permute-start(bf16[48,128]{1,0:T(8,128)(2,1)S(1)} %get-tuple-element.22), channel_id=1, source_target_pairs={{0,4},{2,6},{4,0},{6,2},{1,5},{3,7},{5,1},{7,3},{8,12},{10,14},{12... | collective-permute-start | bytes 36872 | tf_op jit(solution)/shard_map/ppermute | solution.py:382
  10.9 8.0 %collective-permute-start.5 = (bf16[704,128]{1,0:T(8,128)(2,1)S(1)}, bf16[704,128]{1,0:T(8,128)(2,1)S(1)}, u32[]{:S(2)}, u32[]{:S(2)}) collective-permute-start(bf16[704,128]{1,0:T(8,128)(2,1)S(1)} %join.1.refs_0_.refs_1_.packed), channel_id=1, source_target_pairs={{0,24},{8,16},{16,8},{24,0},{1,25},{9,17},{17,9},{25,1},{2,26},{10... | collective-permute-start | bytes 540680 | tf_op jit(solution)/shard_map/ppermute | solution.py:265
  13.5 7.2 %collective-permute-start.3 = (bf16[704,128]{1,0:T(8,128)(2,1)S(1)}, bf16[704,128]{1,0:T(8,128)(2,1)S(1)}, u32[]{:S(2)}, u32[]{:S(2)}) collective-permute-start(bf16[704,128]{1,0:T(8,128)(2,1)S(1)} %join.1.refs_0_.refs_1_.packed), channel_id=1, source_target_pairs={{0,8},{8,0},{16,24},{24,16},{1,9},{9,1},{17,25},{25,17},{2,10},{10... | collective-permute-start | bytes 540680 | tf_op jit(solution)/shard_map/ppermute | solution.py:265
  14.1 6.6 %collective-permute-start.4 = (bf16[704,128]{1,0:T(8,128)(2,1)S(1)}, bf16[704,128]{1,0:T(8,128)(2,1)S(1)}, u32[]{:S(2)}, u32[]{:S(2)}) collective-permute-start(bf16[704,128]{1,0:T(8,128)(2,1)S(1)} %join.1.refs_0_.refs_1_.packed), channel_id=1, source_target_pairs={{0,16},{8,24},{16,0},{24,8},{1,17},{9,25},{17,1},{25,9},{2,18},{10... | collective-permute-start | bytes 540680 | tf_op jit(solution)/shard_map/ppermute | solution.py:265
  20.7 2.8 %collective-permute-start.6 = (bf16[2048,128]{1,0:T(8,128)(2,1)S(1)}, bf16[2048,128]{1,0:T(8,128)(2,1)S(1)}, u32[]{:S(2)}, u32[]{:S(2)}) collective-permute-start(bf16[2048,128]{1,0:T(8,128)(2,1)S(1)} %collect.1.ours), channel_id=1, source_target_pairs={{0,1},{1,0},{2,3},{3,2},{4,5},{5,4},{6,7},{7,6},{8,9},{9,8},{10,11... | collective-permute-start | bytes 1572872 | tf_op jit(solution)/shard_map/ppermute | solution.py:419
  24.6 1.5 %collective-permute-start.7 = (f32[64,256]{1,0:T(8,128)S(1)}, f32[64,256]{1,0:T(8,128)S(1)}, u32[]{:S(2)}, u32[]{:S(2)}) collective-permute-start(f32[64,256]{1,0:T(8,128)S(1)} %get-tuple-element.30), channel_id=1, source_target_pairs={{0,1},{1,0},{2,3},{3,2},{4,5},{5,4},{6,7},{7,6},{8,9},{9,8},{10,11... | collective-permute-start | bytes 196616 | tf_op jit(solution)/shard_map/ppermute | solution.py:435
